TPU v7x, 32 devices: a whole 2x2x4 slice. The times are simulated.
32 devices in a mesh: ctx: 2 (over core), exp: 4 (over y, x), dp: 4 (over z).
Axes of the slice: x: 2, y: 2, z: 4, core: 2. Of those that a mesh axis runs over, the one named last changes fastest.
Arguments:
- queries: bfloat16 [16, 256, 2048], P(('exp', 'dp'), 'ctx'), may hold values from -8 to 8
- keys: bfloat16 [16, 256, 256], P(('exp', 'dp'), 'ctx'), may hold values from -8 to 8
- values: bfloat16 [16, 256, 256], P(('exp', 'dp'), 'ctx'), may hold values from -6 to 6
- resid: bfloat16 [16, 256, 2048], P(('exp', 'dp'), 'ctx'), may hold values from -6 to 6
- block_order: int32 [16], replicated, may hold values from 0 to 15, each once
- norm_gain: float32 [2048], replicated, may hold values from 0.1 to 1.9
- w_gate: bfloat16 [8, 2048, 384], P('exp'), may hold values from -0.125 to 0.125
- w_down: bfloat16 [8, 384, 2048], P('exp'), may hold values from -0.3125 to 0.3125
- routes: int32 [16, 256, 1], P(('exp', 'dp'), 'ctx'), may hold values from 0 to 7; in each aligned block of 128 rows (0 to 127, 128 to 255, ..., all dimensions but the last counted through in order) at most 24 rows name the same one
- route_weight: float32 [16, 256], P(('exp', 'dp'), 'ctx'), may hold values from 0.2 to 1
- d_out: bfloat16 [16, 256, 2048], P(('exp', 'dp'), 'ctx'), may hold values from -6 to 6
Outputs:
- layer_out: bfloat16 [16, 256, 2048], P(('exp', 'dp'), 'ctx')
- d_resid: bfloat16 [16, 256, 2048], P(('exp', 'dp'), 'ctx')
- d_queries: bfloat16 [16, 256, 2048], P(('exp', 'dp'), 'ctx')
- d_keys: bfloat16 [16, 256, 256], P(('exp', 'dp'), 'ctx')
- d_values: bfloat16 [16, 256, 256], P(('exp', 'dp'), 'ctx')
- d_weight: float32 [16, 256], P(('exp', 'dp'), 'ctx')
- d_gain: float32 [2048], replicated
Inputs may be any that keep to these rules, and one draw needn't show every extreme that they name: `routes`: within the rows of one device (aligned blocks of 128 rows) no expert is named more than 24 times, and in every draw some expert is named exactly 24 times in some block.
All inputs are finite; a program needn't handle non-finite values.
Results may differ from a plain program's by a relative error of at most 0.028.
Values may be sent and summed in bfloat16 or wider, within the bound.
No kernel may reach another device: no remote copies, remote signals or barrier semaphores. Data moves between devices by JAX's collectives and lax.ppermute only.
A program may use at most 64 MiB of HBM per device.

v0:
```python
import jax
import jax.numpy as jnp
from jax import lax
from jax.sharding import PartitionSpec as P

D = 2048
HEAD_SIZE = 128
QUERY_HEADS = 16
KEY_VALUE_HEADS = 2
FFE = 384
EXP_DEV = 2


def group_scores(q_group, k_head, allowed):
    raw_scores = jnp.einsum("tgd,kd->tgk", q_group, k_head, preferred_element_type=jnp.float32)
    masked = jnp.where(allowed[:, None, :], raw_scores * HEAD_SIZE ** (-0.5), -1e30)
    peak_score = jnp.max(masked, axis=2, keepdims=True)
    exponent = jnp.exp(masked - peak_score)
    return exponent / jnp.sum(exponent, axis=2, keepdims=True)


def expert_forward(rows_x, gate_mat, down_mat):
    pre_act = jnp.dot(rows_x, gate_mat, preferred_element_type=jnp.float32)
    activity = jax.nn.silu(pre_act).astype(jnp.bfloat16)
    return (
        pre_act,
        jnp.dot(activity, down_mat, preferred_element_type=jnp.float32).astype(jnp.bfloat16),
    )


def expert_backward(pre_act, rows_grad, gate_mat, down_mat):
    d_act = lax.dot_general(
        rows_grad, down_mat, (((1,), (1,)), ((), ())), preferred_element_type=jnp.float32
    )
    sigmoid_pre = jax.nn.sigmoid(pre_act)
    d_pre = (d_act * sigmoid_pre * (1.0 + pre_act * (1.0 - sigmoid_pre))).astype(jnp.bfloat16)
    return lax.dot_general(
        d_pre, gate_mat, (((1,), (1,)), ((), ())), preferred_element_type=jnp.float32
    ).astype(jnp.bfloat16)


def per_device(
    queries,
    keys,
    values,
    resid,
    block_order,
    norm_gain,
    w_gate,
    w_down,
    routes,
    route_weight,
    d_out,
):
    query_rows = queries[0]
    resid_rows = resid[0]
    grad_rows = d_out[0]
    chosen = routes[0, :, 0]
    weight_rows = route_weight[0]
    tokens = query_rows.shape[0]
    span_rows = tokens // 8
    ctx_count = lax.axis_size("ctx")
    exp_count = lax.axis_size("exp")
    experts = EXP_DEV * exp_count
    capacity = 3 * tokens // (2 * experts)
    group_count = QUERY_HEADS // KEY_VALUE_HEADS
    group_width = group_count * HEAD_SIZE
    key_rows, value_rows = (
        lax.all_gather(keys[0], "ctx", axis=0, tiled=True),
        lax.all_gather(values[0], "ctx", axis=0, tiled=True),
    )
    length = key_rows.shape[0]
    block_ids = jnp.arange(8 * ctx_count, dtype=jnp.int32)

    def positions(row_index):
        which = row_index // span_rows
        start_block = jnp.sum(
            jnp.where(which[:, None] == block_ids[None, :], block_order[None, :], 0), axis=1
        )
        return start_block * span_rows + row_index % span_rows

    query_pos = positions(jnp.arange(tokens, dtype=jnp.int32) + lax.axis_index("ctx") * tokens)
    key_pos = positions(jnp.arange(length, dtype=jnp.int32))
    allowed = key_pos[None, :] <= query_pos[:, None]
    attn_parts = []
    saved = []
    for query_group in range(KEY_VALUE_HEADS):
        q_group = query_rows[
            :, query_group * group_width : (query_group + 1) * group_width
        ].reshape(tokens, group_count, HEAD_SIZE)
        k_head = key_rows[:, query_group * HEAD_SIZE : (query_group + 1) * HEAD_SIZE]
        v_head = value_rows[:, query_group * HEAD_SIZE : (query_group + 1) * HEAD_SIZE]
        probability = group_scores(q_group, k_head, allowed)
        prob_low = probability.astype(jnp.bfloat16)
        attn_parts.append(
            jnp.einsum("tgk,kd->tgd", prob_low, v_head, preferred_element_type=jnp.float32).reshape(
                tokens, group_width
            )
        )
        saved.append((q_group, k_head, v_head, probability, prob_low))
    attended = jnp.concatenate(attn_parts, axis=1)
    hidden = (resid_rows.astype(jnp.float32) + attended).astype(jnp.bfloat16)
    hidden_wide = hidden.astype(jnp.float32)
    inv_rms = lax.rsqrt(jnp.mean(hidden_wide * hidden_wide, axis=1, keepdims=True) + 1e-06)
    normed = (hidden_wide * inv_rms * norm_gain[None, :]).astype(jnp.bfloat16)
    grad_wide = grad_rows.astype(jnp.float32)
    scaled_grad = (weight_rows[:, None] * grad_wide).astype(jnp.bfloat16)
    hits = (chosen[:, None] == jnp.arange(experts, dtype=jnp.int32)[None, :]).astype(jnp.int32)
    slot_rank = jnp.sum(hits * (jnp.cumsum(hits, axis=0) - hits), axis=1)
    slot_of = chosen * capacity + slot_rank
    placement = (
        slot_of[None, :] == jnp.arange(experts * capacity, dtype=jnp.int32)[:, None]
    ).astype(jnp.bfloat16)

    def to_slots(token_rows):
        gathered = jnp.dot(placement, token_rows, preferred_element_type=jnp.float32)
        return gathered.astype(jnp.bfloat16).reshape(exp_count, EXP_DEV, capacity, D)

    def from_slots(slot_rows):
        flat = slot_rows.reshape(experts * capacity, D)
        return lax.dot_general(
            placement, flat, (((0,), (0,)), ((), ())), preferred_element_type=jnp.float32
        )

    send_x = to_slots(normed)
    send_grad = to_slots(scaled_grad)
    arrived_x = lax.all_to_all(send_x, "exp", split_axis=0, concat_axis=0, tiled=True)
    sources = arrived_x.shape[0]
    results = []
    kept_pre = []
    for expert_local in range(EXP_DEV):
        pre_act, result = expert_forward(
            arrived_x[:, expert_local].reshape(-1, D), w_gate[expert_local], w_down[expert_local]
        )
        results.append(result.reshape(sources, -1, D))
        kept_pre.append(pre_act.reshape(sources, -1, FFE))
    returned = lax.all_to_all(jnp.stack(results, 1), "exp", split_axis=0, concat_axis=0, tiled=True)
    pre_slots = jnp.stack(kept_pre, 1)
    arrived_grad = lax.all_to_all(send_grad, "exp", split_axis=0, concat_axis=0, tiled=True)
    backs = []
    for local in range(EXP_DEV):
        back = expert_backward(
            pre_slots[:, local].reshape(-1, FFE),
            arrived_grad[:, local].reshape(-1, D),
            w_gate[local],
            w_down[local],
        )
        backs.append(back.reshape(exp_count, capacity, D))
    dn_slots = lax.all_to_all(jnp.stack(backs, 1), "exp", split_axis=0, concat_axis=0, tiled=True)
    y_tok = from_slots(returned)
    dn_tok = from_slots(dn_slots)
    layer_out = (hidden_wide + weight_rows[:, None] * y_tok).astype(jnp.bfloat16)
    d_weight = jnp.sum(y_tok * grad_wide, axis=1)
    gained = norm_gain[None, :] * dn_tok
    mixing = jnp.mean(gained * hidden_wide, axis=1, keepdims=True)
    d_hidden = (grad_wide + inv_rms * gained - hidden_wide * inv_rms**3 * mixing).astype(
        jnp.bfloat16
    )
    gain_local = jnp.sum(dn_tok * hidden_wide * inv_rms, axis=0)
    gain_total = lax.psum(gain_local, ("ctx", "exp", "dp"))
    total_tokens = tokens * ctx_count * exp_count * lax.axis_size("dp")
    d_gain = gain_total / total_tokens
    dq_parts = []
    dk_parts = []
    dv_parts = []
    for query_group in range(KEY_VALUE_HEADS):
        q_group, k_head, v_head, probability, prob_low = saved[query_group]
        grad_group = d_hidden[
            :, query_group * group_width : (query_group + 1) * group_width
        ].reshape(tokens, group_count, HEAD_SIZE)
        attn_group = attended[
            :, query_group * group_width : (query_group + 1) * group_width
        ].reshape(tokens, group_count, HEAD_SIZE)
        row_dot = jnp.sum(grad_group.astype(jnp.float32) * attn_group, axis=2, keepdims=True)
        d_prob = jnp.einsum("tgd,kd->tgk", grad_group, v_head, preferred_element_type=jnp.float32)
        d_score = (probability * (d_prob - row_dot)).astype(jnp.bfloat16)
        dq_group = jnp.einsum(
            "tgk,kd->tgd", d_score, k_head, preferred_element_type=jnp.float32
        ) * HEAD_SIZE ** (-0.5)
        dq_parts.append(dq_group.reshape(tokens, group_width).astype(jnp.bfloat16))
        dk_parts.append(
            jnp.einsum("tgk,tgd->kd", d_score, q_group, preferred_element_type=jnp.float32)
            * HEAD_SIZE ** (-0.5)
        )
        dv_parts.append(
            jnp.einsum("tgk,tgd->kd", prob_low, grad_group, preferred_element_type=jnp.float32)
        )
    key_part = jnp.concatenate(dk_parts, axis=1)
    value_part = jnp.concatenate(dv_parts, axis=1)
    d_keys, d_values = (
        lax.psum_scatter(
            key_part.astype(jnp.bfloat16), "ctx", scatter_dimension=0, tiled=True
        ).astype(jnp.float32),
        lax.psum_scatter(
            value_part.astype(jnp.bfloat16), "ctx", scatter_dimension=0, tiled=True
        ).astype(jnp.float32),
    )
    d_queries = jnp.concatenate(dq_parts, axis=1)
    return (
        layer_out[None],
        d_hidden[None],
        d_queries[None],
        d_keys.astype(jnp.bfloat16)[None],
        d_values.astype(jnp.bfloat16)[None],
        d_weight[None],
        d_gain,
    )


def solution(mesh):
    in_specs = (
        P(("exp", "dp"), "ctx", None),
        P(("exp", "dp"), "ctx", None),
        P(("exp", "dp"), "ctx", None),
        P(("exp", "dp"), "ctx", None),
        P(),
        P(),
        P("exp", None, None),
        P("exp", None, None),
        P(("exp", "dp"), "ctx", None),
        P(("exp", "dp"), "ctx"),
        P(("exp", "dp"), "ctx", None),
    )
    out_specs = (
        P(("exp", "dp"), "ctx", None),
        P(("exp", "dp"), "ctx", None),
        P(("exp", "dp"), "ctx", None),
        P(("exp", "dp"), "ctx", None),
        P(("exp", "dp"), "ctx", None),
        P(("exp", "dp"), "ctx"),
        P(),
    )
    return jax.shard_map(
        per_device, mesh=mesh, in_specs=in_specs, out_specs=out_specs, check_vma=False
    )
```

profile of v0, /device:TPU:0, one launch (start us, length us, event | category | flops | bytes accessed | tf_op | source)
XLA Modules:
  0.0 164.5 jit_solution(1456415482717319893)
XLA Ops:
  9.7 2.0 %all-gather.1 = bf16[1,256,256]{1,2,0:T(8,128)(2,1)S(1)} all-gather(bf16[1,128,256]{1,2,0:T(8,128)(2,1)S(1)} %copy.81), channel_id=3, replica_groups=mesh['ctx'=2,'exp'=4,'dp'=4] {'ctx'}, dimensions={1}, use_global_device_ids=true | all-gather | bytes 196608 | tf_op jit(solution)/shard_map/all_gather | solution.py:70
  14.1 2.1 %all-gather = bf16[1,256,256]{2,1,0:T(8,128)(2,1)S(1)} all-gather(bf16[1,128,256]{2,1,0:T(8,128)(2,1)} %param.12), channel_id=2, replica_groups=mesh['ctx'=2,'exp'=4,'dp'=4] {'ctx'}, dimensions={1}, use_global_device_ids=true | all-gather | bytes 196608 | tf_op jit(solution)/shard_map/all_gather | solution.py:69
  16.2 1.4 copy.79
  19.9 1.5 fusion.123
  21.5 1.0 copy-done.4
  23.0 1.0 copy.83
  24.0 1.4 fusion.66
  26.0 1.3 convolution_convert_fusion.1
  27.3 5.1 %all-to-all-start = ((bf16[4,2,24,2048]{3,2,1,0:T(8,128)(2,1)}), bf16[4,2,24,2048]{3,2,1,0:T(8,128)(2,1)S(1)}, u32[]{:S(2)}, u32[]{:S(2)}) async-start(bf16[4,2,24,2048]{3,2,1,0:T(8,128)(2,1)} %bitcast.171), calls=%async_computation | async-start | bytes 1572864 | tf_op jit(solution)/shard_map/all_to_all | solution.py:127
  32.3 2.4 %convolution_convert_fusion = bf16[192,2048]{1,0:T(8,128)(2,1)} fusion(bf16[1,128,2048]{2,1,0:T(8,128)(2,1)} %param.21, f32[128]{0:T(128)} %bitcast.206, s32[128]{0:T(128)S(1)} %multiply_add_fusion), kind=kOutput, calls=%fused_computation.2 | convolution fusion | flops 101867520 | bytes 1311744 | tf_op jit(solution)/shard_map/dot_general | solution.py:116
  34.8 8.8 %all-to-all-done = bf16[4,2,24,2048]{3,2,1,0:T(8,128)(2,1)S(1)} async-done(((bf16[4,2,24,2048]{3,2,1,0:T(8,128)(2,1)}), bf16[4,2,24,2048]{3,2,1,0:T(8,128)(2,1)S(1)}, u32[]{:S(2)}, u32[]{:S(2)}) %all-to-all-start) | async-done | bytes 786464 | tf_op jit(solution)/shard_map/all_to_all | solution.py:127
  44.4 3.5 %all-to-all-start.2 = ((bf16[4,2,24,2048]{3,2,1,0:T(8,128)(2,1)}), bf16[4,2,24,2048]{3,2,1,0:T(8,128)(2,1)S(1)}, u32[]{:S(2)}, u32[]{:S(2)}) async-start(bf16[4,2,24,2048]{3,2,1,0:T(8,128)(2,1)} %bitcast.170), calls=%async_computation.2 | async-start | bytes 1572864 | tf_op jit(solution)/shard_map/all_to_all | solution.py:139
  47.9 1.3 fusion.119
  49.2 2.5 %fusion.12 = f32[96,384]{1,0:T(8,128)} fusion(bf16[96,2048]{1,0:T(8,128)(2,1)S(1)} %bitcast.197, bf16[2,2048,384]{2,1,0:T(8,128)(2,1)} %param.17), kind=kOutput, calls=%fused_computation.27 | convolution fusion | flops 150994944 | bytes 2113536 | tf_op jit(solution)/shard_map/dot_general | solution.py:23
  51.7 1.1 fusion.6
  52.8 5.4 %all-to-all-done.2 = bf16[4,2,24,2048]{3,2,1,0:T(8,128)(2,1)S(1)} async-done(((bf16[4,2,24,2048]{3,2,1,0:T(8,128)(2,1)}), bf16[4,2,24,2048]{3,2,1,0:T(8,128)(2,1)S(1)}, u32[]{:S(2)}, u32[]{:S(2)}) %all-to-all-start.2) | async-done | bytes 786464 | tf_op jit(solution)/shard_map/all_to_all | solution.py:139
  59.1 3.4 %convolution_convert_fusion.3 = bf16[96,2048]{1,0:T(8,128)(2,1)S(1)} fusion(bf16[2,2048,384]{2,1,0:T(8,128)(2,1)} %param.17, bf16[96,2048]{1,0:T(8,128)(2,1)} %bitcast.198, bf16[2,384,2048]{2,1,0:T(8,128)(2,1)} %param.18, f32[96,384]{1,0:T(8,128)} %fusion.12), kind=kOutput, calls=%fused_computation.11 | convolution fusion | flops 302518272 | bytes 4079616 | tf_op jit(solution)/shard_map/dot_general | solution.py:37
  62.6 4.1 %convolution_convert_fusion.2 = bf16[96,2048]{1,0:T(8,128)(2,1)} fusion(bf16[2,2048,384]{2,1,0:T(8,128)(2,1)} %param.17, bf16[96,2048]{1,0:T(8,128)(2,1)S(1)} %bitcast.195, bf16[2,384,2048]{2,1,0:T(8,128)(2,1)} %param.18, f32[96,384]{1,0:T(8,128)} %fusion.6), kind=kOutput, calls=%fused_computation.10 | convolution fusion | flops 302518272 | bytes 4079616 | tf_op jit(solution)/shard_map/dot_general | solution.py:37
  66.6 2.0 %pad_maximum_fusion.1 = bf16[4,2,24,2048]{3,2,1,0:T(8,128)(2,1)} fusion(bf16[4,1,24,2048]{3,2,1,0:T(8,128)(2,1)} %bitcast.200, bf16[4,1,24,2048]{3,2,1,0:T(8,128)(2,1)S(1)} %bitcast.196), kind=kLoop, calls=%fused_computation.86 | loop fusion | flops 393216 | bytes 1572864 | tf_op jit(solution)/shard_map/stack | solution.py:149
  68.6 3.5 %all-to-all-start.3 = ((bf16[4,2,24,2048]{3,2,1,0:T(8,128)(2,1)}), bf16[4,2,24,2048]{3,2,1,0:T(8,128)(2,1)S(1)}, u32[]{:S(2)}, u32[]{:S(2)}) async-start(bf16[4,2,24,2048]{3,2,1,0:T(8,128)(2,1)} %pad_maximum_fusion.1), calls=%async_computation.3 | async-start | bytes 1572864 | tf_op jit(solution)/shard_map/all_to_all | solution.py:149
  72.1 1.9 %convolution_convert_fusion.4 = bf16[96,2048]{1,0:T(8,128)(2,1)S(1)} fusion(bf16[2,384,2048]{2,1,0:T(8,128)(2,1)} %param.18, f32[96,384]{1,0:T(8,128)} %fusion.6), kind=kOutput, calls=%fused_computation.12 | convolution fusion | flops 151375872 | bytes 2113536 | tf_op jit(solution)/shard_map/dot_general | solution.py:27
  74.0 1.9 %convolution_convert_fusion.5 = bf16[96,2048]{1,0:T(8,128)(2,1)S(1)} fusion(bf16[2,384,2048]{2,1,0:T(8,128)(2,1)} %param.18, f32[96,384]{1,0:T(8,128)} %fusion.12), kind=kOutput, calls=%fused_computation.13 | convolution fusion | flops 151375872 | bytes 2113536 | tf_op jit(solution)/shard_map/dot_general | solution.py:27
  76.0 1.0 pad_maximum_fusion
  76.9 5.4 %all-to-all-done.3 = bf16[4,2,24,2048]{3,2,1,0:T(8,128)(2,1)S(1)} async-done(((bf16[4,2,24,2048]{3,2,1,0:T(8,128)(2,1)}), bf16[4,2,24,2048]{3,2,1,0:T(8,128)(2,1)S(1)}, u32[]{:S(2)}, u32[]{:S(2)}) %all-to-all-start.3) | async-done | bytes 786464 | tf_op jit(solution)/shard_map/all_to_all | solution.py:149
  83.2 3.5 %all-to-all-start.1 = ((bf16[4,2,24,2048]{3,2,1,0:T(8,128)(2,1)}), bf16[4,2,24,2048]{3,2,1,0:T(8,128)(2,1)S(1)}, u32[]{:S(2)}, u32[]{:S(2)}) async-start(bf16[4,2,24,2048]{3,2,1,0:T(8,128)(2,1)} %pad_maximum_fusion), calls=%async_computation.1 | async-start | bytes 1572864 | tf_op jit(solution)/shard_map/all_to_all | solution.py:137
  86.8 2.5 %fusion.73 = (f32[2048]{0:T(1024)S(1)}, f32[128]{0:T(128)S(1)}, f32[128,2048]{1,0:T(8,128)}) fusion(bf16[128,2048]{1,0:T(8,128)(2,1)S(1)} %get-tuple-element.38, f32[128]{0:T(128)} %copy-done.23, f32[2048]{0:T(1024)S(1)} %copy-done.16, bf16[192,2048]{1,0:T(8,128)(2,1)} %bitcast.185, s32[128]{0:T(128)} %copy-done.18), kind=kOutput, calls=%fused_computation.82 | convolution fusion | flops 102520704 | bytes 2377216 | tf_op jit(solution)/shard_map/dot_general | solution.py:121
  89.8 7.1 %all-to-all-done.1 = bf16[4,2,24,2048]{3,2,1,0:T(8,128)(2,1)S(1)} async-done(((bf16[4,2,24,2048]{3,2,1,0:T(8,128)(2,1)}), bf16[4,2,24,2048]{3,2,1,0:T(8,128)(2,1)S(1)}, u32[]{:S(2)}, u32[]{:S(2)}) %all-to-all-start.1) | async-done | bytes 786464 | tf_op jit(solution)/shard_map/all_to_all | solution.py:137
  97.0 3.3 %fusion.65 = (f32[128]{0:T(128)}, bf16[1,128,2048]{2,1,0:T(8,128)(2,1)}, bf16[128,2048]{1,0:T(8,128)(2,1)S(1)}) fusion(bf16[1,128,2048]{2,1,0:T(8,128)(2,1)} %param.21, f32[128]{0:T(128)} %bitcast.207, bf16[128,2048]{1,0:T(8,128)(2,1)S(1)} %get-tuple-element.38, f32[128]{0:T(128)} %broadcast_multiply_fusion.1, f32[128]{0:T(128)} %get-tuple-element.50, ...), kind=kOutput, calls=%fused_computation.74 | convolution fusion | flops 104357760 | bytes 3943424 | tf_op jit(solution)/shard_map/dot_general | solution.py:121
  102.3 1.7 %fusion.30 = bf16[128,8,256]{2,0,1:T(8,128)(2,1)S(1)} fusion(bf16[128,8,128]{0,2,1:T(8,128)(2,1)S(1)} %bitcast.176, f32[128,8]{0,1:T(8,128)S(1)} %multiply_reduce_fusion.1, f32[128,8,256]{2,0,1:T(8,128)} %copy-done.4, f32[128,8]{0,1:T(8,128)S(1)} %copy-done.22, bf16[256,256]{0,1:T(8,128)(2,1)S(1)} %bitcast.188), kind=kOutput, calls=%fused_computation.49 | convolution fusion | flops 68157440 | bytes 1908736 | tf_op jit(solution)/shard_map/tgd,kd->tgk/dot_general | solution.py:175
  107.5 39.6 %psum.7 = f32[2048]{0:T(1024)S(1)} all-reduce(f32[2048]{0:T(1024)S(1)} %get-tuple-element.35), channel_id=1, replica_groups=mesh['ctx'=2,'exp'=4,'dp'=4] {'ctx','exp','dp'}, use_global_device_ids=true, to_apply=%region_16.17 | all-reduce | flops 2048 | bytes 16384 | tf_op jit(solution)/shard_map/psum | solution.py:160
  149.2 0.9 copy.116
  150.9 5.0 %reduce-scatter.7.cloned.1.call-done = bf16[128,256]{1,0:T(8,128)(2,1)} async-done(((bf16[256,256]{1,0:T(8,128)(2,1)}), bf16[128,256]{1,0:T(8,128)(2,1)}) %reduce-scatter.7.cloned.1.call-update) | async-done | bytes 65552
  (99 shorter events, 21.2 us)
Async XLA Ops:
  14.1 18.3 %copy-start.18 = (s32[128]{0:T(128)}, s32[128]{0:T(128)S(1)}, u32[]{:S(2)}) copy-start(s32[128]{0:T(128)S(1)} %multiply_add_fusion) | copy-start | bytes 1540
  16.2 3.5 %copy-start.11 = (bf16[1,256,256]{2,1,0:T(8,128)(2,1)}, bf16[1,256,256]{2,1,0:T(8,128)(2,1)S(1)}, u32[]{:S(2)}) copy-start(bf16[1,256,256]{2,1,0:T(8,128)(2,1)S(1)} %all-gather) | copy-start | bytes 393220
  17.6 2.3 %copy-start.5 = (bf16[128,1024]{0,1:T(8,128)(2,1)}, bf16[128,1024]{0,1:T(8,128)(2,1)S(1)}, u32[]{:S(2)}) copy-start(bf16[128,1024]{0,1:T(8,128)(2,1)S(1)} %get-tuple-element.49) | copy-start | bytes 786436
  17.6 3.8 %copy-start.7 = (bf16[128,1024]{0,1:T(8,128)(2,1)}, bf16[128,1024]{0,1:T(8,128)(2,1)S(1)}, u32[]{:S(2)}) copy-start(bf16[128,1024]{0,1:T(8,128)(2,1)S(1)} %get-tuple-element.48) | copy-start | bytes 786436
  17.7 0.7 copy-start.17
  18.4 1.0 copy-start.2
  18.4 1.5 copy-start.19
  21.4 1.0 copy-start.4
  21.5 5.8 %copy-start.21 = (f32[128,8]{0,1:T(8,128)}, f32[128,8]{0,1:T(8,128)S(1)}, u32[]{:S(2)}) copy-start(f32[128,8]{0,1:T(8,128)S(1)} %get-tuple-element.54) | copy-start | bytes 12292
  21.5 4.5 %copy-start.16 = (f32[2048]{0:T(1024)S(1)}, f32[2048]{0:T(1024)}, u32[]{:S(2)}) copy-start(f32[2048]{0:T(1024)} %param.16) | copy-start | bytes 24580
  26.0 1.3 copy-start.23
  27.3 16.2 %all-to-all-start = ((bf16[4,2,24,2048]{3,2,1,0:T(8,128)(2,1)}), bf16[4,2,24,2048]{3,2,1,0:T(8,128)(2,1)S(1)}, u32[]{:S(2)}, u32[]{:S(2)}) async-start(bf16[4,2,24,2048]{3,2,1,0:T(8,128)(2,1)} %bitcast.171), calls=%async_computation | async-start | bytes 1572864 | tf_op jit(solution)/shard_map/all_to_all | solution.py:127
  43.5 0.9 copy-start
  44.4 13.8 %all-to-all-start.2 = ((bf16[4,2,24,2048]{3,2,1,0:T(8,128)(2,1)}), bf16[4,2,24,2048]{3,2,1,0:T(8,128)(2,1)S(1)}, u32[]{:S(2)}, u32[]{:S(2)}) async-start(bf16[4,2,24,2048]{3,2,1,0:T(8,128)(2,1)} %bitcast.170), calls=%async_computation.2 | async-start | bytes 1572864 | tf_op jit(solution)/shard_map/all_to_all | solution.py:139
  47.9 3.8 %copy-start.24 = (bf16[2,2048,384]{2,1,0:T(8,128)(2,1)S(1)}, bf16[2,2048,384]{2,1,0:T(8,128)(2,1)}, u32[]{:S(2)}) copy-start(bf16[2,2048,384]{2,1,0:T(8,128)(2,1)} %param.17) | copy-start | bytes 9437188
  59.1 3.4 %copy-start.14 = (bf16[4,1,24,2048]{3,2,1,0:T(8,128)(2,1)S(1)}, bf16[4,1,24,2048]{3,2,1,0:T(8,128)(2,1)}, u32[]{:S(2)}) copy-start(bf16[4,1,24,2048]{3,2,1,0:T(8,128)(2,1)} %get-tuple-element.43) | copy-start | bytes 1179652
  68.6 13.7 %all-to-all-start.3 = ((bf16[4,2,24,2048]{3,2,1,0:T(8,128)(2,1)}), bf16[4,2,24,2048]{3,2,1,0:T(8,128)(2,1)S(1)}, u32[]{:S(2)}, u32[]{:S(2)}) async-start(bf16[4,2,24,2048]{3,2,1,0:T(8,128)(2,1)} %pad_maximum_fusion.1), calls=%async_computation.3 | async-start | bytes 1572864 | tf_op jit(solution)/shard_map/all_to_all | solution.py:149
  82.3 0.9 copy-start.10
  83.2 13.7 %all-to-all-start.1 = ((bf16[4,2,24,2048]{3,2,1,0:T(8,128)(2,1)}), bf16[4,2,24,2048]{3,2,1,0:T(8,128)(2,1)S(1)}, u32[]{:S(2)}, u32[]{:S(2)}) async-start(bf16[4,2,24,2048]{3,2,1,0:T(8,128)(2,1)} %pad_maximum_fusion), calls=%async_computation.1 | async-start | bytes 1572864 | tf_op jit(solution)/shard_map/all_to_all | solution.py:137
  86.7 62.5 %reduce-scatter.9.cloned.1.call-start = ((), (), s32[]{:S(2)}) async-start(), calls=%async_computation.7 | async-start | bytes 196608
  100.3 0.9 copy-start.1
  100.3 2.0 %copy-start.22 = (f32[128,8]{0,1:T(8,128)S(1)}, f32[128,8]{0,1:T(8,128)}, u32[]{:S(2)}) copy-start(f32[128,8]{0,1:T(8,128)} %copy-done.21) | copy-start | bytes 12292
  101.3 2.7 %copy-start.8 = (bf16[128,1024]{0,1:T(8,128)(2,1)S(1)}, bf16[128,1024]{0,1:T(8,128)(2,1)}, u32[]{:S(2)}) copy-start(bf16[128,1024]{0,1:T(8,128)(2,1)} %copy-done.7) | copy-start | bytes 786436
  101.4 3.0 %copy-start.12 = (bf16[1,256,256]{2,1,0:T(8,128)(2,1)S(1)}, bf16[1,256,256]{2,1,0:T(8,128)(2,1)}, u32[]{:S(2)}) copy-start(bf16[1,256,256]{2,1,0:T(8,128)(2,1)} %copy-done.11) | copy-start | bytes 393220
  101.4 3.2 %copy-start.9 = (bf16[128,1024]{1,0:T(8,128)(2,1)S(1)}, bf16[128,1024]{1,0:T(8,128)(2,1)}, u32[]{:S(2)}) copy-start(bf16[128,1024]{1,0:T(8,128)(2,1)} %get-tuple-element.47) | copy-start | bytes 786436
  102.3 2.9 %copy-start.3 = (f32[128,8,256]{2,0,1:T(8,128)S(1)}, f32[128,8,256]{2,0,1:T(8,128)}, u32[]{:S(2)}) copy-start(f32[128,8,256]{2,0,1:T(8,128)} %copy-done.2) | copy-start | bytes 3145732
  102.3 2.9 %copy-start.20 = (f32[128,8]{0,1:T(8,128)S(1)}, f32[128,8]{0,1:T(8,128)}, u32[]{:S(2)}) copy-start(f32[128,8]{0,1:T(8,128)} %copy-done.19) | copy-start | bytes 12292
  104.7 1.0 copy-start.6
  104.8 1.0 copy-start.15
  105.2 42.0 %copy-start.13 = (bf16[1,256,256]{2,1,0:T(8,128)(2,1)S(1)}, bf16[1,256,256]{2,1,0:T(8,128)(2,1)}, u32[]{:S(2)}) copy-start(bf16[1,256,256]{2,1,0:T(8,128)(2,1)} %copy-done.11) | copy-start | bytes 393220
  106.7 49.2 %reduce-scatter.7.cloned.1.call-start = ((), (), s32[]{:S(2)}) async-start(), calls=%async_computation.6 | async-start | bytes 196608
Sparse Core Ops, SparseCore 0:
  106.8 7.8 reduce-scatter.8
  147.6 8.2 reduce-scatter.6
where the time goes:
time: 165 us; the launch traced here: 164 us
  blocking collectives  43.7 us (26%)
  waiting for transfers between devices  31.7 us (19%)
  matrix products  31.6 us (19%)
  local copies, waits for them, and re-layouts  15.8 us (10%)
  starting transfers between devices  15.6 us (9%)
  between operations  14.6 us (9%)
  other arithmetic  11.4 us (7%)
    psum x1, blocking collectives, per_device(): gain_total = lax.psum(gain_local, ('ctx', 'exp', 'dp'))  39.6 us
    unnamed x58, local copies, waits for them, and re-layouts  10.9 us
    all_to_all x1, waiting for transfers between devices, per_device(): lax.all_to_all(send_x, 'exp', split_axis=0, concat_axis=0, tiled=True)  8.75 us
    dot_general x2, matrix products, expert_backward(): lax.dot_general(d_pre, gate_mat, (((1,), (1,)), ((), ())), preferred_elem...  7.49 us
    all_to_all x1, waiting for transfers between devices, per_device(): lax.all_to_all(jnp.stack(results, 1), 'exp', split_axis=0, concat_axis=0,...  7.14 us
    dot_general x2, matrix products, from_slots(): lax.dot_general(placement, flat, (((0,), (0,)), ((), ())), preferred_elem...  5.87 us
    all_to_all x1, waiting for transfers between devices, per_device(): lax.all_to_all(jnp.stack(backs, 1), 'exp', split_axis=0, concat_axis=0, t...  5.42 us
    all_to_all x1, waiting for transfers between devices, per_device(): lax.all_to_all(send_grad, 'exp', split_axis=0, concat_axis=0, tiled=True)  5.41 us
  transfers between devices with their start and end apart: 6, of which 5 were waited for; matrix products, arithmetic and copies ran while one was open for 12% of the time, Pallas kernels for 0%

commit v1 on v0

v1 whole, which is shorter than its diff:
```python
import functools

import jax
import jax.numpy as jnp
from jax import lax
from jax.experimental import pallas as pl
from jax.experimental.pallas import tpu as pltpu
from jax.sharding import PartitionSpec as P

D = 2048
HEAD_SIZE = 128
QUERY_HEADS = 16
KEY_VALUE_HEADS = 2
GROUP = QUERY_HEADS // KEY_VALUE_HEADS
FFE = 384
EXP_DEV = 2
COLS = 256
SCALE = HEAD_SIZE ** (-0.5)
EXP2_SCALE = SCALE * 1.4426950408889634
F32 = jnp.float32
BF16 = jnp.bfloat16
NN = (((1,), (0,)), ((), ()))
NT = (((1,), (1,)), ((), ()))
MIB = 1 << 20


def mm(a, b, dims=NN):
    return lax.dot_general(a, b, dims, preferred_element_type=F32)


def iota(shape, dim):
    return lax.broadcasted_iota(jnp.int32, shape, dim)


def row_to_col(row):
    n = row.shape[1]
    eye = iota((n, n), 0) == iota((n, n), 1)
    return jnp.sum(jnp.where(eye, row, jnp.zeros((), row.dtype)), axis=1, keepdims=True)


def col_to_row(col):
    n = col.shape[0]
    eye = iota((n, n), 0) == iota((n, n), 1)
    return jnp.sum(jnp.where(eye, col, jnp.zeros((), col.dtype)), axis=0, keepdims=True)


def block_positions(order_ref, ctx_index, shape, dim):
    span = shape[dim] // 8
    index = iota(shape, dim)
    which = index // span
    start = jnp.zeros(shape, jnp.int32)
    for b in range(8):
        start = jnp.where(which == b, order_ref[ctx_index * 8 + b], start)
    return start * span + index % span


def stacked(refs, cols=slice(None)):
    parts = [r[:, cols] for r in refs]
    return parts[0] if len(parts) == 1 else jnp.concatenate(parts, axis=0)


def column_blocks(width=D, step=COLS):
    return [slice(c, c + step) for c in range(0, width, step)]


def store_pieces(refs, cols, rows_value):
    at = 0
    for r in refs:
        n = r.shape[0]
        r[:, cols] = rows_value[at : at + n]
        at += n


def placement_rows(slot_row, slots):
    tokens = slot_row.shape[1]
    return jnp.where(iota((slots, tokens), 0) == slot_row, 1.0, 0.0).astype(BF16)


def placement_cols(slot_row, slots):
    tokens = slot_row.shape[1]
    slot_col = row_to_col(slot_row)
    return jnp.where(iota((tokens, slots), 1) == slot_col, 1.0, 0.0).astype(BF16)


def dispatch_kernel(experts, capacity, routes_ref, weight_ref, grad_ref, slot_ref, *send_refs):
    tokens = routes_ref.shape[1]
    chosen = routes_ref[...]
    lanes = max(experts, 16)
    hits = jnp.where(iota((lanes, tokens), 0) == chosen, 1.0, 0.0)
    before = jnp.where(iota((tokens, tokens), 0) < iota((tokens, tokens), 1), 1.0, 0.0)
    earlier = mm(hits.astype(BF16), before.astype(BF16))
    rank = jnp.sum(hits * earlier, axis=0, keepdims=True).astype(jnp.int32)
    target = (chosen // EXP_DEV) ^ lax.axis_index("exp")
    slot = (target * EXP_DEV + chosen % EXP_DEV) * capacity + rank
    slot_ref[...] = slot
    place = placement_rows(slot, experts * capacity)
    weight = row_to_col(weight_ref[...])
    for cols in column_blocks():
        scaled = (weight * grad_ref[:, cols].astype(F32)).astype(BF16)
        store_pieces(send_refs, cols, mm(place, scaled).astype(BF16))


def attention_kernel(count, pieces, order_ref, slot_ref, gain_ref, query_ref, resid_ref, *refs):
    kv_refs = refs[:count]
    hidden_ref = refs[count]
    send_refs = refs[count + 1 : count + 1 + pieces]
    tokens = query_ref.shape[0]
    me = lax.axis_index("ctx")
    query_pos = block_positions(order_ref, me, (tokens, 1), 0)
    bias = jnp.concatenate(
        [
            jnp.where(block_positions(order_ref, me ^ s, (1, tokens), 1) <= query_pos, 0.0, -1e30)
            for s in range(count)
        ],
        axis=1,
    )
    length = count * tokens
    ones = jnp.ones((length, HEAD_SIZE), BF16)
    total = jnp.zeros((tokens, HEAD_SIZE), F32)
    for g in range(KEY_VALUE_HEADS):
        k_cols = slice(g * HEAD_SIZE, (g + 1) * HEAD_SIZE)
        v_cols = slice((KEY_VALUE_HEADS + g) * HEAD_SIZE, (KEY_VALUE_HEADS + g + 1) * HEAD_SIZE)
        keys = stacked(kv_refs, k_cols)
        values = jnp.concatenate([stacked(kv_refs, v_cols), ones], axis=1)
        for h in range(g * GROUP, (g + 1) * GROUP):
            cols = slice(h * HEAD_SIZE, (h + 1) * HEAD_SIZE)
            scores = mm(query_ref[:, cols], keys, NT) + bias
            peak = jnp.max(scores, axis=1, keepdims=True)
            weights = jnp.exp2((scores - peak) * EXP2_SCALE).astype(BF16)
            mixed = mm(weights, values)
            attended = mixed[:, :HEAD_SIZE] / mixed[:, HEAD_SIZE:]
            hidden = (resid_ref[:, cols].astype(F32) + attended).astype(BF16)
            hidden_ref[:, cols] = hidden
            wide = hidden.astype(F32)
            total = total + wide * wide
    inv_rms = lax.rsqrt(jnp.sum(total, axis=1, keepdims=True) * (1.0 / D) + 1e-06)
    slots = sum(r.shape[0] for r in send_refs)
    place = placement_rows(slot_ref[...], slots)
    for cols in column_blocks():
        normed = (hidden_ref[:, cols].astype(F32) * inv_rms * gain_ref[:, cols]).astype(BF16)
        store_pieces(send_refs, cols, mm(place, normed).astype(BF16))


def first_expert_rows(slots, capacity):
    return iota((slots, 1), 0) % (EXP_DEV * capacity) < capacity


def expert_grad_kernel(capacity, pieces, down_ref, *refs):
    grads = stacked(refs[:pieces])
    out_ref = refs[pieces]
    first = first_expert_rows(grads.shape[0], capacity)
    out_ref[...] = jnp.where(first, mm(grads, down_ref[0], NT), mm(grads, down_ref[1], NT))


def expert_back_kernel(capacity, pieces, gate_ref, d_act_ref, *refs):
    rows = stacked(refs[:pieces])
    act_ref = refs[pieces]
    out_refs = refs[pieces + 1 :]
    first = first_expert_rows(rows.shape[0], capacity)
    pre = jnp.where(first, mm(rows, gate_ref[0]), mm(rows, gate_ref[1]))
    gate = 1.0 / (1.0 + jnp.exp(-pre))
    act = pre * gate
    act_ref[:, :FFE] = jnp.where(first, act, 0.0).astype(BF16)
    act_ref[:, FFE:] = jnp.where(first, 0.0, act).astype(BF16)
    d_pre = d_act_ref[...] * gate * (1.0 + pre * (1.0 - gate))
    d_first = jnp.where(first, d_pre, 0.0).astype(BF16)
    d_second = jnp.where(first, 0.0, d_pre).astype(BF16)
    for cols in column_blocks():
        back = mm(d_first, gate_ref[0, cols, :], NT) + mm(d_second, gate_ref[1, cols, :], NT)
        store_pieces(out_refs, cols, back.astype(BF16))


def expert_out_kernel(down_ref, act_ref, *out_refs):
    act = act_ref[...]
    for cols in column_blocks():
        y = mm(act[:, :FFE], down_ref[0, :, cols]) + mm(act[:, FFE:], down_ref[1, :, cols])
        store_pieces(out_refs, cols, y.astype(BF16))


def residual_kernel(pieces, slot_ref, gain_ref, hidden_ref, grad_ref, *refs):
    dn_refs = refs[:pieces]
    resid_ref, gain_out_ref, dn_scratch = refs[pieces:]
    tokens = hidden_ref.shape[0]
    slots = sum(r.shape[0] for r in dn_refs)
    place = placement_cols(slot_ref[...], slots)
    square = jnp.zeros((tokens, COLS), F32)
    mixing = jnp.zeros((tokens, COLS), F32)
    for cols in column_blocks():
        dn = mm(place, stacked(dn_refs, cols))
        dn_scratch[:, cols] = dn
        hidden = hidden_ref[:, cols].astype(F32)
        square = square + hidden * hidden
        mixing = mixing + dn * gain_ref[:, cols] * hidden
    inv_rms = lax.rsqrt(jnp.sum(square, axis=1, keepdims=True) * (1.0 / D) + 1e-06)
    mean_mix = jnp.sum(mixing, axis=1, keepdims=True) * (1.0 / D)
    factor = inv_rms * inv_rms * inv_rms * mean_mix
    for cols in column_blocks():
        dn = dn_scratch[:, cols] * inv_rms
        hidden = hidden_ref[:, cols].astype(F32)
        resid_ref[:, cols] = (
            grad_ref[:, cols].astype(F32) + dn * gain_ref[:, cols] - hidden * factor
        ).astype(BF16)
        gain_out_ref[:, cols] = jnp.sum(dn * hidden, axis=0, keepdims=True)


def attention_back_kernel(count, order_ref, query_ref, d_resid_ref, *refs):
    kv_refs = refs[:count]
    dq_ref, own_ref = refs[count : count + 2]
    other_refs = refs[count + 2 :]
    tokens = query_ref.shape[0]
    me = lax.axis_index("ctx")
    query_pos = block_positions(order_ref, me, (1, tokens), 1)
    bias = jnp.concatenate(
        [
            jnp.where(block_positions(order_ref, me ^ s, (tokens, 1), 0) <= query_pos, 0.0, -1e30)
            for s in range(count)
        ],
        axis=0,
    )
    pair_bias = jnp.concatenate([bias, bias], axis=1)
    length = count * tokens
    for g in range(KEY_VALUE_HEADS):
        k_cols = slice(g * HEAD_SIZE, (g + 1) * HEAD_SIZE)
        v_cols = slice((KEY_VALUE_HEADS + g) * HEAD_SIZE, (KEY_VALUE_HEADS + g + 1) * HEAD_SIZE)
        keys = stacked(kv_refs, k_cols)
        values = stacked(kv_refs, v_cols)
        keys_t = jnp.transpose(keys.astype(F32)).astype(BF16)
        d_keys = jnp.zeros((length, HEAD_SIZE), F32)
        d_values = jnp.zeros((length, HEAD_SIZE), F32)
        for h in range(g * GROUP, (g + 1) * GROUP, 2):
            cols_a = slice(h * HEAD_SIZE, (h + 1) * HEAD_SIZE)
            cols_b = slice((h + 1) * HEAD_SIZE, (h + 2) * HEAD_SIZE)
            queries = jnp.concatenate([query_ref[:, cols_a], query_ref[:, cols_b]], axis=0)
            d_out = jnp.concatenate([d_resid_ref[:, cols_a], d_resid_ref[:, cols_b]], axis=0)
            scores = mm(keys, queries, NT) + pair_bias
            peak = jnp.max(scores, axis=0, keepdims=True)
            weights = jnp.exp2((scores - peak) * EXP2_SCALE)
            probs = weights * (1.0 / jnp.sum(weights, axis=0, keepdims=True))
            probs_low = probs.astype(BF16)
            d_probs = mm(values, d_out, NT)
            row_dot = jnp.sum(probs * d_probs, axis=0, keepdims=True)
            d_scores = (probs * (d_probs - row_dot)).astype(BF16)
            d_keys = d_keys + mm(d_scores, queries)
            d_values = d_values + mm(probs_low, d_out)
            d_query_t = mm(keys_t, d_scores) * SCALE
            dq_ref[:, cols_a] = jnp.transpose(d_query_t[:, :tokens]).astype(BF16)
            dq_ref[:, cols_b] = jnp.transpose(d_query_t[:, tokens:]).astype(BF16)
        d_keys = d_keys * SCALE
        own_ref[:, k_cols] = d_keys[:tokens]
        own_ref[:, v_cols] = d_values[:tokens]
        for s, ref in enumerate(other_refs, 1):
            ref[:, k_cols] = d_keys[s * tokens : (s + 1) * tokens].astype(BF16)
            ref[:, v_cols] = d_values[s * tokens : (s + 1) * tokens].astype(BF16)


def output_kernel(pieces, slot_ref, weight_ref, hidden_ref, grad_ref, *refs):
    y_refs = refs[:pieces]
    out_ref, d_weight_ref = refs[pieces:]
    tokens = hidden_ref.shape[0]
    slots = sum(r.shape[0] for r in y_refs)
    place = placement_cols(slot_ref[...], slots)
    weight = row_to_col(weight_ref[...])
    total = jnp.zeros((tokens, COLS), F32)
    for cols in column_blocks():
        y = mm(place, stacked(y_refs, cols))
        out_ref[:, cols] = (hidden_ref[:, cols].astype(F32) + weight * y).astype(BF16)
        total = total + y * grad_ref[:, cols].astype(F32)
    d_weight_ref[...] = col_to_row(jnp.sum(total, axis=1, keepdims=True))


def run(kernel, name, inputs, outputs, flops, smem=0, scratch=(), limit=20 * MIB):
    nbytes = sum(x.size * x.dtype.itemsize for x in inputs) + sum(
        x.size * x.dtype.itemsize for x in outputs
    )
    vmem = pl.BlockSpec(memory_space=pltpu.VMEM)
    scalar = pl.BlockSpec(memory_space=pltpu.SMEM)
    return pl.pallas_call(
        kernel,
        out_shape=list(outputs),
        in_specs=[scalar] * smem + [vmem] * (len(inputs) - smem),
        out_specs=[vmem] * len(outputs),
        scratch_shapes=list(scratch),
        compiler_params=pltpu.CompilerParams(vmem_limit_bytes=limit),
        cost_estimate=pl.CostEstimate(flops=flops, bytes_accessed=nbytes, transcendentals=0),
        name=name,
    )(*inputs)


def pairwise(value, axis, step):
    count = lax.axis_size(axis)
    return lax.ppermute(value, axis, [(i, i ^ step) for i in range(count)])


def exchange(pieces, capacity):
    count = lax.axis_size("exp")
    rows = EXP_DEV * capacity
    if len(pieces) == count:
        return [pieces[0]] + [pairwise(pieces[s], "exp", s) for s in range(1, count)]
    flat = pieces[0]
    blocks = [flat[s * rows : (s + 1) * rows] for s in range(count)]
    moved = [blocks[0]] + [pairwise(blocks[s], "exp", s) for s in range(1, count)]
    return [jnp.concatenate(moved, axis=0)]


def sum_over(value, axis):
    parts = [value] + [pairwise(value, axis, s) for s in range(1, lax.axis_size(axis))]
    while len(parts) > 1:
        parts = [parts[i] + parts[i + 1] for i in range(0, len(parts), 2)]
    return parts[0]


def shaped(shape, dtype):
    return jax.ShapeDtypeStruct(shape, dtype)


def per_device(
    queries,
    keys,
    values,
    resid,
    block_order,
    norm_gain,
    w_gate,
    w_down,
    routes,
    route_weight,
    d_out,
):
    query_rows = queries[0]
    resid_rows = resid[0]
    grad_rows = d_out[0]
    tokens = query_rows.shape[0]
    chosen = routes.reshape(1, tokens)
    gain = norm_gain.reshape(1, D)
    ctx_count = lax.axis_size("ctx")
    exp_count = lax.axis_size("exp")
    experts = EXP_DEV * exp_count
    capacity = 3 * tokens // (2 * experts)
    slots = experts * capacity
    rows = EXP_DEV * capacity
    piece_count = exp_count if rows % 16 == 0 else 1
    piece_shapes = [shaped((slots // piece_count, D), BF16)] * piece_count
    token_shape = shaped((tokens, D), BF16)
    kv_width = 2 * KEY_VALUE_HEADS * HEAD_SIZE
    attn_flops = 4 * tokens * ctx_count * tokens * QUERY_HEADS * HEAD_SIZE
    place_flops = 2 * slots * tokens * D
    expert_flops = 2 * slots * D * FFE * EXP_DEV

    own_kv = jnp.concatenate([keys[0], values[0]], axis=1)
    kv = [own_kv] + [pairwise(own_kv, "ctx", s) for s in range(1, ctx_count)]

    slot, *send_grad = run(
        functools.partial(dispatch_kernel, experts, capacity),
        "dispatch_grads",
        [chosen, route_weight, grad_rows],
        [shaped((1, tokens), jnp.int32)] + piece_shapes,
        place_flops,
    )
    arrived_grad = exchange(send_grad, capacity)

    hidden, *send_x = run(
        functools.partial(attention_kernel, ctx_count, piece_count),
        "attention_forward",
        [block_order, slot, gain, query_rows, resid_rows] + kv,
        [token_shape] + piece_shapes,
        attn_flops + place_flops,
        smem=1,
    )
    arrived_x = exchange(send_x, capacity)

    (d_act,) = run(
        functools.partial(expert_grad_kernel, capacity, piece_count),
        "expert_act_grad",
        [w_down] + arrived_grad,
        [shaped((slots, FFE), F32)],
        expert_flops,
    )
    act, *send_dn = run(
        functools.partial(expert_back_kernel, capacity, piece_count),
        "expert_backward",
        [w_gate, d_act] + arrived_x,
        [shaped((slots, EXP_DEV * FFE), BF16)] + piece_shapes,
        2 * expert_flops,
    )
    dn = exchange(send_dn, capacity)
    send_y = run(
        expert_out_kernel, "expert_output", [w_down, act], piece_shapes, expert_flops
    )
    returned = exchange(send_y, capacity)

    d_hidden, gain_local = run(
        functools.partial(residual_kernel, piece_count),
        "residual_grad",
        [slot, gain, hidden, grad_rows] + dn,
        [token_shape, shaped((1, D), F32)],
        place_flops,
        scratch=[pltpu.VMEM((tokens, D), F32)],
    )
    gain_total = gain_local
    for axis in ("dp", "exp", "ctx"):
        gain_total = sum_over(gain_total, axis)
    total_tokens = tokens * ctx_count * exp_count * lax.axis_size("dp")
    d_gain = gain_total[0] / total_tokens

    d_queries, kv_own, *kv_send = run(
        functools.partial(attention_back_kernel, ctx_count),
        "attention_backward",
        [block_order, query_rows, d_hidden] + kv,
        [token_shape, shaped((tokens, kv_width), F32)]
        + [shaped((tokens, kv_width), BF16)] * (ctx_count - 1),
        5 * attn_flops // 2,
        smem=1,
    )
    kv_grad = kv_own
    for s, part in enumerate(kv_send, 1):
        kv_grad = kv_grad + pairwise(part, "ctx", s).astype(F32)
    kv_grad = kv_grad.astype(BF16)

    layer_out, d_weight = run(
        functools.partial(output_kernel, piece_count),
        "layer_output",
        [slot, route_weight, hidden, grad_rows] + returned,
        [token_shape, shaped((1, tokens), F32)],
        place_flops,
    )
    split = KEY_VALUE_HEADS * HEAD_SIZE
    return (
        layer_out[None],
        d_hidden[None],
        d_queries[None],
        kv_grad[:, :split][None],
        kv_grad[:, split:][None],
        d_weight,
        d_gain,
    )


def solution(mesh):
    in_specs = (
        P(("exp", "dp"), "ctx", None),
        P(("exp", "dp"), "ctx", None),
        P(("exp", "dp"), "ctx", None),
        P(("exp", "dp"), "ctx", None),
        P(),
        P(),
        P("exp", None, None),
        P("exp", None, None),
        P(("exp", "dp"), "ctx", None),
        P(("exp", "dp"), "ctx"),
        P(("exp", "dp"), "ctx", None),
    )
    out_specs = (
        P(("exp", "dp"), "ctx", None),
        P(("exp", "dp"), "ctx", None),
        P(("exp", "dp"), "ctx", None),
        P(("exp", "dp"), "ctx", None),
        P(("exp", "dp"), "ctx", None),
        P(("exp", "dp"), "ctx"),
        P(),
    )
    return jax.shard_map(
        per_device, mesh=mesh, in_specs=in_specs, out_specs=out_specs, check_vma=False
    )
```

time: 165 us -> 67.9 us (0.41)
  blocking collectives: 43.7 us -> 0 us
  matrix products: 31.6 us -> 0 us
  Pallas kernels: 0 us -> 14 us
  between operations: 14.6 us -> 0.78 us
  waiting for transfers between devices: 31.7 us -> 18.4 us
  other arithmetic: 11.4 us -> 1.56 us
  starting transfers between devices: 15.6 us -> 24.5 us
  local copies, waits for them, and re-layouts: 15.8 us -> 8.37 us
    psum x1 -> x0, blocking collectives: 39.6 us -> none  [per_device(): gain_total = lax.psum(gain_local, ('ctx', 'exp', 'dp'))]
    dot_general x20 -> x0, matrix products: 29.4 us -> none  [the longest x2 7.49 us: expert_backward(): lax.dot_general(d_pre, gate_mat, (((1,), (1,)), ((), ())), preferred_elem...]
    all_to_all x4 -> x0, waiting for transfers between devices: 26.7 us -> none  [the longest x1 8.75 us: per_device(): lax.all_to_all(send_x, 'exp', split_axis=0, concat_axis=0, tiled=True)]
    ppermute x0 -> x21, starting transfers between devices: none -> 24.5 us  [pairwise(): return lax.ppermute(value, axis, [(i, i ^ step) for i in range(count)])]
    ppermute x0 -> x21, waiting for transfers between devices: none -> 18.4 us  [pairwise(): return lax.ppermute(value, axis, [(i, i ^ step) for i in range(count)])]
    all_to_all x4 -> x0, starting transfers between devices: 15.5 us -> none  [the longest x1 5.06 us: per_device(): lax.all_to_all(send_x, 'exp', split_axis=0, concat_axis=0, tiled=True)]
    pallas_call x0 -> x8, Pallas kernels: none -> 14 us  [run(): pl.pallas_call(kernel, out_shape=list(outputs), in_specs=[scalar] * smem...]
    unnamed x4 -> x0, waiting for transfers between devices: 5.01 us -> none
  transfers between devices with their start and end apart: 6 -> 21, of which waited for: 5 -> 7; matrix products, arithmetic and copies ran while one was open for 12% -> 2% of each run, Pallas kernels for 0% -> 14%
where the time goes in v1:
time: 67.9 us; the launch traced here: 67.5 us
  starting transfers between devices  24.5 us (36%)
  waiting for transfers between devices  18.4 us (27%)
  Pallas kernels  14 us (21%)
  local copies, waits for them, and re-layouts  8.37 us (12%)
  other arithmetic  1.56 us (2%)
  between operations  0.78 us (1%)
    ppermute x21, starting transfers between devices, pairwise(): return lax.ppermute(value, axis, [(i, i ^ step) for i in range(count)])  24.5 us
    ppermute x21, waiting for transfers between devices, pairwise(): return lax.ppermute(value, axis, [(i, i ^ step) for i in range(count)])  18.4 us
    pallas_call x8, Pallas kernels, run(): pl.pallas_call(kernel, out_shape=list(outputs), in_specs=[scalar] * smem...  14 us
    unnamed x32, local copies, waits for them, and re-layouts  7.71 us
  transfers between devices with their start and end apart: 21, of which 7 were waited for; matrix products, arithmetic and copies ran while one was open for 2% of the time, Pallas kernels for 14%

profile of v1, /device:TPU:0, one launch (start us, length us, event | category | flops | bytes accessed | tf_op | source)
XLA Modules:
  0.0 67.5 jit_solution(13175361761955092484)
XLA Ops:
  0.6 1.0 %copy-done.2 = bf16[1,128,2048]{2,1,0:T(8,128)(2,1)S(1)} copy-done((bf16[1,128,2048]{2,1,0:T(8,128)(2,1)S(1)}, bf16[1,128,2048]{2,1,0:T(8,128)(2,1)}, u32[]{:S(2)}) %copy-start.2) | copy-done | bytes 524312
  3.5 3.0 %collective-permute-start.1 = (bf16[48,2048]{1,0:T(8,128)(2,1)S(1)}, bf16[48,2048]{1,0:T(8,128)(2,1)S(1)}, u32[]{:S(2)}, u32[]{:S(2)}) collective-permute-start(bf16[48,2048]{1,0:T(8,128)(2,1)S(1)} %get-tuple-element.36), channel_id=1, source_target_pairs={{0,4},{4,0},{8,12},{12,8},{1,5},{5,1},{9,13},{13,9},{2,6},{6,2},{1... | collective-permute-start | bytes 589832 | tf_op jit(solution)/shard_map/ppermute | solution.py:291
  6.5 0.9 %pad_maximum_fusion.refs_0_ = bf16[128,512]{1,0:T(8,128)(2,1)S(1)} fusion(bf16[128,256]{1,0:T(8,128)(2,1)} %bitcast.25, bf16[128,256]{1,0:T(8,128)(2,1)} %bitcast.26), kind=kLoop, calls=%fused_computation.1 | loop fusion | flops 262144 | bytes 262144 | tf_op jit(solution)/shard_map/concatenate | solution.py:349
  7.5 1.6 %collective-permute-start.2 = (bf16[48,2048]{1,0:T(8,128)(2,1)S(1)}, bf16[48,2048]{1,0:T(8,128)(2,1)S(1)}, u32[]{:S(2)}, u32[]{:S(2)}) collective-permute-start(bf16[48,2048]{1,0:T(8,128)(2,1)S(1)} %get-tuple-element.37), channel_id=1, source_target_pairs={{0,8},{4,12},{8,0},{12,4},{1,9},{5,13},{9,1},{13,5},{2,10},{6,14},... | collective-permute-start | bytes 589832 | tf_op jit(solution)/shard_map/ppermute | solution.py:291
  9.8 1.0 %copy-done.10 = bf16[1,128,2048]{2,1,0:T(8,128)(2,1)S(1)} copy-done((bf16[1,128,2048]{2,1,0:T(8,128)(2,1)S(1)}, bf16[1,128,2048]{2,1,0:T(8,128)(2,1)}, u32[]{:S(2)}) %copy-start.10) | copy-done | bytes 524312
  10.8 1.0 %copy-done.11 = bf16[1,128,2048]{2,1,0:T(8,128)(2,1)S(1)} copy-done((bf16[1,128,2048]{2,1,0:T(8,128)(2,1)S(1)}, bf16[1,128,2048]{2,1,0:T(8,128)(2,1)}, u32[]{:S(2)}) %copy-start.11) | copy-done | bytes 524312
  12.5 2.0 %attention_forward.1 = (bf16[128,2048]{1,0:T(8,128)(2,1)S(1)}, bf16[48,2048]{1,0:T(8,128)(2,1)S(1)}, bf16[48,2048]{1,0:T(8,128)(2,1)S(1)}, bf16[48,2048]{1,0:T(8,128)(2,1)S(1)}, bf16[48,2048]{1,0:T(8,128)(2,1)S(1)}) custom-call(s32[16]{0:T(128)S(1)} %copy-done.14, s32[1,128]{1,0:T(1,128)S(1)} %get-tuple-element.33.slot_ref, f32[1,2048]{1,0:T(1,128)S(1)} %bitcast.18, ...), custom_call_target="tpu_custom_call" | custom-call | flops 369098752 | bytes 2630208 | tf_op jit(solution)/shard_map/attention_forward/pallas_call | solution.py:277
  14.5 2.0 %collective-permute-start.4 = (bf16[48,2048]{1,0:T(8,128)(2,1)S(1)}, bf16[48,2048]{1,0:T(8,128)(2,1)S(1)}, u32[]{:S(2)}, u32[]{:S(2)}) collective-permute-start(bf16[48,2048]{1,0:T(8,128)(2,1)S(1)} %get-tuple-element.40), channel_id=1, source_target_pairs={{0,4},{4,0},{8,12},{12,8},{1,5},{5,1},{9,13},{13,9},{2,6},{6,2},{1... | collective-permute-start | bytes 589832 | tf_op jit(solution)/shard_map/ppermute | solution.py:291
  16.5 1.5 %collective-permute-start.5 = (bf16[48,2048]{1,0:T(8,128)(2,1)S(1)}, bf16[48,2048]{1,0:T(8,128)(2,1)S(1)}, u32[]{:S(2)}, u32[]{:S(2)}) collective-permute-start(bf16[48,2048]{1,0:T(8,128)(2,1)S(1)} %get-tuple-element.41), channel_id=1, source_target_pairs={{0,8},{4,12},{8,0},{12,4},{1,9},{5,13},{9,1},{13,5},{2,10},{6,14},... | collective-permute-start | bytes 589832 | tf_op jit(solution)/shard_map/ppermute | solution.py:291
  18.1 1.2 %collective-permute-done.2.refs_2_ = bf16[48,2048]{1,0:T(8,128)(2,1)S(1)} collective-permute-done((bf16[48,2048]{1,0:T(8,128)(2,1)S(1)}, bf16[48,2048]{1,0:T(8,128)(2,1)S(1)}, u32[]{:S(2)}, u32[]{:S(2)}) %collective-permute-start.2) | collective-permute-done | bytes 196640 | tf_op jit(solution)/shard_map/ppermute | solution.py:291
  19.2 1.9 %copy-done = bf16[2,384,2048]{2,1,0:T(8,128)(2,1)S(1)} copy-done((bf16[2,384,2048]{2,1,0:T(8,128)(2,1)S(1)}, bf16[2,384,2048]{2,1,0:T(8,128)(2,1)}, u32[]{:S(2)}) %copy-start) | copy-done | bytes 3145752
  21.1 1.2 %expert_act_grad.1.d_act_ref = f32[192,384]{1,0:T(8,128)S(1)} custom-call(bf16[2,384,2048]{2,1,0:T(8,128)(2,1)S(1)} %copy-done, bf16[48,2048]{1,0:T(8,128)(2,1)S(1)} %get-tuple-element.35.refs_0_, bf16[48,2048]{1,0:T(8,128)(2,1)S(1)} %collective-permute-done.1.refs_1_, bf16[48,2048]{1,0:T(8,128)(2,1)S(1)} %collective-permute-done.2.refs_2_, ...), custom_call_target="tpu_custom_call" | custom-call | flops 603979776 | bytes 4227072 | tf_op jit(solution)/shard_map/expert_act_grad/pallas_call | solution.py:277
  22.3 5.1 %collective-permute-done.5.refs_2_ = bf16[48,2048]{1,0:T(8,128)(2,1)S(1)} collective-permute-done((bf16[48,2048]{1,0:T(8,128)(2,1)S(1)}, bf16[48,2048]{1,0:T(8,128)(2,1)S(1)}, u32[]{:S(2)}, u32[]{:S(2)}) %collective-permute-start.5) | collective-permute-done | bytes 196640 | tf_op jit(solution)/shard_map/ppermute | solution.py:291
  27.4 2.3 %expert_backward.1 = (bf16[192,768]{1,0:T(8,128)(2,1)S(1)}, bf16[48,2048]{1,0:T(8,128)(2,1)S(1)}, bf16[48,2048]{1,0:T(8,128)(2,1)S(1)}, bf16[48,2048]{1,0:T(8,128)(2,1)S(1)}, bf16[48,2048]{1,0:T(8,128)(2,1)S(1)}) custom-call(bf16[2,2048,384]{2,1,0:T(8,128)(2,1)S(1)} %copy-done.9, f32[192,384]{1,0:T(8,128)S(1)} %expert_act_grad.1.d_act_ref, ...), custom_call_target="tpu_custom_call" | custom-call | flops 1207959552 | bytes 5308416 | tf_op jit(solution)/shard_map/expert_backward/pallas_call | solution.py:277
  29.7 1.0 %collective-permute-start.10 = (bf16[48,2048]{1,0:T(8,128)(2,1)S(1)}, bf16[48,2048]{1,0:T(8,128)(2,1)S(1)}, u32[]{:S(2)}, u32[]{:S(2)}) collective-permute-start(bf16[48,2048]{1,0:T(8,128)(2,1)S(1)} %get-tuple-element.50), channel_id=1, source_target_pairs={{0,4},{4,0},{8,12},{12,8},{1,5},{5,1},{9,13},{13,9},{2,6},{6,2},{1... | collective-permute-start | bytes 589832 | tf_op jit(solution)/shard_map/ppermute | solution.py:291
  30.7 1.1 %collective-permute-start.11 = (bf16[48,2048]{1,0:T(8,128)(2,1)S(1)}, bf16[48,2048]{1,0:T(8,128)(2,1)S(1)}, u32[]{:S(2)}, u32[]{:S(2)}) collective-permute-start(bf16[48,2048]{1,0:T(8,128)(2,1)S(1)} %get-tuple-element.51), channel_id=1, source_target_pairs={{0,8},{4,12},{8,0},{12,4},{1,9},{5,13},{9,1},{13,5},{2,10},{6,14},... | collective-permute-start | bytes 589832 | tf_op jit(solution)/shard_map/ppermute | solution.py:291
  31.8 1.4 %collective-permute-start.12 = (bf16[48,2048]{1,0:T(8,128)(2,1)S(1)}, bf16[48,2048]{1,0:T(8,128)(2,1)S(1)}, u32[]{:S(2)}, u32[]{:S(2)}) collective-permute-start(bf16[48,2048]{1,0:T(8,128)(2,1)S(1)} %get-tuple-element.52), channel_id=1, source_target_pairs={{0,12},{4,8},{8,4},{12,0},{1,13},{5,9},{9,5},{13,1},{2,14},{6,10},... | collective-permute-start | bytes 589832 | tf_op jit(solution)/shard_map/ppermute | solution.py:291
  33.3 4.2 %collective-permute-done.10.refs_1_ = bf16[48,2048]{1,0:T(8,128)(2,1)S(1)} collective-permute-done((bf16[48,2048]{1,0:T(8,128)(2,1)S(1)}, bf16[48,2048]{1,0:T(8,128)(2,1)S(1)}, u32[]{:S(2)}, u32[]{:S(2)}) %collective-permute-start.10) | collective-permute-done | bytes 196640 | tf_op jit(solution)/shard_map/ppermute | solution.py:291
  37.5 1.5 %collective-permute-done.11.refs_2_ = bf16[48,2048]{1,0:T(8,128)(2,1)S(1)} collective-permute-done((bf16[48,2048]{1,0:T(8,128)(2,1)S(1)}, bf16[48,2048]{1,0:T(8,128)(2,1)S(1)}, u32[]{:S(2)}, u32[]{:S(2)}) %collective-permute-start.11) | collective-permute-done | bytes 196640 | tf_op jit(solution)/shard_map/ppermute | solution.py:291
  38.9 1.8 %collective-permute-done.12.refs_3_ = bf16[48,2048]{1,0:T(8,128)(2,1)S(1)} collective-permute-done((bf16[48,2048]{1,0:T(8,128)(2,1)S(1)}, bf16[48,2048]{1,0:T(8,128)(2,1)S(1)}, u32[]{:S(2)}, u32[]{:S(2)}) %collective-permute-start.12) | collective-permute-done | bytes 196640 | tf_op jit(solution)/shard_map/ppermute | solution.py:291
  40.7 1.5 %residual_grad.1 = (bf16[128,2048]{1,0:T(8,128)(2,1)}, f32[1,2048]{1,0:T(1,128)S(1)}) custom-call(s32[1,128]{1,0:T(1,128)S(1)} %get-tuple-element.33.slot_ref, f32[1,2048]{1,0:T(1,128)S(1)} %bitcast.19, bf16[128,2048]{1,0:T(8,128)(2,1)S(1)} %get-tuple-element.34.hidden_ref, bf16[128,2048]{1,0:T(8,128)(2,1)S(1)} %bitcast.16, ...), custom_call_target="tpu_custom_call" | custom-call | flops 100663296 | bytes 2376192 | tf_op jit(solution)/shard_map/residual_grad/pallas_call | solution.py:277
  42.3 3.6 %collective-permute-start.16 = (f32[1,2048]{1,0:T(1,128)S(1)}, f32[1,2048]{1,0:T(1,128)S(1)}, u32[]{:S(2)}, u32[]{:S(2)}) collective-permute-start(f32[1,2048]{1,0:T(1,128)S(1)} %get-tuple-element.58), channel_id=1, source_target_pairs={{0,3},{1,2},{2,1},{3,0},{4,7},{5,6},{6,5},{7,4},{8,11},{9,10},{10,... | collective-permute-start | bytes 24584 | tf_op jit(solution)/shard_map/ppermute | solution.py:291
  45.9 0.8 %collective-permute-start.14 = (f32[1,2048]{1,0:T(1,128)S(1)}, f32[1,2048]{1,0:T(1,128)S(1)}, u32[]{:S(2)}, u32[]{:S(2)}) collective-permute-start(f32[1,2048]{1,0:T(1,128)S(1)} %get-tuple-element.58), channel_id=1, source_target_pairs={{0,1},{1,0},{2,3},{3,2},{4,5},{5,4},{6,7},{7,6},{8,9},{9,8},{10,11... | collective-permute-start | bytes 24584 | tf_op jit(solution)/shard_map/ppermute | solution.py:291
  46.7 1.0 %expert_output.1 = (bf16[48,2048]{1,0:T(8,128)(2,1)S(1)}, bf16[48,2048]{1,0:T(8,128)(2,1)S(1)}, bf16[48,2048]{1,0:T(8,128)(2,1)S(1)}, bf16[48,2048]{1,0:T(8,128)(2,1)S(1)}) custom-call(bf16[2,384,2048]{2,1,0:T(8,128)(2,1)S(1)} %copy-done.1, bf16[192,768]{1,0:T(8,128)(2,1)S(1)} %get-tuple-element.43.act_ref), custom_call_target="tpu_custom_call" | custom-call | flops 603979776 | bytes 4227072 | tf_op jit(solution)/shard_map/expert_output/pallas_call | solution.py:277
  47.6 0.9 %collective-permute-start.7 = (bf16[48,2048]{1,0:T(8,128)(2,1)S(1)}, bf16[48,2048]{1,0:T(8,128)(2,1)S(1)}, u32[]{:S(2)}, u32[]{:S(2)}) collective-permute-start(bf16[48,2048]{1,0:T(8,128)(2,1)S(1)} %get-tuple-element.45), channel_id=1, source_target_pairs={{0,4},{4,0},{8,12},{12,8},{1,5},{5,1},{9,13},{13,9},{2,6},{6,2},{1... | collective-permute-start | bytes 589832 | tf_op jit(solution)/shard_map/ppermute | solution.py:291
  48.6 1.5 %collective-permute-start.8 = (bf16[48,2048]{1,0:T(8,128)(2,1)S(1)}, bf16[48,2048]{1,0:T(8,128)(2,1)S(1)}, u32[]{:S(2)}, u32[]{:S(2)}) collective-permute-start(bf16[48,2048]{1,0:T(8,128)(2,1)S(1)} %get-tuple-element.46), channel_id=1, source_target_pairs={{0,8},{4,12},{8,0},{12,4},{1,9},{5,13},{9,1},{13,5},{2,10},{6,14},... | collective-permute-start | bytes 589832 | tf_op jit(solution)/shard_map/ppermute | solution.py:291
  50.5 1.8 %collective-permute-start.19 = (f32[1,2048]{1,0:T(1,128)S(1)}, f32[1,2048]{1,0:T(1,128)S(1)}, u32[]{:S(2)}, u32[]{:S(2)}) collective-permute-start(f32[1,2048]{1,0:T(1,128)S(1)} %add_add_fusion.1), channel_id=1, source_target_pairs={{0,12},{4,8},{8,4},{12,0},{1,13},{5,9},{9,5},{13,1},{2,14},{6,10},... | collective-permute-start | bytes 24584 | tf_op jit(solution)/shard_map/ppermute | solution.py:291
  52.8 1.2 %collective-permute-start.17 = (f32[1,2048]{1,0:T(1,128)S(1)}, f32[1,2048]{1,0:T(1,128)S(1)}, u32[]{:S(2)}, u32[]{:S(2)}) collective-permute-start(f32[1,2048]{1,0:T(1,128)S(1)} %add_add_fusion.1), channel_id=1, source_target_pairs={{0,4},{4,0},{8,12},{12,8},{1,5},{5,1},{9,13},{13,9},{2,6},{6,2},{1... | collective-permute-start | bytes 24584 | tf_op jit(solution)/shard_map/ppermute | solution.py:291
  54.0 4.3 %attention_backward.1 = (bf16[128,2048]{1,0:T(8,128)(2,1)}, f32[128,512]{1,0:T(8,128)S(1)}, bf16[128,512]{1,0:T(8,128)(2,1)S(1)}) custom-call(s32[16]{0:T(128)S(1)} %copy-done.15, bf16[128,2048]{1,0:T(8,128)(2,1)S(1)} %bitcast.23, bf16[128,2048]{1,0:T(8,128)(2,1)S(1)} %copy-done.13, bf16[128,512]{1,0:T(8,128)(2,1)S(1)} %pad_maximum_fusion.refs_0_, ...), custom_call_target="tpu_custom_call" | custom-call | flops 671088640 | bytes 2228288 | tf_op jit(solution)/shard_map/attention_backward/pallas_call | solution.py:277
  58.3 1.8 %collective-permute-start.9 = (bf16[48,2048]{1,0:T(8,128)(2,1)S(1)}, bf16[48,2048]{1,0:T(8,128)(2,1)S(1)}, u32[]{:S(2)}, u32[]{:S(2)}) collective-permute-start(bf16[48,2048]{1,0:T(8,128)(2,1)S(1)} %get-tuple-element.47), channel_id=1, source_target_pairs={{0,12},{4,8},{8,4},{12,0},{1,13},{5,9},{9,5},{13,1},{2,14},{6,10},... | collective-permute-start | bytes 589832 | tf_op jit(solution)/shard_map/ppermute | solution.py:291
  60.7 4.2 %collective-permute-done.9.refs_3_ = bf16[48,2048]{1,0:T(8,128)(2,1)S(1)} collective-permute-done((bf16[48,2048]{1,0:T(8,128)(2,1)S(1)}, bf16[48,2048]{1,0:T(8,128)(2,1)S(1)}, u32[]{:S(2)}, u32[]{:S(2)}) %collective-permute-start.9) | collective-permute-done | bytes 196640 | tf_op jit(solution)/shard_map/ppermute | solution.py:291
  64.9 1.3 %layer_output.1 = (bf16[128,2048]{1,0:T(8,128)(2,1)}, f32[1,128]{1,0:T(1,128)}) custom-call(s32[1,128]{1,0:T(1,128)S(1)} %get-tuple-element.33.slot_ref, f32[1,128]{1,0:T(1,128)S(1)} %copy-done.7, bf16[128,2048]{1,0:T(8,128)(2,1)S(1)} %get-tuple-element.34.hidden_ref, bf16[128,2048]{1,0:T(8,128)(2,1)S(1)} %bitcast.17, ...), custom_call_target="tpu_custom_call" | custom-call | flops 100663296 | bytes 2360832 | tf_op jit(solution)/shard_map/layer_output/pallas_call | solution.py:277
  (56 shorter events, 6.3 us)
Async XLA Ops:
  0.6 1.0 %copy-start.2 = (bf16[1,128,2048]{2,1,0:T(8,128)(2,1)S(1)}, bf16[1,128,2048]{2,1,0:T(8,128)(2,1)}, u32[]{:S(2)}) copy-start(bf16[1,128,2048]{2,1,0:T(8,128)(2,1)} %param.21) | copy-start | bytes 1572868
  3.5 14.5 %collective-permute-start.1 = (bf16[48,2048]{1,0:T(8,128)(2,1)S(1)}, bf16[48,2048]{1,0:T(8,128)(2,1)S(1)}, u32[]{:S(2)}, u32[]{:S(2)}) collective-permute-start(bf16[48,2048]{1,0:T(8,128)(2,1)S(1)} %get-tuple-element.36), channel_id=1, source_target_pairs={{0,4},{4,0},{8,12},{12,8},{1,5},{5,1},{9,13},{13,9},{2,6},{6,2},{1... | collective-permute-start | bytes 589832 | tf_op jit(solution)/shard_map/ppermute | solution.py:291
  7.4 1.7 %collective-permute-start = (bf16[128,512]{1,0:T(8,128)(2,1)S(1)}, bf16[128,512]{1,0:T(8,128)(2,1)S(1)}, u32[]{:S(2)}, u32[]{:S(2)}) collective-permute-start(bf16[128,512]{1,0:T(8,128)(2,1)S(1)} %pad_maximum_fusion.refs_0_), channel_id=1, source_target_pairs={{0,16},{16,0},{1,17},{17,1},{2,18},{18,2},{3,19},{19,3},{4,20},{20... | collective-permute-start | bytes 393224 | tf_op jit(solution)/shard_map/ppermute | solution.py:291
  7.5 11.8 %collective-permute-start.2 = (bf16[48,2048]{1,0:T(8,128)(2,1)S(1)}, bf16[48,2048]{1,0:T(8,128)(2,1)S(1)}, u32[]{:S(2)}, u32[]{:S(2)}) collective-permute-start(bf16[48,2048]{1,0:T(8,128)(2,1)S(1)} %get-tuple-element.37), channel_id=1, source_target_pairs={{0,8},{4,12},{8,0},{12,4},{1,9},{5,13},{9,1},{13,5},{2,10},{6,14},... | collective-permute-start | bytes 589832 | tf_op jit(solution)/shard_map/ppermute | solution.py:291
  9.0 10.2 %collective-permute-start.3 = (bf16[48,2048]{1,0:T(8,128)(2,1)S(1)}, bf16[48,2048]{1,0:T(8,128)(2,1)S(1)}, u32[]{:S(2)}, u32[]{:S(2)}) collective-permute-start(bf16[48,2048]{1,0:T(8,128)(2,1)S(1)} %get-tuple-element.38), channel_id=1, source_target_pairs={{0,12},{4,8},{8,4},{12,0},{1,13},{5,9},{9,5},{13,1},{2,14},{6,10},... | collective-permute-start | bytes 589832 | tf_op jit(solution)/shard_map/ppermute | solution.py:291
  10.8 1.0 %copy-start.11 = (bf16[1,128,2048]{2,1,0:T(8,128)(2,1)S(1)}, bf16[1,128,2048]{2,1,0:T(8,128)(2,1)}, u32[]{:S(2)}) copy-start(bf16[1,128,2048]{2,1,0:T(8,128)(2,1)} %param.11) | copy-start | bytes 1572868
  14.5 7.8 %collective-permute-start.4 = (bf16[48,2048]{1,0:T(8,128)(2,1)S(1)}, bf16[48,2048]{1,0:T(8,128)(2,1)S(1)}, u32[]{:S(2)}, u32[]{:S(2)}) collective-permute-start(bf16[48,2048]{1,0:T(8,128)(2,1)S(1)} %get-tuple-element.40), channel_id=1, source_target_pairs={{0,4},{4,0},{8,12},{12,8},{1,5},{5,1},{9,13},{13,9},{2,6},{6,2},{1... | collective-permute-start | bytes 589832 | tf_op jit(solution)/shard_map/ppermute | solution.py:291
  16.5 10.9 %collective-permute-start.5 = (bf16[48,2048]{1,0:T(8,128)(2,1)S(1)}, bf16[48,2048]{1,0:T(8,128)(2,1)S(1)}, u32[]{:S(2)}, u32[]{:S(2)}) collective-permute-start(bf16[48,2048]{1,0:T(8,128)(2,1)S(1)} %get-tuple-element.41), channel_id=1, source_target_pairs={{0,8},{4,12},{8,0},{12,4},{1,9},{5,13},{9,1},{13,5},{2,10},{6,14},... | collective-permute-start | bytes 589832 | tf_op jit(solution)/shard_map/ppermute | solution.py:291
  18.0 9.4 %collective-permute-start.6 = (bf16[48,2048]{1,0:T(8,128)(2,1)S(1)}, bf16[48,2048]{1,0:T(8,128)(2,1)S(1)}, u32[]{:S(2)}, u32[]{:S(2)}) collective-permute-start(bf16[48,2048]{1,0:T(8,128)(2,1)S(1)} %get-tuple-element.42), channel_id=1, source_target_pairs={{0,12},{4,8},{8,4},{12,0},{1,13},{5,9},{9,5},{13,1},{2,14},{6,10},... | collective-permute-start | bytes 589832 | tf_op jit(solution)/shard_map/ppermute | solution.py:291
  19.2 1.9 %copy-start = (bf16[2,384,2048]{2,1,0:T(8,128)(2,1)S(1)}, bf16[2,384,2048]{2,1,0:T(8,128)(2,1)}, u32[]{:S(2)}) copy-start(bf16[2,384,2048]{2,1,0:T(8,128)(2,1)} %down_ref.3) | copy-start | bytes 9437188
  21.1 6.3 %copy-start.9 = (bf16[2,2048,384]{2,1,0:T(8,128)(2,1)S(1)}, bf16[2,2048,384]{2,1,0:T(8,128)(2,1)}, u32[]{:S(2)}) copy-start(bf16[2,2048,384]{2,1,0:T(8,128)(2,1)} %gate_ref.1) | copy-start | bytes 9437188
  22.3 18.5 %copy-start.3 = (bf16[1,128,2048]{2,1,0:T(8,128)(2,1)S(1)}, bf16[1,128,2048]{2,1,0:T(8,128)(2,1)}, u32[]{:S(2)}) copy-start(bf16[1,128,2048]{2,1,0:T(8,128)(2,1)} %param.21) | copy-start | bytes 1572868
  22.3 18.5 %copy-start.5 = (f32[2048]{0:T(1024)S(1)}, f32[2048]{0:T(1024)}, u32[]{:S(2)}) copy-start(f32[2048]{0:T(1024)} %param.16) | copy-start | bytes 24580
  27.4 19.2 %copy-start.1 = (bf16[2,384,2048]{2,1,0:T(8,128)(2,1)S(1)}, bf16[2,384,2048]{2,1,0:T(8,128)(2,1)}, u32[]{:S(2)}) copy-start(bf16[2,384,2048]{2,1,0:T(8,128)(2,1)} %down_ref.3) | copy-start | bytes 9437188
  29.7 24.3 %copy-start.12 = (bf16[1,128,2048]{2,1,0:T(8,128)(2,1)S(1)}, bf16[1,128,2048]{2,1,0:T(8,128)(2,1)}, u32[]{:S(2)}) copy-start(bf16[1,128,2048]{2,1,0:T(8,128)(2,1)} %param.11) | copy-start | bytes 1572868
  29.7 24.3 %copy-start.15 = (s32[16]{0:T(128)S(1)}, s32[16]{0:T(128)}, u32[]{:S(2)}) copy-start(s32[16]{0:T(128)} %order_ref.3) | copy-start | bytes 196
  29.7 7.7 %collective-permute-start.10 = (bf16[48,2048]{1,0:T(8,128)(2,1)S(1)}, bf16[48,2048]{1,0:T(8,128)(2,1)S(1)}, u32[]{:S(2)}, u32[]{:S(2)}) collective-permute-start(bf16[48,2048]{1,0:T(8,128)(2,1)S(1)} %get-tuple-element.50), channel_id=1, source_target_pairs={{0,4},{4,0},{8,12},{12,8},{1,5},{5,1},{9,13},{13,9},{2,6},{6,2},{1... | collective-permute-start | bytes 589832 | tf_op jit(solution)/shard_map/ppermute | solution.py:291
  30.7 8.2 %collective-permute-start.11 = (bf16[48,2048]{1,0:T(8,128)(2,1)S(1)}, bf16[48,2048]{1,0:T(8,128)(2,1)S(1)}, u32[]{:S(2)}, u32[]{:S(2)}) collective-permute-start(bf16[48,2048]{1,0:T(8,128)(2,1)S(1)} %get-tuple-element.51), channel_id=1, source_target_pairs={{0,8},{4,12},{8,0},{12,4},{1,9},{5,13},{9,1},{13,5},{2,10},{6,14},... | collective-permute-start | bytes 589832 | tf_op jit(solution)/shard_map/ppermute | solution.py:291
  31.8 8.9 %collective-permute-start.12 = (bf16[48,2048]{1,0:T(8,128)(2,1)S(1)}, bf16[48,2048]{1,0:T(8,128)(2,1)S(1)}, u32[]{:S(2)}, u32[]{:S(2)}) collective-permute-start(bf16[48,2048]{1,0:T(8,128)(2,1)S(1)} %get-tuple-element.52), channel_id=1, source_target_pairs={{0,12},{4,8},{8,4},{12,0},{1,13},{5,9},{9,5},{13,1},{2,14},{6,10},... | collective-permute-start | bytes 589832 | tf_op jit(solution)/shard_map/ppermute | solution.py:291
  42.3 11.8 %copy-start.13 = (bf16[128,2048]{1,0:T(8,128)(2,1)S(1)}, bf16[128,2048]{1,0:T(8,128)(2,1)}, u32[]{:S(2)}) copy-start(bf16[128,2048]{1,0:T(8,128)(2,1)} %get-tuple-element.53.d_resid_ref) | copy-start | bytes 1572868
  42.3 22.6 %copy-start.7 = (f32[1,128]{1,0:T(1,128)S(1)}, f32[1,128]{1,0:T(1,128)}, u32[]{:S(2)}) copy-start(f32[1,128]{1,0:T(1,128)} %weight_ref.3) | copy-start | bytes 1540
  42.3 7.8 %collective-permute-start.16 = (f32[1,2048]{1,0:T(1,128)S(1)}, f32[1,2048]{1,0:T(1,128)S(1)}, u32[]{:S(2)}, u32[]{:S(2)}) collective-permute-start(f32[1,2048]{1,0:T(1,128)S(1)} %get-tuple-element.58), channel_id=1, source_target_pairs={{0,3},{1,2},{2,1},{3,0},{4,7},{5,6},{6,5},{7,4},{8,11},{9,10},{10,... | collective-permute-start | bytes 24584 | tf_op jit(solution)/shard_map/ppermute | solution.py:291
  45.9 4.5 %collective-permute-start.15 = (f32[1,2048]{1,0:T(1,128)S(1)}, f32[1,2048]{1,0:T(1,128)S(1)}, u32[]{:S(2)}, u32[]{:S(2)}) collective-permute-start(f32[1,2048]{1,0:T(1,128)S(1)} %get-tuple-element.58), channel_id=1, source_target_pairs={{0,2},{1,3},{2,0},{3,1},{4,6},{5,7},{6,4},{7,5},{8,10},{9,11},{10,... | collective-permute-start | bytes 24584 | tf_op jit(solution)/shard_map/ppermute | solution.py:291
  45.9 4.5 %collective-permute-start.14 = (f32[1,2048]{1,0:T(1,128)S(1)}, f32[1,2048]{1,0:T(1,128)S(1)}, u32[]{:S(2)}, u32[]{:S(2)}) collective-permute-start(f32[1,2048]{1,0:T(1,128)S(1)} %get-tuple-element.58), channel_id=1, source_target_pairs={{0,1},{1,0},{2,3},{3,2},{4,5},{5,4},{6,7},{7,6},{8,9},{9,8},{10,11... | collective-permute-start | bytes 24584 | tf_op jit(solution)/shard_map/ppermute | solution.py:291
  47.6 13.0 %collective-permute-start.7 = (bf16[48,2048]{1,0:T(8,128)(2,1)S(1)}, bf16[48,2048]{1,0:T(8,128)(2,1)S(1)}, u32[]{:S(2)}, u32[]{:S(2)}) collective-permute-start(bf16[48,2048]{1,0:T(8,128)(2,1)S(1)} %get-tuple-element.45), channel_id=1, source_target_pairs={{0,4},{4,0},{8,12},{12,8},{1,5},{5,1},{9,13},{13,9},{2,6},{6,2},{1... | collective-permute-start | bytes 589832 | tf_op jit(solution)/shard_map/ppermute | solution.py:291
  48.6 12.1 %collective-permute-start.8 = (bf16[48,2048]{1,0:T(8,128)(2,1)S(1)}, bf16[48,2048]{1,0:T(8,128)(2,1)S(1)}, u32[]{:S(2)}, u32[]{:S(2)}) collective-permute-start(bf16[48,2048]{1,0:T(8,128)(2,1)S(1)} %get-tuple-element.46), channel_id=1, source_target_pairs={{0,8},{4,12},{8,0},{12,4},{1,9},{5,13},{9,1},{13,5},{2,10},{6,14},... | collective-permute-start | bytes 589832 | tf_op jit(solution)/shard_map/ppermute | solution.py:291
  50.5 7.8 %collective-permute-start.19 = (f32[1,2048]{1,0:T(1,128)S(1)}, f32[1,2048]{1,0:T(1,128)S(1)}, u32[]{:S(2)}, u32[]{:S(2)}) collective-permute-start(f32[1,2048]{1,0:T(1,128)S(1)} %add_add_fusion.1), channel_id=1, source_target_pairs={{0,12},{4,8},{8,4},{12,0},{1,13},{5,9},{9,5},{13,1},{2,14},{6,10},... | collective-permute-start | bytes 24584 | tf_op jit(solution)/shard_map/ppermute | solution.py:291
  52.3 7.8 %collective-permute-start.18 = (f32[1,2048]{1,0:T(1,128)S(1)}, f32[1,2048]{1,0:T(1,128)S(1)}, u32[]{:S(2)}, u32[]{:S(2)}) collective-permute-start(f32[1,2048]{1,0:T(1,128)S(1)} %add_add_fusion.1), channel_id=1, source_target_pairs={{0,8},{4,12},{8,0},{12,4},{1,9},{5,13},{9,1},{13,5},{2,10},{6,14},... | collective-permute-start | bytes 24584 | tf_op jit(solution)/shard_map/ppermute | solution.py:291
  52.8 7.2 %collective-permute-start.17 = (f32[1,2048]{1,0:T(1,128)S(1)}, f32[1,2048]{1,0:T(1,128)S(1)}, u32[]{:S(2)}, u32[]{:S(2)}) collective-permute-start(f32[1,2048]{1,0:T(1,128)S(1)} %add_add_fusion.1), channel_id=1, source_target_pairs={{0,4},{4,0},{8,12},{12,8},{1,5},{5,1},{9,13},{13,9},{2,6},{6,2},{1... | collective-permute-start | bytes 24584 | tf_op jit(solution)/shard_map/ppermute | solution.py:291
  58.3 6.6 %collective-permute-start.9 = (bf16[48,2048]{1,0:T(8,128)(2,1)S(1)}, bf16[48,2048]{1,0:T(8,128)(2,1)S(1)}, u32[]{:S(2)}, u32[]{:S(2)}) collective-permute-start(bf16[48,2048]{1,0:T(8,128)(2,1)S(1)} %get-tuple-element.47), channel_id=1, source_target_pairs={{0,12},{4,8},{8,4},{12,0},{1,13},{5,9},{9,5},{13,1},{2,14},{6,10},... | collective-permute-start | bytes 589832 | tf_op jit(solution)/shard_map/ppermute | solution.py:291
  60.1 6.8 %collective-permute-start.13 = (bf16[128,512]{1,0:T(8,128)(2,1)S(1)}, bf16[128,512]{1,0:T(8,128)(2,1)S(1)}, u32[]{:S(2)}, u32[]{:S(2)}) collective-permute-start(bf16[128,512]{1,0:T(8,128)(2,1)S(1)} %get-tuple-element.56), channel_id=1, source_target_pairs={{0,16},{16,0},{1,17},{17,1},{2,18},{18,2},{3,19},{19,3},{4,20},{20... | collective-permute-start | bytes 393224 | tf_op jit(solution)/shard_map/ppermute | solution.py:291
  60.1 6.1 %collective-permute-start.20 = (f32[1,2048]{1,0:T(1,128)S(1)}, f32[1,2048]{1,0:T(1,128)S(1)}, u32[]{:S(2)}, u32[]{:S(2)}) collective-permute-start(f32[1,2048]{1,0:T(1,128)S(1)} %add_add_fusion), channel_id=1, source_target_pairs={{0,16},{16,0},{1,17},{17,1},{2,18},{18,2},{3,19},{19,3},{4,20},{20... | collective-permute-start | bytes 24584 | tf_op jit(solution)/shard_map/ppermute | solution.py:291
  (5 other events, 3.7 us)

commit v2 on v1

v2 whole, which is shorter than its diff:
```python
import functools

import jax
import jax.numpy as jnp
from jax import lax
from jax.experimental import pallas as pl
from jax.experimental.pallas import tpu as pltpu
from jax.sharding import PartitionSpec as P

D = 2048
HEAD_SIZE = 128
QUERY_HEADS = 16
KEY_VALUE_HEADS = 2
GROUP = QUERY_HEADS // KEY_VALUE_HEADS
FFE = 384
EXP_DEV = 2
COLS = 256
SCALE = HEAD_SIZE ** (-0.5)
EXP2_SCALE = SCALE * 1.4426950408889634
F32 = jnp.float32
BF16 = jnp.bfloat16
NN = (((1,), (0,)), ((), ()))
NT = (((1,), (1,)), ((), ()))
MIB = 1 << 20
VMEM, HBM = pltpu.VMEM, pltpu.HBM


def mm(a, b, dims=NN):
    return lax.dot_general(a, b, dims, preferred_element_type=F32)


def iota(shape, dim):
    return lax.broadcasted_iota(jnp.int32, shape, dim)


def row_to_col(row):
    n = row.shape[1]
    eye = iota((n, n), 0) == iota((n, n), 1)
    return jnp.sum(jnp.where(eye, row, jnp.zeros((), row.dtype)), axis=1, keepdims=True)


def col_to_row(col):
    n = col.shape[0]
    eye = iota((n, n), 0) == iota((n, n), 1)
    return jnp.sum(jnp.where(eye, col, jnp.zeros((), col.dtype)), axis=0, keepdims=True)


def block_positions(order_ref, ctx_index, tokens):
    span = tokens // 8
    index = iota((1, tokens), 1)
    which = index // span
    start = jnp.zeros((1, tokens), jnp.int32)
    for b in range(8):
        start = jnp.where(which == b, order_ref[ctx_index * 8 + b], start)
    return start * span + index % span


def stacked(refs, cols=slice(None)):
    parts = [r[:, cols] for r in refs]
    return parts[0] if len(parts) == 1 else jnp.concatenate(parts, axis=0)


def column_blocks(width=D, step=COLS):
    return [slice(c, c + step) for c in range(0, width, step)]


def store_pieces(refs, cols, rows_value):
    at = 0
    for r in refs:
        n = r.shape[0]
        r[:, cols] = rows_value[at : at + n]
        at += n


def pair_cols(pair):
    start = 2 * pair * HEAD_SIZE
    return slice(start, start + HEAD_SIZE), slice(start + HEAD_SIZE, start + 2 * HEAD_SIZE)


def head_pair(ref, pair):
    first, second = pair_cols(pair)
    return jnp.concatenate([ref[:, first], ref[:, second]], axis=0)


def placement_rows(slot_row, slots):
    tokens = slot_row.shape[1]
    return jnp.where(iota((slots, tokens), 0) == slot_row, 1.0, 0.0).astype(BF16)


def placement_cols(slot_row, slots):
    tokens = slot_row.shape[1]
    slot_col = row_to_col(slot_row)
    return jnp.where(iota((tokens, slots), 1) == slot_col, 1.0, 0.0).astype(BF16)


def dispatch_kernel(count, experts, capacity, *refs):
    sources, refs = refs[:9], refs[9:]
    targets, refs = refs[:6], refs[6:]
    grad_ref = targets[0]
    slot_ref, pos_ref, weight_ref = refs[:3]
    send_refs = refs[3:-3]
    order_ref, routes_ref, sems = refs[-3:]
    targets = targets + (weight_ref, routes_ref, order_ref)
    copies = [
        pltpu.make_async_copy(source, target, sems.at[i])
        for i, (source, target) in enumerate(zip(sources, targets))
    ]
    for copy in copies[::-1]:
        copy.start()
    for copy in copies[:5:-1]:
        copy.wait()
    tokens = routes_ref.shape[1]
    chosen = routes_ref[...]
    lanes = max(experts, 16)
    hits = jnp.where(iota((lanes, tokens), 0) == chosen, 1.0, 0.0)
    before = jnp.where(iota((tokens, tokens), 0) < iota((tokens, tokens), 1), 1.0, 0.0)
    earlier = mm(hits.astype(BF16), before.astype(BF16))
    rank = jnp.sum(hits * earlier, axis=0, keepdims=True).astype(jnp.int32)
    target = (chosen // EXP_DEV) ^ lax.axis_index("exp")
    slot = (target * EXP_DEV + chosen % EXP_DEV) * capacity + rank
    slot_ref[...] = slot
    me = lax.axis_index("ctx")
    for s in range(count):
        pos_ref[s : s + 1, :] = block_positions(order_ref, me ^ s, tokens)
    place = placement_rows(slot, experts * capacity)
    weight = row_to_col(weight_ref[...])
    copies[0].wait()
    for cols in column_blocks():
        scaled = (weight * grad_ref[:, cols].astype(F32)).astype(BF16)
        store_pieces(send_refs, cols, mm(place, scaled).astype(BF16))
    for copy in copies[1:6]:
        copy.wait()


def kv_stacks(key_refs, value_refs, g):
    cols = slice(g * HEAD_SIZE, (g + 1) * HEAD_SIZE)
    return stacked(key_refs, cols), stacked(value_refs, cols)


def attention_kernel(
    count, pieces, pos_ref, slot_ref, gain_ref, query_ref, resid_ref, down_hbm, *refs
):
    key_refs, value_refs = refs[:count], refs[count : 2 * count]
    hidden_ref, down_ref = refs[2 * count : 2 * count + 2]
    send_refs = refs[2 * count + 2 : -1]
    down_copy = pltpu.make_async_copy(down_hbm, down_ref, refs[-1])
    down_copy.start()
    tokens = query_ref.shape[0]
    query_pos = row_to_col(pos_ref[:1, :])
    bias = jnp.concatenate(
        [jnp.where(pos_ref[s : s + 1, :] <= query_pos, 0.0, -1e30) for s in range(count)],
        axis=1,
    )
    length = count * tokens
    ones = jnp.ones((length, HEAD_SIZE), BF16)
    total = jnp.zeros((tokens, HEAD_SIZE), F32)
    for g in range(KEY_VALUE_HEADS):
        keys, values = kv_stacks(key_refs, value_refs, g)
        values = jnp.concatenate([values, ones], axis=1)
        for h in range(g * GROUP, (g + 1) * GROUP):
            cols = slice(h * HEAD_SIZE, (h + 1) * HEAD_SIZE)
            scores = mm(query_ref[:, cols], keys, NT) + bias
            peak = jnp.max(scores, axis=1, keepdims=True)
            weights = jnp.exp2((scores - peak) * EXP2_SCALE).astype(BF16)
            mixed = mm(weights, values)
            attended = mixed[:, :HEAD_SIZE] / mixed[:, HEAD_SIZE:]
            hidden = (resid_ref[:, cols].astype(F32) + attended).astype(BF16)
            hidden_ref[:, cols] = hidden
            wide = hidden.astype(F32)
            total = total + wide * wide
    inv_rms = lax.rsqrt(jnp.sum(total, axis=1, keepdims=True) * (1.0 / D) + 1e-06)
    slots = sum(r.shape[0] for r in send_refs)
    place = placement_rows(slot_ref[...], slots)
    for cols in column_blocks():
        normed = (hidden_ref[:, cols].astype(F32) * inv_rms * gain_ref[:, cols]).astype(BF16)
        store_pieces(send_refs, cols, mm(place, normed).astype(BF16))
    down_copy.wait()


def first_expert_rows(slots, capacity):
    return iota((slots, 1), 0) % (EXP_DEV * capacity) < capacity


def probs_kernel(count, capacity, pieces, pos_ref, down_ref, gate_hbm, query_ref, *refs):
    key_refs = refs[:count]
    grad_refs = refs[count : count + pieces]
    d_act_ref, probs_ref, gate_ref, sem = refs[count + pieces :]
    gate_copy = pltpu.make_async_copy(gate_hbm, gate_ref, sem)
    gate_copy.start()
    grads = stacked(grad_refs)
    first = first_expert_rows(grads.shape[0], capacity)
    d_act_ref[...] = jnp.where(first, mm(grads, down_ref[0], NT), mm(grads, down_ref[1], NT))
    query_pos = pos_ref[:1, :]
    bias = jnp.concatenate(
        [
            jnp.where(row_to_col(pos_ref[s : s + 1, :]) <= query_pos, 0.0, -1e30)
            for s in range(count)
        ],
        axis=0,
    )
    bias = jnp.concatenate([bias, bias], axis=1)
    for g in range(KEY_VALUE_HEADS):
        keys = stacked(key_refs, slice(g * HEAD_SIZE, (g + 1) * HEAD_SIZE))
        for pair in range(g * GROUP // 2, (g + 1) * GROUP // 2):
            scores = mm(keys, head_pair(query_ref, pair), NT) + bias
            peak = jnp.max(scores, axis=0, keepdims=True)
            weights = jnp.exp2((scores - peak) * EXP2_SCALE)
            probs_ref[pair] = weights * (1.0 / jnp.sum(weights, axis=0, keepdims=True))
    gate_copy.wait()


def expert_back_kernel(capacity, pieces, gate_ref, d_act_ref, *refs):
    rows = stacked(refs[:pieces])
    act_ref = refs[pieces]
    out_refs = refs[pieces + 1 :]
    first = first_expert_rows(rows.shape[0], capacity)
    pre = jnp.where(first, mm(rows, gate_ref[0]), mm(rows, gate_ref[1]))
    gate = 1.0 / (1.0 + jnp.exp(-pre))
    act = pre * gate
    act_ref[:, :FFE] = jnp.where(first, act, 0.0).astype(BF16)
    act_ref[:, FFE:] = jnp.where(first, 0.0, act).astype(BF16)
    d_pre = d_act_ref[...] * gate * (1.0 + pre * (1.0 - gate))
    d_first = jnp.where(first, d_pre, 0.0).astype(BF16)
    d_second = jnp.where(first, 0.0, d_pre).astype(BF16)
    for cols in column_blocks():
        back = mm(d_first, gate_ref[0, cols, :], NT) + mm(d_second, gate_ref[1, cols, :], NT)
        store_pieces(out_refs, cols, back.astype(BF16))


def expert_out_kernel(pieces, down_ref, act_ref, gain_ref, *refs):
    row_refs, dn_refs = refs[:pieces], refs[pieces : 2 * pieces]
    gain_out_ref = refs[2 * pieces]
    out_refs = refs[2 * pieces + 1 :]
    act = act_ref[...]
    for cols in column_blocks():
        y = mm(act[:, :FFE], down_ref[0, :, cols]) + mm(act[:, FFE:], down_ref[1, :, cols])
        store_pieces(out_refs, cols, y.astype(BF16))
        terms = stacked(row_refs, cols).astype(F32) * stacked(dn_refs, cols).astype(F32)
        gain_out_ref[:, cols] = jnp.sum(terms, axis=0, keepdims=True) / gain_ref[:, cols]


def backward_kernel(count, pieces, slot_ref, gain_ref, hidden_ref, grad_ref, query_ref, probs_ref, *refs):
    dn_refs = refs[:pieces]
    key_refs = refs[pieces : pieces + count]
    value_refs = refs[pieces + count : pieces + 2 * count]
    resid_hbm, dq_hbm, own_ref = refs[pieces + 2 * count : pieces + 2 * count + 3]
    other_refs = refs[pieces + 2 * count + 3 : -4]
    resid_ref, dq_ref, dn_scratch, sems = refs[-4:]
    tokens = hidden_ref.shape[0]
    slots = sum(r.shape[0] for r in dn_refs)
    place = placement_cols(slot_ref[...], slots)
    square = jnp.zeros((tokens, COLS), F32)
    mixing = jnp.zeros((tokens, COLS), F32)
    for cols in column_blocks():
        dn = mm(place, stacked(dn_refs, cols)) * gain_ref[:, cols]
        dn_scratch[:, cols] = dn
        hidden = hidden_ref[:, cols].astype(F32)
        square = square + hidden * hidden
        mixing = mixing + dn * hidden
    inv_rms = lax.rsqrt(jnp.sum(square, axis=1, keepdims=True) * (1.0 / D) + 1e-06)
    mean_mix = jnp.sum(mixing, axis=1, keepdims=True) * (1.0 / D)
    factor = inv_rms * inv_rms * inv_rms * mean_mix
    for cols in column_blocks():
        resid_ref[:, cols] = (
            grad_ref[:, cols].astype(F32)
            + dn_scratch[:, cols] * inv_rms
            - hidden_ref[:, cols].astype(F32) * factor
        ).astype(BF16)
    copies = [pltpu.make_async_copy(resid_ref, resid_hbm, sems.at[0])]
    copies[0].start()
    length = count * tokens
    group_width = GROUP * HEAD_SIZE
    for g in range(KEY_VALUE_HEADS):
        keys, values = kv_stacks(key_refs, value_refs, g)
        keys_t = jnp.transpose(keys.astype(F32)).astype(BF16)
        d_keys = jnp.zeros((length, HEAD_SIZE), F32)
        d_values = jnp.zeros((length, HEAD_SIZE), F32)
        for pair in range(g * GROUP // 2, (g + 1) * GROUP // 2):
            cols_a, cols_b = pair_cols(pair)
            d_out = head_pair(resid_ref, pair)
            probs = probs_ref[pair]
            d_probs = mm(values, d_out, NT)
            row_dot = jnp.sum(probs * d_probs, axis=0, keepdims=True)
            d_scores = (probs * (d_probs - row_dot)).astype(BF16)
            d_keys = d_keys + mm(d_scores, head_pair(query_ref, pair))
            d_values = d_values + mm(probs.astype(BF16), d_out)
            d_query_t = mm(keys_t, d_scores) * SCALE
            dq_ref[:, cols_a] = jnp.transpose(d_query_t[:, :tokens]).astype(BF16)
            dq_ref[:, cols_b] = jnp.transpose(d_query_t[:, tokens:]).astype(BF16)
        cols = slice(g * group_width, (g + 1) * group_width)
        copy = pltpu.make_async_copy(dq_ref.at[:, cols], dq_hbm.at[:, cols], sems.at[1 + g])
        copy.start()
        copies.append(copy)
        k_cols = slice(g * HEAD_SIZE, (g + 1) * HEAD_SIZE)
        v_cols = slice((KEY_VALUE_HEADS + g) * HEAD_SIZE, (KEY_VALUE_HEADS + g + 1) * HEAD_SIZE)
        d_keys = d_keys * SCALE
        own_ref[:, k_cols] = d_keys[:tokens]
        own_ref[:, v_cols] = d_values[:tokens]
        for s, ref in enumerate(other_refs, 1):
            ref[:, k_cols] = d_keys[s * tokens : (s + 1) * tokens].astype(BF16)
            ref[:, v_cols] = d_values[s * tokens : (s + 1) * tokens].astype(BF16)
    for copy in copies:
        copy.wait()


def output_kernel(
    count,
    pieces,
    tokens_in_all,
    slot_ref,
    weight_ref,
    gain_ref,
    hidden_ref,
    grad_ref,
    own_ref,
    *refs,
):
    arrived_refs = refs[: count - 1]
    y_refs = refs[count - 1 : count - 1 + pieces]
    out_hbm, dk_hbm, dv_hbm, d_weight_hbm, d_gain_hbm = refs[count - 1 + pieces : -6]
    out_ref, dk_ref, dv_ref, d_weight_ref, d_gain_ref, sems = refs[-6:]
    split = KEY_VALUE_HEADS * HEAD_SIZE
    d_kv = own_ref[...]
    for ref in arrived_refs:
        d_kv = d_kv + ref[...].astype(F32)
    dk_ref[...] = d_kv[:, :split].astype(BF16)
    dv_ref[...] = d_kv[:, split:].astype(BF16)
    d_gain_ref[...] = gain_ref[...] * (1.0 / tokens_in_all)
    copies = []

    def send(source, target):
        copy = pltpu.make_async_copy(source, target, sems.at[len(copies)])
        copy.start()
        copies.append(copy)

    send(dk_ref, dk_hbm)
    send(dv_ref, dv_hbm)
    send(d_gain_ref, d_gain_hbm)
    tokens = hidden_ref.shape[0]
    slots = sum(r.shape[0] for r in y_refs)
    place = placement_cols(slot_ref[...], slots)
    weight = row_to_col(weight_ref[...])
    total = jnp.zeros((tokens, COLS), F32)
    for cols in column_blocks():
        y = mm(place, stacked(y_refs, cols))
        out_ref[:, cols] = (hidden_ref[:, cols].astype(F32) + weight * y).astype(BF16)
        send(out_ref.at[:, cols], out_hbm.at[:, cols])
        total = total + y * grad_ref[:, cols].astype(F32)
    d_weight_ref[...] = col_to_row(jnp.sum(total, axis=1, keepdims=True))
    send(d_weight_ref, d_weight_hbm)
    for copy in copies:
        copy.wait()


def run(kernel, name, inputs, outputs, flops, scratch=(), limit=20 * MIB):
    nbytes = sum(x.size * x.dtype.itemsize for _, x in inputs) + sum(
        x.size * x.dtype.itemsize for _, x in outputs
    )
    spec = {space: pl.BlockSpec(memory_space=space) for space in (VMEM, HBM)}
    return pl.pallas_call(
        kernel,
        out_shape=[x for _, x in outputs],
        in_specs=[spec[space] for space, _ in inputs],
        out_specs=[spec[space] for space, _ in outputs],
        scratch_shapes=list(scratch),
        compiler_params=pltpu.CompilerParams(vmem_limit_bytes=limit),
        cost_estimate=pl.CostEstimate(flops=flops, bytes_accessed=nbytes, transcendentals=0),
        name=name,
    )(*[pltpu.with_memory_space_constraint(x, HBM) if space is HBM else x for space, x in inputs])


def placed(space, arrays):
    return [(space, x) for x in arrays]


def pairwise(value, axis, step):
    count = lax.axis_size(axis)
    return lax.ppermute(value, axis, [(i, i ^ step) for i in range(count)])


def exchange(pieces, capacity):
    count = lax.axis_size("exp")
    rows = EXP_DEV * capacity
    if len(pieces) == count:
        return [pieces[0]] + [pairwise(pieces[s], "exp", s) for s in range(1, count)]
    flat = pieces[0]
    blocks = [flat[s * rows : (s + 1) * rows] for s in range(count)]
    moved = [blocks[0]] + [pairwise(blocks[s], "exp", s) for s in range(1, count)]
    return [jnp.concatenate(moved, axis=0)]


def sum_over(value, axis):
    step = 1
    while step < lax.axis_size(axis):
        value = value + pairwise(value, axis, step)
        step *= 2
    return value


def shaped(shape, dtype):
    return jax.ShapeDtypeStruct(shape, dtype)


def per_device(
    queries,
    keys,
    values,
    resid,
    block_order,
    norm_gain,
    w_gate,
    w_down,
    routes,
    route_weight,
    d_out,
):
    query_rows = queries[0]
    resid_rows = resid[0]
    grad_rows = d_out[0]
    tokens = query_rows.shape[0]
    chosen = routes.reshape(1, tokens)
    gain = norm_gain.reshape(1, D)
    ctx_count = lax.axis_size("ctx")
    exp_count = lax.axis_size("exp")
    experts = EXP_DEV * exp_count
    capacity = 3 * tokens // (2 * experts)
    slots = experts * capacity
    rows = EXP_DEV * capacity
    piece_count = exp_count if rows % 16 == 0 else 1
    piece_shapes = [shaped((slots // piece_count, D), BF16)] * piece_count
    token_shape = shaped((tokens, D), BF16)
    kv_width = 2 * KEY_VALUE_HEADS * HEAD_SIZE
    attn_flops = 4 * tokens * ctx_count * tokens * QUERY_HEADS * HEAD_SIZE
    place_flops = 2 * slots * tokens * D
    expert_flops = 2 * slots * D * FFE * EXP_DEV

    own_keys, own_values = keys[0], values[0]
    all_keys = [own_keys] + [pairwise(own_keys, "ctx", s) for s in range(1, ctx_count)]
    all_values = [own_values] + [pairwise(own_values, "ctx", s) for s in range(1, ctx_count)]

    near = [grad_rows, query_rows, resid_rows, own_keys, own_values, gain]
    grad_rows, query_rows, resid_rows, own_keys, own_values, gain, slot, pos, weight, *send_grad = run(
        functools.partial(dispatch_kernel, ctx_count, experts, capacity),
        "dispatch_grads",
        placed(HBM, near + [route_weight, chosen, block_order]),
        placed(
            VMEM,
            [shaped(x.shape, x.dtype) for x in near]
            + [
                shaped((1, tokens), jnp.int32),
                shaped((ctx_count, tokens), jnp.int32),
                shaped((1, tokens), F32),
            ]
            + piece_shapes,
        ),
        place_flops,
        scratch=[
            pltpu.SMEM(block_order.shape, jnp.int32),
            pltpu.VMEM((1, tokens), jnp.int32),
            pltpu.SemaphoreType.DMA((9,)),
        ],
    )
    all_keys[0], all_values[0] = own_keys, own_values
    arrived_grad = exchange(send_grad, capacity)

    hidden, down_near, *send_x = run(
        functools.partial(attention_kernel, ctx_count, piece_count),
        "attention_forward",
        placed(VMEM, [pos, slot, gain, query_rows, resid_rows])
        + placed(HBM, [w_down])
        + placed(VMEM, all_keys + all_values),
        placed(VMEM, [token_shape, shaped(w_down.shape, BF16)] + piece_shapes),
        attn_flops + place_flops,
        scratch=[pltpu.SemaphoreType.DMA(())],
    )
    arrived_x = exchange(send_x, capacity)

    d_act, probs, gate_near = run(
        functools.partial(probs_kernel, ctx_count, capacity, piece_count),
        "act_grads_and_probs",
        placed(VMEM, [pos, down_near])
        + placed(HBM, [w_gate])
        + placed(VMEM, [query_rows] + all_keys + arrived_grad),
        placed(
            VMEM,
            [
                shaped((slots, FFE), F32),
                shaped((QUERY_HEADS // 2, ctx_count * tokens, 2 * tokens), F32),
                shaped(w_gate.shape, BF16),
            ],
        ),
        expert_flops + attn_flops // 2,
        scratch=[pltpu.SemaphoreType.DMA(())],
    )
    act, *send_dn = run(
        functools.partial(expert_back_kernel, capacity, piece_count),
        "expert_backward",
        placed(VMEM, [gate_near, d_act] + arrived_x),
        placed(VMEM, [shaped((slots, EXP_DEV * FFE), BF16)] + piece_shapes),
        2 * expert_flops,
    )
    dn = exchange(send_dn, capacity)
    gain_part, *send_y = run(
        functools.partial(expert_out_kernel, piece_count),
        "expert_output",
        placed(VMEM, [down_near, act, gain] + arrived_x + send_dn),
        placed(VMEM, [shaped((1, D), F32)] + piece_shapes),
        expert_flops,
    )
    returned = exchange(send_y, capacity)
    gain_part, slot = lax.optimization_barrier((sum_over(gain_part, "dp"), slot))
    for axis in ("exp", "ctx"):
        gain_part = sum_over(gain_part, axis)

    d_hidden, d_queries, kv_own, *kv_send = run(
        functools.partial(backward_kernel, ctx_count, piece_count),
        "residual_attention_backward",
        placed(VMEM, [slot, gain, hidden, grad_rows, query_rows, probs] + dn + all_keys + all_values),
        placed(HBM, [token_shape] * 2)
        + placed(
            VMEM,
            [shaped((tokens, kv_width), F32)]
            + [shaped((tokens, kv_width), BF16)] * (ctx_count - 1),
        ),
        2 * attn_flops + place_flops,
        scratch=[
            pltpu.VMEM((tokens, D), BF16),
            pltpu.VMEM((tokens, D), BF16),
            pltpu.VMEM((tokens, D), F32),
            pltpu.SemaphoreType.DMA((1 + KEY_VALUE_HEADS,)),
        ],
    )
    kv_arrived = [pairwise(part, "ctx", s) for s, part in enumerate(kv_send, 1)]

    kv_shape = shaped((tokens, kv_width // 2), BF16)
    final_shapes = [token_shape, kv_shape, kv_shape, shaped((1, tokens), F32), shaped((1, D), F32)]
    total_tokens = tokens * ctx_count * exp_count * lax.axis_size("dp")
    layer_out, d_keys, d_values, d_weight, d_gain = run(
        functools.partial(output_kernel, ctx_count, piece_count, total_tokens),
        "layer_output",
        placed(
            VMEM,
            [slot, weight, gain_part, hidden, grad_rows, kv_own] + kv_arrived + returned,
        ),
        placed(HBM, final_shapes),
        place_flops,
        scratch=[pltpu.VMEM(x.shape, x.dtype) for x in final_shapes]
        + [pltpu.SemaphoreType.DMA((4 + D // COLS,))],
    )
    return (
        layer_out[None],
        d_hidden[None],
        d_queries[None],
        d_keys[None],
        d_values[None],
        d_weight,
        d_gain[0],
    )


def solution(mesh):
    in_specs = (
        P(("exp", "dp"), "ctx", None),
        P(("exp", "dp"), "ctx", None),
        P(("exp", "dp"), "ctx", None),
        P(("exp", "dp"), "ctx", None),
        P(),
        P(),
        P("exp", None, None),
        P("exp", None, None),
        P(("exp", "dp"), "ctx", None),
        P(("exp", "dp"), "ctx"),
        P(("exp", "dp"), "ctx", None),
    )
    out_specs = (
        P(("exp", "dp"), "ctx", None),
        P(("exp", "dp"), "ctx", None),
        P(("exp", "dp"), "ctx", None),
        P(("exp", "dp"), "ctx", None),
        P(("exp", "dp"), "ctx", None),
        P(("exp", "dp"), "ctx"),
        P(),
    )
    return jax.shard_map(
        per_device, mesh=mesh, in_specs=in_specs, out_specs=out_specs, check_vma=False
    )
```

time: 67.9 us -> 57 us (0.84)
  local copies, waits for them, and re-layouts: 8.37 us -> 0 us
  starting transfers between devices: 24.5 us -> 22.9 us
  Pallas kernels: 14 us -> 15.6 us
  other arithmetic: 1.56 us -> 0.05 us
  waiting for transfers between devices: 18.4 us -> 17.4 us
    unnamed x32 -> x0, local copies, waits for them, and re-layouts: 7.71 us -> none
    pallas_call x8 -> x7, Pallas kernels: 14 us -> 15.6 us  [run(): pl.pallas_call(kernel, out_shape=[x for _, x in outputs], in_specs=[spec[...]
    ppermute x21 -> x20, starting transfers between devices: 24.5 us -> 22.9 us  [pairwise(): return lax.ppermute(value, axis, [(i, i ^ step) for i in range(count)])]
    ppermute x21 -> x20, waiting for transfers between devices: 18.4 us -> 17.4 us  [pairwise(): return lax.ppermute(value, axis, [(i, i ^ step) for i in range(count)])]
    concatenate x1 -> x0, other arithmetic: 0.88 us -> none  [per_device(): own_kv = jnp.concatenate([keys[0], values[0]], axis=1)]
  transfers between devices with their start and end apart: 21 -> 20, of which waited for: 7 -> 7; matrix products, arithmetic and copies ran while one was open for 2% -> 0% of each run, Pallas kernels for 14% -> 18%
where the time goes in v2:
time: 57 us; the launch traced here: 56.8 us
  starting transfers between devices  22.9 us (40%)
  waiting for transfers between devices  17.4 us (31%)
  Pallas kernels  15.6 us (27%)
  between operations  0.78 us (1%)
    ppermute x20, starting transfers between devices, pairwise(): return lax.ppermute(value, axis, [(i, i ^ step) for i in range(count)])  22.9 us
    ppermute x20, waiting for transfers between devices, pairwise(): return lax.ppermute(value, axis, [(i, i ^ step) for i in range(count)])  17.4 us
    pallas_call x7, Pallas kernels, run(): pl.pallas_call(kernel, out_shape=[x for _, x in outputs], in_specs=[spec[...  15.6 us
  transfers between devices with their start and end apart: 20, of which 7 were waited for; matrix products, arithmetic and copies ran while one was open for 0% of the time, Pallas kernels for 18%

profile of v2, /device:TPU:0, one launch (start us, length us, event | category | flops | bytes accessed | tf_op | source)
XLA Modules:
  0.0 56.8 jit_solution(17434775691231587622)
XLA Ops:
  0.6 1.9 %dispatch_grads.1 = (bf16[128,2048]{1,0:T(8,128)(2,1)S(1)}, bf16[128,2048]{1,0:T(8,128)(2,1)S(1)}, bf16[128,2048]{1,0:T(8,128)(2,1)S(1)}, bf16[128,256]{1,0:T(8,...) custom-call(bf16[128,2048]{1,0:T(8,128)(2,1)} %bitcast.13, ...), custom_call_target="tpu_custom_call" | custom-call | flops 100663296 | bytes 4213824 | tf_op jit(solution)/shard_map/dispatch_grads/pallas_call | solution.py:360
  2.6 3.0 %collective-permute-start.2 = (bf16[48,2048]{1,0:T(8,128)(2,1)S(1)}, bf16[48,2048]{1,0:T(8,128)(2,1)S(1)}, u32[]{:S(2)}, u32[]{:S(2)}) collective-permute-start(bf16[48,2048]{1,0:T(8,128)(2,1)S(1)} %get-tuple-element.59), channel_id=1, source_target_pairs={{0,4},{4,0},{8,12},{12,8},{1,5},{5,1},{9,13},{13,9},{2,6},{6,2},{1... | collective-permute-start | bytes 589832 | tf_op jit(solution)/shard_map/ppermute | solution.py:378
  5.6 0.5 collective-permute-start.1
  6.1 1.5 %collective-permute-start.3 = (bf16[48,2048]{1,0:T(8,128)(2,1)S(1)}, bf16[48,2048]{1,0:T(8,128)(2,1)S(1)}, u32[]{:S(2)}, u32[]{:S(2)}) collective-permute-start(bf16[48,2048]{1,0:T(8,128)(2,1)S(1)} %get-tuple-element.60), channel_id=1, source_target_pairs={{0,8},{4,12},{8,0},{12,4},{1,9},{5,13},{9,1},{13,5},{2,10},{6,14},... | collective-permute-start | bytes 589832 | tf_op jit(solution)/shard_map/ppermute | solution.py:378
  7.6 2.7 %attention_forward.1 = (bf16[128,2048]{1,0:T(8,128)(2,1)S(1)}, bf16[2,384,2048]{2,1,0:T(8,128)(2,1)S(1)}, bf16[48,2048]{1,0:T(8,128)(2,1)S(1)}, bf16[48,2048]{1,...) custom-call(s32[2,128]{1,0:T(2,128)S(1)} %get-tuple-element.50.pos_ref, ...), custom_call_target="tpu_custom_call" | custom-call | flops 369098752 | bytes 8922624 | tf_op jit(solution)/shard_map/attention_forward/pallas_call | solution.py:360
  10.4 2.0 %collective-permute-start.5 = (bf16[48,2048]{1,0:T(8,128)(2,1)S(1)}, bf16[48,2048]{1,0:T(8,128)(2,1)S(1)}, u32[]{:S(2)}, u32[]{:S(2)}) collective-permute-start(bf16[48,2048]{1,0:T(8,128)(2,1)S(1)} %get-tuple-element.65), channel_id=1, source_target_pairs={{0,4},{4,0},{8,12},{12,8},{1,5},{5,1},{9,13},{13,9},{2,6},{6,2},{1... | collective-permute-start | bytes 589832 | tf_op jit(solution)/shard_map/ppermute | solution.py:378
  12.4 1.5 %collective-permute-start.6 = (bf16[48,2048]{1,0:T(8,128)(2,1)S(1)}, bf16[48,2048]{1,0:T(8,128)(2,1)S(1)}, u32[]{:S(2)}, u32[]{:S(2)}) collective-permute-start(bf16[48,2048]{1,0:T(8,128)(2,1)S(1)} %get-tuple-element.66), channel_id=1, source_target_pairs={{0,8},{4,12},{8,0},{12,4},{1,9},{5,13},{9,1},{13,5},{2,10},{6,14},... | collective-permute-start | bytes 589832 | tf_op jit(solution)/shard_map/ppermute | solution.py:378
  13.9 0.4 collective-permute-start.7
  14.3 3.7 %collective-permute-done.3.refs_4_ = bf16[48,2048]{1,0:T(8,128)(2,1)S(1)} collective-permute-done((bf16[48,2048]{1,0:T(8,128)(2,1)S(1)}, bf16[48,2048]{1,0:T(8,128)(2,1)S(1)}, u32[]{:S(2)}, u32[]{:S(2)}) %collective-permute-start.3) | collective-permute-done | bytes 196640 | tf_op jit(solution)/shard_map/ppermute | solution.py:378
  18.1 2.3 %act_grads_and_probs.1 = (f32[192,384]{1,0:T(8,128)S(1)}, f32[8,256,256]{2,1,0:T(8,128)S(1)}, bf16[2,2048,384]{2,1,0:T(8,128)(2,1)S(1)}) custom-call(s32[2,128]{1,0:T(2,128)S(1)} %get-tuple-element.50.pos_ref, bf16[2,384,2048]{2,1,0:T(8,128)(2,1)S(1)} %get-tuple-element.57.down_ref, bf16[2,2048,384]{2,1,0:T(8,128)(2,1)} %gate_hbm.1, ...), custom_call_target="tpu_custom_call" | custom-call | flops 738197504 | bytes 13272064 | tf_op jit(solution)/shard_map/act_grads_and_probs/pallas_call | solution.py:360
  20.4 5.1 %collective-permute-done.6.refs_2_ = bf16[48,2048]{1,0:T(8,128)(2,1)S(1)} collective-permute-done((bf16[48,2048]{1,0:T(8,128)(2,1)S(1)}, bf16[48,2048]{1,0:T(8,128)(2,1)S(1)}, u32[]{:S(2)}, u32[]{:S(2)}) %collective-permute-start.6) | collective-permute-done | bytes 196640 | tf_op jit(solution)/shard_map/ppermute | solution.py:378
  25.5 2.3 %expert_backward.1 = (bf16[192,768]{1,0:T(8,128)(2,1)S(1)}, bf16[48,2048]{1,0:T(8,128)(2,1)S(1)}, bf16[48,2048]{1,0:T(8,128)(2,1)S(1)}, bf16[48,2048]{1,0:T(8,128)(2,1)S(1)}, bf16[48,2048]{1,0:T(8,128)(2,1)S(1)}) custom-call(bf16[2,2048,384]{2,1,0:T(8,128)(2,1)S(1)} %get-tuple-element.62.gate_ref, f32[192,384]{1,0:T(8,128)S(1)} %get-tuple-element.63.d_act_ref, ...), custom_call_target="tpu_custom_call" | custom-call | flops 1207959552 | bytes 5308416 | tf_op jit(solution)/shard_map/expert_backward/pallas_call | solution.py:360
  27.8 0.4 collective-permute-start.13
  28.2 1.7 %collective-permute-start.14 = (bf16[48,2048]{1,0:T(8,128)(2,1)S(1)}, bf16[48,2048]{1,0:T(8,128)(2,1)S(1)}, u32[]{:S(2)}, u32[]{:S(2)}) collective-permute-start(bf16[48,2048]{1,0:T(8,128)(2,1)S(1)} %get-tuple-element.71.refs_6_), channel_id=1, source_target_pairs={{0,8},{4,12},{8,0},{12,4},{1,9},{5,13},{9,1},{13,5},{2,10},{6,14},... | collective-permute-start | bytes 589832 | tf_op jit(solution)/shard_map/ppermute | solution.py:378
  30.0 1.4 %collective-permute-start.15 = (bf16[48,2048]{1,0:T(8,128)(2,1)S(1)}, bf16[48,2048]{1,0:T(8,128)(2,1)S(1)}, u32[]{:S(2)}, u32[]{:S(2)}) collective-permute-start(bf16[48,2048]{1,0:T(8,128)(2,1)S(1)} %get-tuple-element.72.refs_7_), channel_id=1, source_target_pairs={{0,12},{4,8},{8,4},{12,0},{1,13},{5,9},{9,5},{13,1},{2,14},{6,10},... | collective-permute-start | bytes 589832 | tf_op jit(solution)/shard_map/ppermute | solution.py:378
  31.4 1.1 %expert_output.1 = (f32[1,2048]{1,0:T(1,128)S(1)}, bf16[48,2048]{1,0:T(8,128)(2,1)S(1)}, bf16[48,2048]{1,0:T(8,128)(2,1)S(1)}, bf16[48,2048]{1,0:T(8,128)(2,1)S(1)}, bf16[48,2048]{1,0:T(8,128)(2,1)S(1)}) custom-call(bf16[2,384,2048]{2,1,0:T(8,128)(2,1)S(1)} %get-tuple-element.57.down_ref, bf16[192,768]{1,0:T(8,128)(2,1)S(1)} %get-tuple-element.68.act_ref, ...), custom_call_target="tpu_custom_call" | custom-call | flops 603979776 | bytes 5816320 | tf_op jit(solution)/shard_map/expert_output/pallas_call | solution.py:360
  32.5 1.7 %collective-permute-start.8 = (f32[1,2048]{1,0:T(1,128)S(1)}, f32[1,2048]{1,0:T(1,128)S(1)}, u32[]{:S(2)}, u32[]{:S(2)}) collective-permute-start(f32[1,2048]{1,0:T(1,128)S(1)} %get-tuple-element.73), channel_id=1, source_target_pairs={{0,1},{1,0},{2,3},{3,2},{4,5},{5,4},{6,7},{7,6},{8,9},{9,8},{10,11... | collective-permute-start | bytes 24584 | tf_op jit(solution)/shard_map/ppermute | solution.py:378
  34.1 2.1 %collective-permute-done.8 = f32[1,2048]{1,0:T(1,128)S(1)} collective-permute-done((f32[1,2048]{1,0:T(1,128)S(1)}, f32[1,2048]{1,0:T(1,128)S(1)}, u32[]{:S(2)}, u32[]{:S(2)}) %collective-permute-start.8) | collective-permute-done | bytes 8224 | tf_op jit(solution)/shard_map/ppermute | solution.py:378
  36.2 2.7 %collective-permute-start.9 = (f32[1,2048]{1,0:T(1,128)S(1)}, f32[1,2048]{1,0:T(1,128)S(1)}, u32[]{:S(2)}, u32[]{:S(2)}) collective-permute-start(f32[1,2048]{1,0:T(1,128)S(1)} %add.15), channel_id=1, source_target_pairs={{0,2},{1,3},{2,0},{3,1},{4,6},{5,7},{6,4},{7,5},{8,10},{9,11},{10,... | collective-permute-start | bytes 24584 | tf_op jit(solution)/shard_map/ppermute | solution.py:378
  38.9 0.5 collective-permute-start.17
  39.4 1.4 %collective-permute-done.9 = f32[1,2048]{1,0:T(1,128)S(1)} collective-permute-done((f32[1,2048]{1,0:T(1,128)S(1)}, f32[1,2048]{1,0:T(1,128)S(1)}, u32[]{:S(2)}, u32[]{:S(2)}) %collective-permute-start.9) | collective-permute-done | bytes 8224 | tf_op jit(solution)/shard_map/ppermute | solution.py:378
  40.8 1.5 %collective-permute-start.18 = (bf16[48,2048]{1,0:T(8,128)(2,1)S(1)}, bf16[48,2048]{1,0:T(8,128)(2,1)S(1)}, u32[]{:S(2)}, u32[]{:S(2)}) collective-permute-start(bf16[48,2048]{1,0:T(8,128)(2,1)S(1)} %get-tuple-element.84), channel_id=1, source_target_pairs={{0,8},{4,12},{8,0},{12,4},{1,9},{5,13},{9,1},{13,5},{2,10},{6,14},... | collective-permute-start | bytes 589832 | tf_op jit(solution)/shard_map/ppermute | solution.py:378
  42.4 0.3 collective-permute-start.19
  42.7 4.0 %residual_attention_backward.1 = (bf16[128,2048]{1,0:T(8,128)(2,1)}, bf16[128,2048]{1,0:T(8,128)(2,1)}, f32[128,512]{1,0:T(8,128)S(1)}, bf16[128,512]{1,0:T(8,128)(2,1)S(1)}) custom-call(s32[1,128]{1,0:T(1,128)S(1)} %get-tuple-element.74.slot_ref, f32[1,2048]{1,0:T(1,128)S(1)} %get-tuple-element.52.gain_ref, ...), custom_call_target="tpu_custom_call" | custom-call | flops 637534208 | bytes 6169088 | tf_op jit(solution)/shard_map/residual_attention_backward/pallas_call | solution.py:360
  46.7 0.1 collective-permute-start.16
  46.8 1.8 %collective-permute-start.10 = (f32[1,2048]{1,0:T(1,128)S(1)}, f32[1,2048]{1,0:T(1,128)S(1)}, u32[]{:S(2)}, u32[]{:S(2)}) collective-permute-start(f32[1,2048]{1,0:T(1,128)S(1)} %add.16), channel_id=1, source_target_pairs={{0,4},{4,0},{8,12},{12,8},{1,5},{5,1},{9,13},{13,9},{2,6},{6,2},{1... | collective-permute-start | bytes 24584 | tf_op jit(solution)/shard_map/ppermute | solution.py:378
  48.6 2.0 %collective-permute-done.10 = f32[1,2048]{1,0:T(1,128)S(1)} collective-permute-done((f32[1,2048]{1,0:T(1,128)S(1)}, f32[1,2048]{1,0:T(1,128)S(1)}, u32[]{:S(2)}, u32[]{:S(2)}) %collective-permute-start.10) | collective-permute-done | bytes 8224 | tf_op jit(solution)/shard_map/ppermute | solution.py:378
  50.5 1.8 %collective-permute-start.11 = (f32[1,2048]{1,0:T(1,128)S(1)}, f32[1,2048]{1,0:T(1,128)S(1)}, u32[]{:S(2)}, u32[]{:S(2)}) collective-permute-start(f32[1,2048]{1,0:T(1,128)S(1)} %add.17), channel_id=1, source_target_pairs={{0,8},{4,12},{8,0},{12,4},{1,9},{5,13},{9,1},{13,5},{2,10},{6,14},... | collective-permute-start | bytes 24584 | tf_op jit(solution)/shard_map/ppermute | solution.py:378
  52.3 1.9 %collective-permute-done.11 = f32[1,2048]{1,0:T(1,128)S(1)} collective-permute-done((f32[1,2048]{1,0:T(1,128)S(1)}, f32[1,2048]{1,0:T(1,128)S(1)}, u32[]{:S(2)}, u32[]{:S(2)}) %collective-permute-start.11) | collective-permute-done | bytes 8224 | tf_op jit(solution)/shard_map/ppermute | solution.py:378
  54.3 0.1 collective-permute-start.12
  54.3 1.2 %collective-permute-done.12 = f32[1,2048]{1,0:T(1,128)S(1)} collective-permute-done((f32[1,2048]{1,0:T(1,128)S(1)}, f32[1,2048]{1,0:T(1,128)S(1)}, u32[]{:S(2)}, u32[]{:S(2)}) %collective-permute-start.12) | collective-permute-done | bytes 8224 | tf_op jit(solution)/shard_map/ppermute | solution.py:378
  55.6 1.2 %layer_output.1 = (bf16[128,2048]{1,0:T(8,128)(2,1)}, bf16[128,256]{1,0:T(8,128)(2,1)}, bf16[128,256]{1,0:T(8,128)(2,1)}, f32[1,128]{1,0:T(1,128)}, f32[1,2048]{1,0:T(1,128)}) custom-call(s32[1,128]{1,0:T(1,128)S(1)} %get-tuple-element.74.slot_ref, f32[1,128]{1,0:T(1,128)S(1)} %get-tuple-element.75.weight_ref, f32[1,2048]{1,0:T(1,128)S(1)} %add.19.gain_ref, ...), custom_call_target="tpu_custom_call" | custom-call | flops 100663296 | bytes 2901504 | tf_op jit(solution)/shard_map/layer_output/pallas_call | solution.py:360
  (20 shorter events, 0.1 us)
Async XLA Ops:
  2.6 11.3 %collective-permute-start.2 = (bf16[48,2048]{1,0:T(8,128)(2,1)S(1)}, bf16[48,2048]{1,0:T(8,128)(2,1)S(1)}, u32[]{:S(2)}, u32[]{:S(2)}) collective-permute-start(bf16[48,2048]{1,0:T(8,128)(2,1)S(1)} %get-tuple-element.59), channel_id=1, source_target_pairs={{0,4},{4,0},{8,12},{12,8},{1,5},{5,1},{9,13},{13,9},{2,6},{6,2},{1... | collective-permute-start | bytes 589832 | tf_op jit(solution)/shard_map/ppermute | solution.py:378
  5.6 2.1 %collective-permute-start = (bf16[128,256]{1,0:T(8,128)(2,1)}, bf16[128,256]{1,0:T(8,128)(2,1)S(1)}, u32[]{:S(2)}, u32[]{:S(2)}) collective-permute-start(bf16[128,256]{1,0:T(8,128)(2,1)} %bitcast.17), channel_id=1, source_target_pairs={{0,16},{16,0},{1,17},{17,1},{2,18},{18,2},{3,19},{19,3},{4,20},{20... | collective-permute-start | bytes 196616 | tf_op jit(solution)/shard_map/ppermute | solution.py:378
  5.6 2.1 %collective-permute-start.1 = (bf16[128,256]{1,0:T(8,128)(2,1)}, bf16[128,256]{1,0:T(8,128)(2,1)S(1)}, u32[]{:S(2)}, u32[]{:S(2)}) collective-permute-start(bf16[128,256]{1,0:T(8,128)(2,1)} %bitcast.19), channel_id=1, source_target_pairs={{0,16},{16,0},{1,17},{17,1},{2,18},{18,2},{3,19},{19,3},{4,20},{20... | collective-permute-start | bytes 196616 | tf_op jit(solution)/shard_map/ppermute | solution.py:378
  6.1 12.0 %collective-permute-start.3 = (bf16[48,2048]{1,0:T(8,128)(2,1)S(1)}, bf16[48,2048]{1,0:T(8,128)(2,1)S(1)}, u32[]{:S(2)}, u32[]{:S(2)}) collective-permute-start(bf16[48,2048]{1,0:T(8,128)(2,1)S(1)} %get-tuple-element.60), channel_id=1, source_target_pairs={{0,8},{4,12},{8,0},{12,4},{1,9},{5,13},{9,1},{13,5},{2,10},{6,14},... | collective-permute-start | bytes 589832 | tf_op jit(solution)/shard_map/ppermute | solution.py:378
  7.6 10.5 %collective-permute-start.4 = (bf16[48,2048]{1,0:T(8,128)(2,1)S(1)}, bf16[48,2048]{1,0:T(8,128)(2,1)S(1)}, u32[]{:S(2)}, u32[]{:S(2)}) collective-permute-start(bf16[48,2048]{1,0:T(8,128)(2,1)S(1)} %get-tuple-element.61), channel_id=1, source_target_pairs={{0,12},{4,8},{8,4},{12,0},{1,13},{5,9},{9,5},{13,1},{2,14},{6,10},... | collective-permute-start | bytes 589832 | tf_op jit(solution)/shard_map/ppermute | solution.py:378
  10.4 10.1 %collective-permute-start.5 = (bf16[48,2048]{1,0:T(8,128)(2,1)S(1)}, bf16[48,2048]{1,0:T(8,128)(2,1)S(1)}, u32[]{:S(2)}, u32[]{:S(2)}) collective-permute-start(bf16[48,2048]{1,0:T(8,128)(2,1)S(1)} %get-tuple-element.65), channel_id=1, source_target_pairs={{0,4},{4,0},{8,12},{12,8},{1,5},{5,1},{9,13},{13,9},{2,6},{6,2},{1... | collective-permute-start | bytes 589832 | tf_op jit(solution)/shard_map/ppermute | solution.py:378
  12.4 13.2 %collective-permute-start.6 = (bf16[48,2048]{1,0:T(8,128)(2,1)S(1)}, bf16[48,2048]{1,0:T(8,128)(2,1)S(1)}, u32[]{:S(2)}, u32[]{:S(2)}) collective-permute-start(bf16[48,2048]{1,0:T(8,128)(2,1)S(1)} %get-tuple-element.66), channel_id=1, source_target_pairs={{0,8},{4,12},{8,0},{12,4},{1,9},{5,13},{9,1},{13,5},{2,10},{6,14},... | collective-permute-start | bytes 589832 | tf_op jit(solution)/shard_map/ppermute | solution.py:378
  13.9 11.7 %collective-permute-start.7 = (bf16[48,2048]{1,0:T(8,128)(2,1)S(1)}, bf16[48,2048]{1,0:T(8,128)(2,1)S(1)}, u32[]{:S(2)}, u32[]{:S(2)}) collective-permute-start(bf16[48,2048]{1,0:T(8,128)(2,1)S(1)} %get-tuple-element.67), channel_id=1, source_target_pairs={{0,12},{4,8},{8,4},{12,0},{1,13},{5,9},{9,5},{13,1},{2,14},{6,10},... | collective-permute-start | bytes 589832 | tf_op jit(solution)/shard_map/ppermute | solution.py:378
  27.8 14.5 %collective-permute-start.13 = (bf16[48,2048]{1,0:T(8,128)(2,1)S(1)}, bf16[48,2048]{1,0:T(8,128)(2,1)S(1)}, u32[]{:S(2)}, u32[]{:S(2)}) collective-permute-start(bf16[48,2048]{1,0:T(8,128)(2,1)S(1)} %get-tuple-element.70.refs_5_), channel_id=1, source_target_pairs={{0,4},{4,0},{8,12},{12,8},{1,5},{5,1},{9,13},{13,9},{2,6},{6,2},{1... | collective-permute-start | bytes 589832 | tf_op jit(solution)/shard_map/ppermute | solution.py:378
  28.2 14.4 %collective-permute-start.14 = (bf16[48,2048]{1,0:T(8,128)(2,1)S(1)}, bf16[48,2048]{1,0:T(8,128)(2,1)S(1)}, u32[]{:S(2)}, u32[]{:S(2)}) collective-permute-start(bf16[48,2048]{1,0:T(8,128)(2,1)S(1)} %get-tuple-element.71.refs_6_), channel_id=1, source_target_pairs={{0,8},{4,12},{8,0},{12,4},{1,9},{5,13},{9,1},{13,5},{2,10},{6,14},... | collective-permute-start | bytes 589832 | tf_op jit(solution)/shard_map/ppermute | solution.py:378
  30.0 12.7 %collective-permute-start.15 = (bf16[48,2048]{1,0:T(8,128)(2,1)S(1)}, bf16[48,2048]{1,0:T(8,128)(2,1)S(1)}, u32[]{:S(2)}, u32[]{:S(2)}) collective-permute-start(bf16[48,2048]{1,0:T(8,128)(2,1)S(1)} %get-tuple-element.72.refs_7_), channel_id=1, source_target_pairs={{0,12},{4,8},{8,4},{12,0},{1,13},{5,9},{9,5},{13,1},{2,14},{6,10},... | collective-permute-start | bytes 589832 | tf_op jit(solution)/shard_map/ppermute | solution.py:378
  32.5 3.7 %collective-permute-start.8 = (f32[1,2048]{1,0:T(1,128)S(1)}, f32[1,2048]{1,0:T(1,128)S(1)}, u32[]{:S(2)}, u32[]{:S(2)}) collective-permute-start(f32[1,2048]{1,0:T(1,128)S(1)} %get-tuple-element.73), channel_id=1, source_target_pairs={{0,1},{1,0},{2,3},{3,2},{4,5},{5,4},{6,7},{7,6},{8,9},{9,8},{10,11... | collective-permute-start | bytes 24584 | tf_op jit(solution)/shard_map/ppermute | solution.py:378
  36.2 4.6 %collective-permute-start.9 = (f32[1,2048]{1,0:T(1,128)S(1)}, f32[1,2048]{1,0:T(1,128)S(1)}, u32[]{:S(2)}, u32[]{:S(2)}) collective-permute-start(f32[1,2048]{1,0:T(1,128)S(1)} %add.15), channel_id=1, source_target_pairs={{0,2},{1,3},{2,0},{3,1},{4,6},{5,7},{6,4},{7,5},{8,10},{9,11},{10,... | collective-permute-start | bytes 24584 | tf_op jit(solution)/shard_map/ppermute | solution.py:378
  38.9 16.6 %collective-permute-start.17 = (bf16[48,2048]{1,0:T(8,128)(2,1)S(1)}, bf16[48,2048]{1,0:T(8,128)(2,1)S(1)}, u32[]{:S(2)}, u32[]{:S(2)}) collective-permute-start(bf16[48,2048]{1,0:T(8,128)(2,1)S(1)} %get-tuple-element.83), channel_id=1, source_target_pairs={{0,4},{4,0},{8,12},{12,8},{1,5},{5,1},{9,13},{13,9},{2,6},{6,2},{1... | collective-permute-start | bytes 589832 | tf_op jit(solution)/shard_map/ppermute | solution.py:378
  40.8 14.7 %collective-permute-start.18 = (bf16[48,2048]{1,0:T(8,128)(2,1)S(1)}, bf16[48,2048]{1,0:T(8,128)(2,1)S(1)}, u32[]{:S(2)}, u32[]{:S(2)}) collective-permute-start(bf16[48,2048]{1,0:T(8,128)(2,1)S(1)} %get-tuple-element.84), channel_id=1, source_target_pairs={{0,8},{4,12},{8,0},{12,4},{1,9},{5,13},{9,1},{13,5},{2,10},{6,14},... | collective-permute-start | bytes 589832 | tf_op jit(solution)/shard_map/ppermute | solution.py:378
  42.4 13.2 %collective-permute-start.19 = (bf16[48,2048]{1,0:T(8,128)(2,1)S(1)}, bf16[48,2048]{1,0:T(8,128)(2,1)S(1)}, u32[]{:S(2)}, u32[]{:S(2)}) collective-permute-start(bf16[48,2048]{1,0:T(8,128)(2,1)S(1)} %get-tuple-element.85), channel_id=1, source_target_pairs={{0,12},{4,8},{8,4},{12,0},{1,13},{5,9},{9,5},{13,1},{2,14},{6,10},... | collective-permute-start | bytes 589832 | tf_op jit(solution)/shard_map/ppermute | solution.py:378
  46.7 8.8 %collective-permute-start.16 = (bf16[128,512]{1,0:T(8,128)(2,1)S(1)}, bf16[128,512]{1,0:T(8,128)(2,1)S(1)}, u32[]{:S(2)}, u32[]{:S(2)}) collective-permute-start(bf16[128,512]{1,0:T(8,128)(2,1)S(1)} %get-tuple-element.81), channel_id=1, source_target_pairs={{0,16},{16,0},{1,17},{17,1},{2,18},{18,2},{3,19},{19,3},{4,20},{20... | collective-permute-start | bytes 393224 | tf_op jit(solution)/shard_map/ppermute | solution.py:378
  46.8 3.7 %collective-permute-start.10 = (f32[1,2048]{1,0:T(1,128)S(1)}, f32[1,2048]{1,0:T(1,128)S(1)}, u32[]{:S(2)}, u32[]{:S(2)}) collective-permute-start(f32[1,2048]{1,0:T(1,128)S(1)} %add.16), channel_id=1, source_target_pairs={{0,4},{4,0},{8,12},{12,8},{1,5},{5,1},{9,13},{13,9},{2,6},{6,2},{1... | collective-permute-start | bytes 24584 | tf_op jit(solution)/shard_map/ppermute | solution.py:378
  50.5 3.7 %collective-permute-start.11 = (f32[1,2048]{1,0:T(1,128)S(1)}, f32[1,2048]{1,0:T(1,128)S(1)}, u32[]{:S(2)}, u32[]{:S(2)}) collective-permute-start(f32[1,2048]{1,0:T(1,128)S(1)} %add.17), channel_id=1, source_target_pairs={{0,8},{4,12},{8,0},{12,4},{1,9},{5,13},{9,1},{13,5},{2,10},{6,14},... | collective-permute-start | bytes 24584 | tf_op jit(solution)/shard_map/ppermute | solution.py:378
  54.3 1.2 %collective-permute-start.12 = (f32[1,2048]{1,0:T(1,128)S(1)}, f32[1,2048]{1,0:T(1,128)S(1)}, u32[]{:S(2)}, u32[]{:S(2)}) collective-permute-start(f32[1,2048]{1,0:T(1,128)S(1)} %add.18), channel_id=1, source_target_pairs={{0,16},{16,0},{1,17},{17,1},{2,18},{18,2},{3,19},{19,3},{4,20},{20... | collective-permute-start | bytes 24584 | tf_op jit(solution)/shard_map/ppermute | solution.py:378

commit v3 on v2

--- a/solution.py
+++ b/solution.py
@@ -15,6 +15,8 @@
 FFE = 384
 EXP_DEV = 2
 COLS = 256
+LANES = 128
+GAIN_LINES = D // LANES
 SCALE = HEAD_SIZE ** (-0.5)
 EXP2_SCALE = SCALE * 1.4426950408889634
 F32 = jnp.float32
@@ -105,9 +107,9 @@
         pltpu.make_async_copy(source, target, sems.at[i])
         for i, (source, target) in enumerate(zip(sources, targets))
     ]
-    for copy in copies[::-1]:
+    for copy in copies[6:] + copies[:6]:
         copy.start()
-    for copy in copies[:5:-1]:
+    for copy in copies[6:]:
         copy.wait()
     tokens = routes_ref.shape[1]
     chosen = routes_ref[...]
@@ -181,12 +183,16 @@
     return iota((slots, 1), 0) % (EXP_DEV * capacity) < capacity
 
 
-def probs_kernel(count, capacity, pieces, pos_ref, down_ref, gate_hbm, query_ref, *refs):
+def probs_kernel(
+    count, capacity, pieces, pos_ref, slot_ref, weight_ref, down_ref, gate_hbm, query_ref, *refs
+):
     key_refs = refs[:count]
     grad_refs = refs[count : count + pieces]
-    d_act_ref, probs_ref, gate_ref, sem = refs[count + pieces :]
+    d_act_ref, probs_ref, gate_ref, place_ref, wide_ref, sem = refs[count + pieces :]
     gate_copy = pltpu.make_async_copy(gate_hbm, gate_ref, sem)
     gate_copy.start()
+    place_ref[...] = placement_cols(slot_ref[...], place_ref.shape[1])
+    wide_ref[...] = jnp.broadcast_to(row_to_col(weight_ref[...]), wide_ref.shape)
     grads = stacked(grad_refs)
     first = first_expert_rows(grads.shape[0], capacity)
     d_act_ref[...] = jnp.where(first, mm(grads, down_ref[0], NT), mm(grads, down_ref[1], NT))
@@ -209,10 +215,11 @@
     gate_copy.wait()
 
 
-def expert_back_kernel(capacity, pieces, gate_ref, d_act_ref, *refs):
+def expert_back_kernel(capacity, pieces, gate_ref, d_act_ref, gain_ref, *refs):
     rows = stacked(refs[:pieces])
     act_ref = refs[pieces]
-    out_refs = refs[pieces + 1 :]
+    out_refs = refs[pieces + 1 : -1]
+    terms_ref = refs[-1]
     first = first_expert_rows(rows.shape[0], capacity)
     pre = jnp.where(first, mm(rows, gate_ref[0]), mm(rows, gate_ref[1]))
     gate = 1.0 / (1.0 + jnp.exp(-pre))
@@ -224,22 +231,33 @@
     d_second = jnp.where(first, 0.0, d_pre).astype(BF16)
     for cols in column_blocks():
         back = mm(d_first, gate_ref[0, cols, :], NT) + mm(d_second, gate_ref[1, cols, :], NT)
-        store_pieces(out_refs, cols, back.astype(BF16))
-
-
-def expert_out_kernel(pieces, down_ref, act_ref, gain_ref, *refs):
-    row_refs, dn_refs = refs[:pieces], refs[pieces : 2 * pieces]
-    gain_out_ref = refs[2 * pieces]
-    out_refs = refs[2 * pieces + 1 :]
+        back = back.astype(BF16)
+        store_pieces(out_refs, cols, back)
+        products = rows[:, cols].astype(F32) * back.astype(F32)
+        terms = jnp.sum(products, axis=0, keepdims=True) / gain_ref[:, cols]
+        for at in range(0, COLS, LANES):
+            line = (cols.start + at) // LANES
+            terms_ref[line : line + 1, :] = terms[:, at : at + LANES]
+    if pieces > 1:
+        total = terms_ref[...]
+        high = total.astype(BF16)
+        low = (total - high.astype(F32)).astype(BF16)
+        for ref in out_refs:
+            ref[:GAIN_LINES, D:] = high
+            ref[GAIN_LINES : 2 * GAIN_LINES, D:] = low
+            ref[2 * GAIN_LINES :, D:] = jnp.zeros((ref.shape[0] - 2 * GAIN_LINES, LANES), BF16)
+
+
+def expert_out_kernel(down_ref, act_ref, *out_refs):
     act = act_ref[...]
     for cols in column_blocks():
         y = mm(act[:, :FFE], down_ref[0, :, cols]) + mm(act[:, FFE:], down_ref[1, :, cols])
         store_pieces(out_refs, cols, y.astype(BF16))
-        terms = stacked(row_refs, cols).astype(F32) * stacked(dn_refs, cols).astype(F32)
-        gain_out_ref[:, cols] = jnp.sum(terms, axis=0, keepdims=True) / gain_ref[:, cols]
-
-
-def backward_kernel(count, pieces, slot_ref, gain_ref, hidden_ref, grad_ref, query_ref, probs_ref, *refs):
+
+
+def backward_kernel(
+    count, pieces, place_ref, gain_ref, hidden_ref, grad_ref, query_ref, probs_ref, *refs
+):
     dn_refs = refs[:pieces]
     key_refs = refs[pieces : pieces + count]
     value_refs = refs[pieces + count : pieces + 2 * count]
@@ -247,8 +265,7 @@
     other_refs = refs[pieces + 2 * count + 3 : -4]
     resid_ref, dq_ref, dn_scratch, sems = refs[-4:]
     tokens = hidden_ref.shape[0]
-    slots = sum(r.shape[0] for r in dn_refs)
-    place = placement_cols(slot_ref[...], slots)
+    place = place_ref[...]
     square = jnp.zeros((tokens, COLS), F32)
     mixing = jnp.zeros((tokens, COLS), F32)
     for cols in column_blocks():
@@ -303,18 +320,25 @@
         copy.wait()
 
 
+def tree_sum(parts):
+    while len(parts) > 1:
+        parts = [parts[i] + parts[i + 1] for i in range(0, len(parts), 2)]
+    return parts[0]
+
+
 def output_kernel(
     count,
     pieces,
+    gain_parts,
     tokens_in_all,
-    slot_ref,
+    place_ref,
     weight_ref,
-    gain_ref,
     hidden_ref,
     grad_ref,
     own_ref,
     *refs,
 ):
+    gain_refs, refs = refs[:gain_parts], refs[gain_parts:]
     arrived_refs = refs[: count - 1]
     y_refs = refs[count - 1 : count - 1 + pieces]
     out_hbm, dk_hbm, dv_hbm, d_weight_hbm, d_gain_hbm = refs[count - 1 + pieces : -6]
@@ -325,7 +349,7 @@
         d_kv = d_kv + ref[...].astype(F32)
     dk_ref[...] = d_kv[:, :split].astype(BF16)
     dv_ref[...] = d_kv[:, split:].astype(BF16)
-    d_gain_ref[...] = gain_ref[...] * (1.0 / tokens_in_all)
+    d_gain_ref[...] = tree_sum([ref[...] for ref in gain_refs]) * (1.0 / tokens_in_all)
     copies = []
 
     def send(source, target):
@@ -337,9 +361,8 @@
     send(dv_ref, dv_hbm)
     send(d_gain_ref, d_gain_hbm)
     tokens = hidden_ref.shape[0]
-    slots = sum(r.shape[0] for r in y_refs)
-    place = placement_cols(slot_ref[...], slots)
-    weight = row_to_col(weight_ref[...])
+    place = place_ref[...]
+    weight = weight_ref[...]
     total = jnp.zeros((tokens, COLS), F32)
     for cols in column_blocks():
         y = mm(place, stacked(y_refs, cols))
@@ -389,12 +412,17 @@
     return [jnp.concatenate(moved, axis=0)]
 
 
-def sum_over(value, axis):
-    step = 1
-    while step < lax.axis_size(axis):
-        value = value + pairwise(value, axis, step)
-        step *= 2
-    return value
+def with_partners(value, axis):
+    return [value] + [pairwise(value, axis, s) for s in range(1, lax.axis_size(axis))]
+
+
+def in_turns(value, axis, ahead):
+    parts = [value]
+    for s in range(1, lax.axis_size(axis)):
+        parts.append(pairwise(value, axis, s))
+        value, _ = lax.optimization_barrier((value, ahead))
+        ahead = parts[-1]
+    return parts
 
 
 def shaped(shape, dtype):
@@ -438,8 +466,8 @@
     all_keys = [own_keys] + [pairwise(own_keys, "ctx", s) for s in range(1, ctx_count)]
     all_values = [own_values] + [pairwise(own_values, "ctx", s) for s in range(1, ctx_count)]
 
-    near = [grad_rows, query_rows, resid_rows, own_keys, own_values, gain]
-    grad_rows, query_rows, resid_rows, own_keys, own_values, gain, slot, pos, weight, *send_grad = run(
+    near = [grad_rows, own_keys, own_values, gain, query_rows, resid_rows]
+    grad_rows, own_keys, own_values, gain, query_rows, resid_rows, slot, pos, weight, *send_grad = run(
         functools.partial(dispatch_kernel, ctx_count, experts, capacity),
         "dispatch_grads",
         placed(HBM, near + [route_weight, chosen, block_order]),
@@ -475,10 +503,10 @@
     )
     arrived_x = exchange(send_x, capacity)
 
-    d_act, probs, gate_near = run(
+    d_act, probs, gate_near, place, weight_wide = run(
         functools.partial(probs_kernel, ctx_count, capacity, piece_count),
         "act_grads_and_probs",
-        placed(VMEM, [pos, down_near])
+        placed(VMEM, [pos, slot, weight, down_near])
         + placed(HBM, [w_gate])
         + placed(VMEM, [query_rows] + all_keys + arrived_grad),
         placed(
@@ -487,35 +515,48 @@
                 shaped((slots, FFE), F32),
                 shaped((QUERY_HEADS // 2, ctx_count * tokens, 2 * tokens), F32),
                 shaped(w_gate.shape, BF16),
+                shaped((tokens, slots), BF16),
+                shaped((tokens, COLS), F32),
             ],
         ),
         expert_flops + attn_flops // 2,
         scratch=[pltpu.SemaphoreType.DMA(())],
     )
-    act, *send_dn = run(
+    carried = piece_count > 1
+    terms_shape = shaped((GAIN_LINES, LANES), F32)
+    dn_shapes = [shaped((x.shape[0], D + LANES * carried), BF16) for x in piece_shapes]
+    act, *send_dn, terms = run(
         functools.partial(expert_back_kernel, capacity, piece_count),
         "expert_backward",
-        placed(VMEM, [gate_near, d_act] + arrived_x),
-        placed(VMEM, [shaped((slots, EXP_DEV * FFE), BF16)] + piece_shapes),
+        placed(VMEM, [gate_near, d_act, gain] + arrived_x),
+        placed(VMEM, [shaped((slots, EXP_DEV * FFE), BF16)] + dn_shapes + [terms_shape]),
         2 * expert_flops,
     )
     dn = exchange(send_dn, capacity)
-    gain_part, *send_y = run(
-        functools.partial(expert_out_kernel, piece_count),
+    if carried:
+        terms = tree_sum(
+            [
+                x[:GAIN_LINES, D:].astype(F32) + x[GAIN_LINES : 2 * GAIN_LINES, D:].astype(F32)
+                for x in dn
+            ]
+        )
+    else:
+        terms = tree_sum(with_partners(terms, "exp"))
+    terms, place_back = lax.optimization_barrier((terms, place))
+    terms = tree_sum(with_partners(terms, "ctx"))
+    send_y = run(
+        expert_out_kernel,
         "expert_output",
-        placed(VMEM, [down_near, act, gain] + arrived_x + send_dn),
-        placed(VMEM, [shaped((1, D), F32)] + piece_shapes),
+        placed(VMEM, [down_near, act]),
+        placed(VMEM, piece_shapes),
         expert_flops,
     )
     returned = exchange(send_y, capacity)
-    gain_part, slot = lax.optimization_barrier((sum_over(gain_part, "dp"), slot))
-    for axis in ("exp", "ctx"):
-        gain_part = sum_over(gain_part, axis)
 
     d_hidden, d_queries, kv_own, *kv_send = run(
         functools.partial(backward_kernel, ctx_count, piece_count),
         "residual_attention_backward",
-        placed(VMEM, [slot, gain, hidden, grad_rows, query_rows, probs] + dn + all_keys + all_values),
+        placed(VMEM, [place_back, gain, hidden, grad_rows, query_rows, probs] + dn + all_keys + all_values),
         placed(HBM, [token_shape] * 2)
         + placed(
             VMEM,
@@ -531,16 +572,20 @@
         ],
     )
     kv_arrived = [pairwise(part, "ctx", s) for s, part in enumerate(kv_send, 1)]
+    terms, kv_own = lax.optimization_barrier((terms, kv_own))
+    gain_parts = in_turns(terms, "dp", kv_arrived[0])
 
     kv_shape = shaped((tokens, kv_width // 2), BF16)
-    final_shapes = [token_shape, kv_shape, kv_shape, shaped((1, tokens), F32), shaped((1, D), F32)]
+    final_shapes = [token_shape, kv_shape, kv_shape, shaped((1, tokens), F32), terms_shape]
     total_tokens = tokens * ctx_count * exp_count * lax.axis_size("dp")
     layer_out, d_keys, d_values, d_weight, d_gain = run(
-        functools.partial(output_kernel, ctx_count, piece_count, total_tokens),
+        functools.partial(
+            output_kernel, ctx_count, piece_count, len(gain_parts), total_tokens
+        ),
         "layer_output",
         placed(
             VMEM,
-            [slot, weight, gain_part, hidden, grad_rows, kv_own] + kv_arrived + returned,
+            [place, weight_wide, hidden, grad_rows, kv_own] + gain_parts + kv_arrived + returned,
         ),
         placed(HBM, final_shapes),
         place_flops,
@@ -554,7 +599,7 @@
         d_keys[None],
         d_values[None],
         d_weight,
-        d_gain[0],
+        d_gain.reshape(D),
     )
 
 

time: 57 us -> 60.3 us (1.058)
  waiting for transfers between devices: 17.4 us -> 20.5 us
  Pallas kernels: 15.6 us -> 16.9 us
  starting transfers between devices: 22.9 us -> 21.9 us
    ppermute x20 -> x19, waiting for transfers between devices: 17.4 us -> 20.5 us  [pairwise(): return lax.ppermute(value, axis, [(i, i ^ step) for i in range(count)])]
    pallas_call x7, Pallas kernels: 15.6 us -> 16.9 us  [run(): pl.pallas_call(kernel, out_shape=[x for _, x in outputs], in_specs=[spec[...]
    ppermute x20 -> x19, starting transfers between devices: 22.9 us -> 21.9 us  [pairwise(): return lax.ppermute(value, axis, [(i, i ^ step) for i in range(count)])]
  transfers between devices with their start and end apart: 20 -> 19, of which waited for: 7 -> 9; matrix products, arithmetic and copies ran while one was open for 0% -> 0% of each run, Pallas kernels for 18% -> 19%
where the time goes in v3:
time: 60.3 us; the launch traced here: 60 us
  starting transfers between devices  21.9 us (36%)
  waiting for transfers between devices  20.5 us (34%)
  Pallas kernels  16.9 us (28%)
  between operations  0.72 us (1%)
    ppermute x19, starting transfers between devices, pairwise(): return lax.ppermute(value, axis, [(i, i ^ step) for i in range(count)])  21.9 us
    ppermute x19, waiting for transfers between devices, pairwise(): return lax.ppermute(value, axis, [(i, i ^ step) for i in range(count)])  20.5 us
    pallas_call x7, Pallas kernels, run(): pl.pallas_call(kernel, out_shape=[x for _, x in outputs], in_specs=[spec[...  16.9 us
  transfers between devices with their start and end apart: 19, of which 9 were waited for; matrix products, arithmetic and copies ran while one was open for 0% of the time, Pallas kernels for 19%

profile of v3, /device:TPU:0, one launch (start us, length us, event | category | flops | bytes accessed | tf_op | source)
XLA Modules:
  0.0 60.0 jit_solution(3095618062657842169)
XLA Ops:
  0.6 1.5 %dispatch_grads.1 = (bf16[128,2048]{1,0:T(8,128)(2,1)S(1)}, bf16[128,256]{1,0:T(8,128)(2,1)S(1)}, bf16[128,256]{1,0:T(8,128)(2,1)S(1)}, f32[1,2048]{1,0:T(1,128)...) custom-call(bf16[128,2048]{1,0:T(8,128)(2,1)} %bitcast.13, ...), custom_call_target="tpu_custom_call" | custom-call | flops 100663296 | bytes 4213824 | tf_op jit(solution)/shard_map/dispatch_grads/pallas_call | solution.py:383
  2.2 3.0 %collective-permute-start.2 = (bf16[48,2048]{1,0:T(8,128)(2,1)S(1)}, bf16[48,2048]{1,0:T(8,128)(2,1)S(1)}, u32[]{:S(2)}, u32[]{:S(2)}) collective-permute-start(bf16[48,2048]{1,0:T(8,128)(2,1)S(1)} %get-tuple-element.65), channel_id=1, source_target_pairs={{0,4},{4,0},{8,12},{12,8},{1,5},{5,1},{9,13},{13,9},{2,6},{6,2},{1... | collective-permute-start | bytes 589832 | tf_op jit(solution)/shard_map/ppermute | solution.py:401
  5.2 0.5 collective-permute-start.1
  5.7 1.5 %collective-permute-start.3 = (bf16[48,2048]{1,0:T(8,128)(2,1)S(1)}, bf16[48,2048]{1,0:T(8,128)(2,1)S(1)}, u32[]{:S(2)}, u32[]{:S(2)}) collective-permute-start(bf16[48,2048]{1,0:T(8,128)(2,1)S(1)} %get-tuple-element.66), channel_id=1, source_target_pairs={{0,8},{4,12},{8,0},{12,4},{1,9},{5,13},{9,1},{13,5},{2,10},{6,14},... | collective-permute-start | bytes 589832 | tf_op jit(solution)/shard_map/ppermute | solution.py:401
  7.2 2.7 %attention_forward.1 = (bf16[128,2048]{1,0:T(8,128)(2,1)S(1)}, bf16[2,384,2048]{2,1,0:T(8,128)(2,1)S(1)}, bf16[48,2048]{1,0:T(8,128)(2,1)S(1)}, bf16[48,2048]{1,...) custom-call(s32[2,128]{1,0:T(2,128)S(1)} %get-tuple-element.55.pos_ref, ...), custom_call_target="tpu_custom_call" | custom-call | flops 369098752 | bytes 8922624 | tf_op jit(solution)/shard_map/attention_forward/pallas_call | solution.py:383
  9.9 2.0 %collective-permute-start.5 = (bf16[48,2048]{1,0:T(8,128)(2,1)S(1)}, bf16[48,2048]{1,0:T(8,128)(2,1)S(1)}, u32[]{:S(2)}, u32[]{:S(2)}) collective-permute-start(bf16[48,2048]{1,0:T(8,128)(2,1)S(1)} %get-tuple-element.75), channel_id=1, source_target_pairs={{0,4},{4,0},{8,12},{12,8},{1,5},{5,1},{9,13},{13,9},{2,6},{6,2},{1... | collective-permute-start | bytes 589832 | tf_op jit(solution)/shard_map/ppermute | solution.py:401
  12.0 1.5 %collective-permute-start.6 = (bf16[48,2048]{1,0:T(8,128)(2,1)S(1)}, bf16[48,2048]{1,0:T(8,128)(2,1)S(1)}, u32[]{:S(2)}, u32[]{:S(2)}) collective-permute-start(bf16[48,2048]{1,0:T(8,128)(2,1)S(1)} %get-tuple-element.76), channel_id=1, source_target_pairs={{0,8},{4,12},{8,0},{12,4},{1,9},{5,13},{9,1},{13,5},{2,10},{6,14},... | collective-permute-start | bytes 589832 | tf_op jit(solution)/shard_map/ppermute | solution.py:401
  13.5 0.4 collective-permute-start.7
  13.9 3.7 %collective-permute-done.3.refs_4_ = bf16[48,2048]{1,0:T(8,128)(2,1)S(1)} collective-permute-done((bf16[48,2048]{1,0:T(8,128)(2,1)S(1)}, bf16[48,2048]{1,0:T(8,128)(2,1)S(1)}, u32[]{:S(2)}, u32[]{:S(2)}) %collective-permute-start.3) | collective-permute-done | bytes 196640 | tf_op jit(solution)/shard_map/ppermute | solution.py:401
  17.7 3.6 %act_grads_and_probs.1 = (f32[192,384]{1,0:T(8,128)S(1)}, f32[8,256,256]{2,1,0:T(8,128)S(1)}, bf16[2,2048,384]{2,1,0:T(8,128)(2,1)S(1)}, bf16[128,192]{1,0:T(8,128)(2,1)S(1)}, f32[128,256]{1,0:T(8,128)S(1)}) custom-call(s32[2,128]{1,0:T(2,128)S(1)} %get-tuple-element.55.pos_ref, s32[1,128]{1,0:T(1,128)S(1)} %get-tuple-element.56.slot_ref, ...), custom_call_target="tpu_custom_call" | custom-call | flops 738197504 | bytes 13453312 | tf_op jit(solution)/shard_map/act_grads_and_probs/pallas_call | solution.py:383
  21.3 3.9 %collective-permute-done.6.refs_2_ = bf16[48,2048]{1,0:T(8,128)(2,1)S(1)} collective-permute-done((bf16[48,2048]{1,0:T(8,128)(2,1)S(1)}, bf16[48,2048]{1,0:T(8,128)(2,1)S(1)}, u32[]{:S(2)}, u32[]{:S(2)}) %collective-permute-start.6) | collective-permute-done | bytes 196640 | tf_op jit(solution)/shard_map/ppermute | solution.py:401
  25.1 2.9 %expert_backward.1 = (bf16[192,768]{1,0:T(8,128)(2,1)S(1)}, bf16[48,2176]{1,0:T(8,128)(2,1)S(1)}, bf16[48,2176]{1,0:T(8,128)(2,1)S(1)}, bf16[48,2176]{1,0:T(8,12...) custom-call(bf16[2,2048,384]{2,1,0:T(8,128)(2,1)S(1)} %get-tuple-element.72.gate_ref, ...), custom_call_target="tpu_custom_call" | custom-call | flops 1207959552 | bytes 5373952 | tf_op jit(solution)/shard_map/expert_backward/pallas_call | solution.py:383
  28.1 0.3 collective-permute-start.8
  28.4 1.7 %collective-permute-start.9 = (bf16[48,2176]{1,0:T(8,128)(2,1)S(1)}, bf16[48,2176]{1,0:T(8,128)(2,1)S(1)}, u32[]{:S(2)}, u32[]{:S(2)}) collective-permute-start(bf16[48,2176]{1,0:T(8,128)(2,1)S(1)} %get-tuple-element.80), channel_id=1, source_target_pairs={{0,8},{4,12},{8,0},{12,4},{1,9},{5,13},{9,1},{13,5},{2,10},{6,14},... | collective-permute-start | bytes 626696 | tf_op jit(solution)/shard_map/ppermute | solution.py:401
  30.1 1.4 %collective-permute-start.10 = (bf16[48,2176]{1,0:T(8,128)(2,1)S(1)}, bf16[48,2176]{1,0:T(8,128)(2,1)S(1)}, u32[]{:S(2)}, u32[]{:S(2)}) collective-permute-start(bf16[48,2176]{1,0:T(8,128)(2,1)S(1)} %get-tuple-element.81), channel_id=1, source_target_pairs={{0,12},{4,8},{8,4},{12,0},{1,13},{5,9},{9,5},{13,1},{2,14},{6,10},... | collective-permute-start | bytes 626696 | tf_op jit(solution)/shard_map/ppermute | solution.py:401
  31.5 1.0 %expert_output.1 = (bf16[48,2048]{1,0:T(8,128)(2,1)S(1)}, bf16[48,2048]{1,0:T(8,128)(2,1)S(1)}, bf16[48,2048]{1,0:T(8,128)(2,1)S(1)}, bf16[48,2048]{1,0:T(8,128)(2,1)S(1)}) custom-call(bf16[2,384,2048]{2,1,0:T(8,128)(2,1)S(1)} %get-tuple-element.63.down_ref, bf16[192,768]{1,0:T(8,128)(2,1)S(1)} %get-tuple-element.91.act_ref), custom_call_target="tpu_custom_call" | custom-call | flops 603979776 | bytes 4227072 | tf_op jit(solution)/shard_map/expert_output/pallas_call | solution.py:383
  32.5 0.4 collective-permute-start.16
  32.9 1.7 %collective-permute-start.17 = (bf16[48,2048]{1,0:T(8,128)(2,1)S(1)}, bf16[48,2048]{1,0:T(8,128)(2,1)S(1)}, u32[]{:S(2)}, u32[]{:S(2)}) collective-permute-start(bf16[48,2048]{1,0:T(8,128)(2,1)S(1)} %get-tuple-element.94), channel_id=1, source_target_pairs={{0,8},{4,12},{8,0},{12,4},{1,9},{5,13},{9,1},{13,5},{2,10},{6,14},... | collective-permute-start | bytes 589832 | tf_op jit(solution)/shard_map/ppermute | solution.py:401
  34.7 1.5 %collective-permute-done.8.refs_1_ = bf16[48,2176]{1,0:T(8,128)(2,1)S(1)} collective-permute-done((bf16[48,2176]{1,0:T(8,128)(2,1)S(1)}, bf16[48,2176]{1,0:T(8,128)(2,1)S(1)}, u32[]{:S(2)}, u32[]{:S(2)}) %collective-permute-start.8) | collective-permute-done | bytes 208928 | tf_op jit(solution)/shard_map/ppermute | solution.py:401
  36.2 1.5 %collective-permute-start.18 = (bf16[48,2048]{1,0:T(8,128)(2,1)S(1)}, bf16[48,2048]{1,0:T(8,128)(2,1)S(1)}, u32[]{:S(2)}, u32[]{:S(2)}) collective-permute-start(bf16[48,2048]{1,0:T(8,128)(2,1)S(1)} %get-tuple-element.95), channel_id=1, source_target_pairs={{0,12},{4,8},{8,4},{12,0},{1,13},{5,9},{9,5},{13,1},{2,14},{6,10},... | collective-permute-start | bytes 589832 | tf_op jit(solution)/shard_map/ppermute | solution.py:401
  37.6 1.1 %collective-permute-done.9.refs_2_ = bf16[48,2176]{1,0:T(8,128)(2,1)S(1)} collective-permute-done((bf16[48,2176]{1,0:T(8,128)(2,1)S(1)}, bf16[48,2176]{1,0:T(8,128)(2,1)S(1)}, u32[]{:S(2)}, u32[]{:S(2)}) %collective-permute-start.9) | collective-permute-done | bytes 208928 | tf_op jit(solution)/shard_map/ppermute | solution.py:401
  38.8 2.8 %collective-permute-done.10.refs_3_ = bf16[48,2176]{1,0:T(8,128)(2,1)S(1)} collective-permute-done((bf16[48,2176]{1,0:T(8,128)(2,1)S(1)}, bf16[48,2176]{1,0:T(8,128)(2,1)S(1)}, u32[]{:S(2)}, u32[]{:S(2)}) %collective-permute-start.10) | collective-permute-done | bytes 208928 | tf_op jit(solution)/shard_map/ppermute | solution.py:401
  41.6 4.0 %residual_attention_backward.1 = (bf16[128,2048]{1,0:T(8,128)(2,1)}, bf16[128,2048]{1,0:T(8,128)(2,1)}, f32[128,512]{1,0:T(8,128)S(1)}, bf16[128,512]{1,0:T(8,128)(2,1)S(1)}) custom-call(bf16[128,192]{1,0:T(8,128)(2,1)S(1)} %get-tuple-element.83.place_ref, f32[1,2048]{1,0:T(1,128)S(1)} %get-tuple-element.58.gain_ref, ...), custom_call_target="tpu_custom_call" | custom-call | flops 637534208 | bytes 6266880 | tf_op jit(solution)/shard_map/residual_attention_backward/pallas_call | solution.py:383
  45.6 0.1 collective-permute-start.13
  45.7 0.5 collective-permute-start.11
  46.2 0.8 %collective-permute-done.11 = f32[16,128]{1,0:T(8,128)S(1)} collective-permute-done((f32[16,128]{1,0:T(8,128)S(1)}, f32[16,128]{1,0:T(8,128)S(1)}, u32[]{:S(2)}, u32[]{:S(2)}) %collective-permute-start.11) | collective-permute-done | bytes 8224 | tf_op jit(solution)/shard_map/ppermute | solution.py:401
  47.1 1.6 %collective-permute-start.12 = (f32[16,128]{1,0:T(8,128)S(1)}, f32[16,128]{1,0:T(8,128)S(1)}, u32[]{:S(2)}, u32[]{:S(2)}) collective-permute-start(f32[16,128]{1,0:T(8,128)S(1)} %add.31.refs_0_), channel_id=1, source_target_pairs={{0,1},{1,0},{2,3},{3,2},{4,5},{5,4},{6,7},{7,6},{8,9},{9,8},{10,11... | collective-permute-start | bytes 24584 | tf_op jit(solution)/shard_map/ppermute | solution.py:401
  48.6 2.1 %collective-permute-done.12.refs_1_ = f32[16,128]{1,0:T(8,128)S(1)} collective-permute-done((f32[16,128]{1,0:T(8,128)S(1)}, f32[16,128]{1,0:T(8,128)S(1)}, u32[]{:S(2)}, u32[]{:S(2)}) %collective-permute-start.12) | collective-permute-done | bytes 8224 | tf_op jit(solution)/shard_map/ppermute | solution.py:401
  50.7 3.6 %collective-permute-start.15 = (f32[16,128]{1,0:T(8,128)S(1)}, f32[16,128]{1,0:T(8,128)S(1)}, u32[]{:S(2)}, u32[]{:S(2)}) collective-permute-start(f32[16,128]{1,0:T(8,128)S(1)} %add.31.refs_0_), channel_id=1, source_target_pairs={{0,3},{1,2},{2,1},{3,0},{4,7},{5,6},{6,5},{7,4},{8,11},{9,10},{10,... | collective-permute-start | bytes 24584 | tf_op jit(solution)/shard_map/ppermute | solution.py:401
  54.3 1.8 %collective-permute-done.15.refs_3_ = f32[16,128]{1,0:T(8,128)S(1)} collective-permute-done((f32[16,128]{1,0:T(8,128)S(1)}, f32[16,128]{1,0:T(8,128)S(1)}, u32[]{:S(2)}, u32[]{:S(2)}) %collective-permute-start.15) | collective-permute-done | bytes 8224 | tf_op jit(solution)/shard_map/ppermute | solution.py:401
  56.2 2.7 %collective-permute-done.14.refs_2_ = f32[16,128]{1,0:T(8,128)S(1)} collective-permute-done((f32[16,128]{1,0:T(8,128)S(1)}, f32[16,128]{1,0:T(8,128)S(1)}, u32[]{:S(2)}, u32[]{:S(2)}) %collective-permute-start.14) | collective-permute-done | bytes 8224 | tf_op jit(solution)/shard_map/ppermute | solution.py:401
  58.9 1.2 %layer_output.1 = (bf16[128,2048]{1,0:T(8,128)(2,1)}, bf16[128,256]{1,0:T(8,128)(2,1)}, bf16[128,256]{1,0:T(8,128)(2,1)}, f32[1,128]{1,0:T(1,128)}, f32[16,128]{1,0:T(8,128)}) custom-call(bf16[128,192]{1,0:T(8,128)(2,1)S(1)} %get-tuple-element.83.place_ref, f32[128,256]{1,0:T(8,128)S(1)} %get-tuple-element.69.weight_ref, ...), custom_call_target="tpu_custom_call" | custom-call | flops 100663296 | bytes 3105280 | tf_op jit(solution)/shard_map/layer_output/pallas_call | solution.py:383
  (15 shorter events, 0.1 us)
Async XLA Ops:
  2.2 11.3 %collective-permute-start.2 = (bf16[48,2048]{1,0:T(8,128)(2,1)S(1)}, bf16[48,2048]{1,0:T(8,128)(2,1)S(1)}, u32[]{:S(2)}, u32[]{:S(2)}) collective-permute-start(bf16[48,2048]{1,0:T(8,128)(2,1)S(1)} %get-tuple-element.65), channel_id=1, source_target_pairs={{0,4},{4,0},{8,12},{12,8},{1,5},{5,1},{9,13},{13,9},{2,6},{6,2},{1... | collective-permute-start | bytes 589832 | tf_op jit(solution)/shard_map/ppermute | solution.py:401
  5.2 2.1 %collective-permute-start = (bf16[128,256]{1,0:T(8,128)(2,1)}, bf16[128,256]{1,0:T(8,128)(2,1)S(1)}, u32[]{:S(2)}, u32[]{:S(2)}) collective-permute-start(bf16[128,256]{1,0:T(8,128)(2,1)} %bitcast.17), channel_id=1, source_target_pairs={{0,16},{16,0},{1,17},{17,1},{2,18},{18,2},{3,19},{19,3},{4,20},{20... | collective-permute-start | bytes 196616 | tf_op jit(solution)/shard_map/ppermute | solution.py:401
  5.2 2.1 %collective-permute-start.1 = (bf16[128,256]{1,0:T(8,128)(2,1)}, bf16[128,256]{1,0:T(8,128)(2,1)S(1)}, u32[]{:S(2)}, u32[]{:S(2)}) collective-permute-start(bf16[128,256]{1,0:T(8,128)(2,1)} %bitcast.19), channel_id=1, source_target_pairs={{0,16},{16,0},{1,17},{17,1},{2,18},{18,2},{3,19},{19,3},{4,20},{20... | collective-permute-start | bytes 196616 | tf_op jit(solution)/shard_map/ppermute | solution.py:401
  5.7 12.0 %collective-permute-start.3 = (bf16[48,2048]{1,0:T(8,128)(2,1)S(1)}, bf16[48,2048]{1,0:T(8,128)(2,1)S(1)}, u32[]{:S(2)}, u32[]{:S(2)}) collective-permute-start(bf16[48,2048]{1,0:T(8,128)(2,1)S(1)} %get-tuple-element.66), channel_id=1, source_target_pairs={{0,8},{4,12},{8,0},{12,4},{1,9},{5,13},{9,1},{13,5},{2,10},{6,14},... | collective-permute-start | bytes 589832 | tf_op jit(solution)/shard_map/ppermute | solution.py:401
  7.2 10.5 %collective-permute-start.4 = (bf16[48,2048]{1,0:T(8,128)(2,1)S(1)}, bf16[48,2048]{1,0:T(8,128)(2,1)S(1)}, u32[]{:S(2)}, u32[]{:S(2)}) collective-permute-start(bf16[48,2048]{1,0:T(8,128)(2,1)S(1)} %get-tuple-element.67), channel_id=1, source_target_pairs={{0,12},{4,8},{8,4},{12,0},{1,13},{5,9},{9,5},{13,1},{2,14},{6,10},... | collective-permute-start | bytes 589832 | tf_op jit(solution)/shard_map/ppermute | solution.py:401
  9.9 11.3 %collective-permute-start.5 = (bf16[48,2048]{1,0:T(8,128)(2,1)S(1)}, bf16[48,2048]{1,0:T(8,128)(2,1)S(1)}, u32[]{:S(2)}, u32[]{:S(2)}) collective-permute-start(bf16[48,2048]{1,0:T(8,128)(2,1)S(1)} %get-tuple-element.75), channel_id=1, source_target_pairs={{0,4},{4,0},{8,12},{12,8},{1,5},{5,1},{9,13},{13,9},{2,6},{6,2},{1... | collective-permute-start | bytes 589832 | tf_op jit(solution)/shard_map/ppermute | solution.py:401
  12.0 13.2 %collective-permute-start.6 = (bf16[48,2048]{1,0:T(8,128)(2,1)S(1)}, bf16[48,2048]{1,0:T(8,128)(2,1)S(1)}, u32[]{:S(2)}, u32[]{:S(2)}) collective-permute-start(bf16[48,2048]{1,0:T(8,128)(2,1)S(1)} %get-tuple-element.76), channel_id=1, source_target_pairs={{0,8},{4,12},{8,0},{12,4},{1,9},{5,13},{9,1},{13,5},{2,10},{6,14},... | collective-permute-start | bytes 589832 | tf_op jit(solution)/shard_map/ppermute | solution.py:401
  13.5 11.7 %collective-permute-start.7 = (bf16[48,2048]{1,0:T(8,128)(2,1)S(1)}, bf16[48,2048]{1,0:T(8,128)(2,1)S(1)}, u32[]{:S(2)}, u32[]{:S(2)}) collective-permute-start(bf16[48,2048]{1,0:T(8,128)(2,1)S(1)} %get-tuple-element.77), channel_id=1, source_target_pairs={{0,12},{4,8},{8,4},{12,0},{1,13},{5,9},{9,5},{13,1},{2,14},{6,10},... | collective-permute-start | bytes 589832 | tf_op jit(solution)/shard_map/ppermute | solution.py:401
  28.1 8.1 %collective-permute-start.8 = (bf16[48,2176]{1,0:T(8,128)(2,1)S(1)}, bf16[48,2176]{1,0:T(8,128)(2,1)S(1)}, u32[]{:S(2)}, u32[]{:S(2)}) collective-permute-start(bf16[48,2176]{1,0:T(8,128)(2,1)S(1)} %get-tuple-element.79), channel_id=1, source_target_pairs={{0,4},{4,0},{8,12},{12,8},{1,5},{5,1},{9,13},{13,9},{2,6},{6,2},{1... | collective-permute-start | bytes 626696 | tf_op jit(solution)/shard_map/ppermute | solution.py:401
  28.4 10.4 %collective-permute-start.9 = (bf16[48,2176]{1,0:T(8,128)(2,1)S(1)}, bf16[48,2176]{1,0:T(8,128)(2,1)S(1)}, u32[]{:S(2)}, u32[]{:S(2)}) collective-permute-start(bf16[48,2176]{1,0:T(8,128)(2,1)S(1)} %get-tuple-element.80), channel_id=1, source_target_pairs={{0,8},{4,12},{8,0},{12,4},{1,9},{5,13},{9,1},{13,5},{2,10},{6,14},... | collective-permute-start | bytes 626696 | tf_op jit(solution)/shard_map/ppermute | solution.py:401
  30.1 11.5 %collective-permute-start.10 = (bf16[48,2176]{1,0:T(8,128)(2,1)S(1)}, bf16[48,2176]{1,0:T(8,128)(2,1)S(1)}, u32[]{:S(2)}, u32[]{:S(2)}) collective-permute-start(bf16[48,2176]{1,0:T(8,128)(2,1)S(1)} %get-tuple-element.81), channel_id=1, source_target_pairs={{0,12},{4,8},{8,4},{12,0},{1,13},{5,9},{9,5},{13,1},{2,14},{6,10},... | collective-permute-start | bytes 626696 | tf_op jit(solution)/shard_map/ppermute | solution.py:401
  32.5 21.8 %collective-permute-start.16 = (bf16[48,2048]{1,0:T(8,128)(2,1)S(1)}, bf16[48,2048]{1,0:T(8,128)(2,1)S(1)}, u32[]{:S(2)}, u32[]{:S(2)}) collective-permute-start(bf16[48,2048]{1,0:T(8,128)(2,1)S(1)} %get-tuple-element.93), channel_id=1, source_target_pairs={{0,4},{4,0},{8,12},{12,8},{1,5},{5,1},{9,13},{13,9},{2,6},{6,2},{1... | collective-permute-start | bytes 589832 | tf_op jit(solution)/shard_map/ppermute | solution.py:401
  32.9 21.4 %collective-permute-start.17 = (bf16[48,2048]{1,0:T(8,128)(2,1)S(1)}, bf16[48,2048]{1,0:T(8,128)(2,1)S(1)}, u32[]{:S(2)}, u32[]{:S(2)}) collective-permute-start(bf16[48,2048]{1,0:T(8,128)(2,1)S(1)} %get-tuple-element.94), channel_id=1, source_target_pairs={{0,8},{4,12},{8,0},{12,4},{1,9},{5,13},{9,1},{13,5},{2,10},{6,14},... | collective-permute-start | bytes 589832 | tf_op jit(solution)/shard_map/ppermute | solution.py:401
  36.2 18.2 %collective-permute-start.18 = (bf16[48,2048]{1,0:T(8,128)(2,1)S(1)}, bf16[48,2048]{1,0:T(8,128)(2,1)S(1)}, u32[]{:S(2)}, u32[]{:S(2)}) collective-permute-start(bf16[48,2048]{1,0:T(8,128)(2,1)S(1)} %get-tuple-element.95), channel_id=1, source_target_pairs={{0,12},{4,8},{8,4},{12,0},{1,13},{5,9},{9,5},{13,1},{2,14},{6,10},... | collective-permute-start | bytes 589832 | tf_op jit(solution)/shard_map/ppermute | solution.py:401
  45.6 3.0 %collective-permute-start.13 = (bf16[128,512]{1,0:T(8,128)(2,1)S(1)}, bf16[128,512]{1,0:T(8,128)(2,1)S(1)}, u32[]{:S(2)}, u32[]{:S(2)}) collective-permute-start(bf16[128,512]{1,0:T(8,128)(2,1)S(1)} %get-tuple-element.88), channel_id=1, source_target_pairs={{0,16},{16,0},{1,17},{17,1},{2,18},{18,2},{3,19},{19,3},{4,20},{20... | collective-permute-start | bytes 393224 | tf_op jit(solution)/shard_map/ppermute | solution.py:401
  45.7 1.3 %collective-permute-start.11 = (f32[16,128]{1,0:T(8,128)S(1)}, f32[16,128]{1,0:T(8,128)S(1)}, u32[]{:S(2)}, u32[]{:S(2)}) collective-permute-start(f32[16,128]{1,0:T(8,128)S(1)} %add_add_fusion), channel_id=1, source_target_pairs={{0,16},{16,0},{1,17},{17,1},{2,18},{18,2},{3,19},{19,3},{4,20},{20... | collective-permute-start | bytes 24584 | tf_op jit(solution)/shard_map/ppermute | solution.py:401
  47.1 3.7 %collective-permute-start.12 = (f32[16,128]{1,0:T(8,128)S(1)}, f32[16,128]{1,0:T(8,128)S(1)}, u32[]{:S(2)}, u32[]{:S(2)}) collective-permute-start(f32[16,128]{1,0:T(8,128)S(1)} %add.31.refs_0_), channel_id=1, source_target_pairs={{0,1},{1,0},{2,3},{3,2},{4,5},{5,4},{6,7},{7,6},{8,9},{9,8},{10,11... | collective-permute-start | bytes 24584 | tf_op jit(solution)/shard_map/ppermute | solution.py:401
  50.7 5.4 %collective-permute-start.15 = (f32[16,128]{1,0:T(8,128)S(1)}, f32[16,128]{1,0:T(8,128)S(1)}, u32[]{:S(2)}, u32[]{:S(2)}) collective-permute-start(f32[16,128]{1,0:T(8,128)S(1)} %add.31.refs_0_), channel_id=1, source_target_pairs={{0,3},{1,2},{2,1},{3,0},{4,7},{5,6},{6,5},{7,4},{8,11},{9,10},{10,... | collective-permute-start | bytes 24584 | tf_op jit(solution)/shard_map/ppermute | solution.py:401
  54.3 4.5 %collective-permute-start.14 = (f32[16,128]{1,0:T(8,128)S(1)}, f32[16,128]{1,0:T(8,128)S(1)}, u32[]{:S(2)}, u32[]{:S(2)}) collective-permute-start(f32[16,128]{1,0:T(8,128)S(1)} %add.31.refs_0_), channel_id=1, source_target_pairs={{0,2},{1,3},{2,0},{3,1},{4,6},{5,7},{6,4},{7,5},{8,10},{9,11},{10,... | collective-permute-start | bytes 24584 | tf_op jit(solution)/shard_map/ppermute | solution.py:401

commit v4 on v2

--- a/solution.py
+++ b/solution.py
@@ -15,6 +15,9 @@
 FFE = 384
 EXP_DEV = 2
 COLS = 256
+LANES = 128
+GAIN_LINES = D // LANES
+WIDE_LINES = 128
 SCALE = HEAD_SIZE ** (-0.5)
 EXP2_SCALE = SCALE * 1.4426950408889634
 F32 = jnp.float32
@@ -36,13 +39,13 @@
 def row_to_col(row):
     n = row.shape[1]
     eye = iota((n, n), 0) == iota((n, n), 1)
-    return jnp.sum(jnp.where(eye, row, jnp.zeros((), row.dtype)), axis=1, keepdims=True)
+    return jnp.sum(jnp.where(eye, row.astype(F32), 0.0), axis=1, keepdims=True)
 
 
 def col_to_row(col):
     n = col.shape[0]
     eye = iota((n, n), 0) == iota((n, n), 1)
-    return jnp.sum(jnp.where(eye, col, jnp.zeros((), col.dtype)), axis=0, keepdims=True)
+    return jnp.sum(jnp.where(eye, col, 0.0), axis=0, keepdims=True)
 
 
 def block_positions(order_ref, ctx_index, tokens):
@@ -90,7 +93,7 @@
 def placement_cols(slot_row, slots):
     tokens = slot_row.shape[1]
     slot_col = row_to_col(slot_row)
-    return jnp.where(iota((tokens, slots), 1) == slot_col, 1.0, 0.0).astype(BF16)
+    return jnp.where(iota((tokens, slots), 1).astype(F32) == slot_col, 1.0, 0.0).astype(BF16)
 
 
 def dispatch_kernel(count, experts, capacity, *refs):
@@ -105,9 +108,9 @@
         pltpu.make_async_copy(source, target, sems.at[i])
         for i, (source, target) in enumerate(zip(sources, targets))
     ]
-    for copy in copies[::-1]:
+    for copy in copies[6:] + copies[:6]:
         copy.start()
-    for copy in copies[:5:-1]:
+    for copy in copies[6:]:
         copy.wait()
     tokens = routes_ref.shape[1]
     chosen = routes_ref[...]
@@ -138,17 +141,17 @@
 
 
 def attention_kernel(
-    count, pieces, pos_ref, slot_ref, gain_ref, query_ref, resid_ref, down_hbm, *refs
+    count, pos_ref, slot_ref, gain_ref, query_ref, resid_ref, *refs
 ):
     key_refs, value_refs = refs[:count], refs[count : 2 * count]
-    hidden_ref, down_ref = refs[2 * count : 2 * count + 2]
-    send_refs = refs[2 * count + 2 : -1]
-    down_copy = pltpu.make_async_copy(down_hbm, down_ref, refs[-1])
-    down_copy.start()
+    hidden_ref, send_refs = refs[2 * count], refs[2 * count + 1 :]
     tokens = query_ref.shape[0]
     query_pos = row_to_col(pos_ref[:1, :])
     bias = jnp.concatenate(
-        [jnp.where(pos_ref[s : s + 1, :] <= query_pos, 0.0, -1e30) for s in range(count)],
+        [
+            jnp.where(pos_ref[s : s + 1, :].astype(F32) <= query_pos, 0.0, -1e30)
+            for s in range(count)
+        ],
         axis=1,
     )
     length = count * tokens
@@ -174,23 +177,34 @@
     for cols in column_blocks():
         normed = (hidden_ref[:, cols].astype(F32) * inv_rms * gain_ref[:, cols]).astype(BF16)
         store_pieces(send_refs, cols, mm(place, normed).astype(BF16))
-    down_copy.wait()
 
 
 def first_expert_rows(slots, capacity):
     return iota((slots, 1), 0) % (EXP_DEV * capacity) < capacity
 
 
-def probs_kernel(count, capacity, pieces, pos_ref, down_ref, gate_hbm, query_ref, *refs):
+def probs_kernel(
+    count,
+    capacity,
+    pieces,
+    pos_ref,
+    slot_ref,
+    weight_ref,
+    down_hbm,
+    gate_hbm,
+    query_ref,
+    *refs,
+):
     key_refs = refs[:count]
     grad_refs = refs[count : count + pieces]
-    d_act_ref, probs_ref, gate_ref, sem = refs[count + pieces :]
-    gate_copy = pltpu.make_async_copy(gate_hbm, gate_ref, sem)
+    d_act_ref, probs_ref, down_ref, gate_ref, place_ref, wide_ref, sems = refs[count + pieces :]
+    down_copy = pltpu.make_async_copy(down_hbm, down_ref, sems.at[0])
+    gate_copy = pltpu.make_async_copy(gate_hbm, gate_ref, sems.at[1])
+    down_copy.start()
     gate_copy.start()
-    grads = stacked(grad_refs)
-    first = first_expert_rows(grads.shape[0], capacity)
-    d_act_ref[...] = jnp.where(first, mm(grads, down_ref[0], NT), mm(grads, down_ref[1], NT))
-    query_pos = pos_ref[:1, :]
+    place_ref[...] = placement_cols(slot_ref[...], place_ref.shape[1])
+    wide_ref[...] = jnp.broadcast_to(row_to_col(weight_ref[...]), wide_ref.shape)
+    query_pos = pos_ref[:1, :].astype(F32)
     bias = jnp.concatenate(
         [
             jnp.where(row_to_col(pos_ref[s : s + 1, :]) <= query_pos, 0.0, -1e30)
@@ -206,49 +220,76 @@
             peak = jnp.max(scores, axis=0, keepdims=True)
             weights = jnp.exp2((scores - peak) * EXP2_SCALE)
             probs_ref[pair] = weights * (1.0 / jnp.sum(weights, axis=0, keepdims=True))
+    grads = stacked(grad_refs)
+    first = first_expert_rows(grads.shape[0], capacity)
+    down_copy.wait()
+    d_act_ref[...] = jnp.where(first, mm(grads, down_ref[0], NT), mm(grads, down_ref[1], NT))
     gate_copy.wait()
 
 
-def expert_back_kernel(capacity, pieces, gate_ref, d_act_ref, *refs):
+def part_views(refs, rows, part):
+    return [r if r.shape[0] != 2 * rows else r.at[part * rows : (part + 1) * rows] for r in refs]
+
+
+def joined(step, pieces):
+    return pieces > 1 and step > 0 and step & (step - 1) == 0
+
+
+def split_parts(refs, pieces):
+    back, out = [], []
+    at = 0
+    for s in range(pieces):
+        back.append(refs[at])
+        at += not joined(s, pieces)
+        out.append(refs[at])
+        at += 1
+    return back, out
+
+
+def expert_kernel(capacity, pieces, gate_ref, down_ref, d_act_ref, *refs):
     rows = stacked(refs[:pieces])
-    act_ref = refs[pieces]
-    out_refs = refs[pieces + 1 :]
+    back_refs, out_refs = split_parts(refs[pieces:], pieces)
+    back_refs = part_views(back_refs, EXP_DEV * capacity, 0)
+    out_refs = part_views(out_refs, EXP_DEV * capacity, 1)
     first = first_expert_rows(rows.shape[0], capacity)
     pre = jnp.where(first, mm(rows, gate_ref[0]), mm(rows, gate_ref[1]))
     gate = 1.0 / (1.0 + jnp.exp(-pre))
     act = pre * gate
-    act_ref[:, :FFE] = jnp.where(first, act, 0.0).astype(BF16)
-    act_ref[:, FFE:] = jnp.where(first, 0.0, act).astype(BF16)
+    act_first = jnp.where(first, act, 0.0).astype(BF16)
+    act_second = jnp.where(first, 0.0, act).astype(BF16)
     d_pre = d_act_ref[...] * gate * (1.0 + pre * (1.0 - gate))
     d_first = jnp.where(first, d_pre, 0.0).astype(BF16)
     d_second = jnp.where(first, 0.0, d_pre).astype(BF16)
     for cols in column_blocks():
         back = mm(d_first, gate_ref[0, cols, :], NT) + mm(d_second, gate_ref[1, cols, :], NT)
-        store_pieces(out_refs, cols, back.astype(BF16))
-
-
-def expert_out_kernel(pieces, down_ref, act_ref, gain_ref, *refs):
-    row_refs, dn_refs = refs[:pieces], refs[pieces : 2 * pieces]
-    gain_out_ref = refs[2 * pieces]
-    out_refs = refs[2 * pieces + 1 :]
-    act = act_ref[...]
+        store_pieces(back_refs, cols, back.astype(BF16))
+        y = mm(act_first, down_ref[0, :, cols]) + mm(act_second, down_ref[1, :, cols])
+        store_pieces(out_refs, cols, y.astype(BF16))
+
+
+def gain_kernel(pieces, rows, gain_ref, *refs):
+    row_refs = refs[:pieces]
+    back_refs = part_views(refs[pieces:-1], rows, 0)
+    terms_ref = refs[-1]
     for cols in column_blocks():
-        y = mm(act[:, :FFE], down_ref[0, :, cols]) + mm(act[:, FFE:], down_ref[1, :, cols])
-        store_pieces(out_refs, cols, y.astype(BF16))
-        terms = stacked(row_refs, cols).astype(F32) * stacked(dn_refs, cols).astype(F32)
-        gain_out_ref[:, cols] = jnp.sum(terms, axis=0, keepdims=True) / gain_ref[:, cols]
-
-
-def backward_kernel(count, pieces, slot_ref, gain_ref, hidden_ref, grad_ref, query_ref, probs_ref, *refs):
-    dn_refs = refs[:pieces]
+        products = stacked(row_refs, cols).astype(F32) * stacked(back_refs, cols).astype(F32)
+        terms = jnp.sum(products, axis=0, keepdims=True) / gain_ref[:, cols]
+        for at in range(0, COLS, LANES):
+            line = (cols.start + at) // LANES
+            terms_ref[line : line + 1, :] = terms[:, at : at + LANES]
+
+
+def backward_kernel(
+    count, pieces, rows, place_ref, gain_ref, hidden_ref, grad_ref, query_ref, probs_ref, *refs
+):
+    dn_refs = part_views(refs[:pieces], rows, 0)
     key_refs = refs[pieces : pieces + count]
     value_refs = refs[pieces + count : pieces + 2 * count]
     resid_hbm, dq_hbm, own_ref = refs[pieces + 2 * count : pieces + 2 * count + 3]
     other_refs = refs[pieces + 2 * count + 3 : -4]
     resid_ref, dq_ref, dn_scratch, sems = refs[-4:]
     tokens = hidden_ref.shape[0]
-    slots = sum(r.shape[0] for r in dn_refs)
-    place = placement_cols(slot_ref[...], slots)
+    place = place_ref[...]
     square = jnp.zeros((tokens, COLS), F32)
     mixing = jnp.zeros((tokens, COLS), F32)
     for cols in column_blocks():
@@ -304,19 +345,11 @@
 
 
 def output_kernel(
-    count,
-    pieces,
-    tokens_in_all,
-    slot_ref,
-    weight_ref,
-    gain_ref,
-    hidden_ref,
-    grad_ref,
-    own_ref,
-    *refs,
+    count, pieces, rows, tokens_in_all, place_ref, weight_ref, gain_ref, hidden_ref, grad_ref, *refs
 ):
+    own_ref, refs = refs[0], refs[1:]
     arrived_refs = refs[: count - 1]
-    y_refs = refs[count - 1 : count - 1 + pieces]
+    y_refs = part_views(refs[count - 1 : count - 1 + pieces], rows, 1)
     out_hbm, dk_hbm, dv_hbm, d_weight_hbm, d_gain_hbm = refs[count - 1 + pieces : -6]
     out_ref, dk_ref, dv_ref, d_weight_ref, d_gain_ref, sems = refs[-6:]
     split = KEY_VALUE_HEADS * HEAD_SIZE
@@ -337,9 +370,8 @@
     send(dv_ref, dv_hbm)
     send(d_gain_ref, d_gain_hbm)
     tokens = hidden_ref.shape[0]
-    slots = sum(r.shape[0] for r in y_refs)
-    place = placement_cols(slot_ref[...], slots)
-    weight = row_to_col(weight_ref[...])
+    place = place_ref[...]
+    weight = weight_ref[...]
     total = jnp.zeros((tokens, COLS), F32)
     for cols in column_blocks():
         y = mm(place, stacked(y_refs, cols))
@@ -357,7 +389,7 @@
         x.size * x.dtype.itemsize for _, x in outputs
     )
     spec = {space: pl.BlockSpec(memory_space=space) for space in (VMEM, HBM)}
-    return pl.pallas_call(
+    results = pl.pallas_call(
         kernel,
         out_shape=[x for _, x in outputs],
         in_specs=[spec[space] for space, _ in inputs],
@@ -367,6 +399,7 @@
         cost_estimate=pl.CostEstimate(flops=flops, bytes_accessed=nbytes, transcendentals=0),
         name=name,
     )(*[pltpu.with_memory_space_constraint(x, HBM) if space is HBM else x for space, x in inputs])
+    return list(results)
 
 
 def placed(space, arrays):
@@ -389,9 +422,18 @@
     return [jnp.concatenate(moved, axis=0)]
 
 
-def sum_over(value, axis):
-    step = 1
-    while step < lax.axis_size(axis):
+def exchange_apart(pieces, capacity):
+    if len(pieces) == 1:
+        return exchange(pieces, capacity)
+    return [
+        piece if s == 0 or joined(s, len(pieces)) else pairwise(piece, "exp", s)
+        for s, piece in enumerate(pieces)
+    ]
+
+
+def sum_over(value, axis, first=1, last=None):
+    step = first
+    while step < lax.axis_size(axis) and (last is None or step <= last):
         value = value + pairwise(value, axis, step)
         step *= 2
     return value
@@ -438,8 +480,8 @@
     all_keys = [own_keys] + [pairwise(own_keys, "ctx", s) for s in range(1, ctx_count)]
     all_values = [own_values] + [pairwise(own_values, "ctx", s) for s in range(1, ctx_count)]
 
-    near = [grad_rows, query_rows, resid_rows, own_keys, own_values, gain]
-    grad_rows, query_rows, resid_rows, own_keys, own_values, gain, slot, pos, weight, *send_grad = run(
+    near = [grad_rows, own_keys, own_values, gain, query_rows, resid_rows]
+    grad_rows, own_keys, own_values, gain, query_rows, resid_rows, slot, pos, weight, *send_grad = run(
         functools.partial(dispatch_kernel, ctx_count, experts, capacity),
         "dispatch_grads",
         placed(HBM, near + [route_weight, chosen, block_order]),
@@ -463,66 +505,80 @@
     all_keys[0], all_values[0] = own_keys, own_values
     arrived_grad = exchange(send_grad, capacity)
 
-    hidden, down_near, *send_x = run(
-        functools.partial(attention_kernel, ctx_count, piece_count),
+    hidden, *send_x = run(
+        functools.partial(attention_kernel, ctx_count),
         "attention_forward",
-        placed(VMEM, [pos, slot, gain, query_rows, resid_rows])
-        + placed(HBM, [w_down])
-        + placed(VMEM, all_keys + all_values),
-        placed(VMEM, [token_shape, shaped(w_down.shape, BF16)] + piece_shapes),
+        placed(VMEM, [pos, slot, gain, query_rows, resid_rows] + all_keys + all_values),
+        placed(VMEM, [token_shape] + piece_shapes),
         attn_flops + place_flops,
-        scratch=[pltpu.SemaphoreType.DMA(())],
     )
     arrived_x = exchange(send_x, capacity)
 
-    d_act, probs, gate_near = run(
+    d_act, probs, down_near, gate_near, place, weight_wide = run(
         functools.partial(probs_kernel, ctx_count, capacity, piece_count),
         "act_grads_and_probs",
-        placed(VMEM, [pos, down_near])
-        + placed(HBM, [w_gate])
+        placed(VMEM, [pos, slot, weight])
+        + placed(HBM, [w_down, w_gate])
         + placed(VMEM, [query_rows] + all_keys + arrived_grad),
         placed(
             VMEM,
             [
                 shaped((slots, FFE), F32),
                 shaped((QUERY_HEADS // 2, ctx_count * tokens, 2 * tokens), F32),
+                shaped(w_down.shape, BF16),
                 shaped(w_gate.shape, BF16),
+                shaped((tokens, slots), BF16),
+                shaped((tokens, COLS), F32),
             ],
         ),
         expert_flops + attn_flops // 2,
-        scratch=[pltpu.SemaphoreType.DMA(())],
-    )
-    act, *send_dn = run(
-        functools.partial(expert_back_kernel, capacity, piece_count),
-        "expert_backward",
-        placed(VMEM, [gate_near, d_act] + arrived_x),
-        placed(VMEM, [shaped((slots, EXP_DEV * FFE), BF16)] + piece_shapes),
-        2 * expert_flops,
-    )
+        scratch=[pltpu.SemaphoreType.DMA((2,))],
+    )
+
+    return_shapes = []
+    for s in range(piece_count):
+        if joined(s, piece_count):
+            return_shapes.append(shaped((2 * rows, D), BF16))
+        else:
+            return_shapes.extend([piece_shapes[0]] * 2)
+    sent = run(
+        functools.partial(expert_kernel, capacity, piece_count),
+        "experts",
+        placed(VMEM, [gate_near, down_near, d_act] + arrived_x),
+        placed(VMEM, return_shapes),
+        3 * expert_flops,
+    )
+    send_dn, send_y = split_parts(sent, piece_count)
     dn = exchange(send_dn, capacity)
-    gain_part, *send_y = run(
-        functools.partial(expert_out_kernel, piece_count),
-        "expert_output",
-        placed(VMEM, [down_near, act, gain] + arrived_x + send_dn),
-        placed(VMEM, [shaped((1, D), F32)] + piece_shapes),
-        expert_flops,
-    )
-    returned = exchange(send_y, capacity)
-    gain_part, slot = lax.optimization_barrier((sum_over(gain_part, "dp"), slot))
-    for axis in ("exp", "ctx"):
-        gain_part = sum_over(gain_part, axis)
+    y = [
+        dn[s] if joined(s, piece_count) else moved
+        for s, moved in enumerate(exchange_apart(send_y, capacity))
+    ]
+    (terms,) = run(
+        functools.partial(gain_kernel, piece_count, rows),
+        "gain_terms",
+        placed(VMEM, [gain] + arrived_x + send_dn),
+        placed(VMEM, [shaped((GAIN_LINES, LANES), F32)]),
+        2 * slots * D,
+    )
+    terms, place_back = lax.optimization_barrier((sum_over(terms, "dp"), place))
+    terms = sum_over(terms, "exp", last=1)
+
+    terms = jnp.pad(terms, ((0, WIDE_LINES - GAIN_LINES), (0, 0)))
+    terms = sum_over(terms, "exp", first=2)[:GAIN_LINES]
 
     d_hidden, d_queries, kv_own, *kv_send = run(
-        functools.partial(backward_kernel, ctx_count, piece_count),
+        functools.partial(backward_kernel, ctx_count, piece_count, rows),
         "residual_attention_backward",
-        placed(VMEM, [slot, gain, hidden, grad_rows, query_rows, probs] + dn + all_keys + all_values),
+        placed(VMEM, [place_back, gain, hidden, grad_rows, query_rows, probs])
+        + placed(VMEM, dn + all_keys + all_values),
         placed(HBM, [token_shape] * 2)
         + placed(
             VMEM,
             [shaped((tokens, kv_width), F32)]
             + [shaped((tokens, kv_width), BF16)] * (ctx_count - 1),
         ),
-        2 * attn_flops + place_flops,
+        attn_flops + place_flops,
         scratch=[
             pltpu.VMEM((tokens, D), BF16),
             pltpu.VMEM((tokens, D), BF16),
@@ -530,17 +586,22 @@
             pltpu.SemaphoreType.DMA((1 + KEY_VALUE_HEADS,)),
         ],
     )
+    terms, kv_own = lax.optimization_barrier((terms, kv_own))
+    terms = sum_over(terms, "ctx")
     kv_arrived = [pairwise(part, "ctx", s) for s, part in enumerate(kv_send, 1)]
 
     kv_shape = shaped((tokens, kv_width // 2), BF16)
-    final_shapes = [token_shape, kv_shape, kv_shape, shaped((1, tokens), F32), shaped((1, D), F32)]
+    final_shapes = [token_shape, kv_shape, kv_shape]
+    final_shapes += [shaped((1, tokens), F32), shaped((GAIN_LINES, LANES), F32)]
     total_tokens = tokens * ctx_count * exp_count * lax.axis_size("dp")
     layer_out, d_keys, d_values, d_weight, d_gain = run(
-        functools.partial(output_kernel, ctx_count, piece_count, total_tokens),
+        functools.partial(output_kernel, ctx_count, piece_count, rows, total_tokens),
         "layer_output",
         placed(
             VMEM,
-            [slot, weight, gain_part, hidden, grad_rows, kv_own] + kv_arrived + returned,
+            [place, weight_wide, terms, hidden, grad_rows, kv_own]
+            + kv_arrived
+            + y,
         ),
         placed(HBM, final_shapes),
         place_flops,
@@ -554,7 +615,7 @@
         d_keys[None],
         d_values[None],
         d_weight,
-        d_gain[0],
+        d_gain.reshape(D),
     )
 
 

time: 57 us -> 53.5 us (0.939)
  starting transfers between devices: 22.9 us -> 20.9 us
  Pallas kernels: 15.6 us -> 14.6 us
    ppermute x20 -> x18, starting transfers between devices: 22.9 us -> 20.9 us  [pairwise(): return lax.ppermute(value, axis, [(i, i ^ step) for i in range(count)])]
    pallas_call x7, Pallas kernels: 15.6 us -> 14.6 us  [run(): pl.pallas_call(kernel, out_shape=[x for _, x in outputs], in_specs=[spec[...]
    ppermute x20 -> x18, waiting for transfers between devices: 17.4 us -> 17.1 us  [pairwise(): return lax.ppermute(value, axis, [(i, i ^ step) for i in range(count)])]
  transfers between devices with their start and end apart: 20 -> 18, of which waited for: 7 -> 7; matrix products, arithmetic and copies ran while one was open for 0% -> 0% of each run, Pallas kernels for 18% -> 17%
where the time goes in v4:
time: 53.5 us; the launch traced here: 53.3 us
  starting transfers between devices  20.9 us (39%)
  waiting for transfers between devices  17.1 us (32%)
  Pallas kernels  14.6 us (27%)
  between operations  0.73 us (1%)
    ppermute x18, starting transfers between devices, pairwise(): return lax.ppermute(value, axis, [(i, i ^ step) for i in range(count)])  20.9 us
    ppermute x18, waiting for transfers between devices, pairwise(): return lax.ppermute(value, axis, [(i, i ^ step) for i in range(count)])  17.1 us
    pallas_call x7, Pallas kernels, run(): pl.pallas_call(kernel, out_shape=[x for _, x in outputs], in_specs=[spec[...  14.6 us
  transfers between devices with their start and end apart: 18, of which 7 were waited for; matrix products, arithmetic and copies ran while one was open for 0% of the time, Pallas kernels for 17%

profile of v4, /device:TPU:0, one launch (start us, length us, event | category | flops | bytes accessed | tf_op | source)
XLA Modules:
  0.0 53.3 jit_solution(1060877659649074163)
XLA Ops:
  0.6 1.5 %dispatch_grads.1 = (bf16[128,2048]{1,0:T(8,128)(2,1)S(1)}, bf16[128,256]{1,0:T(8,128)(2,1)S(1)}, bf16[128,256]{1,0:T(8,128)(2,1)S(1)}, f32[1,2048]{1,0:T(1,128)...) custom-call(bf16[128,2048]{1,0:T(8,128)(2,1)} %bitcast.13, ...), custom_call_target="tpu_custom_call" | custom-call | flops 100663296 | bytes 4213824 | tf_op jit(solution)/shard_map/dispatch_grads/pallas_call | solution.py:392
  2.2 3.0 %collective-permute-start.1 = (bf16[48,2048]{1,0:T(8,128)(2,1)S(1)}, bf16[48,2048]{1,0:T(8,128)(2,1)S(1)}, u32[]{:S(2)}, u32[]{:S(2)}) collective-permute-start(bf16[48,2048]{1,0:T(8,128)(2,1)S(1)} %get-tuple-element.56), channel_id=1, source_target_pairs={{0,4},{4,0},{8,12},{12,8},{1,5},{5,1},{9,13},{13,9},{2,6},{6,2},{1... | collective-permute-start | bytes 589832 | tf_op jit(solution)/shard_map/ppermute | solution.py:411
  5.2 0.5 collective-permute-start.4
  5.7 1.5 %collective-permute-start.2 = (bf16[48,2048]{1,0:T(8,128)(2,1)S(1)}, bf16[48,2048]{1,0:T(8,128)(2,1)S(1)}, u32[]{:S(2)}, u32[]{:S(2)}) collective-permute-start(bf16[48,2048]{1,0:T(8,128)(2,1)S(1)} %get-tuple-element.57), channel_id=1, source_target_pairs={{0,8},{4,12},{8,0},{12,4},{1,9},{5,13},{9,1},{13,5},{2,10},{6,14},... | collective-permute-start | bytes 589832 | tf_op jit(solution)/shard_map/ppermute | solution.py:411
  7.2 0.0 collective-permute-start.3
  7.2 0.0 collective-permute-done.refs_1_.refs_5_
  7.2 1.4 %attention_forward.1 = (bf16[128,2048]{1,0:T(8,128)(2,1)S(1)}, bf16[48,2048]{1,0:T(8,128)(2,1)S(1)}, bf16[48,2048]{1,0:T(8,128)(2,1)S(1)}, bf16[48,2048]{1,0:T(8,128)(2,1)S(1)}, bf16[48,2048]{1,0:T(8,128)(2,1)S(1)}) custom-call(s32[2,128]{1,0:T(2,128)S(1)} %get-tuple-element.50.pos_ref, s32[1,128]{1,0:T(1,128)S(1)} %get-tuple-element.51.slot_ref, ...), custom_call_target="tpu_custom_call" | custom-call | flops 369098752 | bytes 2631168 | tf_op jit(solution)/shard_map/attention_forward/pallas_call | solution.py:392
  8.7 2.0 %collective-permute-start.5 = (bf16[48,2048]{1,0:T(8,128)(2,1)S(1)}, bf16[48,2048]{1,0:T(8,128)(2,1)S(1)}, u32[]{:S(2)}, u32[]{:S(2)}) collective-permute-start(bf16[48,2048]{1,0:T(8,128)(2,1)S(1)} %get-tuple-element.65), channel_id=1, source_target_pairs={{0,4},{4,0},{8,12},{12,8},{1,5},{5,1},{9,13},{13,9},{2,6},{6,2},{1... | collective-permute-start | bytes 589832 | tf_op jit(solution)/shard_map/ppermute | solution.py:411
  10.7 1.5 %collective-permute-start.6 = (bf16[48,2048]{1,0:T(8,128)(2,1)S(1)}, bf16[48,2048]{1,0:T(8,128)(2,1)S(1)}, u32[]{:S(2)}, u32[]{:S(2)}) collective-permute-start(bf16[48,2048]{1,0:T(8,128)(2,1)S(1)} %get-tuple-element.66), channel_id=1, source_target_pairs={{0,8},{4,12},{8,0},{12,4},{1,9},{5,13},{9,1},{13,5},{2,10},{6,14},... | collective-permute-start | bytes 589832 | tf_op jit(solution)/shard_map/ppermute | solution.py:411
  12.2 1.7 %collective-permute-start.7 = (bf16[48,2048]{1,0:T(8,128)(2,1)S(1)}, bf16[48,2048]{1,0:T(8,128)(2,1)S(1)}, u32[]{:S(2)}, u32[]{:S(2)}) collective-permute-start(bf16[48,2048]{1,0:T(8,128)(2,1)S(1)} %get-tuple-element.67), channel_id=1, source_target_pairs={{0,12},{4,8},{8,4},{12,0},{1,13},{5,9},{9,5},{13,1},{2,14},{6,10},... | collective-permute-start | bytes 589832 | tf_op jit(solution)/shard_map/ppermute | solution.py:411
  13.9 3.7 %collective-permute-done.2.refs_4_ = bf16[48,2048]{1,0:T(8,128)(2,1)S(1)} collective-permute-done((bf16[48,2048]{1,0:T(8,128)(2,1)S(1)}, bf16[48,2048]{1,0:T(8,128)(2,1)S(1)}, u32[]{:S(2)}, u32[]{:S(2)}) %collective-permute-start.2) | collective-permute-done | bytes 196640 | tf_op jit(solution)/shard_map/ppermute | solution.py:411
  17.7 3.1 %act_grads_and_probs.1 = (f32[192,384]{1,0:T(8,128)S(1)}, f32[8,256,256]{2,1,0:T(8,128)S(1)}, bf16[2,384,2048]{2,1,0:T(8,128)(2,1)S(1)}, bf16[2,2048,384]{2,1,0:...) custom-call(s32[2,128]{1,0:T(2,128)S(1)} %get-tuple-element.50.pos_ref, ...), custom_call_target="tpu_custom_call" | custom-call | flops 738197504 | bytes 16599040 | tf_op jit(solution)/shard_map/act_grads_and_probs/pallas_call | solution.py:392
  20.8 4.4 %collective-permute-done.6.refs_2_ = bf16[48,2048]{1,0:T(8,128)(2,1)S(1)} collective-permute-done((bf16[48,2048]{1,0:T(8,128)(2,1)S(1)}, bf16[48,2048]{1,0:T(8,128)(2,1)S(1)}, u32[]{:S(2)}, u32[]{:S(2)}) %collective-permute-start.6) | collective-permute-done | bytes 196640 | tf_op jit(solution)/shard_map/ppermute | solution.py:411
  25.1 3.0 %experts.1 = (bf16[48,2048]{1,0:T(8,128)(2,1)S(1)}, bf16[48,2048]{1,0:T(8,128)(2,1)S(1)}, bf16[96,2048]{1,0:T(8,128)(2,1)S(1)}, bf16[96,2048]{1,0:T(8,128)(2,1)S...) custom-call(bf16[2,2048,384]{2,1,0:T(8,128)(2,1)S(1)} %get-tuple-element.68.gate_ref, ...), custom_call_target="tpu_custom_call" | custom-call | flops 1811939328 | bytes 8945664 | tf_op jit(solution)/shard_map/experts/pallas_call | solution.py:392
  28.1 0.4 collective-permute-start.12
  28.5 1.7 %collective-permute-start.13 = (bf16[96,2048]{1,0:T(8,128)(2,1)S(1)}, bf16[96,2048]{1,0:T(8,128)(2,1)S(1)}, u32[]{:S(2)}, u32[]{:S(2)}) collective-permute-start(bf16[96,2048]{1,0:T(8,128)(2,1)S(1)} %get-tuple-element.73.refs_6_), channel_id=1, source_target_pairs={{0,8},{4,12},{8,0},{12,4},{1,9},{5,13},{9,1},{13,5},{2,10},{6,14},... | collective-permute-start | bytes 1179656 | tf_op jit(solution)/shard_map/ppermute | solution.py:411
  30.3 1.4 %collective-permute-start.14 = (bf16[48,2048]{1,0:T(8,128)(2,1)S(1)}, bf16[48,2048]{1,0:T(8,128)(2,1)S(1)}, u32[]{:S(2)}, u32[]{:S(2)}) collective-permute-start(bf16[48,2048]{1,0:T(8,128)(2,1)S(1)} %get-tuple-element.74.refs_7_), channel_id=1, source_target_pairs={{0,12},{4,8},{8,4},{12,0},{1,13},{5,9},{9,5},{13,1},{2,14},{6,10},... | collective-permute-start | bytes 589832 | tf_op jit(solution)/shard_map/ppermute | solution.py:411
  31.7 0.3 gain_terms.1
  32.0 1.6 %collective-permute-start.8 = (f32[16,128]{1,0:T(8,128)S(1)}, f32[16,128]{1,0:T(8,128)S(1)}, u32[]{:S(2)}, u32[]{:S(2)}) collective-permute-start(f32[16,128]{1,0:T(8,128)S(1)} %gain_terms.1), channel_id=1, source_target_pairs={{0,1},{1,0},{2,3},{3,2},{4,5},{5,4},{6,7},{7,6},{8,9},{9,8},{10,11... | collective-permute-start | bytes 24584 | tf_op jit(solution)/shard_map/ppermute | solution.py:411
  33.6 2.1 %collective-permute-done.8 = f32[16,128]{1,0:T(8,128)S(1)} collective-permute-done((f32[16,128]{1,0:T(8,128)S(1)}, f32[16,128]{1,0:T(8,128)S(1)}, u32[]{:S(2)}, u32[]{:S(2)}) %collective-permute-start.8) | collective-permute-done | bytes 8224 | tf_op jit(solution)/shard_map/ppermute | solution.py:411
  35.7 2.6 %collective-permute-start.9 = (f32[16,128]{1,0:T(8,128)S(1)}, f32[16,128]{1,0:T(8,128)S(1)}, u32[]{:S(2)}, u32[]{:S(2)}) collective-permute-start(f32[16,128]{1,0:T(8,128)S(1)} %add.17), channel_id=1, source_target_pairs={{0,2},{1,3},{2,0},{3,1},{4,6},{5,7},{6,4},{7,5},{8,10},{9,11},{10,... | collective-permute-start | bytes 24584 | tf_op jit(solution)/shard_map/ppermute | solution.py:411
  38.4 1.9 %collective-permute-done.9 = f32[16,128]{1,0:T(8,128)S(1)} collective-permute-done((f32[16,128]{1,0:T(8,128)S(1)}, f32[16,128]{1,0:T(8,128)S(1)}, u32[]{:S(2)}, u32[]{:S(2)}) %collective-permute-start.9) | collective-permute-done | bytes 8224 | tf_op jit(solution)/shard_map/ppermute | solution.py:411
  40.3 0.3 collective-permute-start.10
  40.6 3.3 %collective-permute-done.10 = f32[16,128]{1,0:T(8,128)S(1)} collective-permute-done((f32[16,128]{1,0:T(8,128)S(1)}, f32[16,128]{1,0:T(8,128)S(1)}, u32[]{:S(2)}, u32[]{:S(2)}) %collective-permute-start.10) | collective-permute-done | bytes 8224 | tf_op jit(solution)/shard_map/ppermute | solution.py:411
  43.9 1.6 %collective-permute-start.11 = (f32[128,128]{1,0:T(8,128)S(1)}, f32[128,128]{1,0:T(8,128)S(1)}, u32[]{:S(2)}, u32[]{:S(2)}) collective-permute-start(f32[128,128]{1,0:T(8,128)S(1)} %pad.4), channel_id=1, source_target_pairs={{0,8},{4,12},{8,0},{12,4},{1,9},{5,13},{9,1},{13,5},{2,10},{6,14},... | collective-permute-start | bytes 196616 | tf_op jit(solution)/shard_map/ppermute | solution.py:411
  45.5 0.3 collective-permute-start.17
  45.8 4.0 %residual_attention_backward.1 = (bf16[128,2048]{1,0:T(8,128)(2,1)}, bf16[128,2048]{1,0:T(8,128)(2,1)}, f32[128,512]{1,0:T(8,128)S(1)}, bf16[128,512]{1,0:T(8,128)(2,1)S(1)}) custom-call(bf16[128,192]{1,0:T(8,128)(2,1)S(1)} %get-tuple-element.76.place_ref, f32[1,2048]{1,0:T(1,128)S(1)} %get-tuple-element.61.gain_ref, ...), custom_call_target="tpu_custom_call" | custom-call | flops 369098752 | bytes 6610944 | tf_op jit(solution)/shard_map/residual_attention_backward/pallas_call | solution.py:392
  49.8 0.1 collective-permute-start.16
  49.9 0.5 collective-permute-start.15
  50.4 0.8 %collective-permute-done.15 = f32[16,128]{1,0:T(8,128)S(1)} collective-permute-done((f32[16,128]{1,0:T(8,128)S(1)}, f32[16,128]{1,0:T(8,128)S(1)}, u32[]{:S(2)}, u32[]{:S(2)}) %collective-permute-start.15) | collective-permute-done | bytes 8224 | tf_op jit(solution)/shard_map/ppermute | solution.py:411
  51.3 0.8 %collective-permute-done.17.refs_5_ = bf16[48,2048]{1,0:T(8,128)(2,1)S(1)} collective-permute-done((bf16[48,2048]{1,0:T(8,128)(2,1)S(1)}, bf16[48,2048]{1,0:T(8,128)(2,1)S(1)}, u32[]{:S(2)}, u32[]{:S(2)}) %collective-permute-start.17) | collective-permute-done | bytes 196640 | tf_op jit(solution)/shard_map/ppermute | solution.py:411
  52.1 1.2 %layer_output.1 = (bf16[128,2048]{1,0:T(8,128)(2,1)}, bf16[128,256]{1,0:T(8,128)(2,1)}, bf16[128,256]{1,0:T(8,128)(2,1)}, f32[1,128]{1,0:T(1,128)}, f32[16,128]{1,0:T(8,128)}) custom-call(bf16[128,192]{1,0:T(8,128)(2,1)S(1)} %get-tuple-element.76.place_ref, f32[128,256]{1,0:T(8,128)S(1)} %get-tuple-element.60.weight_ref, f32[16,128]{1,0:T(8,128)S(1)} %add.21.gain_ref, ...), custom_call_target="tpu_custom_call" | custom-call | flops 100663296 | bytes 3473920 | tf_op jit(solution)/shard_map/layer_output/pallas_call | solution.py:392
  (17 shorter events, 0.1 us)
Async XLA Ops:
  2.2 10.0 %collective-permute-start.1 = (bf16[48,2048]{1,0:T(8,128)(2,1)S(1)}, bf16[48,2048]{1,0:T(8,128)(2,1)S(1)}, u32[]{:S(2)}, u32[]{:S(2)}) collective-permute-start(bf16[48,2048]{1,0:T(8,128)(2,1)S(1)} %get-tuple-element.56), channel_id=1, source_target_pairs={{0,4},{4,0},{8,12},{12,8},{1,5},{5,1},{9,13},{13,9},{2,6},{6,2},{1... | collective-permute-start | bytes 589832 | tf_op jit(solution)/shard_map/ppermute | solution.py:411
  5.2 2.1 %collective-permute-start = (bf16[128,256]{1,0:T(8,128)(2,1)}, bf16[128,256]{1,0:T(8,128)(2,1)S(1)}, u32[]{:S(2)}, u32[]{:S(2)}) collective-permute-start(bf16[128,256]{1,0:T(8,128)(2,1)} %bitcast.17), channel_id=1, source_target_pairs={{0,16},{16,0},{1,17},{17,1},{2,18},{18,2},{3,19},{19,3},{4,20},{20... | collective-permute-start | bytes 196616 | tf_op jit(solution)/shard_map/ppermute | solution.py:411
  5.2 2.1 %collective-permute-start.4 = (bf16[128,256]{1,0:T(8,128)(2,1)}, bf16[128,256]{1,0:T(8,128)(2,1)S(1)}, u32[]{:S(2)}, u32[]{:S(2)}) collective-permute-start(bf16[128,256]{1,0:T(8,128)(2,1)} %bitcast.19), channel_id=1, source_target_pairs={{0,16},{16,0},{1,17},{17,1},{2,18},{18,2},{3,19},{19,3},{4,20},{20... | collective-permute-start | bytes 196616 | tf_op jit(solution)/shard_map/ppermute | solution.py:411
  5.7 12.0 %collective-permute-start.2 = (bf16[48,2048]{1,0:T(8,128)(2,1)S(1)}, bf16[48,2048]{1,0:T(8,128)(2,1)S(1)}, u32[]{:S(2)}, u32[]{:S(2)}) collective-permute-start(bf16[48,2048]{1,0:T(8,128)(2,1)S(1)} %get-tuple-element.57), channel_id=1, source_target_pairs={{0,8},{4,12},{8,0},{12,4},{1,9},{5,13},{9,1},{13,5},{2,10},{6,14},... | collective-permute-start | bytes 589832 | tf_op jit(solution)/shard_map/ppermute | solution.py:411
  7.2 10.5 %collective-permute-start.3 = (bf16[48,2048]{1,0:T(8,128)(2,1)S(1)}, bf16[48,2048]{1,0:T(8,128)(2,1)S(1)}, u32[]{:S(2)}, u32[]{:S(2)}) collective-permute-start(bf16[48,2048]{1,0:T(8,128)(2,1)S(1)} %get-tuple-element.58), channel_id=1, source_target_pairs={{0,12},{4,8},{8,4},{12,0},{1,13},{5,9},{9,5},{13,1},{2,14},{6,10},... | collective-permute-start | bytes 589832 | tf_op jit(solution)/shard_map/ppermute | solution.py:411
  8.7 12.1 %collective-permute-start.5 = (bf16[48,2048]{1,0:T(8,128)(2,1)S(1)}, bf16[48,2048]{1,0:T(8,128)(2,1)S(1)}, u32[]{:S(2)}, u32[]{:S(2)}) collective-permute-start(bf16[48,2048]{1,0:T(8,128)(2,1)S(1)} %get-tuple-element.65), channel_id=1, source_target_pairs={{0,4},{4,0},{8,12},{12,8},{1,5},{5,1},{9,13},{13,9},{2,6},{6,2},{1... | collective-permute-start | bytes 589832 | tf_op jit(solution)/shard_map/ppermute | solution.py:411
  10.7 14.5 %collective-permute-start.6 = (bf16[48,2048]{1,0:T(8,128)(2,1)S(1)}, bf16[48,2048]{1,0:T(8,128)(2,1)S(1)}, u32[]{:S(2)}, u32[]{:S(2)}) collective-permute-start(bf16[48,2048]{1,0:T(8,128)(2,1)S(1)} %get-tuple-element.66), channel_id=1, source_target_pairs={{0,8},{4,12},{8,0},{12,4},{1,9},{5,13},{9,1},{13,5},{2,10},{6,14},... | collective-permute-start | bytes 589832 | tf_op jit(solution)/shard_map/ppermute | solution.py:411
  12.2 12.9 %collective-permute-start.7 = (bf16[48,2048]{1,0:T(8,128)(2,1)S(1)}, bf16[48,2048]{1,0:T(8,128)(2,1)S(1)}, u32[]{:S(2)}, u32[]{:S(2)}) collective-permute-start(bf16[48,2048]{1,0:T(8,128)(2,1)S(1)} %get-tuple-element.67), channel_id=1, source_target_pairs={{0,12},{4,8},{8,4},{12,0},{1,13},{5,9},{9,5},{13,1},{2,14},{6,10},... | collective-permute-start | bytes 589832 | tf_op jit(solution)/shard_map/ppermute | solution.py:411
  28.1 17.7 %collective-permute-start.12 = (bf16[96,2048]{1,0:T(8,128)(2,1)S(1)}, bf16[96,2048]{1,0:T(8,128)(2,1)S(1)}, u32[]{:S(2)}, u32[]{:S(2)}) collective-permute-start(bf16[96,2048]{1,0:T(8,128)(2,1)S(1)} %get-tuple-element.72.refs_5_), channel_id=1, source_target_pairs={{0,4},{4,0},{8,12},{12,8},{1,5},{5,1},{9,13},{13,9},{2,6},{6,2},{1... | collective-permute-start | bytes 1179656 | tf_op jit(solution)/shard_map/ppermute | solution.py:411
  28.5 17.3 %collective-permute-start.13 = (bf16[96,2048]{1,0:T(8,128)(2,1)S(1)}, bf16[96,2048]{1,0:T(8,128)(2,1)S(1)}, u32[]{:S(2)}, u32[]{:S(2)}) collective-permute-start(bf16[96,2048]{1,0:T(8,128)(2,1)S(1)} %get-tuple-element.73.refs_6_), channel_id=1, source_target_pairs={{0,8},{4,12},{8,0},{12,4},{1,9},{5,13},{9,1},{13,5},{2,10},{6,14},... | collective-permute-start | bytes 1179656 | tf_op jit(solution)/shard_map/ppermute | solution.py:411
  30.3 15.5 %collective-permute-start.14 = (bf16[48,2048]{1,0:T(8,128)(2,1)S(1)}, bf16[48,2048]{1,0:T(8,128)(2,1)S(1)}, u32[]{:S(2)}, u32[]{:S(2)}) collective-permute-start(bf16[48,2048]{1,0:T(8,128)(2,1)S(1)} %get-tuple-element.74.refs_7_), channel_id=1, source_target_pairs={{0,12},{4,8},{8,4},{12,0},{1,13},{5,9},{9,5},{13,1},{2,14},{6,10},... | collective-permute-start | bytes 589832 | tf_op jit(solution)/shard_map/ppermute | solution.py:411
  32.0 3.7 %collective-permute-start.8 = (f32[16,128]{1,0:T(8,128)S(1)}, f32[16,128]{1,0:T(8,128)S(1)}, u32[]{:S(2)}, u32[]{:S(2)}) collective-permute-start(f32[16,128]{1,0:T(8,128)S(1)} %gain_terms.1), channel_id=1, source_target_pairs={{0,1},{1,0},{2,3},{3,2},{4,5},{5,4},{6,7},{7,6},{8,9},{9,8},{10,11... | collective-permute-start | bytes 24584 | tf_op jit(solution)/shard_map/ppermute | solution.py:411
  35.7 4.5 %collective-permute-start.9 = (f32[16,128]{1,0:T(8,128)S(1)}, f32[16,128]{1,0:T(8,128)S(1)}, u32[]{:S(2)}, u32[]{:S(2)}) collective-permute-start(f32[16,128]{1,0:T(8,128)S(1)} %add.17), channel_id=1, source_target_pairs={{0,2},{1,3},{2,0},{3,1},{4,6},{5,7},{6,4},{7,5},{8,10},{9,11},{10,... | collective-permute-start | bytes 24584 | tf_op jit(solution)/shard_map/ppermute | solution.py:411
  40.3 3.7 %collective-permute-start.10 = (f32[16,128]{1,0:T(8,128)S(1)}, f32[16,128]{1,0:T(8,128)S(1)}, u32[]{:S(2)}, u32[]{:S(2)}) collective-permute-start(f32[16,128]{1,0:T(8,128)S(1)} %add.18), channel_id=1, source_target_pairs={{0,4},{4,0},{8,12},{12,8},{1,5},{5,1},{9,13},{13,9},{2,6},{6,2},{1... | collective-permute-start | bytes 24584 | tf_op jit(solution)/shard_map/ppermute | solution.py:411
  43.9 6.0 %collective-permute-start.11 = (f32[128,128]{1,0:T(8,128)S(1)}, f32[128,128]{1,0:T(8,128)S(1)}, u32[]{:S(2)}, u32[]{:S(2)}) collective-permute-start(f32[128,128]{1,0:T(8,128)S(1)} %pad.4), channel_id=1, source_target_pairs={{0,8},{4,12},{8,0},{12,4},{1,9},{5,13},{9,1},{13,5},{2,10},{6,14},... | collective-permute-start | bytes 196616 | tf_op jit(solution)/shard_map/ppermute | solution.py:411
  45.5 6.6 %collective-permute-start.17 = (bf16[48,2048]{1,0:T(8,128)(2,1)S(1)}, bf16[48,2048]{1,0:T(8,128)(2,1)S(1)}, u32[]{:S(2)}, u32[]{:S(2)}) collective-permute-start(bf16[48,2048]{1,0:T(8,128)(2,1)S(1)} %get-tuple-element.85), channel_id=1, source_target_pairs={{0,12},{4,8},{8,4},{12,0},{1,13},{5,9},{9,5},{13,1},{2,14},{6,10},... | collective-permute-start | bytes 589832 | tf_op jit(solution)/shard_map/ppermute | solution.py:411
  49.8 2.2 %collective-permute-start.16 = (bf16[128,512]{1,0:T(8,128)(2,1)S(1)}, bf16[128,512]{1,0:T(8,128)(2,1)S(1)}, u32[]{:S(2)}, u32[]{:S(2)}) collective-permute-start(bf16[128,512]{1,0:T(8,128)(2,1)S(1)} %get-tuple-element.83), channel_id=1, source_target_pairs={{0,16},{16,0},{1,17},{17,1},{2,18},{18,2},{3,19},{19,3},{4,20},{20... | collective-permute-start | bytes 393224 | tf_op jit(solution)/shard_map/ppermute | solution.py:411
  49.9 1.3 %collective-permute-start.15 = (f32[16,128]{1,0:T(8,128)S(1)}, f32[16,128]{1,0:T(8,128)S(1)}, u32[]{:S(2)}, u32[]{:S(2)}) collective-permute-start(f32[16,128]{1,0:T(8,128)S(1)} %slice_add_fusion), channel_id=1, source_target_pairs={{0,16},{16,0},{1,17},{17,1},{2,18},{18,2},{3,19},{19,3},{4,20},{20... | collective-permute-start | bytes 24584 | tf_op jit(solution)/shard_map/ppermute | solution.py:411

commit v5 on v4

--- a/solution.py
+++ b/solution.py
@@ -17,7 +17,6 @@
 COLS = 256
 LANES = 128
 GAIN_LINES = D // LANES
-WIDE_LINES = 128
 SCALE = HEAD_SIZE ** (-0.5)
 EXP2_SCALE = SCALE * 1.4426950408889634
 F32 = jnp.float32
@@ -198,10 +197,17 @@
     key_refs = refs[:count]
     grad_refs = refs[count : count + pieces]
     d_act_ref, probs_ref, down_ref, gate_ref, place_ref, wide_ref, sems = refs[count + pieces :]
-    down_copy = pltpu.make_async_copy(down_hbm, down_ref, sems.at[0])
-    gate_copy = pltpu.make_async_copy(gate_hbm, gate_ref, sems.at[1])
-    down_copy.start()
-    gate_copy.start()
+    spans = [slice(e * FFE, (e + 1) * FFE) for e in range(EXP_DEV)]
+    down_copies = [
+        pltpu.make_async_copy(down_hbm.at[e], down_ref.at[span, :], sems.at[e])
+        for e, span in enumerate(spans)
+    ]
+    gate_copies = [
+        pltpu.make_async_copy(gate_hbm.at[e], gate_ref.at[:, span], sems.at[EXP_DEV + e])
+        for e, span in enumerate(spans)
+    ]
+    for copy in down_copies + gate_copies:
+        copy.start()
     place_ref[...] = placement_cols(slot_ref[...], place_ref.shape[1])
     wide_ref[...] = jnp.broadcast_to(row_to_col(weight_ref[...]), wide_ref.shape)
     query_pos = pos_ref[:1, :].astype(F32)
@@ -222,9 +228,12 @@
             probs_ref[pair] = weights * (1.0 / jnp.sum(weights, axis=0, keepdims=True))
     grads = stacked(grad_refs)
     first = first_expert_rows(grads.shape[0], capacity)
-    down_copy.wait()
-    d_act_ref[...] = jnp.where(first, mm(grads, down_ref[0], NT), mm(grads, down_ref[1], NT))
-    gate_copy.wait()
+    for copy in down_copies:
+        copy.wait()
+    d_act = mm(grads, down_ref[...], NT)
+    d_act_ref[...] = jnp.where(first, d_act[:, :FFE], d_act[:, FFE:])
+    for copy in gate_copies:
+        copy.wait()
 
 
 def part_views(refs, rows, part):
@@ -252,19 +261,18 @@
     back_refs = part_views(back_refs, EXP_DEV * capacity, 0)
     out_refs = part_views(out_refs, EXP_DEV * capacity, 1)
     first = first_expert_rows(rows.shape[0], capacity)
-    pre = jnp.where(first, mm(rows, gate_ref[0]), mm(rows, gate_ref[1]))
+    both = mm(rows, gate_ref[...])
+    pre = jnp.where(first, both[:, :FFE], both[:, FFE:])
     gate = 1.0 / (1.0 + jnp.exp(-pre))
     act = pre * gate
-    act_first = jnp.where(first, act, 0.0).astype(BF16)
-    act_second = jnp.where(first, 0.0, act).astype(BF16)
     d_pre = d_act_ref[...] * gate * (1.0 + pre * (1.0 - gate))
-    d_first = jnp.where(first, d_pre, 0.0).astype(BF16)
-    d_second = jnp.where(first, 0.0, d_pre).astype(BF16)
+    act, d_pre = [
+        jnp.concatenate([jnp.where(first, x, 0.0), jnp.where(first, 0.0, x)], axis=1).astype(BF16)
+        for x in (act, d_pre)
+    ]
     for cols in column_blocks():
-        back = mm(d_first, gate_ref[0, cols, :], NT) + mm(d_second, gate_ref[1, cols, :], NT)
-        store_pieces(back_refs, cols, back.astype(BF16))
-        y = mm(act_first, down_ref[0, :, cols]) + mm(act_second, down_ref[1, :, cols])
-        store_pieces(out_refs, cols, y.astype(BF16))
+        store_pieces(back_refs, cols, mm(d_pre, gate_ref[cols, :], NT).astype(BF16))
+        store_pieces(out_refs, cols, mm(act, down_ref[:, cols]).astype(BF16))
 
 
 def gain_kernel(pieces, rows, gain_ref, *refs):
@@ -415,7 +423,7 @@
     count = lax.axis_size("exp")
     rows = EXP_DEV * capacity
     if len(pieces) == count:
-        return [pieces[0]] + [pairwise(pieces[s], "exp", s) for s in range(1, count)]
+        return [pieces[0]] + [pairwise(pieces[s], "exp", s) for s in range(count - 1, 0, -1)][::-1]
     flat = pieces[0]
     blocks = [flat[s * rows : (s + 1) * rows] for s in range(count)]
     moved = [blocks[0]] + [pairwise(blocks[s], "exp", s) for s in range(1, count)]
@@ -431,12 +439,18 @@
     ]
 
 
-def sum_over(value, axis, first=1, last=None):
-    step = first
-    while step < lax.axis_size(axis) and (last is None or step <= last):
+def sum_over(value, axis):
+    step = 1
+    while step < lax.axis_size(axis):
         value = value + pairwise(value, axis, step)
         step *= 2
     return value
+
+
+def tree_sum(parts):
+    while len(parts) > 1:
+        parts = [parts[i] + parts[i + 1] for i in range(0, len(parts), 2)]
+    return parts[0]
 
 
 def shaped(shape, dtype):
@@ -503,7 +517,11 @@
         ],
     )
     all_keys[0], all_values[0] = own_keys, own_values
-    arrived_grad = exchange(send_grad, capacity)
+    apart = [s for s in range(1, piece_count) if not joined(s, piece_count)]
+    near = [s for s in range(1, piece_count) if joined(s, piece_count)]
+    arrived_grad = exchange(send_grad, capacity) if piece_count == 1 else list(send_grad)
+    for s in apart:
+        arrived_grad[s] = pairwise(send_grad[s], "exp", s)
 
     hidden, *send_x = run(
         functools.partial(attention_kernel, ctx_count),
@@ -512,7 +530,15 @@
         placed(VMEM, [token_shape] + piece_shapes),
         attn_flops + place_flops,
     )
-    arrived_x = exchange(send_x, capacity)
+    arrived_x = exchange(send_x, capacity) if piece_count == 1 else list(send_x)
+    for s in apart:
+        arrived_x[s] = pairwise(send_x[s], "exp", s)
+    if near:
+        after, _ = lax.optimization_barrier(([send_grad[s] for s in near], send_x[0]))
+        for s, piece in zip(near, after):
+            arrived_grad[s] = pairwise(piece, "exp", s)
+        for s in near:
+            arrived_x[s] = pairwise(send_x[s], "exp", s)
 
     d_act, probs, down_near, gate_near, place, weight_wide = run(
         functools.partial(probs_kernel, ctx_count, capacity, piece_count),
@@ -525,14 +551,14 @@
             [
                 shaped((slots, FFE), F32),
                 shaped((QUERY_HEADS // 2, ctx_count * tokens, 2 * tokens), F32),
-                shaped(w_down.shape, BF16),
-                shaped(w_gate.shape, BF16),
+                shaped((EXP_DEV * FFE, D), BF16),
+                shaped((D, EXP_DEV * FFE), BF16),
                 shaped((tokens, slots), BF16),
                 shaped((tokens, COLS), F32),
             ],
         ),
         expert_flops + attn_flops // 2,
-        scratch=[pltpu.SemaphoreType.DMA((2,))],
+        scratch=[pltpu.SemaphoreType.DMA((2 * EXP_DEV,))],
     )
 
     return_shapes = []
@@ -562,10 +588,11 @@
         2 * slots * D,
     )
     terms, place_back = lax.optimization_barrier((sum_over(terms, "dp"), place))
-    terms = sum_over(terms, "exp", last=1)
-
-    terms = jnp.pad(terms, ((0, WIDE_LINES - GAIN_LINES), (0, 0)))
-    terms = sum_over(terms, "exp", first=2)[:GAIN_LINES]
+
+    if piece_count == 1:
+        terms = sum_over(terms, "exp")
+    else:
+        terms = tree_sum([terms] + [pairwise(terms, "exp", s) for s in range(1, exp_count)])
 
     d_hidden, d_queries, kv_own, *kv_send = run(
         functools.partial(backward_kernel, ctx_count, piece_count, rows),

time: 53.5 us -> 55 us (1.028)
  starting transfers between devices: 20.9 us -> 22.5 us
  waiting for transfers between devices: 17.1 us -> 16.5 us
    ppermute x18 -> x19, starting transfers between devices: 20.9 us -> 22.5 us  [pairwise(): return lax.ppermute(value, axis, [(i, i ^ step) for i in range(count)])]
    ppermute x18 -> x19, waiting for transfers between devices: 17.1 us -> 16.5 us  [pairwise(): return lax.ppermute(value, axis, [(i, i ^ step) for i in range(count)])]
  transfers between devices with their start and end apart: 18 -> 19, of which waited for: 7 -> 10; matrix products, arithmetic and copies ran while one was open for 0% -> 0% of each run, Pallas kernels for 17% -> 17%
where the time goes in v5:
time: 55 us; the launch traced here: 54.9 us
  starting transfers between devices  22.5 us (41%)
  waiting for transfers between devices  16.5 us (30%)
  Pallas kernels  15.1 us (27%)
  between operations  0.74 us (1%)
    ppermute x19, starting transfers between devices, pairwise(): return lax.ppermute(value, axis, [(i, i ^ step) for i in range(count)])  22.5 us
    ppermute x19, waiting for transfers between devices, pairwise(): return lax.ppermute(value, axis, [(i, i ^ step) for i in range(count)])  16.5 us
    pallas_call x7, Pallas kernels, run(): pl.pallas_call(kernel, out_shape=[x for _, x in outputs], in_specs=[spec[...  15.1 us
  transfers between devices with their start and end apart: 19, of which 10 were waited for; matrix products, arithmetic and copies ran while one was open for 0% of the time, Pallas kernels for 17%

profile of v5, /device:TPU:0, one launch (start us, length us, event | category | flops | bytes accessed | tf_op | source)
XLA Modules:
  0.0 54.9 jit_solution(6613305354685395139)
XLA Ops:
  0.6 1.5 %dispatch_grads.1 = (bf16[128,2048]{1,0:T(8,128)(2,1)S(1)}, bf16[128,256]{1,0:T(8,128)(2,1)S(1)}, bf16[128,256]{1,0:T(8,128)(2,1)S(1)}, f32[1,2048]{1,0:T(1,128)...) custom-call(bf16[128,2048]{1,0:T(8,128)(2,1)} %bitcast.13, ...), custom_call_target="tpu_custom_call" | custom-call | flops 100663296 | bytes 4213824 | tf_op jit(solution)/shard_map/dispatch_grads/pallas_call | solution.py:400
  2.2 4.0 %collective-permute-start.4 = (bf16[48,2048]{1,0:T(8,128)(2,1)S(1)}, bf16[48,2048]{1,0:T(8,128)(2,1)S(1)}, u32[]{:S(2)}, u32[]{:S(2)}) collective-permute-start(bf16[48,2048]{1,0:T(8,128)(2,1)S(1)} %get-tuple-element.66), channel_id=1, source_target_pairs={{0,12},{4,8},{8,4},{12,0},{1,13},{5,9},{9,5},{13,1},{2,14},{6,10},... | collective-permute-start | bytes 589832 | tf_op jit(solution)/shard_map/ppermute | solution.py:419
  6.1 0.5 collective-permute-start.1
  6.6 1.0 %collective-permute-done.refs_1_.refs_5_ = bf16[128,256]{1,0:T(8,128)(2,1)S(1)} collective-permute-done((bf16[128,256]{1,0:T(8,128)(2,1)}, bf16[128,256]{1,0:T(8,128)(2,1)S(1)}, u32[]{:S(2)}, u32[]{:S(2)}) %collective-permute-start) | collective-permute-done | bytes 65568 | tf_op jit(solution)/shard_map/ppermute | solution.py:419
  7.8 1.4 %attention_forward.1 = (bf16[128,2048]{1,0:T(8,128)(2,1)S(1)}, bf16[48,2048]{1,0:T(8,128)(2,1)S(1)}, bf16[48,2048]{1,0:T(8,128)(2,1)S(1)}, bf16[48,2048]{1,0:T(8,128)(2,1)S(1)}, bf16[48,2048]{1,0:T(8,128)(2,1)S(1)}) custom-call(s32[2,128]{1,0:T(2,128)S(1)} %get-tuple-element.52.pos_ref, s32[1,128]{1,0:T(1,128)S(1)} %get-tuple-element.53.slot_ref, ...), custom_call_target="tpu_custom_call" | custom-call | flops 369098752 | bytes 2631168 | tf_op jit(solution)/shard_map/attention_forward/pallas_call | solution.py:400
  9.2 0.6 %collective-permute-start.2 = (bf16[48,2048]{1,0:T(8,128)(2,1)S(1)}, bf16[48,2048]{1,0:T(8,128)(2,1)S(1)}, u32[]{:S(2)}, u32[]{:S(2)}) collective-permute-start(bf16[48,2048]{1,0:T(8,128)(2,1)S(1)} %get-tuple-element.64), channel_id=1, source_target_pairs={{0,4},{4,0},{8,12},{12,8},{1,5},{5,1},{9,13},{13,9},{2,6},{6,2},{1... | collective-permute-start | bytes 589832 | tf_op jit(solution)/shard_map/ppermute | solution.py:419
  9.9 1.9 %collective-permute-start.5 = (bf16[48,2048]{1,0:T(8,128)(2,1)S(1)}, bf16[48,2048]{1,0:T(8,128)(2,1)S(1)}, u32[]{:S(2)}, u32[]{:S(2)}) collective-permute-start(bf16[48,2048]{1,0:T(8,128)(2,1)S(1)} %get-tuple-element.69), channel_id=1, source_target_pairs={{0,4},{4,0},{8,12},{12,8},{1,5},{5,1},{9,13},{13,9},{2,6},{6,2},{1... | collective-permute-start | bytes 589832 | tf_op jit(solution)/shard_map/ppermute | solution.py:419
  11.8 1.5 %collective-permute-start.6 = (bf16[48,2048]{1,0:T(8,128)(2,1)S(1)}, bf16[48,2048]{1,0:T(8,128)(2,1)S(1)}, u32[]{:S(2)}, u32[]{:S(2)}) collective-permute-start(bf16[48,2048]{1,0:T(8,128)(2,1)S(1)} %get-tuple-element.70), channel_id=1, source_target_pairs={{0,8},{4,12},{8,0},{12,4},{1,9},{5,13},{9,1},{13,5},{2,10},{6,14},... | collective-permute-start | bytes 589832 | tf_op jit(solution)/shard_map/ppermute | solution.py:419
  13.3 0.4 collective-permute-start.7
  13.7 3.3 %collective-permute-done.2.refs_3_ = bf16[48,2048]{1,0:T(8,128)(2,1)S(1)} collective-permute-done((bf16[48,2048]{1,0:T(8,128)(2,1)S(1)}, bf16[48,2048]{1,0:T(8,128)(2,1)S(1)}, u32[]{:S(2)}, u32[]{:S(2)}) %collective-permute-start.2) | collective-permute-done | bytes 196640 | tf_op jit(solution)/shard_map/ppermute | solution.py:419
  17.0 0.6 %collective-permute-done.3.refs_4_ = bf16[48,2048]{1,0:T(8,128)(2,1)S(1)} collective-permute-done((bf16[48,2048]{1,0:T(8,128)(2,1)S(1)}, bf16[48,2048]{1,0:T(8,128)(2,1)S(1)}, u32[]{:S(2)}, u32[]{:S(2)}) %collective-permute-start.3) | collective-permute-done | bytes 196640 | tf_op jit(solution)/shard_map/ppermute | solution.py:419
  17.5 3.8 %act_grads_and_probs.1 = (f32[192,384]{1,0:T(8,128)S(1)}, f32[8,256,256]{2,1,0:T(8,128)S(1)}, bf16[768,2048]{1,0:T(8,128)(2,1)S(1)}, bf16[2048,768]{1,0:T(8,128)...) custom-call(s32[2,128]{1,0:T(2,128)S(1)} %get-tuple-element.52.pos_ref, ...), custom_call_target="tpu_custom_call" | custom-call | flops 738197504 | bytes 16599040 | tf_op jit(solution)/shard_map/act_grads_and_probs/pallas_call | solution.py:400
  21.4 3.7 %collective-permute-done.6.refs_2_ = bf16[48,2048]{1,0:T(8,128)(2,1)S(1)} collective-permute-done((bf16[48,2048]{1,0:T(8,128)(2,1)S(1)}, bf16[48,2048]{1,0:T(8,128)(2,1)S(1)}, u32[]{:S(2)}, u32[]{:S(2)}) %collective-permute-start.6) | collective-permute-done | bytes 196640 | tf_op jit(solution)/shard_map/ppermute | solution.py:419
  25.1 2.8 %experts.1 = (bf16[48,2048]{1,0:T(8,128)(2,1)S(1)}, bf16[48,2048]{1,0:T(8,128)(2,1)S(1)}, bf16[96,2048]{1,0:T(8,128)(2,1)S(1)}, bf16[96,2048]{1,0:T(8,128)(2,1)S...) custom-call(bf16[2048,768]{1,0:T(8,128)(2,1)S(1)} %get-tuple-element.72.gate_ref, ...), custom_call_target="tpu_custom_call" | custom-call | flops 1811939328 | bytes 8945664 | tf_op jit(solution)/shard_map/experts/pallas_call | solution.py:400
  27.9 1.6 %collective-permute-start.13 = (bf16[96,2048]{1,0:T(8,128)(2,1)S(1)}, bf16[96,2048]{1,0:T(8,128)(2,1)S(1)}, u32[]{:S(2)}, u32[]{:S(2)}) collective-permute-start(bf16[96,2048]{1,0:T(8,128)(2,1)S(1)} %get-tuple-element.76.refs_5_), channel_id=1, source_target_pairs={{0,4},{4,0},{8,12},{12,8},{1,5},{5,1},{9,13},{13,9},{2,6},{6,2},{1... | collective-permute-start | bytes 1179656 | tf_op jit(solution)/shard_map/ppermute | solution.py:419
  29.5 0.5 collective-permute-start.14
  30.0 1.5 %collective-permute-start.15 = (bf16[48,2048]{1,0:T(8,128)(2,1)S(1)}, bf16[48,2048]{1,0:T(8,128)(2,1)S(1)}, u32[]{:S(2)}, u32[]{:S(2)}) collective-permute-start(bf16[48,2048]{1,0:T(8,128)(2,1)S(1)} %get-tuple-element.78.refs_7_), channel_id=1, source_target_pairs={{0,12},{4,8},{8,4},{12,0},{1,13},{5,9},{9,5},{13,1},{2,14},{6,10},... | collective-permute-start | bytes 589832 | tf_op jit(solution)/shard_map/ppermute | solution.py:419
  31.5 0.3 gain_terms.1
  31.8 1.6 %collective-permute-start.8 = (f32[16,128]{1,0:T(8,128)S(1)}, f32[16,128]{1,0:T(8,128)S(1)}, u32[]{:S(2)}, u32[]{:S(2)}) collective-permute-start(f32[16,128]{1,0:T(8,128)S(1)} %gain_terms.1), channel_id=1, source_target_pairs={{0,1},{1,0},{2,3},{3,2},{4,5},{5,4},{6,7},{7,6},{8,9},{9,8},{10,11... | collective-permute-start | bytes 24584 | tf_op jit(solution)/shard_map/ppermute | solution.py:419
  33.4 2.1 %collective-permute-done.8 = f32[16,128]{1,0:T(8,128)S(1)} collective-permute-done((f32[16,128]{1,0:T(8,128)S(1)}, f32[16,128]{1,0:T(8,128)S(1)}, u32[]{:S(2)}, u32[]{:S(2)}) %collective-permute-start.8) | collective-permute-done | bytes 8224 | tf_op jit(solution)/shard_map/ppermute | solution.py:419
  35.5 2.6 %collective-permute-start.9 = (f32[16,128]{1,0:T(8,128)S(1)}, f32[16,128]{1,0:T(8,128)S(1)}, u32[]{:S(2)}, u32[]{:S(2)}) collective-permute-start(f32[16,128]{1,0:T(8,128)S(1)} %add.18), channel_id=1, source_target_pairs={{0,2},{1,3},{2,0},{3,1},{4,6},{5,7},{6,4},{7,5},{8,10},{9,11},{10,... | collective-permute-start | bytes 24584 | tf_op jit(solution)/shard_map/ppermute | solution.py:419
  38.1 1.4 %collective-permute-start.18 = (bf16[48,2048]{1,0:T(8,128)(2,1)S(1)}, bf16[48,2048]{1,0:T(8,128)(2,1)S(1)}, u32[]{:S(2)}, u32[]{:S(2)}) collective-permute-start(bf16[48,2048]{1,0:T(8,128)(2,1)S(1)} %get-tuple-element.89), channel_id=1, source_target_pairs={{0,12},{4,8},{8,4},{12,0},{1,13},{5,9},{9,5},{13,1},{2,14},{6,10},... | collective-permute-start | bytes 589832 | tf_op jit(solution)/shard_map/ppermute | solution.py:419
  39.5 0.5 collective-permute-done.9
  40.1 1.4 %collective-permute-start.12 = (f32[16,128]{1,0:T(8,128)S(1)}, f32[16,128]{1,0:T(8,128)S(1)}, u32[]{:S(2)}, u32[]{:S(2)}) collective-permute-start(f32[16,128]{1,0:T(8,128)S(1)} %add.19), channel_id=1, source_target_pairs={{0,12},{4,8},{8,4},{12,0},{1,13},{5,9},{9,5},{13,1},{2,14},{6,10},... | collective-permute-start | bytes 24584 | tf_op jit(solution)/shard_map/ppermute | solution.py:419
  41.5 3.5 %collective-permute-done.15.refs_3_ = bf16[48,2048]{1,0:T(8,128)(2,1)S(1)} collective-permute-done((bf16[48,2048]{1,0:T(8,128)(2,1)S(1)}, bf16[48,2048]{1,0:T(8,128)(2,1)S(1)}, u32[]{:S(2)}, u32[]{:S(2)}) %collective-permute-start.15) | collective-permute-done | bytes 196640 | tf_op jit(solution)/shard_map/ppermute | solution.py:419
  45.0 0.8 %collective-permute-start.11 = (f32[16,128]{1,0:T(8,128)S(1)}, f32[16,128]{1,0:T(8,128)S(1)}, u32[]{:S(2)}, u32[]{:S(2)}) collective-permute-start(f32[16,128]{1,0:T(8,128)S(1)} %add.19), channel_id=1, source_target_pairs={{0,8},{4,12},{8,0},{12,4},{1,9},{5,13},{9,1},{13,5},{2,10},{6,14},... | collective-permute-start | bytes 24584 | tf_op jit(solution)/shard_map/ppermute | solution.py:419
  45.8 1.5 %collective-permute-start.10 = (f32[16,128]{1,0:T(8,128)S(1)}, f32[16,128]{1,0:T(8,128)S(1)}, u32[]{:S(2)}, u32[]{:S(2)}) collective-permute-start(f32[16,128]{1,0:T(8,128)S(1)} %add.19), channel_id=1, source_target_pairs={{0,4},{4,0},{8,12},{12,8},{1,5},{5,1},{9,13},{13,9},{2,6},{6,2},{1... | collective-permute-start | bytes 24584 | tf_op jit(solution)/shard_map/ppermute | solution.py:419
  47.3 0.8 %collective-permute-done.14.refs_2_.refs_4_ = bf16[96,2048]{1,0:T(8,128)(2,1)S(1)} collective-permute-done((bf16[96,2048]{1,0:T(8,128)(2,1)S(1)}, bf16[96,2048]{1,0:T(8,128)(2,1)S(1)}, u32[]{:S(2)}, u32[]{:S(2)}) %collective-permute-start.14) | collective-permute-done | bytes 393248 | tf_op jit(solution)/shard_map/ppermute | solution.py:419
  48.1 4.0 %residual_attention_backward.1 = (bf16[128,2048]{1,0:T(8,128)(2,1)}, bf16[128,2048]{1,0:T(8,128)(2,1)}, f32[128,512]{1,0:T(8,128)S(1)}, bf16[128,512]{1,0:T(8,128)(2,1)S(1)}) custom-call(bf16[128,192]{1,0:T(8,128)(2,1)S(1)} %get-tuple-element.80.place_ref, f32[1,2048]{1,0:T(1,128)S(1)} %get-tuple-element.60.gain_ref, ...), custom_call_target="tpu_custom_call" | custom-call | flops 369098752 | bytes 6610944 | tf_op jit(solution)/shard_map/residual_attention_backward/pallas_call | solution.py:400
  52.3 0.5 collective-permute-start.16
  52.8 0.8 %collective-permute-done.16 = f32[16,128]{1,0:T(8,128)S(1)} collective-permute-done((f32[16,128]{1,0:T(8,128)S(1)}, f32[16,128]{1,0:T(8,128)S(1)}, u32[]{:S(2)}, u32[]{:S(2)}) %collective-permute-start.16) | collective-permute-done | bytes 8224 | tf_op jit(solution)/shard_map/ppermute | solution.py:419
  53.7 1.2 %layer_output.1 = (bf16[128,2048]{1,0:T(8,128)(2,1)}, bf16[128,256]{1,0:T(8,128)(2,1)}, bf16[128,256]{1,0:T(8,128)(2,1)}, f32[1,128]{1,0:T(1,128)}, f32[16,128]{1,0:T(8,128)}) custom-call(bf16[128,192]{1,0:T(8,128)(2,1)S(1)} %get-tuple-element.80.place_ref, f32[128,256]{1,0:T(8,128)S(1)} %get-tuple-element.68.weight_ref, f32[16,128]{1,0:T(8,128)S(1)} %add.23.gain_ref, ...), custom_call_target="tpu_custom_call" | custom-call | flops 100663296 | bytes 3473920 | tf_op jit(solution)/shard_map/layer_output/pallas_call | solution.py:400
  (17 shorter events, 0.4 us)
Async XLA Ops:
  2.2 11.1 %collective-permute-start.4 = (bf16[48,2048]{1,0:T(8,128)(2,1)S(1)}, bf16[48,2048]{1,0:T(8,128)(2,1)S(1)}, u32[]{:S(2)}, u32[]{:S(2)}) collective-permute-start(bf16[48,2048]{1,0:T(8,128)(2,1)S(1)} %get-tuple-element.66), channel_id=1, source_target_pairs={{0,12},{4,8},{8,4},{12,0},{1,13},{5,9},{9,5},{13,1},{2,14},{6,10},... | collective-permute-start | bytes 589832 | tf_op jit(solution)/shard_map/ppermute | solution.py:419
  6.1 1.5 %collective-permute-start = (bf16[128,256]{1,0:T(8,128)(2,1)}, bf16[128,256]{1,0:T(8,128)(2,1)S(1)}, u32[]{:S(2)}, u32[]{:S(2)}) collective-permute-start(bf16[128,256]{1,0:T(8,128)(2,1)} %bitcast.17), channel_id=1, source_target_pairs={{0,16},{16,0},{1,17},{17,1},{2,18},{18,2},{3,19},{19,3},{4,20},{20... | collective-permute-start | bytes 196616 | tf_op jit(solution)/shard_map/ppermute | solution.py:419
  6.1 1.6 %collective-permute-start.1 = (bf16[128,256]{1,0:T(8,128)(2,1)}, bf16[128,256]{1,0:T(8,128)(2,1)S(1)}, u32[]{:S(2)}, u32[]{:S(2)}) collective-permute-start(bf16[128,256]{1,0:T(8,128)(2,1)} %bitcast.19), channel_id=1, source_target_pairs={{0,16},{16,0},{1,17},{17,1},{2,18},{18,2},{3,19},{19,3},{4,20},{20... | collective-permute-start | bytes 196616 | tf_op jit(solution)/shard_map/ppermute | solution.py:419
  9.2 7.8 %collective-permute-start.2 = (bf16[48,2048]{1,0:T(8,128)(2,1)S(1)}, bf16[48,2048]{1,0:T(8,128)(2,1)S(1)}, u32[]{:S(2)}, u32[]{:S(2)}) collective-permute-start(bf16[48,2048]{1,0:T(8,128)(2,1)S(1)} %get-tuple-element.64), channel_id=1, source_target_pairs={{0,4},{4,0},{8,12},{12,8},{1,5},{5,1},{9,13},{13,9},{2,6},{6,2},{1... | collective-permute-start | bytes 589832 | tf_op jit(solution)/shard_map/ppermute | solution.py:419
  9.8 7.8 %collective-permute-start.3 = (bf16[48,2048]{1,0:T(8,128)(2,1)S(1)}, bf16[48,2048]{1,0:T(8,128)(2,1)S(1)}, u32[]{:S(2)}, u32[]{:S(2)}) collective-permute-start(bf16[48,2048]{1,0:T(8,128)(2,1)S(1)} %get-tuple-element.65), channel_id=1, source_target_pairs={{0,8},{4,12},{8,0},{12,4},{1,9},{5,13},{9,1},{13,5},{2,10},{6,14},... | collective-permute-start | bytes 589832 | tf_op jit(solution)/shard_map/ppermute | solution.py:419
  9.9 11.5 %collective-permute-start.5 = (bf16[48,2048]{1,0:T(8,128)(2,1)S(1)}, bf16[48,2048]{1,0:T(8,128)(2,1)S(1)}, u32[]{:S(2)}, u32[]{:S(2)}) collective-permute-start(bf16[48,2048]{1,0:T(8,128)(2,1)S(1)} %get-tuple-element.69), channel_id=1, source_target_pairs={{0,4},{4,0},{8,12},{12,8},{1,5},{5,1},{9,13},{13,9},{2,6},{6,2},{1... | collective-permute-start | bytes 589832 | tf_op jit(solution)/shard_map/ppermute | solution.py:419
  11.8 13.3 %collective-permute-start.6 = (bf16[48,2048]{1,0:T(8,128)(2,1)S(1)}, bf16[48,2048]{1,0:T(8,128)(2,1)S(1)}, u32[]{:S(2)}, u32[]{:S(2)}) collective-permute-start(bf16[48,2048]{1,0:T(8,128)(2,1)S(1)} %get-tuple-element.70), channel_id=1, source_target_pairs={{0,8},{4,12},{8,0},{12,4},{1,9},{5,13},{9,1},{13,5},{2,10},{6,14},... | collective-permute-start | bytes 589832 | tf_op jit(solution)/shard_map/ppermute | solution.py:419
  13.3 11.8 %collective-permute-start.7 = (bf16[48,2048]{1,0:T(8,128)(2,1)S(1)}, bf16[48,2048]{1,0:T(8,128)(2,1)S(1)}, u32[]{:S(2)}, u32[]{:S(2)}) collective-permute-start(bf16[48,2048]{1,0:T(8,128)(2,1)S(1)} %get-tuple-element.71), channel_id=1, source_target_pairs={{0,12},{4,8},{8,4},{12,0},{1,13},{5,9},{9,5},{13,1},{2,14},{6,10},... | collective-permute-start | bytes 589832 | tf_op jit(solution)/shard_map/ppermute | solution.py:419
  27.9 17.9 %collective-permute-start.13 = (bf16[96,2048]{1,0:T(8,128)(2,1)S(1)}, bf16[96,2048]{1,0:T(8,128)(2,1)S(1)}, u32[]{:S(2)}, u32[]{:S(2)}) collective-permute-start(bf16[96,2048]{1,0:T(8,128)(2,1)S(1)} %get-tuple-element.76.refs_5_), channel_id=1, source_target_pairs={{0,4},{4,0},{8,12},{12,8},{1,5},{5,1},{9,13},{13,9},{2,6},{6,2},{1... | collective-permute-start | bytes 1179656 | tf_op jit(solution)/shard_map/ppermute | solution.py:419
  29.5 18.6 %collective-permute-start.14 = (bf16[96,2048]{1,0:T(8,128)(2,1)S(1)}, bf16[96,2048]{1,0:T(8,128)(2,1)S(1)}, u32[]{:S(2)}, u32[]{:S(2)}) collective-permute-start(bf16[96,2048]{1,0:T(8,128)(2,1)S(1)} %get-tuple-element.77.refs_6_), channel_id=1, source_target_pairs={{0,8},{4,12},{8,0},{12,4},{1,9},{5,13},{9,1},{13,5},{2,10},{6,14},... | collective-permute-start | bytes 1179656 | tf_op jit(solution)/shard_map/ppermute | solution.py:419
  30.0 15.0 %collective-permute-start.15 = (bf16[48,2048]{1,0:T(8,128)(2,1)S(1)}, bf16[48,2048]{1,0:T(8,128)(2,1)S(1)}, u32[]{:S(2)}, u32[]{:S(2)}) collective-permute-start(bf16[48,2048]{1,0:T(8,128)(2,1)S(1)} %get-tuple-element.78.refs_7_), channel_id=1, source_target_pairs={{0,12},{4,8},{8,4},{12,0},{1,13},{5,9},{9,5},{13,1},{2,14},{6,10},... | collective-permute-start | bytes 589832 | tf_op jit(solution)/shard_map/ppermute | solution.py:419
  31.8 3.7 %collective-permute-start.8 = (f32[16,128]{1,0:T(8,128)S(1)}, f32[16,128]{1,0:T(8,128)S(1)}, u32[]{:S(2)}, u32[]{:S(2)}) collective-permute-start(f32[16,128]{1,0:T(8,128)S(1)} %gain_terms.1), channel_id=1, source_target_pairs={{0,1},{1,0},{2,3},{3,2},{4,5},{5,4},{6,7},{7,6},{8,9},{9,8},{10,11... | collective-permute-start | bytes 24584 | tf_op jit(solution)/shard_map/ppermute | solution.py:419
  35.5 4.5 %collective-permute-start.9 = (f32[16,128]{1,0:T(8,128)S(1)}, f32[16,128]{1,0:T(8,128)S(1)}, u32[]{:S(2)}, u32[]{:S(2)}) collective-permute-start(f32[16,128]{1,0:T(8,128)S(1)} %add.18), channel_id=1, source_target_pairs={{0,2},{1,3},{2,0},{3,1},{4,6},{5,7},{6,4},{7,5},{8,10},{9,11},{10,... | collective-permute-start | bytes 24584 | tf_op jit(solution)/shard_map/ppermute | solution.py:419
  38.1 15.6 %collective-permute-start.18 = (bf16[48,2048]{1,0:T(8,128)(2,1)S(1)}, bf16[48,2048]{1,0:T(8,128)(2,1)S(1)}, u32[]{:S(2)}, u32[]{:S(2)}) collective-permute-start(bf16[48,2048]{1,0:T(8,128)(2,1)S(1)} %get-tuple-element.89), channel_id=1, source_target_pairs={{0,12},{4,8},{8,4},{12,0},{1,13},{5,9},{9,5},{13,1},{2,14},{6,10},... | collective-permute-start | bytes 589832 | tf_op jit(solution)/shard_map/ppermute | solution.py:419
  40.1 12.2 %collective-permute-start.12 = (f32[16,128]{1,0:T(8,128)S(1)}, f32[16,128]{1,0:T(8,128)S(1)}, u32[]{:S(2)}, u32[]{:S(2)}) collective-permute-start(f32[16,128]{1,0:T(8,128)S(1)} %add.19), channel_id=1, source_target_pairs={{0,12},{4,8},{8,4},{12,0},{1,13},{5,9},{9,5},{13,1},{2,14},{6,10},... | collective-permute-start | bytes 24584 | tf_op jit(solution)/shard_map/ppermute | solution.py:419
  45.0 7.3 %collective-permute-start.11 = (f32[16,128]{1,0:T(8,128)S(1)}, f32[16,128]{1,0:T(8,128)S(1)}, u32[]{:S(2)}, u32[]{:S(2)}) collective-permute-start(f32[16,128]{1,0:T(8,128)S(1)} %add.19), channel_id=1, source_target_pairs={{0,8},{4,12},{8,0},{12,4},{1,9},{5,13},{9,1},{13,5},{2,10},{6,14},... | collective-permute-start | bytes 24584 | tf_op jit(solution)/shard_map/ppermute | solution.py:419
  45.8 6.4 %collective-permute-start.10 = (f32[16,128]{1,0:T(8,128)S(1)}, f32[16,128]{1,0:T(8,128)S(1)}, u32[]{:S(2)}, u32[]{:S(2)}) collective-permute-start(f32[16,128]{1,0:T(8,128)S(1)} %add.19), channel_id=1, source_target_pairs={{0,4},{4,0},{8,12},{12,8},{1,5},{5,1},{9,13},{13,9},{2,6},{6,2},{1... | collective-permute-start | bytes 24584 | tf_op jit(solution)/shard_map/ppermute | solution.py:419
  52.2 1.5 %collective-permute-start.17 = (bf16[128,512]{1,0:T(8,128)(2,1)S(1)}, bf16[128,512]{1,0:T(8,128)(2,1)S(1)}, u32[]{:S(2)}, u32[]{:S(2)}) collective-permute-start(bf16[128,512]{1,0:T(8,128)(2,1)S(1)} %get-tuple-element.87), channel_id=1, source_target_pairs={{0,16},{16,0},{1,17},{17,1},{2,18},{18,2},{3,19},{19,3},{4,20},{20... | collective-permute-start | bytes 393224 | tf_op jit(solution)/shard_map/ppermute | solution.py:419
  52.3 1.4 %collective-permute-start.16 = (f32[16,128]{1,0:T(8,128)S(1)}, f32[16,128]{1,0:T(8,128)S(1)}, u32[]{:S(2)}, u32[]{:S(2)}) collective-permute-start(f32[16,128]{1,0:T(8,128)S(1)} %add_add_fusion), channel_id=1, source_target_pairs={{0,16},{16,0},{1,17},{17,1},{2,18},{18,2},{3,19},{19,3},{4,20},{20... | collective-permute-start | bytes 24584 | tf_op jit(solution)/shard_map/ppermute | solution.py:419

commit v6 on v5

--- a/solution.py
+++ b/solution.py
@@ -17,6 +17,7 @@
 COLS = 256
 LANES = 128
 GAIN_LINES = D // LANES
+WIDE_LINES = 128
 SCALE = HEAD_SIZE ** (-0.5)
 EXP2_SCALE = SCALE * 1.4426950408889634
 F32 = jnp.float32
@@ -236,50 +237,32 @@
         copy.wait()
 
 
-def part_views(refs, rows, part):
-    return [r if r.shape[0] != 2 * rows else r.at[part * rows : (part + 1) * rows] for r in refs]
-
-
-def joined(step, pieces):
-    return pieces > 1 and step > 0 and step & (step - 1) == 0
-
-
-def split_parts(refs, pieces):
-    back, out = [], []
-    at = 0
-    for s in range(pieces):
-        back.append(refs[at])
-        at += not joined(s, pieces)
-        out.append(refs[at])
-        at += 1
-    return back, out
-
-
-def expert_kernel(capacity, pieces, gate_ref, down_ref, d_act_ref, *refs):
+def expert_back_kernel(capacity, pieces, start, gate_ref, d_act_ref, *refs):
     rows = stacked(refs[:pieces])
-    back_refs, out_refs = split_parts(refs[pieces:], pieces)
-    back_refs = part_views(back_refs, EXP_DEV * capacity, 0)
-    out_refs = part_views(out_refs, EXP_DEV * capacity, 1)
-    first = first_expert_rows(rows.shape[0], capacity)
+    act_ref, back_refs = refs[pieces], refs[pieces + 1 :]
+    count = rows.shape[0]
+    first = first_expert_rows(count, capacity)
     both = mm(rows, gate_ref[...])
     pre = jnp.where(first, both[:, :FFE], both[:, FFE:])
     gate = 1.0 / (1.0 + jnp.exp(-pre))
     act = pre * gate
-    d_pre = d_act_ref[...] * gate * (1.0 + pre * (1.0 - gate))
+    d_pre = d_act_ref[start : start + count, :] * gate * (1.0 + pre * (1.0 - gate))
     act, d_pre = [
         jnp.concatenate([jnp.where(first, x, 0.0), jnp.where(first, 0.0, x)], axis=1).astype(BF16)
         for x in (act, d_pre)
     ]
+    act_ref[...] = act
     for cols in column_blocks():
         store_pieces(back_refs, cols, mm(d_pre, gate_ref[cols, :], NT).astype(BF16))
+
+
+def expert_out_kernel(pieces, acts, down_ref, gain_ref, *refs):
+    act = stacked(refs[:acts])
+    refs = refs[acts:]
+    row_refs, back_refs = refs[:pieces], refs[pieces : 2 * pieces]
+    terms_ref, out_refs = refs[2 * pieces], refs[2 * pieces + 1 :]
+    for cols in column_blocks():
         store_pieces(out_refs, cols, mm(act, down_ref[:, cols]).astype(BF16))
-
-
-def gain_kernel(pieces, rows, gain_ref, *refs):
-    row_refs = refs[:pieces]
-    back_refs = part_views(refs[pieces:-1], rows, 0)
-    terms_ref = refs[-1]
-    for cols in column_blocks():
         products = stacked(row_refs, cols).astype(F32) * stacked(back_refs, cols).astype(F32)
         terms = jnp.sum(products, axis=0, keepdims=True) / gain_ref[:, cols]
         for at in range(0, COLS, LANES):
@@ -288,9 +271,9 @@
 
 
 def backward_kernel(
-    count, pieces, rows, place_ref, gain_ref, hidden_ref, grad_ref, query_ref, probs_ref, *refs
+    count, pieces, place_ref, gain_ref, hidden_ref, grad_ref, query_ref, probs_ref, *refs
 ):
-    dn_refs = part_views(refs[:pieces], rows, 0)
+    dn_refs = refs[:pieces]
     key_refs = refs[pieces : pieces + count]
     value_refs = refs[pieces + count : pieces + 2 * count]
     resid_hbm, dq_hbm, own_ref = refs[pieces + 2 * count : pieces + 2 * count + 3]
@@ -353,11 +336,11 @@
 
 
 def output_kernel(
-    count, pieces, rows, tokens_in_all, place_ref, weight_ref, gain_ref, hidden_ref, grad_ref, *refs
+    count, pieces, tokens_in_all, place_ref, weight_ref, gain_ref, hidden_ref, grad_ref, *refs
 ):
     own_ref, refs = refs[0], refs[1:]
     arrived_refs = refs[: count - 1]
-    y_refs = part_views(refs[count - 1 : count - 1 + pieces], rows, 1)
+    y_refs = refs[count - 1 : count - 1 + pieces]
     out_hbm, dk_hbm, dv_hbm, d_weight_hbm, d_gain_hbm = refs[count - 1 + pieces : -6]
     out_ref, dk_ref, dv_ref, d_weight_ref, d_gain_ref, sems = refs[-6:]
     split = KEY_VALUE_HEADS * HEAD_SIZE
@@ -419,38 +402,28 @@
     return lax.ppermute(value, axis, [(i, i ^ step) for i in range(count)])
 
 
-def exchange(pieces, capacity):
+def exchange_flat(flat, capacity):
     count = lax.axis_size("exp")
     rows = EXP_DEV * capacity
-    if len(pieces) == count:
-        return [pieces[0]] + [pairwise(pieces[s], "exp", s) for s in range(count - 1, 0, -1)][::-1]
-    flat = pieces[0]
     blocks = [flat[s * rows : (s + 1) * rows] for s in range(count)]
     moved = [blocks[0]] + [pairwise(blocks[s], "exp", s) for s in range(1, count)]
-    return [jnp.concatenate(moved, axis=0)]
-
-
-def exchange_apart(pieces, capacity):
-    if len(pieces) == 1:
-        return exchange(pieces, capacity)
+    return jnp.concatenate(moved, axis=0)
+
+
+def exchange(pieces, capacity, steps):
+    if lax.axis_size("exp") != len(pieces):
+        return [exchange_flat(pieces[0], capacity)]
     return [
-        piece if s == 0 or joined(s, len(pieces)) else pairwise(piece, "exp", s)
-        for s, piece in enumerate(pieces)
+        pairwise(piece, "exp", s) if s in steps and s > 0 else piece for s, piece in enumerate(pieces)
     ]
 
 
-def sum_over(value, axis):
-    step = 1
-    while step < lax.axis_size(axis):
+def sum_over(value, axis, first=1, last=None):
+    step = first
+    while step < lax.axis_size(axis) and (last is None or step <= last):
         value = value + pairwise(value, axis, step)
         step *= 2
     return value
-
-
-def tree_sum(parts):
-    while len(parts) > 1:
-        parts = [parts[i] + parts[i + 1] for i in range(0, len(parts), 2)]
-    return parts[0]
 
 
 def shaped(shape, dtype):
@@ -517,11 +490,10 @@
         ],
     )
     all_keys[0], all_values[0] = own_keys, own_values
-    apart = [s for s in range(1, piece_count) if not joined(s, piece_count)]
-    near = [s for s in range(1, piece_count) if joined(s, piece_count)]
-    arrived_grad = exchange(send_grad, capacity) if piece_count == 1 else list(send_grad)
-    for s in apart:
-        arrived_grad[s] = pairwise(send_grad[s], "exp", s)
+    steps = range(piece_count)
+    groups = [[s for s in steps if s & (s - 1) == 0], [s for s in steps if s & (s - 1) != 0]]
+    groups = [group for group in groups if group]
+    arrived_grad = exchange(send_grad, capacity, steps)
 
     hidden, *send_x = run(
         functools.partial(attention_kernel, ctx_count),
@@ -530,15 +502,7 @@
         placed(VMEM, [token_shape] + piece_shapes),
         attn_flops + place_flops,
     )
-    arrived_x = exchange(send_x, capacity) if piece_count == 1 else list(send_x)
-    for s in apart:
-        arrived_x[s] = pairwise(send_x[s], "exp", s)
-    if near:
-        after, _ = lax.optimization_barrier(([send_grad[s] for s in near], send_x[0]))
-        for s, piece in zip(near, after):
-            arrived_grad[s] = pairwise(piece, "exp", s)
-        for s in near:
-            arrived_x[s] = pairwise(send_x[s], "exp", s)
+    arrived_x = exchange(send_x, capacity, steps)
 
     d_act, probs, down_near, gate_near, place, weight_wide = run(
         functools.partial(probs_kernel, ctx_count, capacity, piece_count),
@@ -561,41 +525,47 @@
         scratch=[pltpu.SemaphoreType.DMA((2 * EXP_DEV,))],
     )
 
-    return_shapes = []
-    for s in range(piece_count):
-        if joined(s, piece_count):
-            return_shapes.append(shaped((2 * rows, D), BF16))
-        else:
-            return_shapes.extend([piece_shapes[0]] * 2)
-    sent = run(
-        functools.partial(expert_kernel, capacity, piece_count),
-        "experts",
-        placed(VMEM, [gate_near, down_near, d_act] + arrived_x),
-        placed(VMEM, return_shapes),
-        3 * expert_flops,
-    )
-    send_dn, send_y = split_parts(sent, piece_count)
-    dn = exchange(send_dn, capacity)
-    y = [
-        dn[s] if joined(s, piece_count) else moved
-        for s, moved in enumerate(exchange_apart(send_y, capacity))
-    ]
-    (terms,) = run(
-        functools.partial(gain_kernel, piece_count, rows),
-        "gain_terms",
-        placed(VMEM, [gain] + arrived_x + send_dn),
-        placed(VMEM, [shaped((GAIN_LINES, LANES), F32)]),
-        2 * slots * D,
-    )
-    terms, place_back = lax.optimization_barrier((sum_over(terms, "dp"), place))
-
-    if piece_count == 1:
-        terms = sum_over(terms, "exp")
-    else:
-        terms = tree_sum([terms] + [pairwise(terms, "exp", s) for s in range(1, exp_count)])
+    ordered = [s for group in groups for s in group]
+    dn = [None] * piece_count
+    send_dn = [None] * piece_count
+    acts = []
+    done = 0
+    for group in groups:
+        group_rows = sum(piece_shapes[s].shape[0] for s in group)
+        act, *parts = run(
+            functools.partial(expert_back_kernel, capacity, len(group), done),
+            "expert_backward",
+            placed(VMEM, [gate_near, d_act] + [arrived_x[s] for s in group]),
+            placed(
+                VMEM,
+                [shaped((group_rows, EXP_DEV * FFE), BF16)] + [piece_shapes[s] for s in group],
+            ),
+            2 * expert_flops * group_rows // slots,
+        )
+        acts.append(act)
+        done += group_rows
+        for s, part in zip(group, parts):
+            send_dn[s] = part
+    dn = exchange(send_dn, capacity, steps)
+    terms, *outs = run(
+        functools.partial(expert_out_kernel, piece_count, len(acts)),
+        "expert_output",
+        placed(VMEM, [down_near, gain] + acts)
+        + placed(VMEM, [arrived_x[s] for s in ordered] + [send_dn[s] for s in ordered]),
+        placed(VMEM, [shaped((GAIN_LINES, LANES), F32)] + piece_shapes),
+        expert_flops,
+    )
+    terms = sum_over(sum_over(terms, "ctx"), "dp", last=1)
+    send_y = [outs[ordered.index(s)] for s in steps]
+    terms, send_y, dn = lax.optimization_barrier((terms, send_y, dn))
+    y = exchange(send_y, capacity, steps)
+    terms = jnp.pad(terms, ((0, WIDE_LINES - GAIN_LINES), (0, 0)))
+    terms = sum_over(terms, "dp", first=2)[:GAIN_LINES]
+    terms, place_back = lax.optimization_barrier((terms, place))
+    terms = sum_over(terms, "exp", last=1)
 
     d_hidden, d_queries, kv_own, *kv_send = run(
-        functools.partial(backward_kernel, ctx_count, piece_count, rows),
+        functools.partial(backward_kernel, ctx_count, piece_count),
         "residual_attention_backward",
         placed(VMEM, [place_back, gain, hidden, grad_rows, query_rows, probs])
         + placed(VMEM, dn + all_keys + all_values),
@@ -613,8 +583,8 @@
             pltpu.SemaphoreType.DMA((1 + KEY_VALUE_HEADS,)),
         ],
     )
-    terms, kv_own = lax.optimization_barrier((terms, kv_own))
-    terms = sum_over(terms, "ctx")
+    terms, kv_send = lax.optimization_barrier((terms, kv_send))
+    terms = sum_over(terms, "exp", first=2)
     kv_arrived = [pairwise(part, "ctx", s) for s, part in enumerate(kv_send, 1)]
 
     kv_shape = shaped((tokens, kv_width // 2), BF16)
@@ -622,7 +592,7 @@
     final_shapes += [shaped((1, tokens), F32), shaped((GAIN_LINES, LANES), F32)]
     total_tokens = tokens * ctx_count * exp_count * lax.axis_size("dp")
     layer_out, d_keys, d_values, d_weight, d_gain = run(
-        functools.partial(output_kernel, ctx_count, piece_count, rows, total_tokens),
+        functools.partial(output_kernel, ctx_count, piece_count, total_tokens),
         "layer_output",
         placed(
             VMEM,

time: 55 us -> 57 us (1.036)
  Pallas kernels: 15.1 us -> 16.7 us
  waiting for transfers between devices: 16.5 us -> 17.4 us
  starting transfers between devices: 22.5 us -> 21.9 us
    pallas_call x7 -> x8, Pallas kernels: 15.1 us -> 16.7 us  [run(): pl.pallas_call(kernel, out_shape=[x for _, x in outputs], in_specs=[spec[...]
    ppermute x19 -> x20, waiting for transfers between devices: 16.5 us -> 17.4 us  [pairwise(): return lax.ppermute(value, axis, [(i, i ^ step) for i in range(count)])]
    ppermute x19 -> x20, starting transfers between devices: 22.5 us -> 21.9 us  [pairwise(): return lax.ppermute(value, axis, [(i, i ^ step) for i in range(count)])]
  transfers between devices with their start and end apart: 19 -> 20, of which waited for: 10 -> 5; matrix products, arithmetic and copies ran while one was open for 0% -> 0% of each run, Pallas kernels for 17% -> 25%
where the time goes in v6:
time: 57 us; the launch traced here: 56.9 us
  starting transfers between devices  21.9 us (38%)
  waiting for transfers between devices  17.4 us (31%)
  Pallas kernels  16.7 us (29%)
  between operations  0.78 us (1%)
    ppermute x20, starting transfers between devices, pairwise(): return lax.ppermute(value, axis, [(i, i ^ step) for i in range(count)])  21.9 us
    ppermute x20, waiting for transfers between devices, pairwise(): return lax.ppermute(value, axis, [(i, i ^ step) for i in range(count)])  17.4 us
    pallas_call x8, Pallas kernels, run(): pl.pallas_call(kernel, out_shape=[x for _, x in outputs], in_specs=[spec[...  16.7 us
  transfers between devices with their start and end apart: 20, of which 5 were waited for; matrix products, arithmetic and copies ran while one was open for 0% of the time, Pallas kernels for 25%

profile of v6, /device:TPU:0, one launch (start us, length us, event | category | flops | bytes accessed | tf_op | source)
XLA Modules:
  0.0 56.9 jit_solution(7752801489668353555)
XLA Ops:
  0.6 1.5 %dispatch_grads.1 = (bf16[128,2048]{1,0:T(8,128)(2,1)S(1)}, bf16[128,256]{1,0:T(8,128)(2,1)S(1)}, bf16[128,256]{1,0:T(8,128)(2,1)S(1)}, f32[1,2048]{1,0:T(1,128)...) custom-call(bf16[128,2048]{1,0:T(8,128)(2,1)} %bitcast.13, ...), custom_call_target="tpu_custom_call" | custom-call | flops 100663296 | bytes 4213824 | tf_op jit(solution)/shard_map/dispatch_grads/pallas_call | solution.py:383
  2.2 3.0 %collective-permute-start.1 = (bf16[48,2048]{1,0:T(8,128)(2,1)S(1)}, bf16[48,2048]{1,0:T(8,128)(2,1)S(1)}, u32[]{:S(2)}, u32[]{:S(2)}) collective-permute-start(bf16[48,2048]{1,0:T(8,128)(2,1)S(1)} %get-tuple-element.70), channel_id=1, source_target_pairs={{0,4},{4,0},{8,12},{12,8},{1,5},{5,1},{9,13},{13,9},{2,6},{6,2},{1... | collective-permute-start | bytes 589832 | tf_op jit(solution)/shard_map/ppermute | solution.py:402
  5.2 0.0 collective-permute-start
  5.2 0.5 collective-permute-start.4
  5.7 1.5 %collective-permute-start.2 = (bf16[48,2048]{1,0:T(8,128)(2,1)S(1)}, bf16[48,2048]{1,0:T(8,128)(2,1)S(1)}, u32[]{:S(2)}, u32[]{:S(2)}) collective-permute-start(bf16[48,2048]{1,0:T(8,128)(2,1)S(1)} %get-tuple-element.71), channel_id=1, source_target_pairs={{0,8},{4,12},{8,0},{12,4},{1,9},{5,13},{9,1},{13,5},{2,10},{6,14},... | collective-permute-start | bytes 589832 | tf_op jit(solution)/shard_map/ppermute | solution.py:402
  7.2 0.0 collective-permute-start.3
  7.2 1.4 %attention_forward.1 = (bf16[128,2048]{1,0:T(8,128)(2,1)S(1)}, bf16[48,2048]{1,0:T(8,128)(2,1)S(1)}, bf16[48,2048]{1,0:T(8,128)(2,1)S(1)}, bf16[48,2048]{1,0:T(8,128)(2,1)S(1)}, bf16[48,2048]{1,0:T(8,128)(2,1)S(1)}) custom-call(s32[2,128]{1,0:T(2,128)S(1)} %get-tuple-element.64.pos_ref, s32[1,128]{1,0:T(1,128)S(1)} %get-tuple-element.65.slot_ref, ...), custom_call_target="tpu_custom_call" | custom-call | flops 369098752 | bytes 2631168 | tf_op jit(solution)/shard_map/attention_forward/pallas_call | solution.py:383
  8.7 3.0 %collective-permute-start.7 = (bf16[48,2048]{1,0:T(8,128)(2,1)S(1)}, bf16[48,2048]{1,0:T(8,128)(2,1)S(1)}, u32[]{:S(2)}, u32[]{:S(2)}) collective-permute-start(bf16[48,2048]{1,0:T(8,128)(2,1)S(1)} %get-tuple-element.85), channel_id=1, source_target_pairs={{0,12},{4,8},{8,4},{12,0},{1,13},{5,9},{9,5},{13,1},{2,14},{6,10},... | collective-permute-start | bytes 589832 | tf_op jit(solution)/shard_map/ppermute | solution.py:402
  11.6 0.5 collective-permute-start.5
  12.2 0.5 collective-permute-start.6
  12.6 9.2 %collective-permute-done.2.refs_4_ = bf16[48,2048]{1,0:T(8,128)(2,1)S(1)} collective-permute-done((bf16[48,2048]{1,0:T(8,128)(2,1)S(1)}, bf16[48,2048]{1,0:T(8,128)(2,1)S(1)}, u32[]{:S(2)}, u32[]{:S(2)}) %collective-permute-start.2) | collective-permute-done | bytes 196640 | tf_op jit(solution)/shard_map/ppermute | solution.py:402
  21.9 3.8 %act_grads_and_probs.1 = (f32[192,384]{1,0:T(8,128)S(1)}, f32[8,256,256]{2,1,0:T(8,128)S(1)}, bf16[768,2048]{1,0:T(8,128)(2,1)S(1)}, bf16[2048,768]{1,0:T(8,128)...) custom-call(s32[2,128]{1,0:T(2,128)S(1)} %get-tuple-element.64.pos_ref, ...), custom_call_target="tpu_custom_call" | custom-call | flops 738197504 | bytes 16599040 | tf_op jit(solution)/shard_map/act_grads_and_probs/pallas_call | solution.py:383
  25.7 1.8 %expert_backward.3 = (bf16[48,768]{1,0:T(8,128)(2,1)S(1)}, bf16[48,2048]{1,0:T(8,128)(2,1)S(1)}) custom-call(bf16[2048,768]{1,0:T(8,128)(2,1)S(1)} %get-tuple-element.77.gate_ref, f32[192,384]{1,0:T(8,128)S(1)} %get-tuple-element.78.d_act_ref, bf16[48,2048]{1,0:T(8,128)(2,1)S(1)} %collective-permute-done.7.refs_0_.refs_5_), custom_call_target="tpu_custom_call" | custom-call | flops 301989888 | bytes 3907584 | tf_op jit(solution)/shard_map/expert_backward/pallas_call | solution.py:383
  27.6 1.6 %collective-permute-start.12 = (bf16[48,2048]{1,0:T(8,128)(2,1)S(1)}, bf16[48,2048]{1,0:T(8,128)(2,1)S(1)}, u32[]{:S(2)}, u32[]{:S(2)}) collective-permute-start(bf16[48,2048]{1,0:T(8,128)(2,1)S(1)} %get-tuple-element.90.refs_9_), channel_id=1, source_target_pairs={{0,12},{4,8},{8,4},{12,0},{1,13},{5,9},{9,5},{13,1},{2,14},{6,10},... | collective-permute-start | bytes 589832 | tf_op jit(solution)/shard_map/ppermute | solution.py:402
  29.1 2.1 %expert_backward.2 = (bf16[144,768]{1,0:T(8,128)(2,1)S(1)}, bf16[48,2048]{1,0:T(8,128)(2,1)S(1)}, bf16[48,2048]{1,0:T(8,128)(2,1)S(1)}, bf16[48,2048]{1,0:T(8,128)(2,1)S(1)}) custom-call(bf16[2048,768]{1,0:T(8,128)(2,1)S(1)} %get-tuple-element.77.gate_ref, f32[192,384]{1,0:T(8,128)S(1)} %get-tuple-element.78.d_act_ref, ...), custom_call_target="tpu_custom_call" | custom-call | flops 905969664 | bytes 4841472 | tf_op jit(solution)/shard_map/expert_backward/pallas_call | solution.py:383
  31.2 1.6 %collective-permute-start.10 = (bf16[48,2048]{1,0:T(8,128)(2,1)S(1)}, bf16[48,2048]{1,0:T(8,128)(2,1)S(1)}, u32[]{:S(2)}, u32[]{:S(2)}) collective-permute-start(bf16[48,2048]{1,0:T(8,128)(2,1)S(1)} %get-tuple-element.88.refs_7_), channel_id=1, source_target_pairs={{0,4},{4,0},{8,12},{12,8},{1,5},{5,1},{9,13},{13,9},{2,6},{6,2},{1... | collective-permute-start | bytes 589832 | tf_op jit(solution)/shard_map/ppermute | solution.py:402
  32.8 0.5 collective-permute-start.11
  33.3 0.9 %expert_output.1 = (f32[16,128]{1,0:T(8,128)S(1)}, bf16[48,2048]{1,0:T(8,128)(2,1)S(1)}, bf16[48,2048]{1,0:T(8,128)(2,1)S(1)}, bf16[48,2048]{1,0:T(8,128)(2,1)S(1)}, bf16[48,2048]{1,0:T(8,128)(2,1)S(1)}) custom-call(bf16[768,2048]{1,0:T(8,128)(2,1)S(1)} %get-tuple-element.75.down_ref, f32[1,2048]{1,0:T(1,128)S(1)} %get-tuple-element.76.gain_ref, ...), custom_call_target="tpu_custom_call" | custom-call | flops 603979776 | bytes 5816320 | tf_op jit(solution)/shard_map/expert_output/pallas_call | solution.py:383
  34.2 0.1 collective-permute-start.8
  34.3 1.2 %collective-permute-done.8 = f32[16,128]{1,0:T(8,128)S(1)} collective-permute-done((f32[16,128]{1,0:T(8,128)S(1)}, f32[16,128]{1,0:T(8,128)S(1)}, u32[]{:S(2)}, u32[]{:S(2)}) %collective-permute-start.8) | collective-permute-done | bytes 8224 | tf_op jit(solution)/shard_map/ppermute | solution.py:402
  35.4 1.6 %collective-permute-start.9 = (f32[16,128]{1,0:T(8,128)S(1)}, f32[16,128]{1,0:T(8,128)S(1)}, u32[]{:S(2)}, u32[]{:S(2)}) collective-permute-start(f32[16,128]{1,0:T(8,128)S(1)} %add.17), channel_id=1, source_target_pairs={{0,1},{1,0},{2,3},{3,2},{4,5},{5,4},{6,7},{7,6},{8,9},{9,8},{10,11... | collective-permute-start | bytes 24584 | tf_op jit(solution)/shard_map/ppermute | solution.py:402
  37.0 2.1 %collective-permute-done.9 = f32[16,128]{1,0:T(8,128)S(1)} collective-permute-done((f32[16,128]{1,0:T(8,128)S(1)}, f32[16,128]{1,0:T(8,128)S(1)}, u32[]{:S(2)}, u32[]{:S(2)}) %collective-permute-start.9) | collective-permute-done | bytes 8224 | tf_op jit(solution)/shard_map/ppermute | solution.py:402
  39.1 2.6 %collective-permute-start.13 = (f32[128,128]{1,0:T(8,128)S(1)}, f32[128,128]{1,0:T(8,128)S(1)}, u32[]{:S(2)}, u32[]{:S(2)}) collective-permute-start(f32[128,128]{1,0:T(8,128)S(1)} %pad.4), channel_id=1, source_target_pairs={{0,2},{1,3},{2,0},{3,1},{4,6},{5,7},{6,4},{7,5},{8,10},{9,11},{10,... | collective-permute-start | bytes 196616 | tf_op jit(solution)/shard_map/ppermute | solution.py:402
  41.8 0.1 collective-permute-start.17
  41.9 2.0 %collective-permute-start.18 = (bf16[48,2048]{1,0:T(8,128)(2,1)S(1)}, bf16[48,2048]{1,0:T(8,128)(2,1)S(1)}, u32[]{:S(2)}, u32[]{:S(2)}) collective-permute-start(bf16[48,2048]{1,0:T(8,128)(2,1)S(1)} %get-tuple-element.112), channel_id=1, source_target_pairs={{0,8},{4,12},{8,0},{12,4},{1,9},{5,13},{9,1},{13,5},{2,10},{6,14},... | collective-permute-start | bytes 589832 | tf_op jit(solution)/shard_map/ppermute | solution.py:402
  43.8 1.4 %collective-permute-start.19 = (bf16[48,2048]{1,0:T(8,128)(2,1)S(1)}, bf16[48,2048]{1,0:T(8,128)(2,1)S(1)}, u32[]{:S(2)}, u32[]{:S(2)}) collective-permute-start(bf16[48,2048]{1,0:T(8,128)(2,1)S(1)} %get-tuple-element.113), channel_id=1, source_target_pairs={{0,12},{4,8},{8,4},{12,0},{1,13},{5,9},{9,5},{13,1},{2,14},{6,10},... | collective-permute-start | bytes 589832 | tf_op jit(solution)/shard_map/ppermute | solution.py:402
  45.3 0.1 collective-permute-start.14
  45.4 4.0 %residual_attention_backward.1 = (bf16[128,2048]{1,0:T(8,128)(2,1)}, bf16[128,2048]{1,0:T(8,128)(2,1)}, f32[128,512]{1,0:T(8,128)S(1)}, bf16[128,512]{1,0:T(8,128)(2,1)S(1)}) custom-call(bf16[128,192]{1,0:T(8,128)(2,1)S(1)} %get-tuple-element.98.place_ref, f32[1,2048]{1,0:T(1,128)S(1)} %get-tuple-element.76.gain_ref, ...), custom_call_target="tpu_custom_call" | custom-call | flops 369098752 | bytes 6217728 | tf_op jit(solution)/shard_map/residual_attention_backward/pallas_call | solution.py:383
  49.4 2.6 %collective-permute-done.14 = f32[16,128]{1,0:T(8,128)S(1)} collective-permute-done((f32[16,128]{1,0:T(8,128)S(1)}, f32[16,128]{1,0:T(8,128)S(1)}, u32[]{:S(2)}, u32[]{:S(2)}) %collective-permute-start.14) | collective-permute-done | bytes 8224 | tf_op jit(solution)/shard_map/ppermute | solution.py:402
  52.0 1.3 %collective-permute-start.15 = (f32[16,128]{1,0:T(8,128)S(1)}, f32[16,128]{1,0:T(8,128)S(1)}, u32[]{:S(2)}, u32[]{:S(2)}) collective-permute-start(f32[16,128]{1,0:T(8,128)S(1)} %add.20), channel_id=1, source_target_pairs={{0,8},{4,12},{8,0},{12,4},{1,9},{5,13},{9,1},{13,5},{2,10},{6,14},... | collective-permute-start | bytes 24584 | tf_op jit(solution)/shard_map/ppermute | solution.py:402
  53.3 2.3 %collective-permute-done.15 = f32[16,128]{1,0:T(8,128)S(1)} collective-permute-done((f32[16,128]{1,0:T(8,128)S(1)}, f32[16,128]{1,0:T(8,128)S(1)}, u32[]{:S(2)}, u32[]{:S(2)}) %collective-permute-start.15) | collective-permute-done | bytes 8224 | tf_op jit(solution)/shard_map/ppermute | solution.py:402
  55.7 1.2 %layer_output.1 = (bf16[128,2048]{1,0:T(8,128)(2,1)}, bf16[128,256]{1,0:T(8,128)(2,1)}, bf16[128,256]{1,0:T(8,128)(2,1)}, f32[1,128]{1,0:T(1,128)}, f32[16,128]{1,0:T(8,128)}) custom-call(bf16[128,192]{1,0:T(8,128)(2,1)S(1)} %get-tuple-element.98.place_ref, f32[128,256]{1,0:T(8,128)S(1)} %get-tuple-element.74.weight_ref, f32[16,128]{1,0:T(8,128)S(1)} %add.21.gain_ref, ...), custom_call_target="tpu_custom_call" | custom-call | flops 100663296 | bytes 3080704 | tf_op jit(solution)/shard_map/layer_output/pallas_call | solution.py:383
  (22 shorter events, 0.1 us)
Async XLA Ops:
  2.2 10.0 %collective-permute-start.1 = (bf16[48,2048]{1,0:T(8,128)(2,1)S(1)}, bf16[48,2048]{1,0:T(8,128)(2,1)S(1)}, u32[]{:S(2)}, u32[]{:S(2)}) collective-permute-start(bf16[48,2048]{1,0:T(8,128)(2,1)S(1)} %get-tuple-element.70), channel_id=1, source_target_pairs={{0,4},{4,0},{8,12},{12,8},{1,5},{5,1},{9,13},{13,9},{2,6},{6,2},{1... | collective-permute-start | bytes 589832 | tf_op jit(solution)/shard_map/ppermute | solution.py:402
  5.2 2.1 %collective-permute-start = (bf16[128,256]{1,0:T(8,128)(2,1)}, bf16[128,256]{1,0:T(8,128)(2,1)S(1)}, u32[]{:S(2)}, u32[]{:S(2)}) collective-permute-start(bf16[128,256]{1,0:T(8,128)(2,1)} %bitcast.17), channel_id=1, source_target_pairs={{0,16},{16,0},{1,17},{17,1},{2,18},{18,2},{3,19},{19,3},{4,20},{20... | collective-permute-start | bytes 196616 | tf_op jit(solution)/shard_map/ppermute | solution.py:402
  5.2 2.1 %collective-permute-start.4 = (bf16[128,256]{1,0:T(8,128)(2,1)}, bf16[128,256]{1,0:T(8,128)(2,1)S(1)}, u32[]{:S(2)}, u32[]{:S(2)}) collective-permute-start(bf16[128,256]{1,0:T(8,128)(2,1)} %bitcast.19), channel_id=1, source_target_pairs={{0,16},{16,0},{1,17},{17,1},{2,18},{18,2},{3,19},{19,3},{4,20},{20... | collective-permute-start | bytes 196616 | tf_op jit(solution)/shard_map/ppermute | solution.py:402
  5.7 16.2 %collective-permute-start.2 = (bf16[48,2048]{1,0:T(8,128)(2,1)S(1)}, bf16[48,2048]{1,0:T(8,128)(2,1)S(1)}, u32[]{:S(2)}, u32[]{:S(2)}) collective-permute-start(bf16[48,2048]{1,0:T(8,128)(2,1)S(1)} %get-tuple-element.71), channel_id=1, source_target_pairs={{0,8},{4,12},{8,0},{12,4},{1,9},{5,13},{9,1},{13,5},{2,10},{6,14},... | collective-permute-start | bytes 589832 | tf_op jit(solution)/shard_map/ppermute | solution.py:402
  7.2 14.7 %collective-permute-start.3 = (bf16[48,2048]{1,0:T(8,128)(2,1)S(1)}, bf16[48,2048]{1,0:T(8,128)(2,1)S(1)}, u32[]{:S(2)}, u32[]{:S(2)}) collective-permute-start(bf16[48,2048]{1,0:T(8,128)(2,1)S(1)} %get-tuple-element.72), channel_id=1, source_target_pairs={{0,12},{4,8},{8,4},{12,0},{1,13},{5,9},{9,5},{13,1},{2,14},{6,10},... | collective-permute-start | bytes 589832 | tf_op jit(solution)/shard_map/ppermute | solution.py:402
  8.7 17.0 %collective-permute-start.7 = (bf16[48,2048]{1,0:T(8,128)(2,1)S(1)}, bf16[48,2048]{1,0:T(8,128)(2,1)S(1)}, u32[]{:S(2)}, u32[]{:S(2)}) collective-permute-start(bf16[48,2048]{1,0:T(8,128)(2,1)S(1)} %get-tuple-element.85), channel_id=1, source_target_pairs={{0,12},{4,8},{8,4},{12,0},{1,13},{5,9},{9,5},{13,1},{2,14},{6,10},... | collective-permute-start | bytes 589832 | tf_op jit(solution)/shard_map/ppermute | solution.py:402
  11.6 17.5 %collective-permute-start.5 = (bf16[48,2048]{1,0:T(8,128)(2,1)S(1)}, bf16[48,2048]{1,0:T(8,128)(2,1)S(1)}, u32[]{:S(2)}, u32[]{:S(2)}) collective-permute-start(bf16[48,2048]{1,0:T(8,128)(2,1)S(1)} %get-tuple-element.82), channel_id=1, source_target_pairs={{0,4},{4,0},{8,12},{12,8},{1,5},{5,1},{9,13},{13,9},{2,6},{6,2},{1... | collective-permute-start | bytes 589832 | tf_op jit(solution)/shard_map/ppermute | solution.py:402
  12.2 17.0 %collective-permute-start.6 = (bf16[48,2048]{1,0:T(8,128)(2,1)S(1)}, bf16[48,2048]{1,0:T(8,128)(2,1)S(1)}, u32[]{:S(2)}, u32[]{:S(2)}) collective-permute-start(bf16[48,2048]{1,0:T(8,128)(2,1)S(1)} %get-tuple-element.83), channel_id=1, source_target_pairs={{0,8},{4,12},{8,0},{12,4},{1,9},{5,13},{9,1},{13,5},{2,10},{6,14},... | collective-permute-start | bytes 589832 | tf_op jit(solution)/shard_map/ppermute | solution.py:402
  27.6 11.5 %collective-permute-start.12 = (bf16[48,2048]{1,0:T(8,128)(2,1)S(1)}, bf16[48,2048]{1,0:T(8,128)(2,1)S(1)}, u32[]{:S(2)}, u32[]{:S(2)}) collective-permute-start(bf16[48,2048]{1,0:T(8,128)(2,1)S(1)} %get-tuple-element.90.refs_9_), channel_id=1, source_target_pairs={{0,12},{4,8},{8,4},{12,0},{1,13},{5,9},{9,5},{13,1},{2,14},{6,10},... | collective-permute-start | bytes 589832 | tf_op jit(solution)/shard_map/ppermute | solution.py:402
  31.2 7.9 %collective-permute-start.10 = (bf16[48,2048]{1,0:T(8,128)(2,1)S(1)}, bf16[48,2048]{1,0:T(8,128)(2,1)S(1)}, u32[]{:S(2)}, u32[]{:S(2)}) collective-permute-start(bf16[48,2048]{1,0:T(8,128)(2,1)S(1)} %get-tuple-element.88.refs_7_), channel_id=1, source_target_pairs={{0,4},{4,0},{8,12},{12,8},{1,5},{5,1},{9,13},{13,9},{2,6},{6,2},{1... | collective-permute-start | bytes 589832 | tf_op jit(solution)/shard_map/ppermute | solution.py:402
  32.8 6.3 %collective-permute-start.11 = (bf16[48,2048]{1,0:T(8,128)(2,1)S(1)}, bf16[48,2048]{1,0:T(8,128)(2,1)S(1)}, u32[]{:S(2)}, u32[]{:S(2)}) collective-permute-start(bf16[48,2048]{1,0:T(8,128)(2,1)S(1)} %get-tuple-element.89.refs_8_), channel_id=1, source_target_pairs={{0,8},{4,12},{8,0},{12,4},{1,9},{5,13},{9,1},{13,5},{2,10},{6,14},... | collective-permute-start | bytes 589832 | tf_op jit(solution)/shard_map/ppermute | solution.py:402
  34.2 1.2 %collective-permute-start.8 = (f32[16,128]{1,0:T(8,128)S(1)}, f32[16,128]{1,0:T(8,128)S(1)}, u32[]{:S(2)}, u32[]{:S(2)}) collective-permute-start(f32[16,128]{1,0:T(8,128)S(1)} %get-tuple-element.91), channel_id=1, source_target_pairs={{0,16},{16,0},{1,17},{17,1},{2,18},{18,2},{3,19},{19,3},{4,20},{20... | collective-permute-start | bytes 24584 | tf_op jit(solution)/shard_map/ppermute | solution.py:402
  35.4 3.7 %collective-permute-start.9 = (f32[16,128]{1,0:T(8,128)S(1)}, f32[16,128]{1,0:T(8,128)S(1)}, u32[]{:S(2)}, u32[]{:S(2)}) collective-permute-start(f32[16,128]{1,0:T(8,128)S(1)} %add.17), channel_id=1, source_target_pairs={{0,1},{1,0},{2,3},{3,2},{4,5},{5,4},{6,7},{7,6},{8,9},{9,8},{10,11... | collective-permute-start | bytes 24584 | tf_op jit(solution)/shard_map/ppermute | solution.py:402
  39.1 6.1 %collective-permute-start.13 = (f32[128,128]{1,0:T(8,128)S(1)}, f32[128,128]{1,0:T(8,128)S(1)}, u32[]{:S(2)}, u32[]{:S(2)}) collective-permute-start(f32[128,128]{1,0:T(8,128)S(1)} %pad.4), channel_id=1, source_target_pairs={{0,2},{1,3},{2,0},{3,1},{4,6},{5,7},{6,4},{7,5},{8,10},{9,11},{10,... | collective-permute-start | bytes 196616 | tf_op jit(solution)/shard_map/ppermute | solution.py:402
  41.8 13.9 %collective-permute-start.17 = (bf16[48,2048]{1,0:T(8,128)(2,1)S(1)}, bf16[48,2048]{1,0:T(8,128)(2,1)S(1)}, u32[]{:S(2)}, u32[]{:S(2)}) collective-permute-start(bf16[48,2048]{1,0:T(8,128)(2,1)S(1)} %get-tuple-element.111), channel_id=1, source_target_pairs={{0,4},{4,0},{8,12},{12,8},{1,5},{5,1},{9,13},{13,9},{2,6},{6,2},{1... | collective-permute-start | bytes 589832 | tf_op jit(solution)/shard_map/ppermute | solution.py:402
  41.9 13.8 %collective-permute-start.18 = (bf16[48,2048]{1,0:T(8,128)(2,1)S(1)}, bf16[48,2048]{1,0:T(8,128)(2,1)S(1)}, u32[]{:S(2)}, u32[]{:S(2)}) collective-permute-start(bf16[48,2048]{1,0:T(8,128)(2,1)S(1)} %get-tuple-element.112), channel_id=1, source_target_pairs={{0,8},{4,12},{8,0},{12,4},{1,9},{5,13},{9,1},{13,5},{2,10},{6,14},... | collective-permute-start | bytes 589832 | tf_op jit(solution)/shard_map/ppermute | solution.py:402
  43.8 11.8 %collective-permute-start.19 = (bf16[48,2048]{1,0:T(8,128)(2,1)S(1)}, bf16[48,2048]{1,0:T(8,128)(2,1)S(1)}, u32[]{:S(2)}, u32[]{:S(2)}) collective-permute-start(bf16[48,2048]{1,0:T(8,128)(2,1)S(1)} %get-tuple-element.113), channel_id=1, source_target_pairs={{0,12},{4,8},{8,4},{12,0},{1,13},{5,9},{9,5},{13,1},{2,14},{6,10},... | collective-permute-start | bytes 589832 | tf_op jit(solution)/shard_map/ppermute | solution.py:402
  45.3 6.7 %collective-permute-start.14 = (f32[16,128]{1,0:T(8,128)S(1)}, f32[16,128]{1,0:T(8,128)S(1)}, u32[]{:S(2)}, u32[]{:S(2)}) collective-permute-start(f32[16,128]{1,0:T(8,128)S(1)} %slice_add_fusion), channel_id=1, source_target_pairs={{0,4},{4,0},{8,12},{12,8},{1,5},{5,1},{9,13},{13,9},{2,6},{6,2},{1... | collective-permute-start | bytes 24584 | tf_op jit(solution)/shard_map/ppermute | solution.py:402
  52.0 3.7 %collective-permute-start.16 = (bf16[128,512]{1,0:T(8,128)(2,1)S(1)}, bf16[128,512]{1,0:T(8,128)(2,1)S(1)}, u32[]{:S(2)}, u32[]{:S(2)}) collective-permute-start(bf16[128,512]{1,0:T(8,128)(2,1)S(1)} %get-tuple-element.109), channel_id=1, source_target_pairs={{0,16},{16,0},{1,17},{17,1},{2,18},{18,2},{3,19},{19,3},{4,20},{20... | collective-permute-start | bytes 393224 | tf_op jit(solution)/shard_map/ppermute | solution.py:402
  52.0 3.7 %collective-permute-start.15 = (f32[16,128]{1,0:T(8,128)S(1)}, f32[16,128]{1,0:T(8,128)S(1)}, u32[]{:S(2)}, u32[]{:S(2)}) collective-permute-start(f32[16,128]{1,0:T(8,128)S(1)} %add.20), channel_id=1, source_target_pairs={{0,8},{4,12},{8,0},{12,4},{1,9},{5,13},{9,1},{13,5},{2,10},{6,14},... | collective-permute-start | bytes 24584 | tf_op jit(solution)/shard_map/ppermute | solution.py:402

commit v7 on v6

--- a/solution.py
+++ b/solution.py
@@ -17,7 +17,7 @@
 COLS = 256
 LANES = 128
 GAIN_LINES = D // LANES
-WIDE_LINES = 128
+WIDE_LINES = 32
 SCALE = HEAD_SIZE ** (-0.5)
 EXP2_SCALE = SCALE * 1.4426950408889634
 F32 = jnp.float32
@@ -183,21 +183,9 @@
     return iota((slots, 1), 0) % (EXP_DEV * capacity) < capacity
 
 
-def probs_kernel(
-    count,
-    capacity,
-    pieces,
-    pos_ref,
-    slot_ref,
-    weight_ref,
-    down_hbm,
-    gate_hbm,
-    query_ref,
-    *refs,
-):
+def probs_kernel(count, pos_ref, slot_ref, weight_ref, down_hbm, gate_hbm, query_ref, *refs):
     key_refs = refs[:count]
-    grad_refs = refs[count : count + pieces]
-    d_act_ref, probs_ref, down_ref, gate_ref, place_ref, wide_ref, sems = refs[count + pieces :]
+    probs_ref, down_ref, gate_ref, place_ref, wide_ref, sems = refs[count:]
     spans = [slice(e * FFE, (e + 1) * FFE) for e in range(EXP_DEV)]
     down_copies = [
         pltpu.make_async_copy(down_hbm.at[e], down_ref.at[span, :], sems.at[e])
@@ -227,26 +215,26 @@
             peak = jnp.max(scores, axis=0, keepdims=True)
             weights = jnp.exp2((scores - peak) * EXP2_SCALE)
             probs_ref[pair] = weights * (1.0 / jnp.sum(weights, axis=0, keepdims=True))
-    grads = stacked(grad_refs)
+    for copy in down_copies + gate_copies:
+        copy.wait()
+
+
+def expert_grad_kernel(capacity, down_ref, *refs):
+    grads = stacked(refs[:-1])
     first = first_expert_rows(grads.shape[0], capacity)
-    for copy in down_copies:
-        copy.wait()
-    d_act = mm(grads, down_ref[...], NT)
-    d_act_ref[...] = jnp.where(first, d_act[:, :FFE], d_act[:, FFE:])
-    for copy in gate_copies:
-        copy.wait()
-
-
-def expert_back_kernel(capacity, pieces, start, gate_ref, d_act_ref, *refs):
+    both = mm(grads, down_ref[...], NT)
+    refs[-1][...] = jnp.where(first, both[:, :FFE], both[:, FFE:])
+
+
+def expert_back_kernel(capacity, pieces, gate_ref, d_act_ref, *refs):
     rows = stacked(refs[:pieces])
     act_ref, back_refs = refs[pieces], refs[pieces + 1 :]
-    count = rows.shape[0]
-    first = first_expert_rows(count, capacity)
+    first = first_expert_rows(rows.shape[0], capacity)
     both = mm(rows, gate_ref[...])
     pre = jnp.where(first, both[:, :FFE], both[:, FFE:])
     gate = 1.0 / (1.0 + jnp.exp(-pre))
     act = pre * gate
-    d_pre = d_act_ref[start : start + count, :] * gate * (1.0 + pre * (1.0 - gate))
+    d_pre = d_act_ref[...] * gate * (1.0 + pre * (1.0 - gate))
     act, d_pre = [
         jnp.concatenate([jnp.where(first, x, 0.0), jnp.where(first, 0.0, x)], axis=1).astype(BF16)
         for x in (act, d_pre)
@@ -256,9 +244,8 @@
         store_pieces(back_refs, cols, mm(d_pre, gate_ref[cols, :], NT).astype(BF16))
 
 
-def expert_out_kernel(pieces, acts, down_ref, gain_ref, *refs):
-    act = stacked(refs[:acts])
-    refs = refs[acts:]
+def expert_out_kernel(pieces, down_ref, gain_ref, act_ref, *refs):
+    act = act_ref[...]
     row_refs, back_refs = refs[:pieces], refs[pieces : 2 * pieces]
     terms_ref, out_refs = refs[2 * pieces], refs[2 * pieces + 1 :]
     for cols in column_blocks():
@@ -410,20 +397,28 @@
     return jnp.concatenate(moved, axis=0)
 
 
-def exchange(pieces, capacity, steps):
+def exchange(pieces, capacity):
     if lax.axis_size("exp") != len(pieces):
         return [exchange_flat(pieces[0], capacity)]
-    return [
-        pairwise(piece, "exp", s) if s in steps and s > 0 else piece for s, piece in enumerate(pieces)
-    ]
-
-
-def sum_over(value, axis, first=1, last=None):
+    return [pairwise(piece, "exp", s) if s > 0 else piece for s, piece in enumerate(pieces)]
+
+
+def doubled(value, axis, step):
+    return value + pairwise(value, axis, step)
+
+
+def sum_over(value, axis, first=1):
     step = first
-    while step < lax.axis_size(axis) and (last is None or step <= last):
-        value = value + pairwise(value, axis, step)
+    while step < lax.axis_size(axis):
+        value = doubled(value, axis, step)
         step *= 2
     return value
+
+
+def widened(act, value, axis, step):
+    rows = value.shape[0]
+    wide = jnp.pad(value, ((0, WIDE_LINES - rows), (0, 0)))
+    return act(wide, axis, step)[:rows]
 
 
 def shaped(shape, dtype):
@@ -490,10 +485,7 @@
         ],
     )
     all_keys[0], all_values[0] = own_keys, own_values
-    steps = range(piece_count)
-    groups = [[s for s in steps if s & (s - 1) == 0], [s for s in steps if s & (s - 1) != 0]]
-    groups = [group for group in groups if group]
-    arrived_grad = exchange(send_grad, capacity, steps)
+    arrived_grad = exchange(send_grad, capacity)
 
     hidden, *send_x = run(
         functools.partial(attention_kernel, ctx_count),
@@ -502,18 +494,17 @@
         placed(VMEM, [token_shape] + piece_shapes),
         attn_flops + place_flops,
     )
-    arrived_x = exchange(send_x, capacity, steps)
-
-    d_act, probs, down_near, gate_near, place, weight_wide = run(
-        functools.partial(probs_kernel, ctx_count, capacity, piece_count),
-        "act_grads_and_probs",
+    arrived_x = exchange(send_x, capacity)
+
+    probs, down_near, gate_near, place, weight_wide = run(
+        functools.partial(probs_kernel, ctx_count),
+        "probs_and_weights",
         placed(VMEM, [pos, slot, weight])
         + placed(HBM, [w_down, w_gate])
-        + placed(VMEM, [query_rows] + all_keys + arrived_grad),
+        + placed(VMEM, [query_rows] + all_keys),
         placed(
             VMEM,
             [
-                shaped((slots, FFE), F32),
                 shaped((QUERY_HEADS // 2, ctx_count * tokens, 2 * tokens), F32),
                 shaped((EXP_DEV * FFE, D), BF16),
                 shaped((D, EXP_DEV * FFE), BF16),
@@ -521,48 +512,38 @@
                 shaped((tokens, COLS), F32),
             ],
         ),
-        expert_flops + attn_flops // 2,
+        attn_flops // 2,
         scratch=[pltpu.SemaphoreType.DMA((2 * EXP_DEV,))],
     )
 
-    ordered = [s for group in groups for s in group]
-    dn = [None] * piece_count
-    send_dn = [None] * piece_count
-    acts = []
-    done = 0
-    for group in groups:
-        group_rows = sum(piece_shapes[s].shape[0] for s in group)
-        act, *parts = run(
-            functools.partial(expert_back_kernel, capacity, len(group), done),
-            "expert_backward",
-            placed(VMEM, [gate_near, d_act] + [arrived_x[s] for s in group]),
-            placed(
-                VMEM,
-                [shaped((group_rows, EXP_DEV * FFE), BF16)] + [piece_shapes[s] for s in group],
-            ),
-            2 * expert_flops * group_rows // slots,
-        )
-        acts.append(act)
-        done += group_rows
-        for s, part in zip(group, parts):
-            send_dn[s] = part
-    dn = exchange(send_dn, capacity, steps)
-    terms, *outs = run(
-        functools.partial(expert_out_kernel, piece_count, len(acts)),
+    (d_act,) = run(
+        functools.partial(expert_grad_kernel, capacity),
+        "act_grads",
+        placed(VMEM, [down_near] + arrived_grad),
+        placed(VMEM, [shaped((slots, FFE), F32)]),
+        expert_flops,
+    )
+    act, *send_dn = run(
+        functools.partial(expert_back_kernel, capacity, piece_count),
+        "expert_backward",
+        placed(VMEM, [gate_near, d_act] + arrived_x),
+        placed(VMEM, [shaped((slots, EXP_DEV * FFE), BF16)] + piece_shapes),
+        2 * expert_flops,
+    )
+    dn = exchange(send_dn, capacity)
+    terms, *send_y = run(
+        functools.partial(expert_out_kernel, piece_count),
         "expert_output",
-        placed(VMEM, [down_near, gain] + acts)
-        + placed(VMEM, [arrived_x[s] for s in ordered] + [send_dn[s] for s in ordered]),
+        placed(VMEM, [down_near, gain, act] + arrived_x + send_dn),
         placed(VMEM, [shaped((GAIN_LINES, LANES), F32)] + piece_shapes),
         expert_flops,
     )
-    terms = sum_over(sum_over(terms, "ctx"), "dp", last=1)
-    send_y = [outs[ordered.index(s)] for s in steps]
+    terms = doubled(sum_over(terms, "ctx"), "exp", 2)
     terms, send_y, dn = lax.optimization_barrier((terms, send_y, dn))
-    y = exchange(send_y, capacity, steps)
-    terms = jnp.pad(terms, ((0, WIDE_LINES - GAIN_LINES), (0, 0)))
-    terms = sum_over(terms, "dp", first=2)[:GAIN_LINES]
+    y = exchange(send_y, capacity)
+    terms = widened(doubled, terms, "dp", 2)
     terms, place_back = lax.optimization_barrier((terms, place))
-    terms = sum_over(terms, "exp", last=1)
+    terms = doubled(terms, "exp", 1)
 
     d_hidden, d_queries, kv_own, *kv_send = run(
         functools.partial(backward_kernel, ctx_count, piece_count),
@@ -584,7 +565,8 @@
         ],
     )
     terms, kv_send = lax.optimization_barrier((terms, kv_send))
-    terms = sum_over(terms, "exp", first=2)
+    terms = sum_over(sum_over(terms, "exp", first=4), "dp", first=4)
+    terms = doubled(terms, "dp", 1)
     kv_arrived = [pairwise(part, "ctx", s) for s, part in enumerate(kv_send, 1)]
 
     kv_shape = shaped((tokens, kv_width // 2), BF16)

time: 57 us -> 55.9 us (0.981)
  starting transfers between devices: 21.9 us -> 24.1 us
  waiting for transfers between devices: 17.4 us -> 15.4 us
  Pallas kernels: 16.7 us -> 15.5 us
    ppermute x20, starting transfers between devices: 21.9 us -> 24.1 us  [pairwise(): return lax.ppermute(value, axis, [(i, i ^ step) for i in range(count)])]
    ppermute x20, waiting for transfers between devices: 17.4 us -> 15.4 us  [pairwise(): return lax.ppermute(value, axis, [(i, i ^ step) for i in range(count)])]
    pallas_call x8, Pallas kernels: 16.7 us -> 15.5 us  [run(): pl.pallas_call(kernel, out_shape=[x for _, x in outputs], in_specs=[spec[...]
  transfers between devices with their start and end apart: 20 -> 20, of which waited for: 5 -> 8; matrix products, arithmetic and copies ran while one was open for 0% -> 0% of each run, Pallas kernels for 25% -> 19%
where the time goes in v7:
time: 55.9 us; the launch traced here: 55.7 us
  starting transfers between devices  24.1 us (43%)
  Pallas kernels  15.5 us (28%)
  waiting for transfers between devices  15.4 us (28%)
  between operations  0.74 us (1%)
    ppermute x20, starting transfers between devices, pairwise(): return lax.ppermute(value, axis, [(i, i ^ step) for i in range(count)])  24.1 us
    pallas_call x8, Pallas kernels, run(): pl.pallas_call(kernel, out_shape=[x for _, x in outputs], in_specs=[spec[...  15.5 us
    ppermute x20, waiting for transfers between devices, pairwise(): return lax.ppermute(value, axis, [(i, i ^ step) for i in range(count)])  15.4 us
  transfers between devices with their start and end apart: 20, of which 8 were waited for; matrix products, arithmetic and copies ran while one was open for 0% of the time, Pallas kernels for 19%

profile of v7, /device:TPU:0, one launch (start us, length us, event | category | flops | bytes accessed | tf_op | source)
XLA Modules:
  0.0 55.7 jit_solution(5197730939245458131)
XLA Ops:
  0.6 1.5 %dispatch_grads.1 = (bf16[128,2048]{1,0:T(8,128)(2,1)S(1)}, bf16[128,256]{1,0:T(8,128)(2,1)S(1)}, bf16[128,256]{1,0:T(8,128)(2,1)S(1)}, f32[1,2048]{1,0:T(1,128)...) custom-call(bf16[128,2048]{1,0:T(8,128)(2,1)} %bitcast.13, ...), custom_call_target="tpu_custom_call" | custom-call | flops 100663296 | bytes 4213824 | tf_op jit(solution)/shard_map/dispatch_grads/pallas_call | solution.py:370
  2.2 3.0 %collective-permute-start.1 = (bf16[48,2048]{1,0:T(8,128)(2,1)S(1)}, bf16[48,2048]{1,0:T(8,128)(2,1)S(1)}, u32[]{:S(2)}, u32[]{:S(2)}) collective-permute-start(bf16[48,2048]{1,0:T(8,128)(2,1)S(1)} %get-tuple-element.73), channel_id=1, source_target_pairs={{0,4},{4,0},{8,12},{12,8},{1,5},{5,1},{9,13},{13,9},{2,6},{6,2},{1... | collective-permute-start | bytes 589832 | tf_op jit(solution)/shard_map/ppermute | solution.py:389
  5.2 0.5 collective-permute-start.4
  5.7 1.5 %collective-permute-start.2 = (bf16[48,2048]{1,0:T(8,128)(2,1)S(1)}, bf16[48,2048]{1,0:T(8,128)(2,1)S(1)}, u32[]{:S(2)}, u32[]{:S(2)}) collective-permute-start(bf16[48,2048]{1,0:T(8,128)(2,1)S(1)} %get-tuple-element.74), channel_id=1, source_target_pairs={{0,8},{4,12},{8,0},{12,4},{1,9},{5,13},{9,1},{13,5},{2,10},{6,14},... | collective-permute-start | bytes 589832 | tf_op jit(solution)/shard_map/ppermute | solution.py:389
  7.2 1.4 %attention_forward.1 = (bf16[128,2048]{1,0:T(8,128)(2,1)S(1)}, bf16[48,2048]{1,0:T(8,128)(2,1)S(1)}, bf16[48,2048]{1,0:T(8,128)(2,1)S(1)}, bf16[48,2048]{1,0:T(8,128)(2,1)S(1)}, bf16[48,2048]{1,0:T(8,128)(2,1)S(1)}) custom-call(s32[2,128]{1,0:T(2,128)S(1)} %get-tuple-element.62.pos_ref, s32[1,128]{1,0:T(1,128)S(1)} %get-tuple-element.63.slot_ref, ...), custom_call_target="tpu_custom_call" | custom-call | flops 369098752 | bytes 2631168 | tf_op jit(solution)/shard_map/attention_forward/pallas_call | solution.py:370
  8.7 2.0 %collective-permute-start.5 = (bf16[48,2048]{1,0:T(8,128)(2,1)S(1)}, bf16[48,2048]{1,0:T(8,128)(2,1)S(1)}, u32[]{:S(2)}, u32[]{:S(2)}) collective-permute-start(bf16[48,2048]{1,0:T(8,128)(2,1)S(1)} %get-tuple-element.79), channel_id=1, source_target_pairs={{0,4},{4,0},{8,12},{12,8},{1,5},{5,1},{9,13},{13,9},{2,6},{6,2},{1... | collective-permute-start | bytes 589832 | tf_op jit(solution)/shard_map/ppermute | solution.py:389
  10.7 1.5 %collective-permute-start.6 = (bf16[48,2048]{1,0:T(8,128)(2,1)S(1)}, bf16[48,2048]{1,0:T(8,128)(2,1)S(1)}, u32[]{:S(2)}, u32[]{:S(2)}) collective-permute-start(bf16[48,2048]{1,0:T(8,128)(2,1)S(1)} %get-tuple-element.80), channel_id=1, source_target_pairs={{0,8},{4,12},{8,0},{12,4},{1,9},{5,13},{9,1},{13,5},{2,10},{6,14},... | collective-permute-start | bytes 589832 | tf_op jit(solution)/shard_map/ppermute | solution.py:389
  12.2 1.7 %collective-permute-start.7 = (bf16[48,2048]{1,0:T(8,128)(2,1)S(1)}, bf16[48,2048]{1,0:T(8,128)(2,1)S(1)}, u32[]{:S(2)}, u32[]{:S(2)}) collective-permute-start(bf16[48,2048]{1,0:T(8,128)(2,1)S(1)} %get-tuple-element.81), channel_id=1, source_target_pairs={{0,12},{4,8},{8,4},{12,0},{1,13},{5,9},{9,5},{13,1},{2,14},{6,10},... | collective-permute-start | bytes 589832 | tf_op jit(solution)/shard_map/ppermute | solution.py:389
  13.9 2.9 %probs_and_weights.1 = (f32[8,256,256]{2,1,0:T(8,128)S(1)}, bf16[768,2048]{1,0:T(8,128)(2,1)S(1)}, bf16[2048,768]{1,0:T(8,128)(2,1)S(1)}, bf16[128,192]{1,0:T(8,128)(2,1)S(1)}, f32[128,256]{1,0:T(8,128)S(1)}) custom-call(s32[2,128]{1,0:T(2,128)S(1)} %get-tuple-element.62.pos_ref, s32[1,128]{1,0:T(1,128)S(1)} %get-tuple-element.63.slot_ref, ...), custom_call_target="tpu_custom_call" | custom-call | flops 134217728 | bytes 15517696 | tf_op jit(solution)/shard_map/probs_and_weights/pallas_call | solution.py:370
  16.8 0.9 %collective-permute-done.2.refs_2_ = bf16[48,2048]{1,0:T(8,128)(2,1)S(1)} collective-permute-done((bf16[48,2048]{1,0:T(8,128)(2,1)S(1)}, bf16[48,2048]{1,0:T(8,128)(2,1)S(1)}, u32[]{:S(2)}, u32[]{:S(2)}) %collective-permute-start.2) | collective-permute-done | bytes 196640 | tf_op jit(solution)/shard_map/ppermute | solution.py:389
  17.7 1.2 %act_grads.1.d_act_ref = f32[192,384]{1,0:T(8,128)S(1)} custom-call(bf16[768,2048]{1,0:T(8,128)(2,1)S(1)} %get-tuple-element.69.down_ref, bf16[48,2048]{1,0:T(8,128)(2,1)S(1)} %get-tuple-element.72.refs_0_, bf16[48,2048]{1,0:T(8,128)(2,1)S(1)} %collective-permute-done.1.refs_1_, bf16[48,2048]{1,0:T(8,128)(2,1)S(1)} %collective-permute-done.2.refs_2_, ...), custom_call_target="tpu_custom_call" | custom-call | flops 603979776 | bytes 4227072 | tf_op jit(solution)/shard_map/act_grads/pallas_call | solution.py:370
  18.9 0.3 collective-permute-done.5.refs_1_
  19.2 5.9 %collective-permute-done.6.refs_2_ = bf16[48,2048]{1,0:T(8,128)(2,1)S(1)} collective-permute-done((bf16[48,2048]{1,0:T(8,128)(2,1)S(1)}, bf16[48,2048]{1,0:T(8,128)(2,1)S(1)}, u32[]{:S(2)}, u32[]{:S(2)}) %collective-permute-start.6) | collective-permute-done | bytes 196640 | tf_op jit(solution)/shard_map/ppermute | solution.py:389
  25.1 2.3 %expert_backward.1 = (bf16[192,768]{1,0:T(8,128)(2,1)S(1)}, bf16[48,2048]{1,0:T(8,128)(2,1)S(1)}, bf16[48,2048]{1,0:T(8,128)(2,1)S(1)}, bf16[48,2048]{1,0:T(8,128)(2,1)S(1)}, bf16[48,2048]{1,0:T(8,128)(2,1)S(1)}) custom-call(bf16[2048,768]{1,0:T(8,128)(2,1)S(1)} %get-tuple-element.71.gate_ref, f32[192,384]{1,0:T(8,128)S(1)} %act_grads.1.d_act_ref, ...), custom_call_target="tpu_custom_call" | custom-call | flops 1207959552 | bytes 5308416 | tf_op jit(solution)/shard_map/expert_backward/pallas_call | solution.py:370
  27.4 0.4 collective-permute-start.10
  27.8 1.7 %collective-permute-start.11 = (bf16[48,2048]{1,0:T(8,128)(2,1)S(1)}, bf16[48,2048]{1,0:T(8,128)(2,1)S(1)}, u32[]{:S(2)}, u32[]{:S(2)}) collective-permute-start(bf16[48,2048]{1,0:T(8,128)(2,1)S(1)} %get-tuple-element.85.refs_6_), channel_id=1, source_target_pairs={{0,8},{4,12},{8,0},{12,4},{1,9},{5,13},{9,1},{13,5},{2,10},{6,14},... | collective-permute-start | bytes 589832 | tf_op jit(solution)/shard_map/ppermute | solution.py:389
  29.6 1.4 %collective-permute-start.12 = (bf16[48,2048]{1,0:T(8,128)(2,1)S(1)}, bf16[48,2048]{1,0:T(8,128)(2,1)S(1)}, u32[]{:S(2)}, u32[]{:S(2)}) collective-permute-start(bf16[48,2048]{1,0:T(8,128)(2,1)S(1)} %get-tuple-element.86.refs_7_), channel_id=1, source_target_pairs={{0,12},{4,8},{8,4},{12,0},{1,13},{5,9},{9,5},{13,1},{2,14},{6,10},... | collective-permute-start | bytes 589832 | tf_op jit(solution)/shard_map/ppermute | solution.py:389
  31.0 0.9 %expert_output.1 = (f32[16,128]{1,0:T(8,128)S(1)}, bf16[48,2048]{1,0:T(8,128)(2,1)S(1)}, bf16[48,2048]{1,0:T(8,128)(2,1)S(1)}, bf16[48,2048]{1,0:T(8,128)(2,1)S(1)}, bf16[48,2048]{1,0:T(8,128)(2,1)S(1)}) custom-call(bf16[768,2048]{1,0:T(8,128)(2,1)S(1)} %get-tuple-element.69.down_ref, f32[1,2048]{1,0:T(1,128)S(1)} %get-tuple-element.70.gain_ref, ...), custom_call_target="tpu_custom_call" | custom-call | flops 603979776 | bytes 5816320 | tf_op jit(solution)/shard_map/expert_output/pallas_call | solution.py:370
  32.0 1.2 %collective-permute-done.8 = f32[16,128]{1,0:T(8,128)S(1)} collective-permute-done((f32[16,128]{1,0:T(8,128)S(1)}, f32[16,128]{1,0:T(8,128)S(1)}, u32[]{:S(2)}, u32[]{:S(2)}) %collective-permute-start.8) | collective-permute-done | bytes 8224 | tf_op jit(solution)/shard_map/ppermute | solution.py:389
  33.1 1.5 %collective-permute-start.9 = (f32[16,128]{1,0:T(8,128)S(1)}, f32[16,128]{1,0:T(8,128)S(1)}, u32[]{:S(2)}, u32[]{:S(2)}) collective-permute-start(f32[16,128]{1,0:T(8,128)S(1)} %add.17), channel_id=1, source_target_pairs={{0,8},{4,12},{8,0},{12,4},{1,9},{5,13},{9,1},{13,5},{2,10},{6,14},... | collective-permute-start | bytes 24584 | tf_op jit(solution)/shard_map/ppermute | solution.py:389
  34.7 2.9 %collective-permute-done.9 = f32[16,128]{1,0:T(8,128)S(1)} collective-permute-done((f32[16,128]{1,0:T(8,128)S(1)}, f32[16,128]{1,0:T(8,128)S(1)}, u32[]{:S(2)}, u32[]{:S(2)}) %collective-permute-start.9) | collective-permute-done | bytes 8224 | tf_op jit(solution)/shard_map/ppermute | solution.py:389
  37.6 1.1 %collective-permute-done.12.refs_3_ = bf16[48,2048]{1,0:T(8,128)(2,1)S(1)} collective-permute-done((bf16[48,2048]{1,0:T(8,128)(2,1)S(1)}, bf16[48,2048]{1,0:T(8,128)(2,1)S(1)}, u32[]{:S(2)}, u32[]{:S(2)}) %collective-permute-start.12) | collective-permute-done | bytes 196640 | tf_op jit(solution)/shard_map/ppermute | solution.py:389
  38.7 2.6 %collective-permute-start.13 = (f32[32,128]{1,0:T(8,128)S(1)}, f32[32,128]{1,0:T(8,128)S(1)}, u32[]{:S(2)}, u32[]{:S(2)}) collective-permute-start(f32[32,128]{1,0:T(8,128)S(1)} %pad.4), channel_id=1, source_target_pairs={{0,2},{1,3},{2,0},{3,1},{4,6},{5,7},{6,4},{7,5},{8,10},{9,11},{10,... | collective-permute-start | bytes 49160 | tf_op jit(solution)/shard_map/ppermute | solution.py:389
  41.3 1.0 %collective-permute-start.17 = (bf16[48,2048]{1,0:T(8,128)(2,1)S(1)}, bf16[48,2048]{1,0:T(8,128)(2,1)S(1)}, u32[]{:S(2)}, u32[]{:S(2)}) collective-permute-start(bf16[48,2048]{1,0:T(8,128)(2,1)S(1)} %get-tuple-element.107), channel_id=1, source_target_pairs={{0,4},{4,0},{8,12},{12,8},{1,5},{5,1},{9,13},{13,9},{2,6},{6,2},{1... | collective-permute-start | bytes 589832 | tf_op jit(solution)/shard_map/ppermute | solution.py:389
  42.3 1.5 %collective-permute-start.18 = (bf16[48,2048]{1,0:T(8,128)(2,1)S(1)}, bf16[48,2048]{1,0:T(8,128)(2,1)S(1)}, u32[]{:S(2)}, u32[]{:S(2)}) collective-permute-start(bf16[48,2048]{1,0:T(8,128)(2,1)S(1)} %get-tuple-element.108), channel_id=1, source_target_pairs={{0,8},{4,12},{8,0},{12,4},{1,9},{5,13},{9,1},{13,5},{2,10},{6,14},... | collective-permute-start | bytes 589832 | tf_op jit(solution)/shard_map/ppermute | solution.py:389
  43.8 1.0 %collective-permute-start.19 = (bf16[48,2048]{1,0:T(8,128)(2,1)S(1)}, bf16[48,2048]{1,0:T(8,128)(2,1)S(1)}, u32[]{:S(2)}, u32[]{:S(2)}) collective-permute-start(bf16[48,2048]{1,0:T(8,128)(2,1)S(1)} %get-tuple-element.109), channel_id=1, source_target_pairs={{0,12},{4,8},{8,4},{12,0},{1,13},{5,9},{9,5},{13,1},{2,14},{6,10},... | collective-permute-start | bytes 589832 | tf_op jit(solution)/shard_map/ppermute | solution.py:389
  44.8 1.0 %collective-permute-start.14 = (f32[16,128]{1,0:T(8,128)S(1)}, f32[16,128]{1,0:T(8,128)S(1)}, u32[]{:S(2)}, u32[]{:S(2)}) collective-permute-start(f32[16,128]{1,0:T(8,128)S(1)} %slice_add_fusion), channel_id=1, source_target_pairs={{0,4},{4,0},{8,12},{12,8},{1,5},{5,1},{9,13},{13,9},{2,6},{6,2},{1... | collective-permute-start | bytes 24584 | tf_op jit(solution)/shard_map/ppermute | solution.py:389
  45.8 4.0 %residual_attention_backward.1 = (bf16[128,2048]{1,0:T(8,128)(2,1)}, bf16[128,2048]{1,0:T(8,128)(2,1)}, f32[128,512]{1,0:T(8,128)S(1)}, bf16[128,512]{1,0:T(8,128)(2,1)S(1)}) custom-call(bf16[128,192]{1,0:T(8,128)(2,1)S(1)} %get-tuple-element.94.place_ref, f32[1,2048]{1,0:T(1,128)S(1)} %get-tuple-element.70.gain_ref, ...), custom_call_target="tpu_custom_call" | custom-call | flops 369098752 | bytes 6217728 | tf_op jit(solution)/shard_map/residual_attention_backward/pallas_call | solution.py:370
  49.8 1.0 %collective-permute-done.14 = f32[16,128]{1,0:T(8,128)S(1)} collective-permute-done((f32[16,128]{1,0:T(8,128)S(1)}, f32[16,128]{1,0:T(8,128)S(1)}, u32[]{:S(2)}, u32[]{:S(2)}) %collective-permute-start.14) | collective-permute-done | bytes 8224 | tf_op jit(solution)/shard_map/ppermute | solution.py:389
  50.9 1.6 %collective-permute-start.15 = (f32[16,128]{1,0:T(8,128)S(1)}, f32[16,128]{1,0:T(8,128)S(1)}, u32[]{:S(2)}, u32[]{:S(2)}) collective-permute-start(f32[16,128]{1,0:T(8,128)S(1)} %add.20), channel_id=1, source_target_pairs={{0,1},{1,0},{2,3},{3,2},{4,5},{5,4},{6,7},{7,6},{8,9},{9,8},{10,11... | collective-permute-start | bytes 24584 | tf_op jit(solution)/shard_map/ppermute | solution.py:389
  52.4 2.1 %collective-permute-done.15 = f32[16,128]{1,0:T(8,128)S(1)} collective-permute-done((f32[16,128]{1,0:T(8,128)S(1)}, f32[16,128]{1,0:T(8,128)S(1)}, u32[]{:S(2)}, u32[]{:S(2)}) %collective-permute-start.15) | collective-permute-done | bytes 8224 | tf_op jit(solution)/shard_map/ppermute | solution.py:389
  54.5 1.2 %layer_output.1 = (bf16[128,2048]{1,0:T(8,128)(2,1)}, bf16[128,256]{1,0:T(8,128)(2,1)}, bf16[128,256]{1,0:T(8,128)(2,1)}, f32[1,128]{1,0:T(1,128)}, f32[16,128]{1,0:T(8,128)}) custom-call(bf16[128,192]{1,0:T(8,128)(2,1)S(1)} %get-tuple-element.94.place_ref, f32[128,256]{1,0:T(8,128)S(1)} %get-tuple-element.68.weight_ref, f32[16,128]{1,0:T(8,128)S(1)} %add.21.gain_ref, ...), custom_call_target="tpu_custom_call" | custom-call | flops 100663296 | bytes 3080704 | tf_op jit(solution)/shard_map/layer_output/pallas_call | solution.py:370
  (22 shorter events, 0.1 us)
Async XLA Ops:
  2.2 10.0 %collective-permute-start.1 = (bf16[48,2048]{1,0:T(8,128)(2,1)S(1)}, bf16[48,2048]{1,0:T(8,128)(2,1)S(1)}, u32[]{:S(2)}, u32[]{:S(2)}) collective-permute-start(bf16[48,2048]{1,0:T(8,128)(2,1)S(1)} %get-tuple-element.73), channel_id=1, source_target_pairs={{0,4},{4,0},{8,12},{12,8},{1,5},{5,1},{9,13},{13,9},{2,6},{6,2},{1... | collective-permute-start | bytes 589832 | tf_op jit(solution)/shard_map/ppermute | solution.py:389
  5.2 2.1 %collective-permute-start = (bf16[128,256]{1,0:T(8,128)(2,1)}, bf16[128,256]{1,0:T(8,128)(2,1)S(1)}, u32[]{:S(2)}, u32[]{:S(2)}) collective-permute-start(bf16[128,256]{1,0:T(8,128)(2,1)} %bitcast.17), channel_id=1, source_target_pairs={{0,16},{16,0},{1,17},{17,1},{2,18},{18,2},{3,19},{19,3},{4,20},{20... | collective-permute-start | bytes 196616 | tf_op jit(solution)/shard_map/ppermute | solution.py:389
  5.2 2.1 %collective-permute-start.4 = (bf16[128,256]{1,0:T(8,128)(2,1)}, bf16[128,256]{1,0:T(8,128)(2,1)S(1)}, u32[]{:S(2)}, u32[]{:S(2)}) collective-permute-start(bf16[128,256]{1,0:T(8,128)(2,1)} %bitcast.19), channel_id=1, source_target_pairs={{0,16},{16,0},{1,17},{17,1},{2,18},{18,2},{3,19},{19,3},{4,20},{20... | collective-permute-start | bytes 196616 | tf_op jit(solution)/shard_map/ppermute | solution.py:389
  5.7 12.0 %collective-permute-start.2 = (bf16[48,2048]{1,0:T(8,128)(2,1)S(1)}, bf16[48,2048]{1,0:T(8,128)(2,1)S(1)}, u32[]{:S(2)}, u32[]{:S(2)}) collective-permute-start(bf16[48,2048]{1,0:T(8,128)(2,1)S(1)} %get-tuple-element.74), channel_id=1, source_target_pairs={{0,8},{4,12},{8,0},{12,4},{1,9},{5,13},{9,1},{13,5},{2,10},{6,14},... | collective-permute-start | bytes 589832 | tf_op jit(solution)/shard_map/ppermute | solution.py:389
  7.2 10.5 %collective-permute-start.3 = (bf16[48,2048]{1,0:T(8,128)(2,1)S(1)}, bf16[48,2048]{1,0:T(8,128)(2,1)S(1)}, u32[]{:S(2)}, u32[]{:S(2)}) collective-permute-start(bf16[48,2048]{1,0:T(8,128)(2,1)S(1)} %get-tuple-element.75), channel_id=1, source_target_pairs={{0,12},{4,8},{8,4},{12,0},{1,13},{5,9},{9,5},{13,1},{2,14},{6,10},... | collective-permute-start | bytes 589832 | tf_op jit(solution)/shard_map/ppermute | solution.py:389
  8.7 10.5 %collective-permute-start.5 = (bf16[48,2048]{1,0:T(8,128)(2,1)S(1)}, bf16[48,2048]{1,0:T(8,128)(2,1)S(1)}, u32[]{:S(2)}, u32[]{:S(2)}) collective-permute-start(bf16[48,2048]{1,0:T(8,128)(2,1)S(1)} %get-tuple-element.79), channel_id=1, source_target_pairs={{0,4},{4,0},{8,12},{12,8},{1,5},{5,1},{9,13},{13,9},{2,6},{6,2},{1... | collective-permute-start | bytes 589832 | tf_op jit(solution)/shard_map/ppermute | solution.py:389
  10.7 14.5 %collective-permute-start.6 = (bf16[48,2048]{1,0:T(8,128)(2,1)S(1)}, bf16[48,2048]{1,0:T(8,128)(2,1)S(1)}, u32[]{:S(2)}, u32[]{:S(2)}) collective-permute-start(bf16[48,2048]{1,0:T(8,128)(2,1)S(1)} %get-tuple-element.80), channel_id=1, source_target_pairs={{0,8},{4,12},{8,0},{12,4},{1,9},{5,13},{9,1},{13,5},{2,10},{6,14},... | collective-permute-start | bytes 589832 | tf_op jit(solution)/shard_map/ppermute | solution.py:389
  12.2 12.9 %collective-permute-start.7 = (bf16[48,2048]{1,0:T(8,128)(2,1)S(1)}, bf16[48,2048]{1,0:T(8,128)(2,1)S(1)}, u32[]{:S(2)}, u32[]{:S(2)}) collective-permute-start(bf16[48,2048]{1,0:T(8,128)(2,1)S(1)} %get-tuple-element.81), channel_id=1, source_target_pairs={{0,12},{4,8},{8,4},{12,0},{1,13},{5,9},{9,5},{13,1},{2,14},{6,10},... | collective-permute-start | bytes 589832 | tf_op jit(solution)/shard_map/ppermute | solution.py:389
  27.4 10.2 %collective-permute-start.10 = (bf16[48,2048]{1,0:T(8,128)(2,1)S(1)}, bf16[48,2048]{1,0:T(8,128)(2,1)S(1)}, u32[]{:S(2)}, u32[]{:S(2)}) collective-permute-start(bf16[48,2048]{1,0:T(8,128)(2,1)S(1)} %get-tuple-element.84.refs_5_), channel_id=1, source_target_pairs={{0,4},{4,0},{8,12},{12,8},{1,5},{5,1},{9,13},{13,9},{2,6},{6,2},{1... | collective-permute-start | bytes 589832 | tf_op jit(solution)/shard_map/ppermute | solution.py:389
  27.8 9.8 %collective-permute-start.11 = (bf16[48,2048]{1,0:T(8,128)(2,1)S(1)}, bf16[48,2048]{1,0:T(8,128)(2,1)S(1)}, u32[]{:S(2)}, u32[]{:S(2)}) collective-permute-start(bf16[48,2048]{1,0:T(8,128)(2,1)S(1)} %get-tuple-element.85.refs_6_), channel_id=1, source_target_pairs={{0,8},{4,12},{8,0},{12,4},{1,9},{5,13},{9,1},{13,5},{2,10},{6,14},... | collective-permute-start | bytes 589832 | tf_op jit(solution)/shard_map/ppermute | solution.py:389
  29.6 9.2 %collective-permute-start.12 = (bf16[48,2048]{1,0:T(8,128)(2,1)S(1)}, bf16[48,2048]{1,0:T(8,128)(2,1)S(1)}, u32[]{:S(2)}, u32[]{:S(2)}) collective-permute-start(bf16[48,2048]{1,0:T(8,128)(2,1)S(1)} %get-tuple-element.86.refs_7_), channel_id=1, source_target_pairs={{0,12},{4,8},{8,4},{12,0},{1,13},{5,9},{9,5},{13,1},{2,14},{6,10},... | collective-permute-start | bytes 589832 | tf_op jit(solution)/shard_map/ppermute | solution.py:389
  31.9 1.2 %collective-permute-start.8 = (f32[16,128]{1,0:T(8,128)S(1)}, f32[16,128]{1,0:T(8,128)S(1)}, u32[]{:S(2)}, u32[]{:S(2)}) collective-permute-start(f32[16,128]{1,0:T(8,128)S(1)} %get-tuple-element.87), channel_id=1, source_target_pairs={{0,16},{16,0},{1,17},{17,1},{2,18},{18,2},{3,19},{19,3},{4,20},{20... | collective-permute-start | bytes 24584 | tf_op jit(solution)/shard_map/ppermute | solution.py:389
  33.1 4.4 %collective-permute-start.9 = (f32[16,128]{1,0:T(8,128)S(1)}, f32[16,128]{1,0:T(8,128)S(1)}, u32[]{:S(2)}, u32[]{:S(2)}) collective-permute-start(f32[16,128]{1,0:T(8,128)S(1)} %add.17), channel_id=1, source_target_pairs={{0,8},{4,12},{8,0},{12,4},{1,9},{5,13},{9,1},{13,5},{2,10},{6,14},... | collective-permute-start | bytes 24584 | tf_op jit(solution)/shard_map/ppermute | solution.py:389
  38.7 6.1 %collective-permute-start.13 = (f32[32,128]{1,0:T(8,128)S(1)}, f32[32,128]{1,0:T(8,128)S(1)}, u32[]{:S(2)}, u32[]{:S(2)}) collective-permute-start(f32[32,128]{1,0:T(8,128)S(1)} %pad.4), channel_id=1, source_target_pairs={{0,2},{1,3},{2,0},{3,1},{4,6},{5,7},{6,4},{7,5},{8,10},{9,11},{10,... | collective-permute-start | bytes 49160 | tf_op jit(solution)/shard_map/ppermute | solution.py:389
  41.3 13.2 %collective-permute-start.17 = (bf16[48,2048]{1,0:T(8,128)(2,1)S(1)}, bf16[48,2048]{1,0:T(8,128)(2,1)S(1)}, u32[]{:S(2)}, u32[]{:S(2)}) collective-permute-start(bf16[48,2048]{1,0:T(8,128)(2,1)S(1)} %get-tuple-element.107), channel_id=1, source_target_pairs={{0,4},{4,0},{8,12},{12,8},{1,5},{5,1},{9,13},{13,9},{2,6},{6,2},{1... | collective-permute-start | bytes 589832 | tf_op jit(solution)/shard_map/ppermute | solution.py:389
  42.3 12.2 %collective-permute-start.18 = (bf16[48,2048]{1,0:T(8,128)(2,1)S(1)}, bf16[48,2048]{1,0:T(8,128)(2,1)S(1)}, u32[]{:S(2)}, u32[]{:S(2)}) collective-permute-start(bf16[48,2048]{1,0:T(8,128)(2,1)S(1)} %get-tuple-element.108), channel_id=1, source_target_pairs={{0,8},{4,12},{8,0},{12,4},{1,9},{5,13},{9,1},{13,5},{2,10},{6,14},... | collective-permute-start | bytes 589832 | tf_op jit(solution)/shard_map/ppermute | solution.py:389
  43.8 10.7 %collective-permute-start.19 = (bf16[48,2048]{1,0:T(8,128)(2,1)S(1)}, bf16[48,2048]{1,0:T(8,128)(2,1)S(1)}, u32[]{:S(2)}, u32[]{:S(2)}) collective-permute-start(bf16[48,2048]{1,0:T(8,128)(2,1)S(1)} %get-tuple-element.109), channel_id=1, source_target_pairs={{0,12},{4,8},{8,4},{12,0},{1,13},{5,9},{9,5},{13,1},{2,14},{6,10},... | collective-permute-start | bytes 589832 | tf_op jit(solution)/shard_map/ppermute | solution.py:389
  44.8 6.1 %collective-permute-start.14 = (f32[16,128]{1,0:T(8,128)S(1)}, f32[16,128]{1,0:T(8,128)S(1)}, u32[]{:S(2)}, u32[]{:S(2)}) collective-permute-start(f32[16,128]{1,0:T(8,128)S(1)} %slice_add_fusion), channel_id=1, source_target_pairs={{0,4},{4,0},{8,12},{12,8},{1,5},{5,1},{9,13},{13,9},{2,6},{6,2},{1... | collective-permute-start | bytes 24584 | tf_op jit(solution)/shard_map/ppermute | solution.py:389
  50.9 3.7 %collective-permute-start.16 = (bf16[128,512]{1,0:T(8,128)(2,1)S(1)}, bf16[128,512]{1,0:T(8,128)(2,1)S(1)}, u32[]{:S(2)}, u32[]{:S(2)}) collective-permute-start(bf16[128,512]{1,0:T(8,128)(2,1)S(1)} %get-tuple-element.105), channel_id=1, source_target_pairs={{0,16},{16,0},{1,17},{17,1},{2,18},{18,2},{3,19},{19,3},{4,20},{20... | collective-permute-start | bytes 393224 | tf_op jit(solution)/shard_map/ppermute | solution.py:389
  50.9 3.7 %collective-permute-start.15 = (f32[16,128]{1,0:T(8,128)S(1)}, f32[16,128]{1,0:T(8,128)S(1)}, u32[]{:S(2)}, u32[]{:S(2)}) collective-permute-start(f32[16,128]{1,0:T(8,128)S(1)} %add.20), channel_id=1, source_target_pairs={{0,1},{1,0},{2,3},{3,2},{4,5},{5,4},{6,7},{7,6},{8,9},{9,8},{10,11... | collective-permute-start | bytes 24584 | tf_op jit(solution)/shard_map/ppermute | solution.py:389

commit v8 on v7

--- a/solution.py
+++ b/solution.py
@@ -226,15 +226,16 @@
     refs[-1][...] = jnp.where(first, both[:, :FFE], both[:, FFE:])
 
 
-def expert_back_kernel(capacity, pieces, gate_ref, d_act_ref, *refs):
+def expert_back_kernel(capacity, pieces, start, gate_ref, d_act_ref, *refs):
     rows = stacked(refs[:pieces])
     act_ref, back_refs = refs[pieces], refs[pieces + 1 :]
-    first = first_expert_rows(rows.shape[0], capacity)
+    count = rows.shape[0]
+    first = first_expert_rows(count, capacity)
     both = mm(rows, gate_ref[...])
     pre = jnp.where(first, both[:, :FFE], both[:, FFE:])
     gate = 1.0 / (1.0 + jnp.exp(-pre))
     act = pre * gate
-    d_pre = d_act_ref[...] * gate * (1.0 + pre * (1.0 - gate))
+    d_pre = d_act_ref[start : start + count, :] * gate * (1.0 + pre * (1.0 - gate))
     act, d_pre = [
         jnp.concatenate([jnp.where(first, x, 0.0), jnp.where(first, 0.0, x)], axis=1).astype(BF16)
         for x in (act, d_pre)
@@ -244,8 +245,9 @@
         store_pieces(back_refs, cols, mm(d_pre, gate_ref[cols, :], NT).astype(BF16))
 
 
-def expert_out_kernel(pieces, down_ref, gain_ref, act_ref, *refs):
-    act = act_ref[...]
+def expert_out_kernel(pieces, acts, down_ref, gain_ref, *refs):
+    act = stacked(refs[:acts])
+    refs = refs[acts:]
     row_refs, back_refs = refs[:pieces], refs[pieces : 2 * pieces]
     terms_ref, out_refs = refs[2 * pieces], refs[2 * pieces + 1 :]
     for cols in column_blocks():
@@ -397,10 +399,13 @@
     return jnp.concatenate(moved, axis=0)
 
 
-def exchange(pieces, capacity):
+def exchange(pieces, capacity, steps):
     if lax.axis_size("exp") != len(pieces):
         return [exchange_flat(pieces[0], capacity)]
-    return [pairwise(piece, "exp", s) if s > 0 else piece for s, piece in enumerate(pieces)]
+    return [
+        pairwise(piece, "exp", s) if s > 0 and s in steps else piece
+        for s, piece in enumerate(pieces)
+    ]
 
 
 def doubled(value, axis, step):
@@ -459,9 +464,6 @@
     expert_flops = 2 * slots * D * FFE * EXP_DEV
 
     own_keys, own_values = keys[0], values[0]
-    all_keys = [own_keys] + [pairwise(own_keys, "ctx", s) for s in range(1, ctx_count)]
-    all_values = [own_values] + [pairwise(own_values, "ctx", s) for s in range(1, ctx_count)]
-
     near = [grad_rows, own_keys, own_values, gain, query_rows, resid_rows]
     grad_rows, own_keys, own_values, gain, query_rows, resid_rows, slot, pos, weight, *send_grad = run(
         functools.partial(dispatch_kernel, ctx_count, experts, capacity),
@@ -484,8 +486,14 @@
             pltpu.SemaphoreType.DMA((9,)),
         ],
     )
-    all_keys[0], all_values[0] = own_keys, own_values
-    arrived_grad = exchange(send_grad, capacity)
+    all_keys = [own_keys] + [pairwise(own_keys, "ctx", s) for s in range(1, ctx_count)]
+    all_values = [own_values] + [pairwise(own_values, "ctx", s) for s in range(1, ctx_count)]
+    steps = range(piece_count)
+    near = [s for s in steps if s & (s - 1) == 0]
+    far = [s for s in steps if s & (s - 1) != 0]
+    groups = [group for group in (far, near) if group]
+    ordered = [s for group in groups for s in group]
+    arrived_grad = exchange(send_grad, capacity, steps)
 
     hidden, *send_x = run(
         functools.partial(attention_kernel, ctx_count),
@@ -494,8 +502,6 @@
         placed(VMEM, [token_shape] + piece_shapes),
         attn_flops + place_flops,
     )
-    arrived_x = exchange(send_x, capacity)
-
     probs, down_near, gate_near, place, weight_wide = run(
         functools.partial(probs_kernel, ctx_count),
         "probs_and_weights",
@@ -516,31 +522,56 @@
         scratch=[pltpu.SemaphoreType.DMA((2 * EXP_DEV,))],
     )
 
+    if far:
+        arrived_x = exchange(send_x, capacity, far)
+        after = [arrived_grad[s] for s in near]
+        start, place, after = lax.optimization_barrier(([send_x[s] for s in near], place, after))
+        for s, grad_piece, piece in zip(near, after, start):
+            arrived_grad[s] = grad_piece
+            arrived_x[s] = piece
+        arrived_x = exchange(arrived_x, capacity, near)
+    else:
+        arrived_x = exchange(send_x, capacity, steps)
+
     (d_act,) = run(
         functools.partial(expert_grad_kernel, capacity),
         "act_grads",
-        placed(VMEM, [down_near] + arrived_grad),
+        placed(VMEM, [down_near] + [arrived_grad[s] for s in ordered]),
         placed(VMEM, [shaped((slots, FFE), F32)]),
         expert_flops,
     )
-    act, *send_dn = run(
-        functools.partial(expert_back_kernel, capacity, piece_count),
-        "expert_backward",
-        placed(VMEM, [gate_near, d_act] + arrived_x),
-        placed(VMEM, [shaped((slots, EXP_DEV * FFE), BF16)] + piece_shapes),
-        2 * expert_flops,
-    )
-    dn = exchange(send_dn, capacity)
-    terms, *send_y = run(
-        functools.partial(expert_out_kernel, piece_count),
+    send_dn = [None] * piece_count
+    acts = []
+    done = 0
+    for group in groups:
+        group_rows = sum(piece_shapes[s].shape[0] for s in group)
+        act, *parts = run(
+            functools.partial(expert_back_kernel, capacity, len(group), done),
+            "expert_backward",
+            placed(VMEM, [gate_near, d_act] + [arrived_x[s] for s in group]),
+            placed(
+                VMEM,
+                [shaped((group_rows, EXP_DEV * FFE), BF16)] + [piece_shapes[s] for s in group],
+            ),
+            2 * expert_flops * group_rows // slots,
+        )
+        acts.append(act)
+        done += group_rows
+        for s, part in zip(group, parts):
+            send_dn[s] = part
+    dn = exchange(send_dn, capacity, steps)
+    terms, *outs = run(
+        functools.partial(expert_out_kernel, piece_count, len(acts)),
         "expert_output",
-        placed(VMEM, [down_near, gain, act] + arrived_x + send_dn),
+        placed(VMEM, [down_near, gain] + acts)
+        + placed(VMEM, [arrived_x[s] for s in ordered] + [send_dn[s] for s in ordered]),
         placed(VMEM, [shaped((GAIN_LINES, LANES), F32)] + piece_shapes),
         expert_flops,
     )
+    send_y = [outs[ordered.index(s)] for s in steps]
     terms = doubled(sum_over(terms, "ctx"), "exp", 2)
     terms, send_y, dn = lax.optimization_barrier((terms, send_y, dn))
-    y = exchange(send_y, capacity)
+    y = exchange(send_y, capacity, steps)
     terms = widened(doubled, terms, "dp", 2)
     terms, place_back = lax.optimization_barrier((terms, place))
     terms = doubled(terms, "exp", 1)

time: 55.9 us -> 60.5 us (1.082)
  waiting for transfers between devices: 15.4 us -> 17.8 us
  Pallas kernels: 15.5 us -> 17.1 us
    ppermute x20, waiting for transfers between devices: 15.4 us -> 17.8 us  [pairwise(): return lax.ppermute(value, axis, [(i, i ^ step) for i in range(count)])]
    pallas_call x8 -> x9, Pallas kernels: 15.5 us -> 17.1 us  [run(): pl.pallas_call(kernel, out_shape=[x for _, x in outputs], in_specs=[spec[...]
  transfers between devices with their start and end apart: 20 -> 20, of which waited for: 8 -> 9; matrix products, arithmetic and copies ran while one was open for 0% -> 0% of each run, Pallas kernels for 19% -> 24%
where the time goes in v8:
time: 60.5 us; the launch traced here: 60.4 us
  starting transfers between devices  24.6 us (41%)
  waiting for transfers between devices  17.8 us (29%)
  Pallas kernels  17.1 us (28%)
  between operations  0.8 us (1%)
    ppermute x20, starting transfers between devices, pairwise(): return lax.ppermute(value, axis, [(i, i ^ step) for i in range(count)])  24.6 us
    ppermute x20, waiting for transfers between devices, pairwise(): return lax.ppermute(value, axis, [(i, i ^ step) for i in range(count)])  17.8 us
    pallas_call x9, Pallas kernels, run(): pl.pallas_call(kernel, out_shape=[x for _, x in outputs], in_specs=[spec[...  17.1 us
  transfers between devices with their start and end apart: 20, of which 9 were waited for; matrix products, arithmetic and copies ran while one was open for 0% of the time, Pallas kernels for 24%

profile of v8, /device:TPU:0, one launch (start us, length us, event | category | flops | bytes accessed | tf_op | source)
XLA Modules:
  0.0 60.4 jit_solution(4808073270243484520)
XLA Ops:
  0.6 1.5 %dispatch_grads.1 = (bf16[128,2048]{1,0:T(8,128)(2,1)S(1)}, bf16[128,256]{1,0:T(8,128)(2,1)S(1)}, bf16[128,256]{1,0:T(8,128)(2,1)S(1)}, f32[1,2048]{1,0:T(1,128)...) custom-call(bf16[128,2048]{1,0:T(8,128)(2,1)} %bitcast.13, ...), custom_call_target="tpu_custom_call" | custom-call | flops 100663296 | bytes 4213824 | tf_op jit(solution)/shard_map/dispatch_grads/pallas_call | solution.py:372
  2.2 3.0 %collective-permute-start.2 = (bf16[48,2048]{1,0:T(8,128)(2,1)S(1)}, bf16[48,2048]{1,0:T(8,128)(2,1)S(1)}, u32[]{:S(2)}, u32[]{:S(2)}) collective-permute-start(bf16[48,2048]{1,0:T(8,128)(2,1)S(1)} %get-tuple-element.83), channel_id=1, source_target_pairs={{0,4},{4,0},{8,12},{12,8},{1,5},{5,1},{9,13},{13,9},{2,6},{6,2},{1... | collective-permute-start | bytes 589832 | tf_op jit(solution)/shard_map/ppermute | solution.py:391
  5.2 1.5 %collective-permute-start.3 = (bf16[48,2048]{1,0:T(8,128)(2,1)S(1)}, bf16[48,2048]{1,0:T(8,128)(2,1)S(1)}, u32[]{:S(2)}, u32[]{:S(2)}) collective-permute-start(bf16[48,2048]{1,0:T(8,128)(2,1)S(1)} %get-tuple-element.84), channel_id=1, source_target_pairs={{0,8},{4,12},{8,0},{12,4},{1,9},{5,13},{9,1},{13,5},{2,10},{6,14},... | collective-permute-start | bytes 589832 | tf_op jit(solution)/shard_map/ppermute | solution.py:391
  6.7 0.5 collective-permute-start
  7.2 0.7 %collective-permute-done.1.refs_3_.refs_7_ = bf16[128,256]{1,0:T(8,128)(2,1)S(1)} collective-permute-done((bf16[128,256]{1,0:T(8,128)(2,1)S(1)}, bf16[128,256]{1,0:T(8,128)(2,1)S(1)}, u32[]{:S(2)}, u32[]{:S(2)}) %collective-permute-start.1) | collective-permute-done | bytes 65568 | tf_op jit(solution)/shard_map/ppermute | solution.py:391
  8.0 0.2 collective-permute-done.refs_1_.refs_5_
  8.1 1.4 %attention_forward.1 = (bf16[128,2048]{1,0:T(8,128)(2,1)S(1)}, bf16[48,2048]{1,0:T(8,128)(2,1)S(1)}, bf16[48,2048]{1,0:T(8,128)(2,1)S(1)}, bf16[48,2048]{1,0:T(8,128)(2,1)S(1)}, bf16[48,2048]{1,0:T(8,128)(2,1)S(1)}) custom-call(s32[2,128]{1,0:T(2,128)S(1)} %get-tuple-element.70.pos_ref, s32[1,128]{1,0:T(1,128)S(1)} %get-tuple-element.71.slot_ref, ...), custom_call_target="tpu_custom_call" | custom-call | flops 369098752 | bytes 2631168 | tf_op jit(solution)/shard_map/attention_forward/pallas_call | solution.py:372
  9.6 2.1 %collective-permute-start.5 = (bf16[48,2048]{1,0:T(8,128)(2,1)S(1)}, bf16[48,2048]{1,0:T(8,128)(2,1)S(1)}, u32[]{:S(2)}, u32[]{:S(2)}) collective-permute-start(bf16[48,2048]{1,0:T(8,128)(2,1)S(1)} %get-tuple-element.93), channel_id=1, source_target_pairs={{0,12},{4,8},{8,4},{12,0},{1,13},{5,9},{9,5},{13,1},{2,14},{6,10},... | collective-permute-start | bytes 589832 | tf_op jit(solution)/shard_map/ppermute | solution.py:391
  11.6 2.9 %probs_and_weights.1 = (f32[8,256,256]{2,1,0:T(8,128)S(1)}, bf16[768,2048]{1,0:T(8,128)(2,1)S(1)}, bf16[2048,768]{1,0:T(8,128)(2,1)S(1)}, bf16[128,192]{1,0:T(8,128)(2,1)S(1)}, f32[128,256]{1,0:T(8,128)S(1)}) custom-call(s32[2,128]{1,0:T(2,128)S(1)} %get-tuple-element.70.pos_ref, s32[1,128]{1,0:T(1,128)S(1)} %get-tuple-element.71.slot_ref, ...), custom_call_target="tpu_custom_call" | custom-call | flops 134217728 | bytes 15517696 | tf_op jit(solution)/shard_map/probs_and_weights/pallas_call | solution.py:372
  14.6 5.8 %collective-permute-done.3.refs_3_ = bf16[48,2048]{1,0:T(8,128)(2,1)S(1)} collective-permute-done((bf16[48,2048]{1,0:T(8,128)(2,1)S(1)}, bf16[48,2048]{1,0:T(8,128)(2,1)S(1)}, u32[]{:S(2)}, u32[]{:S(2)}) %collective-permute-start.3) | collective-permute-done | bytes 196640 | tf_op jit(solution)/shard_map/ppermute | solution.py:391
  20.4 2.5 %collective-permute-start.7 = (bf16[48,2048]{1,0:T(8,128)(2,1)S(1)}, bf16[48,2048]{1,0:T(8,128)(2,1)S(1)}, u32[]{:S(2)}, u32[]{:S(2)}) collective-permute-start(bf16[48,2048]{1,0:T(8,128)(2,1)S(1)} %get-tuple-element.97), channel_id=1, source_target_pairs={{0,8},{4,12},{8,0},{12,4},{1,9},{5,13},{9,1},{13,5},{2,10},{6,14},... | collective-permute-start | bytes 589832 | tf_op jit(solution)/shard_map/ppermute | solution.py:391
  22.8 1.2 %act_grads.1.d_act_ref = f32[192,384]{1,0:T(8,128)S(1)} custom-call(bf16[768,2048]{1,0:T(8,128)(2,1)S(1)} %get-tuple-element.87.down_ref, bf16[48,2048]{1,0:T(8,128)(2,1)S(1)} %collective-permute-done.4.refs_0_, bf16[48,2048]{1,0:T(8,128)(2,1)S(1)} %get-tuple-element.90.refs_1_, bf16[48,2048]{1,0:T(8,128)(2,1)S(1)} %collective-permute-done.2.refs_2_, ...), custom_call_target="tpu_custom_call" | custom-call | flops 603979776 | bytes 4227072 | tf_op jit(solution)/shard_map/act_grads/pallas_call | solution.py:372
  24.0 1.8 %expert_backward.2 = (bf16[48,768]{1,0:T(8,128)(2,1)S(1)}, bf16[48,2048]{1,0:T(8,128)(2,1)S(1)}) custom-call(bf16[2048,768]{1,0:T(8,128)(2,1)S(1)} %get-tuple-element.88.gate_ref, f32[192,384]{1,0:T(8,128)S(1)} %act_grads.1.d_act_ref, bf16[48,2048]{1,0:T(8,128)(2,1)S(1)} %collective-permute-done.5.refs_0_.refs_2_), custom_call_target="tpu_custom_call" | custom-call | flops 301989888 | bytes 3907584 | tf_op jit(solution)/shard_map/expert_backward/pallas_call | solution.py:372
  25.9 1.5 %collective-permute-start.12 = (bf16[48,2048]{1,0:T(8,128)(2,1)S(1)}, bf16[48,2048]{1,0:T(8,128)(2,1)S(1)}, u32[]{:S(2)}, u32[]{:S(2)}) collective-permute-start(bf16[48,2048]{1,0:T(8,128)(2,1)S(1)} %get-tuple-element.99.refs_6_), channel_id=1, source_target_pairs={{0,12},{4,8},{8,4},{12,0},{1,13},{5,9},{9,5},{13,1},{2,14},{6,10},... | collective-permute-start | bytes 589832 | tf_op jit(solution)/shard_map/ppermute | solution.py:391
  27.4 0.6 %collective-permute-done.6.refs_1_.refs_4_ = bf16[48,2048]{1,0:T(8,128)(2,1)S(1)} collective-permute-done((bf16[48,2048]{1,0:T(8,128)(2,1)S(1)}, bf16[48,2048]{1,0:T(8,128)(2,1)S(1)}, u32[]{:S(2)}, u32[]{:S(2)}) %collective-permute-start.6) | collective-permute-done | bytes 196640 | tf_op jit(solution)/shard_map/ppermute | solution.py:391
  28.1 1.3 %collective-permute-done.7.refs_2_.refs_5_ = bf16[48,2048]{1,0:T(8,128)(2,1)S(1)} collective-permute-done((bf16[48,2048]{1,0:T(8,128)(2,1)S(1)}, bf16[48,2048]{1,0:T(8,128)(2,1)S(1)}, u32[]{:S(2)}, u32[]{:S(2)}) %collective-permute-start.7) | collective-permute-done | bytes 196640 | tf_op jit(solution)/shard_map/ppermute | solution.py:391
  29.3 2.1 %expert_backward.3 = (bf16[144,768]{1,0:T(8,128)(2,1)S(1)}, bf16[48,2048]{1,0:T(8,128)(2,1)S(1)}, bf16[48,2048]{1,0:T(8,128)(2,1)S(1)}, bf16[48,2048]{1,0:T(8,128)(2,1)S(1)}) custom-call(bf16[2048,768]{1,0:T(8,128)(2,1)S(1)} %get-tuple-element.88.gate_ref, f32[192,384]{1,0:T(8,128)S(1)} %act_grads.1.d_act_ref, ...), custom_call_target="tpu_custom_call" | custom-call | flops 905969664 | bytes 4841472 | tf_op jit(solution)/shard_map/expert_backward/pallas_call | solution.py:372
  31.4 3.2 %collective-permute-start.10 = (bf16[48,2048]{1,0:T(8,128)(2,1)S(1)}, bf16[48,2048]{1,0:T(8,128)(2,1)S(1)}, u32[]{:S(2)}, u32[]{:S(2)}) collective-permute-start(bf16[48,2048]{1,0:T(8,128)(2,1)S(1)} %get-tuple-element.101.refs_8_), channel_id=1, source_target_pairs={{0,4},{4,0},{8,12},{12,8},{1,5},{5,1},{9,13},{13,9},{2,6},{6,2},{1... | collective-permute-start | bytes 589832 | tf_op jit(solution)/shard_map/ppermute | solution.py:391
  34.6 2.6 %collective-permute-start.11 = (bf16[48,2048]{1,0:T(8,128)(2,1)S(1)}, bf16[48,2048]{1,0:T(8,128)(2,1)S(1)}, u32[]{:S(2)}, u32[]{:S(2)}) collective-permute-start(bf16[48,2048]{1,0:T(8,128)(2,1)S(1)} %get-tuple-element.102.refs_9_), channel_id=1, source_target_pairs={{0,8},{4,12},{8,0},{12,4},{1,9},{5,13},{9,1},{13,5},{2,10},{6,14},... | collective-permute-start | bytes 589832 | tf_op jit(solution)/shard_map/ppermute | solution.py:391
  37.2 0.9 %expert_output.1 = (f32[16,128]{1,0:T(8,128)S(1)}, bf16[48,2048]{1,0:T(8,128)(2,1)S(1)}, bf16[48,2048]{1,0:T(8,128)(2,1)S(1)}, bf16[48,2048]{1,0:T(8,128)(2,1)S(1)}, bf16[48,2048]{1,0:T(8,128)(2,1)S(1)}) custom-call(bf16[768,2048]{1,0:T(8,128)(2,1)S(1)} %get-tuple-element.87.down_ref, f32[1,2048]{1,0:T(1,128)S(1)} %get-tuple-element.72.gain_ref, ...), custom_call_target="tpu_custom_call" | custom-call | flops 603979776 | bytes 5816320 | tf_op jit(solution)/shard_map/expert_output/pallas_call | solution.py:372
  38.2 0.1 collective-permute-start.8
  38.2 1.2 %collective-permute-done.8 = f32[16,128]{1,0:T(8,128)S(1)} collective-permute-done((f32[16,128]{1,0:T(8,128)S(1)}, f32[16,128]{1,0:T(8,128)S(1)}, u32[]{:S(2)}, u32[]{:S(2)}) %collective-permute-start.8) | collective-permute-done | bytes 8224 | tf_op jit(solution)/shard_map/ppermute | solution.py:391
  39.4 3.6 %collective-permute-done.9 = f32[16,128]{1,0:T(8,128)S(1)} collective-permute-done((f32[16,128]{1,0:T(8,128)S(1)}, f32[16,128]{1,0:T(8,128)S(1)}, u32[]{:S(2)}, u32[]{:S(2)}) %collective-permute-start.9) | collective-permute-done | bytes 8224 | tf_op jit(solution)/shard_map/ppermute | solution.py:391
  43.1 2.4 %collective-permute-start.13 = (f32[32,128]{1,0:T(8,128)S(1)}, f32[32,128]{1,0:T(8,128)S(1)}, u32[]{:S(2)}, u32[]{:S(2)}) collective-permute-start(f32[32,128]{1,0:T(8,128)S(1)} %pad.4), channel_id=1, source_target_pairs={{0,2},{1,3},{2,0},{3,1},{4,6},{5,7},{6,4},{7,5},{8,10},{9,11},{10,... | collective-permute-start | bytes 49160 | tf_op jit(solution)/shard_map/ppermute | solution.py:391
  45.5 0.1 collective-permute-start.17
  45.6 3.4 %collective-permute-start.19 = (bf16[48,2048]{1,0:T(8,128)(2,1)S(1)}, bf16[48,2048]{1,0:T(8,128)(2,1)S(1)}, u32[]{:S(2)}, u32[]{:S(2)}) collective-permute-start(bf16[48,2048]{1,0:T(8,128)(2,1)S(1)} %get-tuple-element.125), channel_id=1, source_target_pairs={{0,12},{4,8},{8,4},{12,0},{1,13},{5,9},{9,5},{13,1},{2,14},{6,10},... | collective-permute-start | bytes 589832 | tf_op jit(solution)/shard_map/ppermute | solution.py:391
  49.0 0.1 collective-permute-start.14
  49.1 4.0 %residual_attention_backward.1 = (bf16[128,2048]{1,0:T(8,128)(2,1)}, bf16[128,2048]{1,0:T(8,128)(2,1)}, f32[128,512]{1,0:T(8,128)S(1)}, bf16[128,512]{1,0:T(8,128)(2,1)S(1)}) custom-call(bf16[128,192]{1,0:T(8,128)(2,1)S(1)} %get-tuple-element.110.place_ref, f32[1,2048]{1,0:T(1,128)S(1)} %get-tuple-element.72.gain_ref, ...), custom_call_target="tpu_custom_call" | custom-call | flops 369098752 | bytes 6217728 | tf_op jit(solution)/shard_map/residual_attention_backward/pallas_call | solution.py:372
  53.1 2.3 %collective-permute-done.14 = f32[16,128]{1,0:T(8,128)S(1)} collective-permute-done((f32[16,128]{1,0:T(8,128)S(1)}, f32[16,128]{1,0:T(8,128)S(1)}, u32[]{:S(2)}, u32[]{:S(2)}) %collective-permute-start.14) | collective-permute-done | bytes 8224 | tf_op jit(solution)/shard_map/ppermute | solution.py:391
  55.5 1.6 %collective-permute-start.15 = (f32[16,128]{1,0:T(8,128)S(1)}, f32[16,128]{1,0:T(8,128)S(1)}, u32[]{:S(2)}, u32[]{:S(2)}) collective-permute-start(f32[16,128]{1,0:T(8,128)S(1)} %add.20), channel_id=1, source_target_pairs={{0,1},{1,0},{2,3},{3,2},{4,5},{5,4},{6,7},{7,6},{8,9},{9,8},{10,11... | collective-permute-start | bytes 24584 | tf_op jit(solution)/shard_map/ppermute | solution.py:391
  57.0 2.1 %collective-permute-done.15 = f32[16,128]{1,0:T(8,128)S(1)} collective-permute-done((f32[16,128]{1,0:T(8,128)S(1)}, f32[16,128]{1,0:T(8,128)S(1)}, u32[]{:S(2)}, u32[]{:S(2)}) %collective-permute-start.15) | collective-permute-done | bytes 8224 | tf_op jit(solution)/shard_map/ppermute | solution.py:391
  59.1 1.2 %layer_output.1 = (bf16[128,2048]{1,0:T(8,128)(2,1)}, bf16[128,256]{1,0:T(8,128)(2,1)}, bf16[128,256]{1,0:T(8,128)(2,1)}, f32[1,128]{1,0:T(1,128)}, f32[16,128]{1,0:T(8,128)}) custom-call(bf16[128,192]{1,0:T(8,128)(2,1)S(1)} %get-tuple-element.110.place_ref, f32[128,256]{1,0:T(8,128)S(1)} %get-tuple-element.86.weight_ref, f32[16,128]{1,0:T(8,128)S(1)} %add.21.gain_ref, ...), custom_call_target="tpu_custom_call" | custom-call | flops 100663296 | bytes 3080704 | tf_op jit(solution)/shard_map/layer_output/pallas_call | solution.py:372
  (23 shorter events, 0.1 us)
Async XLA Ops:
  2.2 12.4 %collective-permute-start.2 = (bf16[48,2048]{1,0:T(8,128)(2,1)S(1)}, bf16[48,2048]{1,0:T(8,128)(2,1)S(1)}, u32[]{:S(2)}, u32[]{:S(2)}) collective-permute-start(bf16[48,2048]{1,0:T(8,128)(2,1)S(1)} %get-tuple-element.83), channel_id=1, source_target_pairs={{0,4},{4,0},{8,12},{12,8},{1,5},{5,1},{9,13},{13,9},{2,6},{6,2},{1... | collective-permute-start | bytes 589832 | tf_op jit(solution)/shard_map/ppermute | solution.py:391
  5.2 15.2 %collective-permute-start.3 = (bf16[48,2048]{1,0:T(8,128)(2,1)S(1)}, bf16[48,2048]{1,0:T(8,128)(2,1)S(1)}, u32[]{:S(2)}, u32[]{:S(2)}) collective-permute-start(bf16[48,2048]{1,0:T(8,128)(2,1)S(1)} %get-tuple-element.84), channel_id=1, source_target_pairs={{0,8},{4,12},{8,0},{12,4},{1,9},{5,13},{9,1},{13,5},{2,10},{6,14},... | collective-permute-start | bytes 589832 | tf_op jit(solution)/shard_map/ppermute | solution.py:391
  6.7 1.3 %collective-permute-start.1 = (bf16[128,256]{1,0:T(8,128)(2,1)S(1)}, bf16[128,256]{1,0:T(8,128)(2,1)S(1)}, u32[]{:S(2)}, u32[]{:S(2)}) collective-permute-start(bf16[128,256]{1,0:T(8,128)(2,1)S(1)} %get-tuple-element.76.refs_2_.refs_6_), channel_id=1, source_target_pairs={{0,16},{16,0},{1,17},{17,1},{2,18},{18,2},{3,19},{19,3},{4,20},{20... | collective-permute-start | bytes 196616 | tf_op jit(solution)/shard_map/ppermute | solution.py:391
  6.7 1.4 %collective-permute-start = (bf16[128,256]{1,0:T(8,128)(2,1)S(1)}, bf16[128,256]{1,0:T(8,128)(2,1)S(1)}, u32[]{:S(2)}, u32[]{:S(2)}) collective-permute-start(bf16[128,256]{1,0:T(8,128)(2,1)S(1)} %get-tuple-element.75.refs_0_.refs_4_), channel_id=1, source_target_pairs={{0,16},{16,0},{1,17},{17,1},{2,18},{18,2},{3,19},{19,3},{4,20},{20... | collective-permute-start | bytes 196616 | tf_op jit(solution)/shard_map/ppermute | solution.py:391
  7.2 15.6 %collective-permute-start.4 = (bf16[48,2048]{1,0:T(8,128)(2,1)S(1)}, bf16[48,2048]{1,0:T(8,128)(2,1)S(1)}, u32[]{:S(2)}, u32[]{:S(2)}) collective-permute-start(bf16[48,2048]{1,0:T(8,128)(2,1)S(1)} %get-tuple-element.89), channel_id=1, source_target_pairs={{0,12},{4,8},{8,4},{12,0},{1,13},{5,9},{9,5},{13,1},{2,14},{6,10},... | collective-permute-start | bytes 589832 | tf_op jit(solution)/shard_map/ppermute | solution.py:391
  9.6 14.5 %collective-permute-start.5 = (bf16[48,2048]{1,0:T(8,128)(2,1)S(1)}, bf16[48,2048]{1,0:T(8,128)(2,1)S(1)}, u32[]{:S(2)}, u32[]{:S(2)}) collective-permute-start(bf16[48,2048]{1,0:T(8,128)(2,1)S(1)} %get-tuple-element.93), channel_id=1, source_target_pairs={{0,12},{4,8},{8,4},{12,0},{1,13},{5,9},{9,5},{13,1},{2,14},{6,10},... | collective-permute-start | bytes 589832 | tf_op jit(solution)/shard_map/ppermute | solution.py:391
  20.4 7.7 %collective-permute-start.6 = (bf16[48,2048]{1,0:T(8,128)(2,1)S(1)}, bf16[48,2048]{1,0:T(8,128)(2,1)S(1)}, u32[]{:S(2)}, u32[]{:S(2)}) collective-permute-start(bf16[48,2048]{1,0:T(8,128)(2,1)S(1)} %get-tuple-element.96), channel_id=1, source_target_pairs={{0,4},{4,0},{8,12},{12,8},{1,5},{5,1},{9,13},{13,9},{2,6},{6,2},{1... | collective-permute-start | bytes 589832 | tf_op jit(solution)/shard_map/ppermute | solution.py:391
  20.4 9.0 %collective-permute-start.7 = (bf16[48,2048]{1,0:T(8,128)(2,1)S(1)}, bf16[48,2048]{1,0:T(8,128)(2,1)S(1)}, u32[]{:S(2)}, u32[]{:S(2)}) collective-permute-start(bf16[48,2048]{1,0:T(8,128)(2,1)S(1)} %get-tuple-element.97), channel_id=1, source_target_pairs={{0,8},{4,12},{8,0},{12,4},{1,9},{5,13},{9,1},{13,5},{2,10},{6,14},... | collective-permute-start | bytes 589832 | tf_op jit(solution)/shard_map/ppermute | solution.py:391
  25.9 17.1 %collective-permute-start.12 = (bf16[48,2048]{1,0:T(8,128)(2,1)S(1)}, bf16[48,2048]{1,0:T(8,128)(2,1)S(1)}, u32[]{:S(2)}, u32[]{:S(2)}) collective-permute-start(bf16[48,2048]{1,0:T(8,128)(2,1)S(1)} %get-tuple-element.99.refs_6_), channel_id=1, source_target_pairs={{0,12},{4,8},{8,4},{12,0},{1,13},{5,9},{9,5},{13,1},{2,14},{6,10},... | collective-permute-start | bytes 589832 | tf_op jit(solution)/shard_map/ppermute | solution.py:391
  31.4 11.6 %collective-permute-start.10 = (bf16[48,2048]{1,0:T(8,128)(2,1)S(1)}, bf16[48,2048]{1,0:T(8,128)(2,1)S(1)}, u32[]{:S(2)}, u32[]{:S(2)}) collective-permute-start(bf16[48,2048]{1,0:T(8,128)(2,1)S(1)} %get-tuple-element.101.refs_8_), channel_id=1, source_target_pairs={{0,4},{4,0},{8,12},{12,8},{1,5},{5,1},{9,13},{13,9},{2,6},{6,2},{1... | collective-permute-start | bytes 589832 | tf_op jit(solution)/shard_map/ppermute | solution.py:391
  34.6 8.5 %collective-permute-start.11 = (bf16[48,2048]{1,0:T(8,128)(2,1)S(1)}, bf16[48,2048]{1,0:T(8,128)(2,1)S(1)}, u32[]{:S(2)}, u32[]{:S(2)}) collective-permute-start(bf16[48,2048]{1,0:T(8,128)(2,1)S(1)} %get-tuple-element.102.refs_9_), channel_id=1, source_target_pairs={{0,8},{4,12},{8,0},{12,4},{1,9},{5,13},{9,1},{13,5},{2,10},{6,14},... | collective-permute-start | bytes 589832 | tf_op jit(solution)/shard_map/ppermute | solution.py:391
  38.2 1.2 %collective-permute-start.8 = (f32[16,128]{1,0:T(8,128)S(1)}, f32[16,128]{1,0:T(8,128)S(1)}, u32[]{:S(2)}, u32[]{:S(2)}) collective-permute-start(f32[16,128]{1,0:T(8,128)S(1)} %get-tuple-element.103), channel_id=1, source_target_pairs={{0,16},{16,0},{1,17},{17,1},{2,18},{18,2},{3,19},{19,3},{4,20},{20... | collective-permute-start | bytes 24584 | tf_op jit(solution)/shard_map/ppermute | solution.py:391
  39.4 3.7 %collective-permute-start.9 = (f32[16,128]{1,0:T(8,128)S(1)}, f32[16,128]{1,0:T(8,128)S(1)}, u32[]{:S(2)}, u32[]{:S(2)}) collective-permute-start(f32[16,128]{1,0:T(8,128)S(1)} %add.17), channel_id=1, source_target_pairs={{0,8},{4,12},{8,0},{12,4},{1,9},{5,13},{9,1},{13,5},{2,10},{6,14},... | collective-permute-start | bytes 24584 | tf_op jit(solution)/shard_map/ppermute | solution.py:391
  43.1 5.9 %collective-permute-start.13 = (f32[32,128]{1,0:T(8,128)S(1)}, f32[32,128]{1,0:T(8,128)S(1)}, u32[]{:S(2)}, u32[]{:S(2)}) collective-permute-start(f32[32,128]{1,0:T(8,128)S(1)} %pad.4), channel_id=1, source_target_pairs={{0,2},{1,3},{2,0},{3,1},{4,6},{5,7},{6,4},{7,5},{8,10},{9,11},{10,... | collective-permute-start | bytes 49160 | tf_op jit(solution)/shard_map/ppermute | solution.py:391
  45.5 13.6 %collective-permute-start.17 = (bf16[48,2048]{1,0:T(8,128)(2,1)S(1)}, bf16[48,2048]{1,0:T(8,128)(2,1)S(1)}, u32[]{:S(2)}, u32[]{:S(2)}) collective-permute-start(bf16[48,2048]{1,0:T(8,128)(2,1)S(1)} %get-tuple-element.123), channel_id=1, source_target_pairs={{0,4},{4,0},{8,12},{12,8},{1,5},{5,1},{9,13},{13,9},{2,6},{6,2},{1... | collective-permute-start | bytes 589832 | tf_op jit(solution)/shard_map/ppermute | solution.py:391
  45.6 13.5 %collective-permute-start.18 = (bf16[48,2048]{1,0:T(8,128)(2,1)S(1)}, bf16[48,2048]{1,0:T(8,128)(2,1)S(1)}, u32[]{:S(2)}, u32[]{:S(2)}) collective-permute-start(bf16[48,2048]{1,0:T(8,128)(2,1)S(1)} %get-tuple-element.124), channel_id=1, source_target_pairs={{0,8},{4,12},{8,0},{12,4},{1,9},{5,13},{9,1},{13,5},{2,10},{6,14},... | collective-permute-start | bytes 589832 | tf_op jit(solution)/shard_map/ppermute | solution.py:391
  45.6 13.5 %collective-permute-start.19 = (bf16[48,2048]{1,0:T(8,128)(2,1)S(1)}, bf16[48,2048]{1,0:T(8,128)(2,1)S(1)}, u32[]{:S(2)}, u32[]{:S(2)}) collective-permute-start(bf16[48,2048]{1,0:T(8,128)(2,1)S(1)} %get-tuple-element.125), channel_id=1, source_target_pairs={{0,12},{4,8},{8,4},{12,0},{1,13},{5,9},{9,5},{13,1},{2,14},{6,10},... | collective-permute-start | bytes 589832 | tf_op jit(solution)/shard_map/ppermute | solution.py:391
  49.0 6.4 %collective-permute-start.14 = (f32[16,128]{1,0:T(8,128)S(1)}, f32[16,128]{1,0:T(8,128)S(1)}, u32[]{:S(2)}, u32[]{:S(2)}) collective-permute-start(f32[16,128]{1,0:T(8,128)S(1)} %slice_add_fusion), channel_id=1, source_target_pairs={{0,4},{4,0},{8,12},{12,8},{1,5},{5,1},{9,13},{13,9},{2,6},{6,2},{1... | collective-permute-start | bytes 24584 | tf_op jit(solution)/shard_map/ppermute | solution.py:391
  55.5 3.7 %collective-permute-start.16 = (bf16[128,512]{1,0:T(8,128)(2,1)S(1)}, bf16[128,512]{1,0:T(8,128)(2,1)S(1)}, u32[]{:S(2)}, u32[]{:S(2)}) collective-permute-start(bf16[128,512]{1,0:T(8,128)(2,1)S(1)} %get-tuple-element.121), channel_id=1, source_target_pairs={{0,16},{16,0},{1,17},{17,1},{2,18},{18,2},{3,19},{19,3},{4,20},{20... | collective-permute-start | bytes 393224 | tf_op jit(solution)/shard_map/ppermute | solution.py:391
  55.5 3.7 %collective-permute-start.15 = (f32[16,128]{1,0:T(8,128)S(1)}, f32[16,128]{1,0:T(8,128)S(1)}, u32[]{:S(2)}, u32[]{:S(2)}) collective-permute-start(f32[16,128]{1,0:T(8,128)S(1)} %add.20), channel_id=1, source_target_pairs={{0,1},{1,0},{2,3},{3,2},{4,5},{5,4},{6,7},{7,6},{8,9},{9,8},{10,11... | collective-permute-start | bytes 24584 | tf_op jit(solution)/shard_map/ppermute | solution.py:391

commit v9 on v7

--- a/solution.py
+++ b/solution.py
@@ -254,7 +254,8 @@
         terms = jnp.sum(products, axis=0, keepdims=True) / gain_ref[:, cols]
         for at in range(0, COLS, LANES):
             line = (cols.start + at) // LANES
-            terms_ref[line : line + 1, :] = terms[:, at : at + LANES]
+            part = jnp.broadcast_to(terms[:, at : at + LANES], (terms_ref.shape[0], LANES))
+            terms_ref[:, line, :] = part
 
 
 def backward_kernel(
@@ -531,24 +532,22 @@
         2 * expert_flops,
     )
     dn = exchange(send_dn, capacity)
+    group = exp_count * lax.axis_size("dp")
     terms, *send_y = run(
         functools.partial(expert_out_kernel, piece_count),
         "expert_output",
         placed(VMEM, [down_near, gain, act] + arrived_x + send_dn),
-        placed(VMEM, [shaped((GAIN_LINES, LANES), F32)] + piece_shapes),
+        placed(VMEM, [shaped((group, GAIN_LINES, LANES), F32)] + piece_shapes),
         expert_flops,
     )
-    terms = doubled(sum_over(terms, "ctx"), "exp", 2)
-    terms, send_y, dn = lax.optimization_barrier((terms, send_y, dn))
+    terms = lax.all_to_all(terms, ("exp", "dp"), split_axis=0, concat_axis=0, tiled=True)
+    terms, send_y = lax.optimization_barrier((terms, send_y))
     y = exchange(send_y, capacity)
-    terms = widened(doubled, terms, "dp", 2)
-    terms, place_back = lax.optimization_barrier((terms, place))
-    terms = doubled(terms, "exp", 1)
 
     d_hidden, d_queries, kv_own, *kv_send = run(
         functools.partial(backward_kernel, ctx_count, piece_count),
         "residual_attention_backward",
-        placed(VMEM, [place_back, gain, hidden, grad_rows, query_rows, probs])
+        placed(VMEM, [place, gain, hidden, grad_rows, query_rows, probs])
         + placed(VMEM, dn + all_keys + all_values),
         placed(HBM, [token_shape] * 2)
         + placed(
@@ -564,9 +563,8 @@
             pltpu.SemaphoreType.DMA((1 + KEY_VALUE_HEADS,)),
         ],
     )
-    terms, kv_send = lax.optimization_barrier((terms, kv_send))
-    terms = sum_over(sum_over(terms, "exp", first=4), "dp", first=4)
-    terms = doubled(terms, "dp", 1)
+    terms, kv_own = lax.optimization_barrier((terms, kv_own))
+    terms = sum_over(jnp.sum(terms, axis=0), "ctx")
     kv_arrived = [pairwise(part, "ctx", s) for s, part in enumerate(kv_send, 1)]
 
     kv_shape = shaped((tokens, kv_width // 2), BF16)

time: 55.9 us -> 65.1 us (1.16)
  local copies, waits for them, and re-layouts: 0.01 us -> 8.24 us
  Pallas kernels: 15.5 us -> 17.8 us
  waiting for transfers between devices: 15.4 us -> 13.1 us
  other arithmetic: 0.02 us -> 0.93 us
    unnamed x0 -> x24, local copies, waits for them, and re-layouts: none -> 8.24 us
    ppermute x20 -> x16, waiting for transfers between devices: 15.4 us -> 8.91 us  [pairwise(): return lax.ppermute(value, axis, [(i, i ^ step) for i in range(count)])]
    ppermute x20 -> x16, starting transfers between devices: 24.1 us -> 17.9 us  [pairwise(): return lax.ppermute(value, axis, [(i, i ^ step) for i in range(count)])]
    all_to_all x0 -> x1, starting transfers between devices: none -> 5.93 us  [per_device(): lax.all_to_all(terms, ('exp', 'dp'), split_axis=0, concat_axis=0, tiled=T...]
    all_to_all x0 -> x1, waiting for transfers between devices: none -> 4.18 us  [per_device(): lax.all_to_all(terms, ('exp', 'dp'), split_axis=0, concat_axis=0, tiled=T...]
    pallas_call x8, Pallas kernels: 15.5 us -> 17.8 us  [run(): pl.pallas_call(kernel, out_shape=[x for _, x in outputs], in_specs=[spec[...]
    reduce_sum x0 -> x1, other arithmetic: none -> 0.93 us  [per_device(): terms = sum_over(jnp.sum(terms, axis=0), 'ctx')]
  transfers between devices with their start and end apart: 20 -> 17, of which waited for: 8 -> 4; matrix products, arithmetic and copies ran while one was open for 0% -> 1% of each run, Pallas kernels for 19% -> 16%
where the time goes in v9:
time: 65.1 us; the launch traced here: 64.7 us
  starting transfers between devices  23.9 us (37%)
  Pallas kernels  17.8 us (27%)
  waiting for transfers between devices  13.1 us (20%)
  local copies, waits for them, and re-layouts  8.24 us (13%)
  other arithmetic  0.93 us (1%)
  between operations  0.79 us (1%)
    ppermute x16, starting transfers between devices, pairwise(): return lax.ppermute(value, axis, [(i, i ^ step) for i in range(count)])  17.9 us
    pallas_call x8, Pallas kernels, run(): pl.pallas_call(kernel, out_shape=[x for _, x in outputs], in_specs=[spec[...  17.8 us
    ppermute x16, waiting for transfers between devices, pairwise(): return lax.ppermute(value, axis, [(i, i ^ step) for i in range(count)])  8.91 us
    unnamed x24, local copies, waits for them, and re-layouts  8.24 us
    all_to_all x1, starting transfers between devices, per_device(): lax.all_to_all(terms, ('exp', 'dp'), split_axis=0, concat_axis=0, tiled=T...  5.93 us
    all_to_all x1, waiting for transfers between devices, per_device(): lax.all_to_all(terms, ('exp', 'dp'), split_axis=0, concat_axis=0, tiled=T...  4.18 us
  transfers between devices with their start and end apart: 17, of which 4 were waited for; matrix products, arithmetic and copies ran while one was open for 1% of the time, Pallas kernels for 16%

profile of v9, /device:TPU:0, one launch (start us, length us, event | category | flops | bytes accessed | tf_op | source)
XLA Modules:
  0.0 64.7 jit_solution(124479693846806684)
XLA Ops:
  0.6 1.5 %dispatch_grads.1 = (bf16[128,2048]{1,0:T(8,128)(2,1)S(1)}, bf16[128,256]{1,0:T(8,128)(2,1)S(1)}, bf16[128,256]{1,0:T(8,128)(2,1)S(1)}, f32[1,2048]{1,0:T(1,128)...) custom-call(bf16[128,2048]{1,0:T(8,128)(2,1)} %bitcast.13, ...), custom_call_target="tpu_custom_call" | custom-call | flops 100663296 | bytes 4213824 | tf_op jit(solution)/shard_map/dispatch_grads/pallas_call | solution.py:371
  2.2 3.0 %collective-permute-start.1 = (bf16[48,2048]{1,0:T(8,128)(2,1)S(1)}, bf16[48,2048]{1,0:T(8,128)(2,1)S(1)}, u32[]{:S(2)}, u32[]{:S(2)}) collective-permute-start(bf16[48,2048]{1,0:T(8,128)(2,1)S(1)} %get-tuple-element.67), channel_id=1, source_target_pairs={{0,4},{4,0},{8,12},{12,8},{1,5},{5,1},{9,13},{13,9},{2,6},{6,2},{1... | collective-permute-start | bytes 589832 | tf_op jit(solution)/shard_map/ppermute | solution.py:390
  5.7 1.5 %collective-permute-start.2 = (bf16[48,2048]{1,0:T(8,128)(2,1)S(1)}, bf16[48,2048]{1,0:T(8,128)(2,1)S(1)}, u32[]{:S(2)}, u32[]{:S(2)}) collective-permute-start(bf16[48,2048]{1,0:T(8,128)(2,1)S(1)} %get-tuple-element.68), channel_id=1, source_target_pairs={{0,8},{4,12},{8,0},{12,4},{1,9},{5,13},{9,1},{13,5},{2,10},{6,14},... | collective-permute-start | bytes 589832 | tf_op jit(solution)/shard_map/ppermute | solution.py:390
  7.3 1.5 %attention_forward.1 = (bf16[128,2048]{1,0:T(8,128)(2,1)S(1)}, bf16[48,2048]{1,0:T(8,128)(2,1)S(1)}, bf16[48,2048]{1,0:T(8,128)(2,1)S(1)}, bf16[48,2048]{1,0:T(8,128)(2,1)S(1)}, bf16[48,2048]{1,0:T(8,128)(2,1)S(1)}) custom-call(s32[2,128]{1,0:T(2,128)S(1)} %get-tuple-element.56.pos_ref, s32[1,128]{1,0:T(1,128)S(1)} %get-tuple-element.57.slot_ref, ...), custom_call_target="tpu_custom_call" | custom-call | flops 369098752 | bytes 2631168 | tf_op jit(solution)/shard_map/attention_forward/pallas_call | solution.py:371
  8.7 2.0 %collective-permute-start.5 = (bf16[48,2048]{1,0:T(8,128)(2,1)S(1)}, bf16[48,2048]{1,0:T(8,128)(2,1)S(1)}, u32[]{:S(2)}, u32[]{:S(2)}) collective-permute-start(bf16[48,2048]{1,0:T(8,128)(2,1)S(1)} %get-tuple-element.73), channel_id=1, source_target_pairs={{0,4},{4,0},{8,12},{12,8},{1,5},{5,1},{9,13},{13,9},{2,6},{6,2},{1... | collective-permute-start | bytes 589832 | tf_op jit(solution)/shard_map/ppermute | solution.py:390
  10.7 1.5 %collective-permute-start.6 = (bf16[48,2048]{1,0:T(8,128)(2,1)S(1)}, bf16[48,2048]{1,0:T(8,128)(2,1)S(1)}, u32[]{:S(2)}, u32[]{:S(2)}) collective-permute-start(bf16[48,2048]{1,0:T(8,128)(2,1)S(1)} %get-tuple-element.74), channel_id=1, source_target_pairs={{0,8},{4,12},{8,0},{12,4},{1,9},{5,13},{9,1},{13,5},{2,10},{6,14},... | collective-permute-start | bytes 589832 | tf_op jit(solution)/shard_map/ppermute | solution.py:390
  12.3 1.7 %collective-permute-start.7 = (bf16[48,2048]{1,0:T(8,128)(2,1)S(1)}, bf16[48,2048]{1,0:T(8,128)(2,1)S(1)}, u32[]{:S(2)}, u32[]{:S(2)}) collective-permute-start(bf16[48,2048]{1,0:T(8,128)(2,1)S(1)} %get-tuple-element.75), channel_id=1, source_target_pairs={{0,12},{4,8},{8,4},{12,0},{1,13},{5,9},{9,5},{13,1},{2,14},{6,10},... | collective-permute-start | bytes 589832 | tf_op jit(solution)/shard_map/ppermute | solution.py:390
  13.9 2.9 %probs_and_weights.1 = (f32[8,256,256]{2,1,0:T(8,128)S(1)}, bf16[768,2048]{1,0:T(8,128)(2,1)S(1)}, bf16[2048,768]{1,0:T(8,128)(2,1)S(1)}, bf16[128,192]{1,0:T(8,128)(2,1)S(1)}, f32[128,256]{1,0:T(8,128)S(1)}) custom-call(s32[2,128]{1,0:T(2,128)S(1)} %get-tuple-element.56.pos_ref, s32[1,128]{1,0:T(1,128)S(1)} %get-tuple-element.57.slot_ref, ...), custom_call_target="tpu_custom_call" | custom-call | flops 134217728 | bytes 15517696 | tf_op jit(solution)/shard_map/probs_and_weights/pallas_call | solution.py:371
  16.9 1.3 %copy-done = f32[8,256,256]{2,1,0:T(8,128)} copy-done((f32[8,256,256]{2,1,0:T(8,128)}, f32[8,256,256]{2,1,0:T(8,128)S(1)}, u32[]{:S(2)}) %copy-start) | copy-done | bytes 2097176
  18.2 1.2 %act_grads.1.d_act_ref = f32[192,384]{1,0:T(8,128)S(1)} custom-call(bf16[768,2048]{1,0:T(8,128)(2,1)S(1)} %get-tuple-element.63.down_ref, bf16[48,2048]{1,0:T(8,128)(2,1)S(1)} %get-tuple-element.66.refs_0_, bf16[48,2048]{1,0:T(8,128)(2,1)S(1)} %collective-permute-done.1.refs_1_, bf16[48,2048]{1,0:T(8,128)(2,1)S(1)} %collective-permute-done.2.refs_2_, ...), custom_call_target="tpu_custom_call" | custom-call | flops 603979776 | bytes 4227072 | tf_op jit(solution)/shard_map/act_grads/pallas_call | solution.py:371
  19.4 5.7 %collective-permute-done.6.refs_2_ = bf16[48,2048]{1,0:T(8,128)(2,1)S(1)} collective-permute-done((bf16[48,2048]{1,0:T(8,128)(2,1)S(1)}, bf16[48,2048]{1,0:T(8,128)(2,1)S(1)}, u32[]{:S(2)}, u32[]{:S(2)}) %collective-permute-start.6) | collective-permute-done | bytes 196640 | tf_op jit(solution)/shard_map/ppermute | solution.py:390
  25.2 2.3 %expert_backward.1 = (bf16[192,768]{1,0:T(8,128)(2,1)S(1)}, bf16[48,2048]{1,0:T(8,128)(2,1)S(1)}, bf16[48,2048]{1,0:T(8,128)(2,1)S(1)}, bf16[48,2048]{1,0:T(8,128)(2,1)S(1)}, bf16[48,2048]{1,0:T(8,128)(2,1)S(1)}) custom-call(bf16[2048,768]{1,0:T(8,128)(2,1)S(1)} %get-tuple-element.65.gate_ref, f32[192,384]{1,0:T(8,128)S(1)} %act_grads.1.d_act_ref, ...), custom_call_target="tpu_custom_call" | custom-call | flops 1207959552 | bytes 5308416 | tf_op jit(solution)/shard_map/expert_backward/pallas_call | solution.py:371
  27.4 1.7 %expert_output.1 = (f32[16,16,128]{2,1,0:T(8,128)}, bf16[48,2048]{1,0:T(8,128)(2,1)S(1)}, bf16[48,2048]{1,0:T(8,128)(2,1)S(1)}, bf16[48,2048]{1,0:T(8,128)(2,1)S(1)}, bf16[48,2048]{1,0:T(8,128)(2,1)S(1)}) custom-call(bf16[768,2048]{1,0:T(8,128)(2,1)S(1)} %get-tuple-element.63.down_ref, f32[1,2048]{1,0:T(1,128)S(1)} %get-tuple-element.64.gain_ref, ...), custom_call_target="tpu_custom_call" | custom-call | flops 603979776 | bytes 5939200 | tf_op jit(solution)/shard_map/expert_output/pallas_call | solution.py:371
  29.2 0.7 %copy-done.8 = bf16[48,2048]{1,0:T(8,128)(2,1)} copy-done((bf16[48,2048]{1,0:T(8,128)(2,1)}, bf16[48,2048]{1,0:T(8,128)(2,1)S(1)}, u32[]{:S(2)}) %copy-start.8) | copy-done | bytes 196632
  29.9 0.7 %copy-done.9 = bf16[48,2048]{1,0:T(8,128)(2,1)} copy-done((bf16[48,2048]{1,0:T(8,128)(2,1)}, bf16[48,2048]{1,0:T(8,128)(2,1)S(1)}, u32[]{:S(2)}) %copy-start.9) | copy-done | bytes 196632
  30.5 0.7 %copy-done.10 = bf16[48,2048]{1,0:T(8,128)(2,1)} copy-done((bf16[48,2048]{1,0:T(8,128)(2,1)}, bf16[48,2048]{1,0:T(8,128)(2,1)S(1)}, u32[]{:S(2)}) %copy-start.10) | copy-done | bytes 196632
  31.2 5.9 %all-to-all-start = ((f32[16,16,128]{2,1,0:T(8,128)}), f32[16,16,128]{2,1,0:T(8,128)S(1)}, u32[]{:S(2)}, u32[]{:S(2)}) async-start(f32[16,16,128]{2,1,0:T(8,128)} %get-tuple-element.81), calls=%async_computation | async-start | bytes 262144 | tf_op jit(solution)/shard_map/all_to_all | solution.py:543
  37.2 1.9 %collective-permute-start.8 = (bf16[48,2048]{1,0:T(8,128)(2,1)S(1)}, bf16[48,2048]{1,0:T(8,128)(2,1)S(1)}, u32[]{:S(2)}, u32[]{:S(2)}) collective-permute-start(bf16[48,2048]{1,0:T(8,128)(2,1)S(1)} %get-tuple-element.78.refs_5_), channel_id=1, source_target_pairs={{0,4},{4,0},{8,12},{12,8},{1,5},{5,1},{9,13},{13,9},{2,6},{6,2},{1... | collective-permute-start | bytes 589832 | tf_op jit(solution)/shard_map/ppermute | solution.py:390
  39.1 1.5 %collective-permute-start.9 = (bf16[48,2048]{1,0:T(8,128)(2,1)S(1)}, bf16[48,2048]{1,0:T(8,128)(2,1)S(1)}, u32[]{:S(2)}, u32[]{:S(2)}) collective-permute-start(bf16[48,2048]{1,0:T(8,128)(2,1)S(1)} %get-tuple-element.79.refs_6_), channel_id=1, source_target_pairs={{0,8},{4,12},{8,0},{12,4},{1,9},{5,13},{9,1},{13,5},{2,10},{6,14},... | collective-permute-start | bytes 589832 | tf_op jit(solution)/shard_map/ppermute | solution.py:390
  40.7 4.2 %all-to-all-done = f32[16,16,128]{2,1,0:T(8,128)S(1)} async-done(((f32[16,16,128]{2,1,0:T(8,128)}), f32[16,16,128]{2,1,0:T(8,128)S(1)}, u32[]{:S(2)}, u32[]{:S(2)}) %all-to-all-start) | async-done | bytes 131104 | tf_op jit(solution)/shard_map/all_to_all | solution.py:543
  45.6 0.8 %collective-permute-start.13 = (bf16[48,2048]{1,0:T(8,128)(2,1)}, bf16[48,2048]{1,0:T(8,128)(2,1)S(1)}, u32[]{:S(2)}, u32[]{:S(2)}) collective-permute-start(bf16[48,2048]{1,0:T(8,128)(2,1)} %copy-done.10), channel_id=1, source_target_pairs={{0,4},{4,0},{8,12},{12,8},{1,5},{5,1},{9,13},{13,9},{2,6},{6,2},{1... | collective-permute-start | bytes 589832 | tf_op jit(solution)/shard_map/ppermute | solution.py:390
  46.4 0.7 %collective-permute-start.14 = (bf16[48,2048]{1,0:T(8,128)(2,1)}, bf16[48,2048]{1,0:T(8,128)(2,1)}, u32[]{:S(2)}, u32[]{:S(2)}) collective-permute-start(bf16[48,2048]{1,0:T(8,128)(2,1)} %copy-done.9), channel_id=1, source_target_pairs={{0,8},{4,12},{8,0},{12,4},{1,9},{5,13},{9,1},{13,5},{2,10},{6,14},... | collective-permute-start | bytes 589832 | tf_op jit(solution)/shard_map/ppermute | solution.py:390
  47.1 1.9 %collective-permute-start.15 = (bf16[48,2048]{1,0:T(8,128)(2,1)}, bf16[48,2048]{1,0:T(8,128)(2,1)S(1)}, u32[]{:S(2)}, u32[]{:S(2)}) collective-permute-start(bf16[48,2048]{1,0:T(8,128)(2,1)} %copy-done.8), channel_id=1, source_target_pairs={{0,12},{4,8},{8,4},{12,0},{1,13},{5,9},{9,5},{13,1},{2,14},{6,10},... | collective-permute-start | bytes 589832 | tf_op jit(solution)/shard_map/ppermute | solution.py:390
  49.1 2.3 %collective-permute-done.10.refs_3_ = bf16[48,2048]{1,0:T(8,128)(2,1)S(1)} collective-permute-done((bf16[48,2048]{1,0:T(8,128)(2,1)S(1)}, bf16[48,2048]{1,0:T(8,128)(2,1)S(1)}, u32[]{:S(2)}, u32[]{:S(2)}) %collective-permute-start.10) | collective-permute-done | bytes 196640 | tf_op jit(solution)/shard_map/ppermute | solution.py:390
  51.4 1.6 %copy-done.1 = f32[8,256,256]{2,1,0:T(8,128)S(1)} copy-done((f32[8,256,256]{2,1,0:T(8,128)S(1)}, f32[8,256,256]{2,1,0:T(8,128)}, u32[]{:S(2)}) %copy-start.1) | copy-done | bytes 2097176
  53.0 0.8 %copy-done.5 = bf16[128,256]{1,0:T(8,128)(2,1)S(1)} copy-done((bf16[128,256]{1,0:T(8,128)(2,1)S(1)}, bf16[128,256]{1,0:T(8,128)(2,1)}, u32[]{:S(2)}) %copy-start.5) | copy-done | bytes 65560
  53.8 0.8 %copy-done.7 = bf16[128,256]{1,0:T(8,128)(2,1)S(1)} copy-done((bf16[128,256]{1,0:T(8,128)(2,1)S(1)}, bf16[128,256]{1,0:T(8,128)(2,1)}, u32[]{:S(2)}) %copy-start.7) | copy-done | bytes 65560
  54.6 4.7 %residual_attention_backward.1 = (bf16[128,2048]{1,0:T(8,128)(2,1)}, bf16[128,2048]{1,0:T(8,128)(2,1)}, f32[128,512]{1,0:T(8,128)S(1)}, bf16[128,512]{1,0:T(8,128)(2,1)}) custom-call(bf16[128,192]{1,0:T(8,128)(2,1)S(1)} %get-tuple-element.61.place_ref, f32[1,2048]{1,0:T(1,128)S(1)} %get-tuple-element.64.gain_ref, ...), custom_call_target="tpu_custom_call" | custom-call | flops 369098752 | bytes 6217728 | tf_op jit(solution)/shard_map/residual_attention_backward/pallas_call | solution.py:371
  59.4 0.9 %reduce_sum.9 = f32[16,128]{1,0:T(8,128)S(1)} reduce(f32[16,16,128]{2,1,0:T(8,128)} %copy-done.11, f32[]{:T(128)} %constant.0.clone.1), dimensions={0}, to_apply=%region_0.0 | reduce | flops 30720 | bytes 139268 | tf_op jit(solution)/shard_map/reduce_sum | solution.py:567
  60.9 0.8 %collective-permute-done.11 = f32[16,128]{1,0:T(8,128)S(1)} collective-permute-done((f32[16,128]{1,0:T(8,128)S(1)}, f32[16,128]{1,0:T(8,128)S(1)}, u32[]{:S(2)}, u32[]{:S(2)}) %collective-permute-start.11) | collective-permute-done | bytes 8224 | tf_op jit(solution)/shard_map/ppermute | solution.py:390
  61.7 0.9 %copy-done.3 = f32[128,256]{1,0:T(8,128)S(1)} copy-done((f32[128,256]{1,0:T(8,128)S(1)}, f32[128,256]{1,0:T(8,128)}, u32[]{:S(2)}) %copy-start.3) | copy-done | bytes 131096
  62.6 2.1 %layer_output.1 = (bf16[128,2048]{1,0:T(8,128)(2,1)}, bf16[128,256]{1,0:T(8,128)(2,1)}, bf16[128,256]{1,0:T(8,128)(2,1)}, f32[1,128]{1,0:T(1,128)}, f32[16,128]{1,0:T(8,128)}) custom-call(bf16[128,192]{1,0:T(8,128)(2,1)S(1)} %get-tuple-element.61.place_ref, f32[128,256]{1,0:T(8,128)S(1)} %copy-done.3, f32[16,128]{1,0:T(8,128)S(1)} %add.3.gain_ref, ...), custom_call_target="tpu_custom_call" | custom-call | flops 100663296 | bytes 3080704 | tf_op jit(solution)/shard_map/layer_output/pallas_call | solution.py:371
  (36 shorter events, 2.0 us)
Async XLA Ops:
  2.2 14.7 %copy-start.4 = (bf16[128,256]{1,0:T(8,128)(2,1)}, bf16[128,256]{1,0:T(8,128)(2,1)S(1)}, u32[]{:S(2)}) copy-start(bf16[128,256]{1,0:T(8,128)(2,1)S(1)} %get-tuple-element.71.refs_2_.refs_6_) | copy-start | bytes 196612
  2.2 10.1 %collective-permute-start.1 = (bf16[48,2048]{1,0:T(8,128)(2,1)S(1)}, bf16[48,2048]{1,0:T(8,128)(2,1)S(1)}, u32[]{:S(2)}, u32[]{:S(2)}) collective-permute-start(bf16[48,2048]{1,0:T(8,128)(2,1)S(1)} %get-tuple-element.67), channel_id=1, source_target_pairs={{0,4},{4,0},{8,12},{12,8},{1,5},{5,1},{9,13},{13,9},{2,6},{6,2},{1... | collective-permute-start | bytes 589832 | tf_op jit(solution)/shard_map/ppermute | solution.py:390
  5.2 2.1 %collective-permute-start = (bf16[128,256]{1,0:T(8,128)(2,1)}, bf16[128,256]{1,0:T(8,128)(2,1)S(1)}, u32[]{:S(2)}, u32[]{:S(2)}) collective-permute-start(bf16[128,256]{1,0:T(8,128)(2,1)} %bitcast.17), channel_id=1, source_target_pairs={{0,16},{16,0},{1,17},{17,1},{2,18},{18,2},{3,19},{19,3},{4,20},{20... | collective-permute-start | bytes 196616 | tf_op jit(solution)/shard_map/ppermute | solution.py:390
  5.2 2.1 %collective-permute-start.4 = (bf16[128,256]{1,0:T(8,128)(2,1)}, bf16[128,256]{1,0:T(8,128)(2,1)S(1)}, u32[]{:S(2)}, u32[]{:S(2)}) collective-permute-start(bf16[128,256]{1,0:T(8,128)(2,1)} %bitcast.19), channel_id=1, source_target_pairs={{0,16},{16,0},{1,17},{17,1},{2,18},{18,2},{3,19},{19,3},{4,20},{20... | collective-permute-start | bytes 196616 | tf_op jit(solution)/shard_map/ppermute | solution.py:390
  5.7 12.5 %collective-permute-start.2 = (bf16[48,2048]{1,0:T(8,128)(2,1)S(1)}, bf16[48,2048]{1,0:T(8,128)(2,1)S(1)}, u32[]{:S(2)}, u32[]{:S(2)}) collective-permute-start(bf16[48,2048]{1,0:T(8,128)(2,1)S(1)} %get-tuple-element.68), channel_id=1, source_target_pairs={{0,8},{4,12},{8,0},{12,4},{1,9},{5,13},{9,1},{13,5},{2,10},{6,14},... | collective-permute-start | bytes 589832 | tf_op jit(solution)/shard_map/ppermute | solution.py:390
  7.2 11.0 %collective-permute-start.3 = (bf16[48,2048]{1,0:T(8,128)(2,1)S(1)}, bf16[48,2048]{1,0:T(8,128)(2,1)S(1)}, u32[]{:S(2)}, u32[]{:S(2)}) collective-permute-start(bf16[48,2048]{1,0:T(8,128)(2,1)S(1)} %get-tuple-element.69), channel_id=1, source_target_pairs={{0,12},{4,8},{8,4},{12,0},{1,13},{5,9},{9,5},{13,1},{2,14},{6,10},... | collective-permute-start | bytes 589832 | tf_op jit(solution)/shard_map/ppermute | solution.py:390
  7.3 6.7 %copy-start.6 = (bf16[128,256]{1,0:T(8,128)(2,1)}, bf16[128,256]{1,0:T(8,128)(2,1)S(1)}, u32[]{:S(2)}) copy-start(bf16[128,256]{1,0:T(8,128)(2,1)S(1)} %collective-permute-done.4.refs_3_.refs_7_) | copy-start | bytes 196612
  8.7 10.7 %collective-permute-start.5 = (bf16[48,2048]{1,0:T(8,128)(2,1)S(1)}, bf16[48,2048]{1,0:T(8,128)(2,1)S(1)}, u32[]{:S(2)}, u32[]{:S(2)}) collective-permute-start(bf16[48,2048]{1,0:T(8,128)(2,1)S(1)} %get-tuple-element.73), channel_id=1, source_target_pairs={{0,4},{4,0},{8,12},{12,8},{1,5},{5,1},{9,13},{13,9},{2,6},{6,2},{1... | collective-permute-start | bytes 589832 | tf_op jit(solution)/shard_map/ppermute | solution.py:390
  10.7 14.4 %collective-permute-start.6 = (bf16[48,2048]{1,0:T(8,128)(2,1)S(1)}, bf16[48,2048]{1,0:T(8,128)(2,1)S(1)}, u32[]{:S(2)}, u32[]{:S(2)}) collective-permute-start(bf16[48,2048]{1,0:T(8,128)(2,1)S(1)} %get-tuple-element.74), channel_id=1, source_target_pairs={{0,8},{4,12},{8,0},{12,4},{1,9},{5,13},{9,1},{13,5},{2,10},{6,14},... | collective-permute-start | bytes 589832 | tf_op jit(solution)/shard_map/ppermute | solution.py:390
  12.3 12.9 %collective-permute-start.7 = (bf16[48,2048]{1,0:T(8,128)(2,1)S(1)}, bf16[48,2048]{1,0:T(8,128)(2,1)S(1)}, u32[]{:S(2)}, u32[]{:S(2)}) collective-permute-start(bf16[48,2048]{1,0:T(8,128)(2,1)S(1)} %get-tuple-element.75), channel_id=1, source_target_pairs={{0,12},{4,8},{8,4},{12,0},{1,13},{5,9},{9,5},{13,1},{2,14},{6,10},... | collective-permute-start | bytes 589832 | tf_op jit(solution)/shard_map/ppermute | solution.py:390
  16.9 1.4 %copy-start = (f32[8,256,256]{2,1,0:T(8,128)}, f32[8,256,256]{2,1,0:T(8,128)S(1)}, u32[]{:S(2)}) copy-start(f32[8,256,256]{2,1,0:T(8,128)S(1)} %get-tuple-element.89.probs_ref) | copy-start | bytes 6291460
  18.2 7.0 %copy-start.2 = (f32[128,256]{1,0:T(8,128)}, f32[128,256]{1,0:T(8,128)S(1)}, u32[]{:S(2)}) copy-start(f32[128,256]{1,0:T(8,128)S(1)} %get-tuple-element.62.weight_ref) | copy-start | bytes 393220
  29.2 0.7 %copy-start.8 = (bf16[48,2048]{1,0:T(8,128)(2,1)}, bf16[48,2048]{1,0:T(8,128)(2,1)S(1)}, u32[]{:S(2)}) copy-start(bf16[48,2048]{1,0:T(8,128)(2,1)S(1)} %get-tuple-element.97) | copy-start | bytes 589828
  29.9 0.7 %copy-start.9 = (bf16[48,2048]{1,0:T(8,128)(2,1)}, bf16[48,2048]{1,0:T(8,128)(2,1)S(1)}, u32[]{:S(2)}) copy-start(bf16[48,2048]{1,0:T(8,128)(2,1)S(1)} %get-tuple-element.96) | copy-start | bytes 589828
  30.5 0.7 %copy-start.10 = (bf16[48,2048]{1,0:T(8,128)(2,1)}, bf16[48,2048]{1,0:T(8,128)(2,1)S(1)}, u32[]{:S(2)}) copy-start(bf16[48,2048]{1,0:T(8,128)(2,1)S(1)} %get-tuple-element.95) | copy-start | bytes 589828
  31.2 13.7 %all-to-all-start = ((f32[16,16,128]{2,1,0:T(8,128)}), f32[16,16,128]{2,1,0:T(8,128)S(1)}, u32[]{:S(2)}, u32[]{:S(2)}) async-start(f32[16,16,128]{2,1,0:T(8,128)} %get-tuple-element.81), calls=%async_computation | async-start | bytes 262144 | tf_op jit(solution)/shard_map/all_to_all | solution.py:543
  37.2 9.9 %collective-permute-start.8 = (bf16[48,2048]{1,0:T(8,128)(2,1)S(1)}, bf16[48,2048]{1,0:T(8,128)(2,1)S(1)}, u32[]{:S(2)}, u32[]{:S(2)}) collective-permute-start(bf16[48,2048]{1,0:T(8,128)(2,1)S(1)} %get-tuple-element.78.refs_5_), channel_id=1, source_target_pairs={{0,4},{4,0},{8,12},{12,8},{1,5},{5,1},{9,13},{13,9},{2,6},{6,2},{1... | collective-permute-start | bytes 589832 | tf_op jit(solution)/shard_map/ppermute | solution.py:390
  39.1 10.0 %collective-permute-start.9 = (bf16[48,2048]{1,0:T(8,128)(2,1)S(1)}, bf16[48,2048]{1,0:T(8,128)(2,1)S(1)}, u32[]{:S(2)}, u32[]{:S(2)}) collective-permute-start(bf16[48,2048]{1,0:T(8,128)(2,1)S(1)} %get-tuple-element.79.refs_6_), channel_id=1, source_target_pairs={{0,8},{4,12},{8,0},{12,4},{1,9},{5,13},{9,1},{13,5},{2,10},{6,14},... | collective-permute-start | bytes 589832 | tf_op jit(solution)/shard_map/ppermute | solution.py:390
  40.6 10.8 %collective-permute-start.10 = (bf16[48,2048]{1,0:T(8,128)(2,1)S(1)}, bf16[48,2048]{1,0:T(8,128)(2,1)S(1)}, u32[]{:S(2)}, u32[]{:S(2)}) collective-permute-start(bf16[48,2048]{1,0:T(8,128)(2,1)S(1)} %get-tuple-element.80.refs_7_), channel_id=1, source_target_pairs={{0,12},{4,8},{8,4},{12,0},{1,13},{5,9},{9,5},{13,1},{2,14},{6,10},... | collective-permute-start | bytes 589832 | tf_op jit(solution)/shard_map/ppermute | solution.py:390
  44.9 0.7 %copy-start.11 = (f32[16,16,128]{2,1,0:T(8,128)}, f32[16,16,128]{2,1,0:T(8,128)S(1)}, u32[]{:S(2)}) copy-start(f32[16,16,128]{2,1,0:T(8,128)S(1)} %all-to-all-done) | copy-start | bytes 393220
  45.6 16.1 %collective-permute-start.13 = (bf16[48,2048]{1,0:T(8,128)(2,1)}, bf16[48,2048]{1,0:T(8,128)(2,1)S(1)}, u32[]{:S(2)}, u32[]{:S(2)}) collective-permute-start(bf16[48,2048]{1,0:T(8,128)(2,1)} %copy-done.10), channel_id=1, source_target_pairs={{0,4},{4,0},{8,12},{12,8},{1,5},{5,1},{9,13},{13,9},{2,6},{6,2},{1... | collective-permute-start | bytes 589832 | tf_op jit(solution)/shard_map/ppermute | solution.py:390
  46.4 15.3 %collective-permute-start.14 = (bf16[48,2048]{1,0:T(8,128)(2,1)}, bf16[48,2048]{1,0:T(8,128)(2,1)}, u32[]{:S(2)}, u32[]{:S(2)}) collective-permute-start(bf16[48,2048]{1,0:T(8,128)(2,1)} %copy-done.9), channel_id=1, source_target_pairs={{0,8},{4,12},{8,0},{12,4},{1,9},{5,13},{9,1},{13,5},{2,10},{6,14},... | collective-permute-start | bytes 589832 | tf_op jit(solution)/shard_map/ppermute | solution.py:390
  47.1 14.6 %collective-permute-start.15 = (bf16[48,2048]{1,0:T(8,128)(2,1)}, bf16[48,2048]{1,0:T(8,128)(2,1)S(1)}, u32[]{:S(2)}, u32[]{:S(2)}) collective-permute-start(bf16[48,2048]{1,0:T(8,128)(2,1)} %copy-done.8), channel_id=1, source_target_pairs={{0,12},{4,8},{8,4},{12,0},{1,13},{5,9},{9,5},{13,1},{2,14},{6,10},... | collective-permute-start | bytes 589832 | tf_op jit(solution)/shard_map/ppermute | solution.py:390
  51.4 1.6 %copy-start.1 = (f32[8,256,256]{2,1,0:T(8,128)S(1)}, f32[8,256,256]{2,1,0:T(8,128)}, u32[]{:S(2)}) copy-start(f32[8,256,256]{2,1,0:T(8,128)} %copy-done) | copy-start | bytes 6291460
  53.0 0.8 %copy-start.5 = (bf16[128,256]{1,0:T(8,128)(2,1)S(1)}, bf16[128,256]{1,0:T(8,128)(2,1)}, u32[]{:S(2)}) copy-start(bf16[128,256]{1,0:T(8,128)(2,1)} %copy-done.4) | copy-start | bytes 196612
  53.8 0.8 %copy-start.7 = (bf16[128,256]{1,0:T(8,128)(2,1)S(1)}, bf16[128,256]{1,0:T(8,128)(2,1)}, u32[]{:S(2)}) copy-start(bf16[128,256]{1,0:T(8,128)(2,1)} %copy-done.6) | copy-start | bytes 196612
  59.3 2.4 %collective-permute-start.12 = (bf16[128,512]{1,0:T(8,128)(2,1)}, bf16[128,512]{1,0:T(8,128)(2,1)S(1)}, u32[]{:S(2)}, u32[]{:S(2)}) collective-permute-start(bf16[128,512]{1,0:T(8,128)(2,1)} %get-tuple-element.93), channel_id=1, source_target_pairs={{0,16},{16,0},{1,17},{17,1},{2,18},{18,2},{3,19},{19,3},{4,20},{20... | collective-permute-start | bytes 393224 | tf_op jit(solution)/shard_map/ppermute | solution.py:390
  60.3 1.4 %collective-permute-start.11 = (f32[16,128]{1,0:T(8,128)S(1)}, f32[16,128]{1,0:T(8,128)S(1)}, u32[]{:S(2)}, u32[]{:S(2)}) collective-permute-start(f32[16,128]{1,0:T(8,128)S(1)} %reduce_sum.9), channel_id=1, source_target_pairs={{0,16},{16,0},{1,17},{17,1},{2,18},{18,2},{3,19},{19,3},{4,20},{20... | collective-permute-start | bytes 24584 | tf_op jit(solution)/shard_map/ppermute | solution.py:390
  61.7 0.9 %copy-start.3 = (f32[128,256]{1,0:T(8,128)S(1)}, f32[128,256]{1,0:T(8,128)}, u32[]{:S(2)}) copy-start(f32[128,256]{1,0:T(8,128)} %copy-done.2) | copy-start | bytes 393220

commit v10 on v5

--- a/solution.py
+++ b/solution.py
@@ -17,6 +17,9 @@
 COLS = 256
 LANES = 128
 GAIN_LINES = D // LANES
+WIDE_LINES = 32
+A_COST = 4000000000
+B_COST = 0
 SCALE = HEAD_SIZE ** (-0.5)
 EXP2_SCALE = SCALE * 1.4426950408889634
 F32 = jnp.float32
@@ -287,15 +290,45 @@
             terms_ref[line : line + 1, :] = terms[:, at : at + LANES]
 
 
-def backward_kernel(
+def group_back(g, key_refs, value_refs, query_ref, probs_ref, d_resid, dq_ref, own_ref, shared):
+    length = len(key_refs) * own_ref.shape[0]
+    tokens = own_ref.shape[0]
+    keys, values = kv_stacks(key_refs, value_refs, g)
+    keys_t = jnp.transpose(keys.astype(F32)).astype(BF16)
+    d_keys = jnp.zeros((length, HEAD_SIZE), F32)
+    d_values = jnp.zeros((length, HEAD_SIZE), F32)
+    for local in range(GROUP // 2):
+        pair = g * GROUP // 2 + local
+        cols_a, cols_b = pair_cols(local)
+        d_out = head_pair(d_resid, local)
+        probs = probs_ref[pair]
+        d_probs = mm(values, d_out, NT)
+        row_dot = jnp.sum(probs * d_probs, axis=0, keepdims=True)
+        d_scores = (probs * (d_probs - row_dot)).astype(BF16)
+        d_keys = d_keys + mm(d_scores, head_pair(query_ref, pair))
+        d_values = d_values + mm(probs.astype(BF16), d_out)
+        d_query_t = mm(keys_t, d_scores) * SCALE
+        dq_ref[:, cols_a] = jnp.transpose(d_query_t[:, :tokens]).astype(BF16)
+        dq_ref[:, cols_b] = jnp.transpose(d_query_t[:, tokens:]).astype(BF16)
+    d_keys = d_keys * SCALE
+    own_ref[:, :HEAD_SIZE] = d_keys[:tokens]
+    own_ref[:, HEAD_SIZE:] = d_values[:tokens]
+    start = 2 * g * HEAD_SIZE
+    for s, ref in enumerate(shared, 1):
+        span = slice(s * tokens, (s + 1) * tokens)
+        ref[:, start : start + HEAD_SIZE] = d_keys[span].astype(BF16)
+        ref[:, start + HEAD_SIZE : start + 2 * HEAD_SIZE] = d_values[span].astype(BF16)
+
+
+def first_back_kernel(
     count, pieces, rows, place_ref, gain_ref, hidden_ref, grad_ref, query_ref, probs_ref, *refs
 ):
+    key_refs, value_refs = refs[:count], refs[count : 2 * count]
+    refs = refs[2 * count :]
     dn_refs = part_views(refs[:pieces], rows, 0)
-    key_refs = refs[pieces : pieces + count]
-    value_refs = refs[pieces + count : pieces + 2 * count]
-    resid_hbm, dq_hbm, own_ref = refs[pieces + 2 * count : pieces + 2 * count + 3]
-    other_refs = refs[pieces + 2 * count + 3 : -4]
-    resid_ref, dq_ref, dn_scratch, sems = refs[-4:]
+    resid_hbm, dq_ref, rest_ref, own_ref = refs[pieces : pieces + 4]
+    shared = refs[pieces + 4 : -3]
+    resid_ref, dn_scratch, sem = refs[-3:]
     tokens = hidden_ref.shape[0]
     place = place_ref[...]
     square = jnp.zeros((tokens, COLS), F32)
@@ -309,64 +342,41 @@
     inv_rms = lax.rsqrt(jnp.sum(square, axis=1, keepdims=True) * (1.0 / D) + 1e-06)
     mean_mix = jnp.sum(mixing, axis=1, keepdims=True) * (1.0 / D)
     factor = inv_rms * inv_rms * inv_rms * mean_mix
+    half = GROUP * HEAD_SIZE
     for cols in column_blocks():
-        resid_ref[:, cols] = (
+        part = (
             grad_ref[:, cols].astype(F32)
             + dn_scratch[:, cols] * inv_rms
             - hidden_ref[:, cols].astype(F32) * factor
         ).astype(BF16)
-    copies = [pltpu.make_async_copy(resid_ref, resid_hbm, sems.at[0])]
-    copies[0].start()
-    length = count * tokens
-    group_width = GROUP * HEAD_SIZE
-    for g in range(KEY_VALUE_HEADS):
-        keys, values = kv_stacks(key_refs, value_refs, g)
-        keys_t = jnp.transpose(keys.astype(F32)).astype(BF16)
-        d_keys = jnp.zeros((length, HEAD_SIZE), F32)
-        d_values = jnp.zeros((length, HEAD_SIZE), F32)
-        for pair in range(g * GROUP // 2, (g + 1) * GROUP // 2):
-            cols_a, cols_b = pair_cols(pair)
-            d_out = head_pair(resid_ref, pair)
-            probs = probs_ref[pair]
-            d_probs = mm(values, d_out, NT)
-            row_dot = jnp.sum(probs * d_probs, axis=0, keepdims=True)
-            d_scores = (probs * (d_probs - row_dot)).astype(BF16)
-            d_keys = d_keys + mm(d_scores, head_pair(query_ref, pair))
-            d_values = d_values + mm(probs.astype(BF16), d_out)
-            d_query_t = mm(keys_t, d_scores) * SCALE
-            dq_ref[:, cols_a] = jnp.transpose(d_query_t[:, :tokens]).astype(BF16)
-            dq_ref[:, cols_b] = jnp.transpose(d_query_t[:, tokens:]).astype(BF16)
-        cols = slice(g * group_width, (g + 1) * group_width)
-        copy = pltpu.make_async_copy(dq_ref.at[:, cols], dq_hbm.at[:, cols], sems.at[1 + g])
-        copy.start()
-        copies.append(copy)
-        k_cols = slice(g * HEAD_SIZE, (g + 1) * HEAD_SIZE)
-        v_cols = slice((KEY_VALUE_HEADS + g) * HEAD_SIZE, (KEY_VALUE_HEADS + g + 1) * HEAD_SIZE)
-        d_keys = d_keys * SCALE
-        own_ref[:, k_cols] = d_keys[:tokens]
-        own_ref[:, v_cols] = d_values[:tokens]
-        for s, ref in enumerate(other_refs, 1):
-            ref[:, k_cols] = d_keys[s * tokens : (s + 1) * tokens].astype(BF16)
-            ref[:, v_cols] = d_values[s * tokens : (s + 1) * tokens].astype(BF16)
-    for copy in copies:
-        copy.wait()
+        resid_ref[:, cols] = part
+        if cols.start >= half:
+            rest_ref[:, cols.start - half : cols.stop - half] = part
+    resid_copy = pltpu.make_async_copy(resid_ref, resid_hbm, sem)
+    resid_copy.start()
+    group_back(0, key_refs, value_refs, query_ref, probs_ref, resid_ref, dq_ref, own_ref, shared)
+    resid_copy.wait()
+
+
+def second_back_kernel(count, query_ref, probs_ref, rest_ref, *refs):
+    key_refs, value_refs = refs[:count], refs[count : 2 * count]
+    first_shared = refs[2 * count : 3 * count - 1]
+    dq_ref, own_ref = refs[3 * count - 1 : 3 * count + 1]
+    shared = refs[3 * count + 1 :]
+    for source, target in zip(first_shared, shared):
+        target[:, : 2 * HEAD_SIZE] = source[...]
+    group_back(1, key_refs, value_refs, query_ref, probs_ref, rest_ref, dq_ref, own_ref, shared)
 
 
 def output_kernel(
     count, pieces, rows, tokens_in_all, place_ref, weight_ref, gain_ref, hidden_ref, grad_ref, *refs
 ):
-    own_ref, refs = refs[0], refs[1:]
+    own_refs, refs = refs[:KEY_VALUE_HEADS], refs[KEY_VALUE_HEADS:]
+    dq_refs, refs = refs[:KEY_VALUE_HEADS], refs[KEY_VALUE_HEADS:]
     arrived_refs = refs[: count - 1]
     y_refs = part_views(refs[count - 1 : count - 1 + pieces], rows, 1)
-    out_hbm, dk_hbm, dv_hbm, d_weight_hbm, d_gain_hbm = refs[count - 1 + pieces : -6]
+    out_hbm, dq_hbm, dk_hbm, dv_hbm, d_weight_hbm, d_gain_hbm = refs[count - 1 + pieces : -6]
     out_ref, dk_ref, dv_ref, d_weight_ref, d_gain_ref, sems = refs[-6:]
-    split = KEY_VALUE_HEADS * HEAD_SIZE
-    d_kv = own_ref[...]
-    for ref in arrived_refs:
-        d_kv = d_kv + ref[...].astype(F32)
-    dk_ref[...] = d_kv[:, :split].astype(BF16)
-    dv_ref[...] = d_kv[:, split:].astype(BF16)
-    d_gain_ref[...] = gain_ref[...] * (1.0 / tokens_in_all)
     copies = []
 
     def send(source, target):
@@ -374,6 +384,17 @@
         copy.start()
         copies.append(copy)
 
+    width = GROUP * HEAD_SIZE
+    for g, dq_ref in enumerate(dq_refs):
+        send(dq_ref, dq_hbm.at[:, g * width : (g + 1) * width])
+    for g, own_ref in enumerate(own_refs):
+        d_kv = own_ref[...]
+        for ref in arrived_refs:
+            d_kv = d_kv + ref[:, 2 * g * HEAD_SIZE : 2 * (g + 1) * HEAD_SIZE].astype(F32)
+        cols = slice(g * HEAD_SIZE, (g + 1) * HEAD_SIZE)
+        dk_ref[:, cols] = d_kv[:, :HEAD_SIZE].astype(BF16)
+        dv_ref[:, cols] = d_kv[:, HEAD_SIZE:].astype(BF16)
+    d_gain_ref[...] = gain_ref[...] * (1.0 / tokens_in_all)
     send(dk_ref, dk_hbm)
     send(dv_ref, dv_hbm)
     send(d_gain_ref, d_gain_hbm)
@@ -393,9 +414,7 @@
 
 
 def run(kernel, name, inputs, outputs, flops, scratch=(), limit=20 * MIB):
-    nbytes = sum(x.size * x.dtype.itemsize for _, x in inputs) + sum(
-        x.size * x.dtype.itemsize for _, x in outputs
-    )
+    nbytes = sum(x.size * x.dtype.itemsize for _, x in inputs + outputs) if flops else 0
     spec = {space: pl.BlockSpec(memory_space=space) for space in (VMEM, HBM)}
     results = pl.pallas_call(
         kernel,
@@ -419,38 +438,36 @@
     return lax.ppermute(value, axis, [(i, i ^ step) for i in range(count)])
 
 
-def exchange(pieces, capacity):
+def exchange_flat(flat, capacity):
     count = lax.axis_size("exp")
     rows = EXP_DEV * capacity
-    if len(pieces) == count:
-        return [pieces[0]] + [pairwise(pieces[s], "exp", s) for s in range(count - 1, 0, -1)][::-1]
-    flat = pieces[0]
     blocks = [flat[s * rows : (s + 1) * rows] for s in range(count)]
     moved = [blocks[0]] + [pairwise(blocks[s], "exp", s) for s in range(1, count)]
-    return [jnp.concatenate(moved, axis=0)]
-
-
-def exchange_apart(pieces, capacity):
-    if len(pieces) == 1:
-        return exchange(pieces, capacity)
-    return [
-        piece if s == 0 or joined(s, len(pieces)) else pairwise(piece, "exp", s)
-        for s, piece in enumerate(pieces)
-    ]
-
-
-def sum_over(value, axis):
-    step = 1
+    return jnp.concatenate(moved, axis=0)
+
+
+def exchange(pieces, capacity):
+    if lax.axis_size("exp") != len(pieces):
+        return [exchange_flat(pieces[0], capacity)]
+    return [pairwise(piece, "exp", s) if s > 0 else piece for s, piece in enumerate(pieces)]
+
+
+def doubled(value, axis, step):
+    return value + pairwise(value, axis, step)
+
+
+def sum_over(value, axis, first=1):
+    step = first
     while step < lax.axis_size(axis):
-        value = value + pairwise(value, axis, step)
+        value = doubled(value, axis, step)
         step *= 2
     return value
 
 
-def tree_sum(parts):
-    while len(parts) > 1:
-        parts = [parts[i] + parts[i + 1] for i in range(0, len(parts), 2)]
-    return parts[0]
+def widened(act, value, axis, step):
+    rows = value.shape[0]
+    wide = jnp.pad(value, ((0, WIDE_LINES - rows), (0, 0)))
+    return act(wide, axis, step)[:rows]
 
 
 def shaped(shape, dtype):
@@ -517,11 +534,7 @@
         ],
     )
     all_keys[0], all_values[0] = own_keys, own_values
-    apart = [s for s in range(1, piece_count) if not joined(s, piece_count)]
-    near = [s for s in range(1, piece_count) if joined(s, piece_count)]
-    arrived_grad = exchange(send_grad, capacity) if piece_count == 1 else list(send_grad)
-    for s in apart:
-        arrived_grad[s] = pairwise(send_grad[s], "exp", s)
+    arrived_grad = exchange(send_grad, capacity)
 
     hidden, *send_x = run(
         functools.partial(attention_kernel, ctx_count),
@@ -530,15 +543,7 @@
         placed(VMEM, [token_shape] + piece_shapes),
         attn_flops + place_flops,
     )
-    arrived_x = exchange(send_x, capacity) if piece_count == 1 else list(send_x)
-    for s in apart:
-        arrived_x[s] = pairwise(send_x[s], "exp", s)
-    if near:
-        after, _ = lax.optimization_barrier(([send_grad[s] for s in near], send_x[0]))
-        for s, piece in zip(near, after):
-            arrived_grad[s] = pairwise(piece, "exp", s)
-        for s in near:
-            arrived_x[s] = pairwise(send_x[s], "exp", s)
+    arrived_x = exchange(send_x, capacity)
 
     d_act, probs, down_near, gate_near, place, weight_wide = run(
         functools.partial(probs_kernel, ctx_count, capacity, piece_count),
@@ -576,10 +581,9 @@
     )
     send_dn, send_y = split_parts(sent, piece_count)
     dn = exchange(send_dn, capacity)
-    y = [
-        dn[s] if joined(s, piece_count) else moved
-        for s, moved in enumerate(exchange_apart(send_y, capacity))
-    ]
+    far = [s for s in range(1, piece_count) if not joined(s, piece_count)]
+    y = list(dn) if piece_count > 1 else [exchange_flat(send_y[0], capacity)]
+    y[0] = send_y[0] if piece_count > 1 else y[0]
     (terms,) = run(
         functools.partial(gain_kernel, piece_count, rows),
         "gain_terms",
@@ -587,53 +591,65 @@
         placed(VMEM, [shaped((GAIN_LINES, LANES), F32)]),
         2 * slots * D,
     )
-    terms, place_back = lax.optimization_barrier((sum_over(terms, "dp"), place))
-
-    if piece_count == 1:
-        terms = sum_over(terms, "exp")
-    else:
-        terms = tree_sum([terms] + [pairwise(terms, "exp", s) for s in range(1, exp_count)])
-
-    d_hidden, d_queries, kv_own, *kv_send = run(
-        functools.partial(backward_kernel, ctx_count, piece_count, rows),
-        "residual_attention_backward",
-        placed(VMEM, [place_back, gain, hidden, grad_rows, query_rows, probs])
-        + placed(VMEM, dn + all_keys + all_values),
-        placed(HBM, [token_shape] * 2)
+    terms = sum_over(sum_over(terms, "dp"), "ctx")
+    send_far, terms, dn = lax.optimization_barrier(([send_y[s] for s in far], terms, dn))
+    for s, piece in zip(far, send_far):
+        y[s] = pairwise(piece, "exp", s)
+    terms = doubled(terms, "exp", 1)
+
+    half_shape = shaped((tokens, D // 2), BF16)
+    own_shape = shaped((tokens, 2 * HEAD_SIZE), F32)
+    d_hidden, dq_first, rest, own_first, *shared_first = run(
+        functools.partial(first_back_kernel, ctx_count, piece_count, rows),
+        "residual_and_first_group",
+        placed(VMEM, [place, gain, hidden, grad_rows, query_rows, probs])
+        + placed(VMEM, all_keys + all_values + dn),
+        placed(HBM, [token_shape])
         + placed(
             VMEM,
-            [shaped((tokens, kv_width), F32)]
-            + [shaped((tokens, kv_width), BF16)] * (ctx_count - 1),
+            [half_shape, half_shape, own_shape]
+            + [shaped((tokens, 2 * HEAD_SIZE), BF16)] * (ctx_count - 1),
         ),
-        attn_flops + place_flops,
+        A_COST,
         scratch=[
             pltpu.VMEM((tokens, D), BF16),
-            pltpu.VMEM((tokens, D), BF16),
             pltpu.VMEM((tokens, D), F32),
-            pltpu.SemaphoreType.DMA((1 + KEY_VALUE_HEADS,)),
+            pltpu.SemaphoreType.DMA(()),
         ],
     )
-    terms, kv_own = lax.optimization_barrier((terms, kv_own))
-    terms = sum_over(terms, "ctx")
-    kv_arrived = [pairwise(part, "ctx", s) for s, part in enumerate(kv_send, 1)]
+    arrived_far, terms, rest = lax.optimization_barrier(([y[s] for s in far], terms, rest))
+    for s, piece in zip(far, arrived_far):
+        y[s] = piece
+    terms = widened(doubled, terms, "exp", 2)
+    dq_second, own_second, *shared = run(
+        functools.partial(second_back_kernel, ctx_count),
+        "second_group",
+        placed(VMEM, [query_rows, probs, rest] + all_keys + all_values + shared_first),
+        placed(VMEM, [half_shape, own_shape])
+        + placed(VMEM, [shaped((tokens, kv_width), BF16)] * (ctx_count - 1)),
+        B_COST,
+    )
+    terms = sum_over(terms, "exp", first=4)
+    kv_arrived = [pairwise(part, "ctx", s) for s, part in enumerate(shared, 1)]
 
     kv_shape = shaped((tokens, kv_width // 2), BF16)
-    final_shapes = [token_shape, kv_shape, kv_shape]
+    final_shapes = [token_shape, token_shape, kv_shape, kv_shape]
     final_shapes += [shaped((1, tokens), F32), shaped((GAIN_LINES, LANES), F32)]
     total_tokens = tokens * ctx_count * exp_count * lax.axis_size("dp")
-    layer_out, d_keys, d_values, d_weight, d_gain = run(
+    layer_out, d_queries, d_keys, d_values, d_weight, d_gain = run(
         functools.partial(output_kernel, ctx_count, piece_count, rows, total_tokens),
         "layer_output",
         placed(
             VMEM,
-            [place, weight_wide, terms, hidden, grad_rows, kv_own]
+            [place, weight_wide, terms, hidden, grad_rows, own_first, own_second]
+            + [dq_first, dq_second]
             + kv_arrived
             + y,
         ),
         placed(HBM, final_shapes),
         place_flops,
-        scratch=[pltpu.VMEM(x.shape, x.dtype) for x in final_shapes]
-        + [pltpu.SemaphoreType.DMA((4 + D // COLS,))],
+        scratch=[pltpu.VMEM(x.shape, x.dtype) for x in final_shapes[:1] + final_shapes[2:]]
+        + [pltpu.SemaphoreType.DMA((4 + KEY_VALUE_HEADS + D // COLS,))],
     )
     return (
         layer_out[None],

time: 55 us -> 56.7 us (1.031)
  waiting for transfers between devices: 16.5 us -> 19 us
    ppermute x19 -> x18, waiting for transfers between devices: 16.5 us -> 19 us  [pairwise(): return lax.ppermute(value, axis, [(i, i ^ step) for i in range(count)])]
    ppermute x19 -> x18, starting transfers between devices: 22.5 us -> 22 us  [pairwise(): return lax.ppermute(value, axis, [(i, i ^ step) for i in range(count)])]
    pallas_call x7 -> x8, Pallas kernels: 15.1 us -> 14.7 us  [run(): pl.pallas_call(kernel, out_shape=[x for _, x in outputs], in_specs=[spec[...]
  transfers between devices with their start and end apart: 19 -> 18, of which waited for: 10 -> 9; matrix products, arithmetic and copies ran while one was open for 0% -> 0% of each run, Pallas kernels for 17% -> 16%
where the time goes in v10:
time: 56.7 us; the launch traced here: 56.5 us
  starting transfers between devices  22 us (39%)
  waiting for transfers between devices  19 us (34%)
  Pallas kernels  14.7 us (26%)
  between operations  0.73 us (1%)
    ppermute x18, starting transfers between devices, pairwise(): return lax.ppermute(value, axis, [(i, i ^ step) for i in range(count)])  22 us
    ppermute x18, waiting for transfers between devices, pairwise(): return lax.ppermute(value, axis, [(i, i ^ step) for i in range(count)])  19 us
    pallas_call x8, Pallas kernels, run(): pl.pallas_call(kernel, out_shape=[x for _, x in outputs], in_specs=[spec[...  14.7 us
  transfers between devices with their start and end apart: 18, of which 9 were waited for; matrix products, arithmetic and copies ran while one was open for 0% of the time, Pallas kernels for 16%

profile of v10, /device:TPU:0, one launch (start us, length us, event | category | flops | bytes accessed | tf_op | source)
XLA Modules:
  0.0 56.5 jit_solution(16218176959830639152)
XLA Ops:
  0.6 1.5 %dispatch_grads.1 = (bf16[128,2048]{1,0:T(8,128)(2,1)S(1)}, bf16[128,256]{1,0:T(8,128)(2,1)S(1)}, bf16[128,256]{1,0:T(8,128)(2,1)S(1)}, f32[1,2048]{1,0:T(1,128)...) custom-call(bf16[128,2048]{1,0:T(8,128)(2,1)} %bitcast.13, ...), custom_call_target="tpu_custom_call" | custom-call | flops 100663296 | bytes 4213824 | tf_op jit(solution)/shard_map/dispatch_grads/pallas_call | solution.py:419
  2.2 3.0 %collective-permute-start.1 = (bf16[48,2048]{1,0:T(8,128)(2,1)S(1)}, bf16[48,2048]{1,0:T(8,128)(2,1)S(1)}, u32[]{:S(2)}, u32[]{:S(2)}) collective-permute-start(bf16[48,2048]{1,0:T(8,128)(2,1)S(1)} %get-tuple-element.66), channel_id=1, source_target_pairs={{0,4},{4,0},{8,12},{12,8},{1,5},{5,1},{9,13},{13,9},{2,6},{6,2},{1... | collective-permute-start | bytes 589832 | tf_op jit(solution)/shard_map/ppermute | solution.py:438
  5.2 0.5 collective-permute-start.4
  5.7 1.5 %collective-permute-start.2 = (bf16[48,2048]{1,0:T(8,128)(2,1)S(1)}, bf16[48,2048]{1,0:T(8,128)(2,1)S(1)}, u32[]{:S(2)}, u32[]{:S(2)}) collective-permute-start(bf16[48,2048]{1,0:T(8,128)(2,1)S(1)} %get-tuple-element.67), channel_id=1, source_target_pairs={{0,8},{4,12},{8,0},{12,4},{1,9},{5,13},{9,1},{13,5},{2,10},{6,14},... | collective-permute-start | bytes 589832 | tf_op jit(solution)/shard_map/ppermute | solution.py:438
  7.2 1.4 %attention_forward.1 = (bf16[128,2048]{1,0:T(8,128)(2,1)S(1)}, bf16[48,2048]{1,0:T(8,128)(2,1)S(1)}, bf16[48,2048]{1,0:T(8,128)(2,1)S(1)}, bf16[48,2048]{1,0:T(8,128)(2,1)S(1)}, bf16[48,2048]{1,0:T(8,128)(2,1)S(1)}) custom-call(s32[2,128]{1,0:T(2,128)S(1)} %get-tuple-element.60.pos_ref, s32[1,128]{1,0:T(1,128)S(1)} %get-tuple-element.61.slot_ref, ...), custom_call_target="tpu_custom_call" | custom-call | flops 369098752 | bytes 2631168 | tf_op jit(solution)/shard_map/attention_forward/pallas_call | solution.py:419
  8.7 2.0 %collective-permute-start.5 = (bf16[48,2048]{1,0:T(8,128)(2,1)S(1)}, bf16[48,2048]{1,0:T(8,128)(2,1)S(1)}, u32[]{:S(2)}, u32[]{:S(2)}) collective-permute-start(bf16[48,2048]{1,0:T(8,128)(2,1)S(1)} %get-tuple-element.78), channel_id=1, source_target_pairs={{0,4},{4,0},{8,12},{12,8},{1,5},{5,1},{9,13},{13,9},{2,6},{6,2},{1... | collective-permute-start | bytes 589832 | tf_op jit(solution)/shard_map/ppermute | solution.py:438
  10.7 1.5 %collective-permute-start.6 = (bf16[48,2048]{1,0:T(8,128)(2,1)S(1)}, bf16[48,2048]{1,0:T(8,128)(2,1)S(1)}, u32[]{:S(2)}, u32[]{:S(2)}) collective-permute-start(bf16[48,2048]{1,0:T(8,128)(2,1)S(1)} %get-tuple-element.79), channel_id=1, source_target_pairs={{0,8},{4,12},{8,0},{12,4},{1,9},{5,13},{9,1},{13,5},{2,10},{6,14},... | collective-permute-start | bytes 589832 | tf_op jit(solution)/shard_map/ppermute | solution.py:438
  12.2 1.7 %collective-permute-start.7 = (bf16[48,2048]{1,0:T(8,128)(2,1)S(1)}, bf16[48,2048]{1,0:T(8,128)(2,1)S(1)}, u32[]{:S(2)}, u32[]{:S(2)}) collective-permute-start(bf16[48,2048]{1,0:T(8,128)(2,1)S(1)} %get-tuple-element.80), channel_id=1, source_target_pairs={{0,12},{4,8},{8,4},{12,0},{1,13},{5,9},{9,5},{13,1},{2,14},{6,10},... | collective-permute-start | bytes 589832 | tf_op jit(solution)/shard_map/ppermute | solution.py:438
  13.9 3.7 %collective-permute-done.2.refs_4_ = bf16[48,2048]{1,0:T(8,128)(2,1)S(1)} collective-permute-done((bf16[48,2048]{1,0:T(8,128)(2,1)S(1)}, bf16[48,2048]{1,0:T(8,128)(2,1)S(1)}, u32[]{:S(2)}, u32[]{:S(2)}) %collective-permute-start.2) | collective-permute-done | bytes 196640 | tf_op jit(solution)/shard_map/ppermute | solution.py:438
  17.7 3.8 %act_grads_and_probs.1 = (f32[192,384]{1,0:T(8,128)S(1)}, f32[8,256,256]{2,1,0:T(8,128)S(1)}, bf16[768,2048]{1,0:T(8,128)(2,1)S(1)}, bf16[2048,768]{1,0:T(8,128)...) custom-call(s32[2,128]{1,0:T(2,128)S(1)} %get-tuple-element.60.pos_ref, ...), custom_call_target="tpu_custom_call" | custom-call | flops 738197504 | bytes 16599040 | tf_op jit(solution)/shard_map/act_grads_and_probs/pallas_call | solution.py:419
  21.5 3.6 %collective-permute-done.6.refs_2_ = bf16[48,2048]{1,0:T(8,128)(2,1)S(1)} collective-permute-done((bf16[48,2048]{1,0:T(8,128)(2,1)S(1)}, bf16[48,2048]{1,0:T(8,128)(2,1)S(1)}, u32[]{:S(2)}, u32[]{:S(2)}) %collective-permute-start.6) | collective-permute-done | bytes 196640 | tf_op jit(solution)/shard_map/ppermute | solution.py:438
  25.1 2.8 %experts.1 = (bf16[48,2048]{1,0:T(8,128)(2,1)S(1)}, bf16[48,2048]{1,0:T(8,128)(2,1)S(1)}, bf16[96,2048]{1,0:T(8,128)(2,1)S(1)}, bf16[96,2048]{1,0:T(8,128)(2,1)S...) custom-call(bf16[2048,768]{1,0:T(8,128)(2,1)S(1)} %get-tuple-element.71.gate_ref, ...), custom_call_target="tpu_custom_call" | custom-call | flops 1811939328 | bytes 8945664 | tf_op jit(solution)/shard_map/experts/pallas_call | solution.py:419
  28.0 0.4 collective-permute-start.11
  28.4 1.7 %collective-permute-start.12 = (bf16[96,2048]{1,0:T(8,128)(2,1)S(1)}, bf16[96,2048]{1,0:T(8,128)(2,1)S(1)}, u32[]{:S(2)}, u32[]{:S(2)}) collective-permute-start(bf16[96,2048]{1,0:T(8,128)(2,1)S(1)} %get-tuple-element.84.refs_6_), channel_id=1, source_target_pairs={{0,8},{4,12},{8,0},{12,4},{1,9},{5,13},{9,1},{13,5},{2,10},{6,14},... | collective-permute-start | bytes 1179656 | tf_op jit(solution)/shard_map/ppermute | solution.py:438
  30.1 1.4 %collective-permute-start.13 = (bf16[48,2048]{1,0:T(8,128)(2,1)S(1)}, bf16[48,2048]{1,0:T(8,128)(2,1)S(1)}, u32[]{:S(2)}, u32[]{:S(2)}) collective-permute-start(bf16[48,2048]{1,0:T(8,128)(2,1)S(1)} %get-tuple-element.85.refs_7_), channel_id=1, source_target_pairs={{0,12},{4,8},{8,4},{12,0},{1,13},{5,9},{9,5},{13,1},{2,14},{6,10},... | collective-permute-start | bytes 589832 | tf_op jit(solution)/shard_map/ppermute | solution.py:438
  31.5 0.3 gain_terms.1
  31.8 1.6 %collective-permute-start.8 = (f32[16,128]{1,0:T(8,128)S(1)}, f32[16,128]{1,0:T(8,128)S(1)}, u32[]{:S(2)}, u32[]{:S(2)}) collective-permute-start(f32[16,128]{1,0:T(8,128)S(1)} %gain_terms.1), channel_id=1, source_target_pairs={{0,1},{1,0},{2,3},{3,2},{4,5},{5,4},{6,7},{7,6},{8,9},{9,8},{10,11... | collective-permute-start | bytes 24584 | tf_op jit(solution)/shard_map/ppermute | solution.py:438
  33.5 2.1 %collective-permute-done.8 = f32[16,128]{1,0:T(8,128)S(1)} collective-permute-done((f32[16,128]{1,0:T(8,128)S(1)}, f32[16,128]{1,0:T(8,128)S(1)}, u32[]{:S(2)}, u32[]{:S(2)}) %collective-permute-start.8) | collective-permute-done | bytes 8224 | tf_op jit(solution)/shard_map/ppermute | solution.py:438
  35.6 2.6 %collective-permute-start.9 = (f32[16,128]{1,0:T(8,128)S(1)}, f32[16,128]{1,0:T(8,128)S(1)}, u32[]{:S(2)}, u32[]{:S(2)}) collective-permute-start(f32[16,128]{1,0:T(8,128)S(1)} %add.17), channel_id=1, source_target_pairs={{0,2},{1,3},{2,0},{3,1},{4,6},{5,7},{6,4},{7,5},{8,10},{9,11},{10,... | collective-permute-start | bytes 24584 | tf_op jit(solution)/shard_map/ppermute | solution.py:438
  38.2 1.9 %collective-permute-done.9 = f32[16,128]{1,0:T(8,128)S(1)} collective-permute-done((f32[16,128]{1,0:T(8,128)S(1)}, f32[16,128]{1,0:T(8,128)S(1)}, u32[]{:S(2)}, u32[]{:S(2)}) %collective-permute-start.9) | collective-permute-done | bytes 8224 | tf_op jit(solution)/shard_map/ppermute | solution.py:438
  40.1 1.2 %collective-permute-done.10 = f32[16,128]{1,0:T(8,128)S(1)} collective-permute-done((f32[16,128]{1,0:T(8,128)S(1)}, f32[16,128]{1,0:T(8,128)S(1)}, u32[]{:S(2)}, u32[]{:S(2)}) %collective-permute-start.10) | collective-permute-done | bytes 8224 | tf_op jit(solution)/shard_map/ppermute | solution.py:438
  41.3 2.1 %collective-permute-done.13.refs_7_ = bf16[48,2048]{1,0:T(8,128)(2,1)S(1)} collective-permute-done((bf16[48,2048]{1,0:T(8,128)(2,1)S(1)}, bf16[48,2048]{1,0:T(8,128)(2,1)S(1)}, u32[]{:S(2)}, u32[]{:S(2)}) %collective-permute-start.13) | collective-permute-done | bytes 196640 | tf_op jit(solution)/shard_map/ppermute | solution.py:438
  43.4 0.8 %collective-permute-start.15 = (f32[16,128]{1,0:T(8,128)S(1)}, f32[16,128]{1,0:T(8,128)S(1)}, u32[]{:S(2)}, u32[]{:S(2)}) collective-permute-start(f32[16,128]{1,0:T(8,128)S(1)} %add.19), channel_id=1, source_target_pairs={{0,4},{4,0},{8,12},{12,8},{1,5},{5,1},{9,13},{13,9},{2,6},{6,2},{1... | collective-permute-start | bytes 24584 | tf_op jit(solution)/shard_map/ppermute | solution.py:438
  44.2 1.5 %collective-permute-start.14 = (bf16[48,2048]{1,0:T(8,128)(2,1)S(1)}, bf16[48,2048]{1,0:T(8,128)(2,1)S(1)}, u32[]{:S(2)}, u32[]{:S(2)}) collective-permute-start(bf16[48,2048]{1,0:T(8,128)(2,1)S(1)} %get-tuple-element.86), channel_id=1, source_target_pairs={{0,12},{4,8},{8,4},{12,0},{1,13},{5,9},{9,5},{13,1},{2,14},{6,10},... | collective-permute-start | bytes 589832 | tf_op jit(solution)/shard_map/ppermute | solution.py:438
  45.7 2.1 %residual_and_first_group.1 = (bf16[128,2048]{1,0:T(8,128)(2,1)}, bf16[128,1024]{1,0:T(8,128)(2,1)S(1)}, bf16[128,1024]{1,0:T(8,128)(2,1)S(1)}, f32[128,256]{1,0:T(8,128)S(1)}, bf16[128,256]{1,0:T(8,128)(2,1)S(1)}) custom-call(bf16[128,192]{1,0:T(8,128)(2,1)S(1)} %get-tuple-element.69.place_ref, f32[1,2048]{1,0:T(1,128)S(1)} %get-tuple-element.74.gain_ref, ...), custom_call_target="tpu_custom_call" | custom-call | flops 4000000000 | bytes 6414336 | tf_op jit(solution)/shard_map/residual_and_first_group/pallas_call | solution.py:419
  47.8 3.0 %collective-permute-done.14.refs_8_ = bf16[48,2048]{1,0:T(8,128)(2,1)S(1)} collective-permute-done((bf16[48,2048]{1,0:T(8,128)(2,1)S(1)}, bf16[48,2048]{1,0:T(8,128)(2,1)S(1)}, u32[]{:S(2)}, u32[]{:S(2)}) %collective-permute-start.14) | collective-permute-done | bytes 196640 | tf_op jit(solution)/shard_map/ppermute | solution.py:438
  50.8 1.5 %collective-permute-start.16 = (f32[32,128]{1,0:T(8,128)S(1)}, f32[32,128]{1,0:T(8,128)S(1)}, u32[]{:S(2)}, u32[]{:S(2)}) collective-permute-start(f32[32,128]{1,0:T(8,128)S(1)} %pad.4), channel_id=1, source_target_pairs={{0,8},{4,12},{8,0},{12,4},{1,9},{5,13},{9,1},{13,5},{2,10},{6,14},... | collective-permute-start | bytes 49160 | tf_op jit(solution)/shard_map/ppermute | solution.py:438
  52.4 1.5 %second_group.1 = (bf16[128,1024]{1,0:T(8,128)(2,1)S(1)}, f32[128,256]{1,0:T(8,128)S(1)}, bf16[128,512]{1,0:T(8,128)(2,1)S(1)}) custom-call(bf16[128,2048]{1,0:T(8,128)(2,1)S(1)} %get-tuple-element.63.query_ref, f32[8,256,256]{2,1,0:T(8,128)S(1)} %get-tuple-element.90.probs_ref, bf16[128,1024]{1,0:T(8,128)(2,1)S(1)} %get-tuple-element.98.rest_ref, ...), custom_call_target="tpu_custom_call" | custom-call | tf_op jit(solution)/shard_map/second_group/pallas_call | solution.py:419
  53.9 0.1 collective-permute-start.17
  53.9 0.6 %collective-permute-done.16 = f32[32,128]{1,0:T(8,128)S(1)} collective-permute-done((f32[32,128]{1,0:T(8,128)S(1)}, f32[32,128]{1,0:T(8,128)S(1)}, u32[]{:S(2)}, u32[]{:S(2)}) %collective-permute-start.16) | collective-permute-done | bytes 16416 | tf_op jit(solution)/shard_map/ppermute | solution.py:438
  54.6 0.7 %collective-permute-done.17.refs_4_ = bf16[128,512]{1,0:T(8,128)(2,1)S(1)} collective-permute-done((bf16[128,512]{1,0:T(8,128)(2,1)S(1)}, bf16[128,512]{1,0:T(8,128)(2,1)S(1)}, u32[]{:S(2)}, u32[]{:S(2)}) %collective-permute-start.17) | collective-permute-done | bytes 131104 | tf_op jit(solution)/shard_map/ppermute | solution.py:438
  55.3 1.2 %layer_output.1 = (bf16[128,2048]{1,0:T(8,128)(2,1)}, bf16[128,2048]{1,0:T(8,128)(2,1)}, bf16[128,256]{1,0:T(8,128)(2,1)}, bf16[128,256]{1,0:T(8,128)(2,1)}, f32[1,128]{1,0:T(1,128)}, /*index=5*/f32[16,128]{1,0:T(8,128)}) custom-call(bf16[128,192]{1,0:T(8,128)(2,1)S(1)} %get-tuple-element.69.place_ref, f32[128,256]{1,0:T(8,128)S(1)} %get-tuple-element.70.weight_ref, ...), custom_call_target="tpu_custom_call" | custom-call | flops 100663296 | bytes 4522496 | tf_op jit(solution)/shard_map/layer_output/pallas_call | solution.py:419
  (18 shorter events, 0.1 us)
Async XLA Ops:
  2.2 10.0 %collective-permute-start.1 = (bf16[48,2048]{1,0:T(8,128)(2,1)S(1)}, bf16[48,2048]{1,0:T(8,128)(2,1)S(1)}, u32[]{:S(2)}, u32[]{:S(2)}) collective-permute-start(bf16[48,2048]{1,0:T(8,128)(2,1)S(1)} %get-tuple-element.66), channel_id=1, source_target_pairs={{0,4},{4,0},{8,12},{12,8},{1,5},{5,1},{9,13},{13,9},{2,6},{6,2},{1... | collective-permute-start | bytes 589832 | tf_op jit(solution)/shard_map/ppermute | solution.py:438
  5.2 2.1 %collective-permute-start = (bf16[128,256]{1,0:T(8,128)(2,1)}, bf16[128,256]{1,0:T(8,128)(2,1)S(1)}, u32[]{:S(2)}, u32[]{:S(2)}) collective-permute-start(bf16[128,256]{1,0:T(8,128)(2,1)} %bitcast.17), channel_id=1, source_target_pairs={{0,16},{16,0},{1,17},{17,1},{2,18},{18,2},{3,19},{19,3},{4,20},{20... | collective-permute-start | bytes 196616 | tf_op jit(solution)/shard_map/ppermute | solution.py:438
  5.2 2.1 %collective-permute-start.4 = (bf16[128,256]{1,0:T(8,128)(2,1)}, bf16[128,256]{1,0:T(8,128)(2,1)S(1)}, u32[]{:S(2)}, u32[]{:S(2)}) collective-permute-start(bf16[128,256]{1,0:T(8,128)(2,1)} %bitcast.19), channel_id=1, source_target_pairs={{0,16},{16,0},{1,17},{17,1},{2,18},{18,2},{3,19},{19,3},{4,20},{20... | collective-permute-start | bytes 196616 | tf_op jit(solution)/shard_map/ppermute | solution.py:438
  5.7 12.0 %collective-permute-start.2 = (bf16[48,2048]{1,0:T(8,128)(2,1)S(1)}, bf16[48,2048]{1,0:T(8,128)(2,1)S(1)}, u32[]{:S(2)}, u32[]{:S(2)}) collective-permute-start(bf16[48,2048]{1,0:T(8,128)(2,1)S(1)} %get-tuple-element.67), channel_id=1, source_target_pairs={{0,8},{4,12},{8,0},{12,4},{1,9},{5,13},{9,1},{13,5},{2,10},{6,14},... | collective-permute-start | bytes 589832 | tf_op jit(solution)/shard_map/ppermute | solution.py:438
  7.2 10.5 %collective-permute-start.3 = (bf16[48,2048]{1,0:T(8,128)(2,1)S(1)}, bf16[48,2048]{1,0:T(8,128)(2,1)S(1)}, u32[]{:S(2)}, u32[]{:S(2)}) collective-permute-start(bf16[48,2048]{1,0:T(8,128)(2,1)S(1)} %get-tuple-element.68), channel_id=1, source_target_pairs={{0,12},{4,8},{8,4},{12,0},{1,13},{5,9},{9,5},{13,1},{2,14},{6,10},... | collective-permute-start | bytes 589832 | tf_op jit(solution)/shard_map/ppermute | solution.py:438
  8.7 12.8 %collective-permute-start.5 = (bf16[48,2048]{1,0:T(8,128)(2,1)S(1)}, bf16[48,2048]{1,0:T(8,128)(2,1)S(1)}, u32[]{:S(2)}, u32[]{:S(2)}) collective-permute-start(bf16[48,2048]{1,0:T(8,128)(2,1)S(1)} %get-tuple-element.78), channel_id=1, source_target_pairs={{0,4},{4,0},{8,12},{12,8},{1,5},{5,1},{9,13},{13,9},{2,6},{6,2},{1... | collective-permute-start | bytes 589832 | tf_op jit(solution)/shard_map/ppermute | solution.py:438
  10.7 14.5 %collective-permute-start.6 = (bf16[48,2048]{1,0:T(8,128)(2,1)S(1)}, bf16[48,2048]{1,0:T(8,128)(2,1)S(1)}, u32[]{:S(2)}, u32[]{:S(2)}) collective-permute-start(bf16[48,2048]{1,0:T(8,128)(2,1)S(1)} %get-tuple-element.79), channel_id=1, source_target_pairs={{0,8},{4,12},{8,0},{12,4},{1,9},{5,13},{9,1},{13,5},{2,10},{6,14},... | collective-permute-start | bytes 589832 | tf_op jit(solution)/shard_map/ppermute | solution.py:438
  12.2 12.9 %collective-permute-start.7 = (bf16[48,2048]{1,0:T(8,128)(2,1)S(1)}, bf16[48,2048]{1,0:T(8,128)(2,1)S(1)}, u32[]{:S(2)}, u32[]{:S(2)}) collective-permute-start(bf16[48,2048]{1,0:T(8,128)(2,1)S(1)} %get-tuple-element.80), channel_id=1, source_target_pairs={{0,12},{4,8},{8,4},{12,0},{1,13},{5,9},{9,5},{13,1},{2,14},{6,10},... | collective-permute-start | bytes 589832 | tf_op jit(solution)/shard_map/ppermute | solution.py:438
  28.0 15.4 %collective-permute-start.11 = (bf16[96,2048]{1,0:T(8,128)(2,1)S(1)}, bf16[96,2048]{1,0:T(8,128)(2,1)S(1)}, u32[]{:S(2)}, u32[]{:S(2)}) collective-permute-start(bf16[96,2048]{1,0:T(8,128)(2,1)S(1)} %get-tuple-element.83.refs_5_), channel_id=1, source_target_pairs={{0,4},{4,0},{8,12},{12,8},{1,5},{5,1},{9,13},{13,9},{2,6},{6,2},{1... | collective-permute-start | bytes 1179656 | tf_op jit(solution)/shard_map/ppermute | solution.py:438
  28.4 15.0 %collective-permute-start.12 = (bf16[96,2048]{1,0:T(8,128)(2,1)S(1)}, bf16[96,2048]{1,0:T(8,128)(2,1)S(1)}, u32[]{:S(2)}, u32[]{:S(2)}) collective-permute-start(bf16[96,2048]{1,0:T(8,128)(2,1)S(1)} %get-tuple-element.84.refs_6_), channel_id=1, source_target_pairs={{0,8},{4,12},{8,0},{12,4},{1,9},{5,13},{9,1},{13,5},{2,10},{6,14},... | collective-permute-start | bytes 1179656 | tf_op jit(solution)/shard_map/ppermute | solution.py:438
  30.1 13.3 %collective-permute-start.13 = (bf16[48,2048]{1,0:T(8,128)(2,1)S(1)}, bf16[48,2048]{1,0:T(8,128)(2,1)S(1)}, u32[]{:S(2)}, u32[]{:S(2)}) collective-permute-start(bf16[48,2048]{1,0:T(8,128)(2,1)S(1)} %get-tuple-element.85.refs_7_), channel_id=1, source_target_pairs={{0,12},{4,8},{8,4},{12,0},{1,13},{5,9},{9,5},{13,1},{2,14},{6,10},... | collective-permute-start | bytes 589832 | tf_op jit(solution)/shard_map/ppermute | solution.py:438
  31.8 3.7 %collective-permute-start.8 = (f32[16,128]{1,0:T(8,128)S(1)}, f32[16,128]{1,0:T(8,128)S(1)}, u32[]{:S(2)}, u32[]{:S(2)}) collective-permute-start(f32[16,128]{1,0:T(8,128)S(1)} %gain_terms.1), channel_id=1, source_target_pairs={{0,1},{1,0},{2,3},{3,2},{4,5},{5,4},{6,7},{7,6},{8,9},{9,8},{10,11... | collective-permute-start | bytes 24584 | tf_op jit(solution)/shard_map/ppermute | solution.py:438
  35.6 4.5 %collective-permute-start.9 = (f32[16,128]{1,0:T(8,128)S(1)}, f32[16,128]{1,0:T(8,128)S(1)}, u32[]{:S(2)}, u32[]{:S(2)}) collective-permute-start(f32[16,128]{1,0:T(8,128)S(1)} %add.17), channel_id=1, source_target_pairs={{0,2},{1,3},{2,0},{3,1},{4,6},{5,7},{6,4},{7,5},{8,10},{9,11},{10,... | collective-permute-start | bytes 24584 | tf_op jit(solution)/shard_map/ppermute | solution.py:438
  40.1 1.2 %collective-permute-start.10 = (f32[16,128]{1,0:T(8,128)S(1)}, f32[16,128]{1,0:T(8,128)S(1)}, u32[]{:S(2)}, u32[]{:S(2)}) collective-permute-start(f32[16,128]{1,0:T(8,128)S(1)} %add.18), channel_id=1, source_target_pairs={{0,16},{16,0},{1,17},{17,1},{2,18},{18,2},{3,19},{19,3},{4,20},{20... | collective-permute-start | bytes 24584 | tf_op jit(solution)/shard_map/ppermute | solution.py:438
  43.4 4.4 %collective-permute-start.15 = (f32[16,128]{1,0:T(8,128)S(1)}, f32[16,128]{1,0:T(8,128)S(1)}, u32[]{:S(2)}, u32[]{:S(2)}) collective-permute-start(f32[16,128]{1,0:T(8,128)S(1)} %add.19), channel_id=1, source_target_pairs={{0,4},{4,0},{8,12},{12,8},{1,5},{5,1},{9,13},{13,9},{2,6},{6,2},{1... | collective-permute-start | bytes 24584 | tf_op jit(solution)/shard_map/ppermute | solution.py:438
  44.2 6.7 %collective-permute-start.14 = (bf16[48,2048]{1,0:T(8,128)(2,1)S(1)}, bf16[48,2048]{1,0:T(8,128)(2,1)S(1)}, u32[]{:S(2)}, u32[]{:S(2)}) collective-permute-start(bf16[48,2048]{1,0:T(8,128)(2,1)S(1)} %get-tuple-element.86), channel_id=1, source_target_pairs={{0,12},{4,8},{8,4},{12,0},{1,13},{5,9},{9,5},{13,1},{2,14},{6,10},... | collective-permute-start | bytes 589832 | tf_op jit(solution)/shard_map/ppermute | solution.py:438
  50.8 3.7 %collective-permute-start.16 = (f32[32,128]{1,0:T(8,128)S(1)}, f32[32,128]{1,0:T(8,128)S(1)}, u32[]{:S(2)}, u32[]{:S(2)}) collective-permute-start(f32[32,128]{1,0:T(8,128)S(1)} %pad.4), channel_id=1, source_target_pairs={{0,8},{4,12},{8,0},{12,4},{1,9},{5,13},{9,1},{13,5},{2,10},{6,14},... | collective-permute-start | bytes 49160 | tf_op jit(solution)/shard_map/ppermute | solution.py:438
  53.9 1.4 %collective-permute-start.17 = (bf16[128,512]{1,0:T(8,128)(2,1)S(1)}, bf16[128,512]{1,0:T(8,128)(2,1)S(1)}, u32[]{:S(2)}, u32[]{:S(2)}) collective-permute-start(bf16[128,512]{1,0:T(8,128)(2,1)S(1)} %get-tuple-element.103), channel_id=1, source_target_pairs={{0,16},{16,0},{1,17},{17,1},{2,18},{18,2},{3,19},{19,3},{4,20},{20... | collective-permute-start | bytes 393224 | tf_op jit(solution)/shard_map/ppermute | solution.py:438

commit v11 on v5

--- a/solution.py
+++ b/solution.py
@@ -293,9 +293,9 @@
     dn_refs = part_views(refs[:pieces], rows, 0)
     key_refs = refs[pieces : pieces + count]
     value_refs = refs[pieces + count : pieces + 2 * count]
-    resid_hbm, dq_hbm, own_ref = refs[pieces + 2 * count : pieces + 2 * count + 3]
-    other_refs = refs[pieces + 2 * count + 3 : -4]
-    resid_ref, dq_ref, dn_scratch, sems = refs[-4:]
+    resid_hbm, dq_ref, own_ref = refs[pieces + 2 * count : pieces + 2 * count + 3]
+    other_refs = refs[pieces + 2 * count + 3 : -3]
+    resid_ref, dn_scratch, sem = refs[-3:]
     tokens = hidden_ref.shape[0]
     place = place_ref[...]
     square = jnp.zeros((tokens, COLS), F32)
@@ -315,10 +315,9 @@
             + dn_scratch[:, cols] * inv_rms
             - hidden_ref[:, cols].astype(F32) * factor
         ).astype(BF16)
-    copies = [pltpu.make_async_copy(resid_ref, resid_hbm, sems.at[0])]
-    copies[0].start()
+    resid_copy = pltpu.make_async_copy(resid_ref, resid_hbm, sem)
+    resid_copy.start()
     length = count * tokens
-    group_width = GROUP * HEAD_SIZE
     for g in range(KEY_VALUE_HEADS):
         keys, values = kv_stacks(key_refs, value_refs, g)
         keys_t = jnp.transpose(keys.astype(F32)).astype(BF16)
@@ -336,10 +335,6 @@
             d_query_t = mm(keys_t, d_scores) * SCALE
             dq_ref[:, cols_a] = jnp.transpose(d_query_t[:, :tokens]).astype(BF16)
             dq_ref[:, cols_b] = jnp.transpose(d_query_t[:, tokens:]).astype(BF16)
-        cols = slice(g * group_width, (g + 1) * group_width)
-        copy = pltpu.make_async_copy(dq_ref.at[:, cols], dq_hbm.at[:, cols], sems.at[1 + g])
-        copy.start()
-        copies.append(copy)
         k_cols = slice(g * HEAD_SIZE, (g + 1) * HEAD_SIZE)
         v_cols = slice((KEY_VALUE_HEADS + g) * HEAD_SIZE, (KEY_VALUE_HEADS + g + 1) * HEAD_SIZE)
         d_keys = d_keys * SCALE
@@ -348,18 +343,25 @@
         for s, ref in enumerate(other_refs, 1):
             ref[:, k_cols] = d_keys[s * tokens : (s + 1) * tokens].astype(BF16)
             ref[:, v_cols] = d_values[s * tokens : (s + 1) * tokens].astype(BF16)
-    for copy in copies:
-        copy.wait()
+    resid_copy.wait()
 
 
 def output_kernel(
     count, pieces, rows, tokens_in_all, place_ref, weight_ref, gain_ref, hidden_ref, grad_ref, *refs
 ):
-    own_ref, refs = refs[0], refs[1:]
+    own_ref, dq_ref, refs = refs[0], refs[1], refs[2:]
     arrived_refs = refs[: count - 1]
     y_refs = part_views(refs[count - 1 : count - 1 + pieces], rows, 1)
-    out_hbm, dk_hbm, dv_hbm, d_weight_hbm, d_gain_hbm = refs[count - 1 + pieces : -6]
+    out_hbm, dq_hbm, dk_hbm, dv_hbm, d_weight_hbm, d_gain_hbm = refs[count - 1 + pieces : -6]
     out_ref, dk_ref, dv_ref, d_weight_ref, d_gain_ref, sems = refs[-6:]
+    copies = []
+
+    def send(source, target):
+        copy = pltpu.make_async_copy(source, target, sems.at[len(copies)])
+        copy.start()
+        copies.append(copy)
+
+    send(dq_ref, dq_hbm)
     split = KEY_VALUE_HEADS * HEAD_SIZE
     d_kv = own_ref[...]
     for ref in arrived_refs:
@@ -367,13 +369,6 @@
     dk_ref[...] = d_kv[:, :split].astype(BF16)
     dv_ref[...] = d_kv[:, split:].astype(BF16)
     d_gain_ref[...] = gain_ref[...] * (1.0 / tokens_in_all)
-    copies = []
-
-    def send(source, target):
-        copy = pltpu.make_async_copy(source, target, sems.at[len(copies)])
-        copy.start()
-        copies.append(copy)
-
     send(dk_ref, dk_hbm)
     send(dv_ref, dv_hbm)
     send(d_gain_ref, d_gain_hbm)
@@ -393,9 +388,7 @@
 
 
 def run(kernel, name, inputs, outputs, flops, scratch=(), limit=20 * MIB):
-    nbytes = sum(x.size * x.dtype.itemsize for _, x in inputs) + sum(
-        x.size * x.dtype.itemsize for _, x in outputs
-    )
+    nbytes = sum(x.size * x.dtype.itemsize for _, x in inputs + outputs)
     spec = {space: pl.BlockSpec(memory_space=space) for space in (VMEM, HBM)}
     results = pl.pallas_call(
         kernel,
@@ -419,38 +412,30 @@
     return lax.ppermute(value, axis, [(i, i ^ step) for i in range(count)])
 
 
-def exchange(pieces, capacity):
+def exchange_flat(flat, capacity):
     count = lax.axis_size("exp")
     rows = EXP_DEV * capacity
-    if len(pieces) == count:
-        return [pieces[0]] + [pairwise(pieces[s], "exp", s) for s in range(count - 1, 0, -1)][::-1]
-    flat = pieces[0]
     blocks = [flat[s * rows : (s + 1) * rows] for s in range(count)]
     moved = [blocks[0]] + [pairwise(blocks[s], "exp", s) for s in range(1, count)]
-    return [jnp.concatenate(moved, axis=0)]
-
-
-def exchange_apart(pieces, capacity):
-    if len(pieces) == 1:
-        return exchange(pieces, capacity)
-    return [
-        piece if s == 0 or joined(s, len(pieces)) else pairwise(piece, "exp", s)
-        for s, piece in enumerate(pieces)
-    ]
-
-
-def sum_over(value, axis):
-    step = 1
+    return jnp.concatenate(moved, axis=0)
+
+
+def exchange(pieces, capacity):
+    if lax.axis_size("exp") != len(pieces):
+        return [exchange_flat(pieces[0], capacity)]
+    return [pairwise(piece, "exp", s) if s > 0 else piece for s, piece in enumerate(pieces)]
+
+
+def doubled(value, axis, step):
+    return value + pairwise(value, axis, step)
+
+
+def sum_over(value, axis, first=1):
+    step = first
     while step < lax.axis_size(axis):
-        value = value + pairwise(value, axis, step)
+        value = doubled(value, axis, step)
         step *= 2
     return value
-
-
-def tree_sum(parts):
-    while len(parts) > 1:
-        parts = [parts[i] + parts[i + 1] for i in range(0, len(parts), 2)]
-    return parts[0]
 
 
 def shaped(shape, dtype):
@@ -517,11 +502,7 @@
         ],
     )
     all_keys[0], all_values[0] = own_keys, own_values
-    apart = [s for s in range(1, piece_count) if not joined(s, piece_count)]
-    near = [s for s in range(1, piece_count) if joined(s, piece_count)]
-    arrived_grad = exchange(send_grad, capacity) if piece_count == 1 else list(send_grad)
-    for s in apart:
-        arrived_grad[s] = pairwise(send_grad[s], "exp", s)
+    arrived_grad = exchange(send_grad, capacity)
 
     hidden, *send_x = run(
         functools.partial(attention_kernel, ctx_count),
@@ -530,15 +511,7 @@
         placed(VMEM, [token_shape] + piece_shapes),
         attn_flops + place_flops,
     )
-    arrived_x = exchange(send_x, capacity) if piece_count == 1 else list(send_x)
-    for s in apart:
-        arrived_x[s] = pairwise(send_x[s], "exp", s)
-    if near:
-        after, _ = lax.optimization_barrier(([send_grad[s] for s in near], send_x[0]))
-        for s, piece in zip(near, after):
-            arrived_grad[s] = pairwise(piece, "exp", s)
-        for s in near:
-            arrived_x[s] = pairwise(send_x[s], "exp", s)
+    arrived_x = exchange(send_x, capacity)
 
     d_act, probs, down_near, gate_near, place, weight_wide = run(
         functools.partial(probs_kernel, ctx_count, capacity, piece_count),
@@ -576,10 +549,9 @@
     )
     send_dn, send_y = split_parts(sent, piece_count)
     dn = exchange(send_dn, capacity)
-    y = [
-        dn[s] if joined(s, piece_count) else moved
-        for s, moved in enumerate(exchange_apart(send_y, capacity))
-    ]
+    far = [s for s in range(1, piece_count) if not joined(s, piece_count)]
+    y = list(dn) if piece_count > 1 else [exchange_flat(send_y[0], capacity)]
+    y[0] = send_y[0] if piece_count > 1 else y[0]
     (terms,) = run(
         functools.partial(gain_kernel, piece_count, rows),
         "gain_terms",
@@ -587,53 +559,52 @@
         placed(VMEM, [shaped((GAIN_LINES, LANES), F32)]),
         2 * slots * D,
     )
-    terms, place_back = lax.optimization_barrier((sum_over(terms, "dp"), place))
-
-    if piece_count == 1:
-        terms = sum_over(terms, "exp")
-    else:
-        terms = tree_sum([terms] + [pairwise(terms, "exp", s) for s in range(1, exp_count)])
+    terms = sum_over(sum_over(terms, "dp"), "ctx")
+    send_far, terms = lax.optimization_barrier(([send_y[s] for s in far], terms))
+    for s, piece in zip(far, send_far):
+        y[s] = pairwise(piece, "exp", s)
+    terms, dn = lax.optimization_barrier((terms, dn))
+    terms = doubled(terms, "exp", 1)
 
     d_hidden, d_queries, kv_own, *kv_send = run(
         functools.partial(backward_kernel, ctx_count, piece_count, rows),
         "residual_attention_backward",
-        placed(VMEM, [place_back, gain, hidden, grad_rows, query_rows, probs])
+        placed(VMEM, [place, gain, hidden, grad_rows, query_rows, probs])
         + placed(VMEM, dn + all_keys + all_values),
-        placed(HBM, [token_shape] * 2)
+        placed(HBM, [token_shape])
         + placed(
             VMEM,
-            [shaped((tokens, kv_width), F32)]
+            [token_shape, shaped((tokens, kv_width), F32)]
             + [shaped((tokens, kv_width), BF16)] * (ctx_count - 1),
         ),
         attn_flops + place_flops,
         scratch=[
             pltpu.VMEM((tokens, D), BF16),
-            pltpu.VMEM((tokens, D), BF16),
             pltpu.VMEM((tokens, D), F32),
-            pltpu.SemaphoreType.DMA((1 + KEY_VALUE_HEADS,)),
+            pltpu.SemaphoreType.DMA(()),
         ],
     )
-    terms, kv_own = lax.optimization_barrier((terms, kv_own))
-    terms = sum_over(terms, "ctx")
+    terms, kv_send = lax.optimization_barrier((terms, kv_send))
+    terms = sum_over(terms, "exp", first=2)
     kv_arrived = [pairwise(part, "ctx", s) for s, part in enumerate(kv_send, 1)]
 
     kv_shape = shaped((tokens, kv_width // 2), BF16)
-    final_shapes = [token_shape, kv_shape, kv_shape]
+    final_shapes = [token_shape, token_shape, kv_shape, kv_shape]
     final_shapes += [shaped((1, tokens), F32), shaped((GAIN_LINES, LANES), F32)]
     total_tokens = tokens * ctx_count * exp_count * lax.axis_size("dp")
-    layer_out, d_keys, d_values, d_weight, d_gain = run(
+    layer_out, d_queries, d_keys, d_values, d_weight, d_gain = run(
         functools.partial(output_kernel, ctx_count, piece_count, rows, total_tokens),
         "layer_output",
         placed(
             VMEM,
-            [place, weight_wide, terms, hidden, grad_rows, kv_own]
+            [place, weight_wide, terms, hidden, grad_rows, kv_own, d_queries]
             + kv_arrived
             + y,
         ),
         placed(HBM, final_shapes),
         place_flops,
-        scratch=[pltpu.VMEM(x.shape, x.dtype) for x in final_shapes]
-        + [pltpu.SemaphoreType.DMA((4 + D // COLS,))],
+        scratch=[pltpu.VMEM(x.shape, x.dtype) for x in final_shapes[:1] + final_shapes[2:]]
+        + [pltpu.SemaphoreType.DMA((5 + D // COLS,))],
     )
     return (
         layer_out[None],

time: 55 us -> 54.4 us (0.989)
  waiting for transfers between devices: 16.5 us -> 18 us
  starting transfers between devices: 22.5 us -> 21.1 us
  Pallas kernels: 15.1 us -> 14.4 us
    ppermute x19 -> x18, waiting for transfers between devices: 16.5 us -> 18 us  [pairwise(): return lax.ppermute(value, axis, [(i, i ^ step) for i in range(count)])]
    ppermute x19 -> x18, starting transfers between devices: 22.5 us -> 21.1 us  [pairwise(): return lax.ppermute(value, axis, [(i, i ^ step) for i in range(count)])]
    pallas_call x7, Pallas kernels: 15.1 us -> 14.4 us  [run(): pl.pallas_call(kernel, out_shape=[x for _, x in outputs], in_specs=[spec[...]
  transfers between devices with their start and end apart: 19 -> 18, of which waited for: 10 -> 8; matrix products, arithmetic and copies ran while one was open for 0% -> 0% of each run, Pallas kernels for 17% -> 16%
where the time goes in v11:
time: 54.4 us; the launch traced here: 54.3 us
  starting transfers between devices  21.1 us (39%)
  waiting for transfers between devices  18 us (33%)
  Pallas kernels  14.4 us (26%)
  between operations  0.71 us (1%)
    ppermute x18, starting transfers between devices, pairwise(): return lax.ppermute(value, axis, [(i, i ^ step) for i in range(count)])  21.1 us
    ppermute x18, waiting for transfers between devices, pairwise(): return lax.ppermute(value, axis, [(i, i ^ step) for i in range(count)])  18 us
    pallas_call x7, Pallas kernels, run(): pl.pallas_call(kernel, out_shape=[x for _, x in outputs], in_specs=[spec[...  14.4 us
  transfers between devices with their start and end apart: 18, of which 8 were waited for; matrix products, arithmetic and copies ran while one was open for 0% of the time, Pallas kernels for 16%

profile of v11, /device:TPU:0, one launch (start us, length us, event | category | flops | bytes accessed | tf_op | source)
XLA Modules:
  0.0 54.3 jit_solution(18272436677395557798)
XLA Ops:
  0.6 1.5 %dispatch_grads.1 = (bf16[128,2048]{1,0:T(8,128)(2,1)S(1)}, bf16[128,256]{1,0:T(8,128)(2,1)S(1)}, bf16[128,256]{1,0:T(8,128)(2,1)S(1)}, f32[1,2048]{1,0:T(1,128)...) custom-call(bf16[128,2048]{1,0:T(8,128)(2,1)} %bitcast.13, ...), custom_call_target="tpu_custom_call" | custom-call | flops 100663296 | bytes 4213824 | tf_op jit(solution)/shard_map/dispatch_grads/pallas_call | solution.py:393
  2.2 3.0 %collective-permute-start.1 = (bf16[48,2048]{1,0:T(8,128)(2,1)S(1)}, bf16[48,2048]{1,0:T(8,128)(2,1)S(1)}, u32[]{:S(2)}, u32[]{:S(2)}) collective-permute-start(bf16[48,2048]{1,0:T(8,128)(2,1)S(1)} %get-tuple-element.62), channel_id=1, source_target_pairs={{0,4},{4,0},{8,12},{12,8},{1,5},{5,1},{9,13},{13,9},{2,6},{6,2},{1... | collective-permute-start | bytes 589832 | tf_op jit(solution)/shard_map/ppermute | solution.py:412
  5.2 0.5 collective-permute-start.4
  5.7 1.5 %collective-permute-start.2 = (bf16[48,2048]{1,0:T(8,128)(2,1)S(1)}, bf16[48,2048]{1,0:T(8,128)(2,1)S(1)}, u32[]{:S(2)}, u32[]{:S(2)}) collective-permute-start(bf16[48,2048]{1,0:T(8,128)(2,1)S(1)} %get-tuple-element.63), channel_id=1, source_target_pairs={{0,8},{4,12},{8,0},{12,4},{1,9},{5,13},{9,1},{13,5},{2,10},{6,14},... | collective-permute-start | bytes 589832 | tf_op jit(solution)/shard_map/ppermute | solution.py:412
  7.2 0.0 collective-permute-start.3
  7.2 0.0 collective-permute-done.refs_1_.refs_5_
  7.2 0.0 collective-permute-done.4.refs_3_.refs_7_
  7.2 1.4 %attention_forward.1 = (bf16[128,2048]{1,0:T(8,128)(2,1)S(1)}, bf16[48,2048]{1,0:T(8,128)(2,1)S(1)}, bf16[48,2048]{1,0:T(8,128)(2,1)S(1)}, bf16[48,2048]{1,0:T(8,128)(2,1)S(1)}, bf16[48,2048]{1,0:T(8,128)(2,1)S(1)}) custom-call(s32[2,128]{1,0:T(2,128)S(1)} %get-tuple-element.56.pos_ref, s32[1,128]{1,0:T(1,128)S(1)} %get-tuple-element.57.slot_ref, ...), custom_call_target="tpu_custom_call" | custom-call | flops 369098752 | bytes 2631168 | tf_op jit(solution)/shard_map/attention_forward/pallas_call | solution.py:393
  8.6 2.0 %collective-permute-start.5 = (bf16[48,2048]{1,0:T(8,128)(2,1)S(1)}, bf16[48,2048]{1,0:T(8,128)(2,1)S(1)}, u32[]{:S(2)}, u32[]{:S(2)}) collective-permute-start(bf16[48,2048]{1,0:T(8,128)(2,1)S(1)} %get-tuple-element.74), channel_id=1, source_target_pairs={{0,4},{4,0},{8,12},{12,8},{1,5},{5,1},{9,13},{13,9},{2,6},{6,2},{1... | collective-permute-start | bytes 589832 | tf_op jit(solution)/shard_map/ppermute | solution.py:412
  10.7 1.5 %collective-permute-start.6 = (bf16[48,2048]{1,0:T(8,128)(2,1)S(1)}, bf16[48,2048]{1,0:T(8,128)(2,1)S(1)}, u32[]{:S(2)}, u32[]{:S(2)}) collective-permute-start(bf16[48,2048]{1,0:T(8,128)(2,1)S(1)} %get-tuple-element.75), channel_id=1, source_target_pairs={{0,8},{4,12},{8,0},{12,4},{1,9},{5,13},{9,1},{13,5},{2,10},{6,14},... | collective-permute-start | bytes 589832 | tf_op jit(solution)/shard_map/ppermute | solution.py:412
  12.2 1.8 %collective-permute-start.7 = (bf16[48,2048]{1,0:T(8,128)(2,1)S(1)}, bf16[48,2048]{1,0:T(8,128)(2,1)S(1)}, u32[]{:S(2)}, u32[]{:S(2)}) collective-permute-start(bf16[48,2048]{1,0:T(8,128)(2,1)S(1)} %get-tuple-element.76), channel_id=1, source_target_pairs={{0,12},{4,8},{8,4},{12,0},{1,13},{5,9},{9,5},{13,1},{2,14},{6,10},... | collective-permute-start | bytes 589832 | tf_op jit(solution)/shard_map/ppermute | solution.py:412
  13.9 3.7 %collective-permute-done.2.refs_4_ = bf16[48,2048]{1,0:T(8,128)(2,1)S(1)} collective-permute-done((bf16[48,2048]{1,0:T(8,128)(2,1)S(1)}, bf16[48,2048]{1,0:T(8,128)(2,1)S(1)}, u32[]{:S(2)}, u32[]{:S(2)}) %collective-permute-start.2) | collective-permute-done | bytes 196640 | tf_op jit(solution)/shard_map/ppermute | solution.py:412
  17.7 3.8 %act_grads_and_probs.1 = (f32[192,384]{1,0:T(8,128)S(1)}, f32[8,256,256]{2,1,0:T(8,128)S(1)}, bf16[768,2048]{1,0:T(8,128)(2,1)S(1)}, bf16[2048,768]{1,0:T(8,128)...) custom-call(s32[2,128]{1,0:T(2,128)S(1)} %get-tuple-element.56.pos_ref, ...), custom_call_target="tpu_custom_call" | custom-call | flops 738197504 | bytes 16599040 | tf_op jit(solution)/shard_map/act_grads_and_probs/pallas_call | solution.py:393
  21.5 3.6 %collective-permute-done.6.refs_2_ = bf16[48,2048]{1,0:T(8,128)(2,1)S(1)} collective-permute-done((bf16[48,2048]{1,0:T(8,128)(2,1)S(1)}, bf16[48,2048]{1,0:T(8,128)(2,1)S(1)}, u32[]{:S(2)}, u32[]{:S(2)}) %collective-permute-start.6) | collective-permute-done | bytes 196640 | tf_op jit(solution)/shard_map/ppermute | solution.py:412
  25.1 2.8 %experts.1 = (bf16[48,2048]{1,0:T(8,128)(2,1)S(1)}, bf16[48,2048]{1,0:T(8,128)(2,1)S(1)}, bf16[96,2048]{1,0:T(8,128)(2,1)S(1)}, bf16[96,2048]{1,0:T(8,128)(2,1)S...) custom-call(bf16[2048,768]{1,0:T(8,128)(2,1)S(1)} %get-tuple-element.67.gate_ref, ...), custom_call_target="tpu_custom_call" | custom-call | flops 1811939328 | bytes 8945664 | tf_op jit(solution)/shard_map/experts/pallas_call | solution.py:393
  28.0 0.4 collective-permute-start.11
  28.4 1.7 %collective-permute-start.12 = (bf16[96,2048]{1,0:T(8,128)(2,1)S(1)}, bf16[96,2048]{1,0:T(8,128)(2,1)S(1)}, u32[]{:S(2)}, u32[]{:S(2)}) collective-permute-start(bf16[96,2048]{1,0:T(8,128)(2,1)S(1)} %get-tuple-element.80.refs_6_), channel_id=1, source_target_pairs={{0,8},{4,12},{8,0},{12,4},{1,9},{5,13},{9,1},{13,5},{2,10},{6,14},... | collective-permute-start | bytes 1179656 | tf_op jit(solution)/shard_map/ppermute | solution.py:412
  30.1 1.4 %collective-permute-start.13 = (bf16[48,2048]{1,0:T(8,128)(2,1)S(1)}, bf16[48,2048]{1,0:T(8,128)(2,1)S(1)}, u32[]{:S(2)}, u32[]{:S(2)}) collective-permute-start(bf16[48,2048]{1,0:T(8,128)(2,1)S(1)} %get-tuple-element.81.refs_7_), channel_id=1, source_target_pairs={{0,12},{4,8},{8,4},{12,0},{1,13},{5,9},{9,5},{13,1},{2,14},{6,10},... | collective-permute-start | bytes 589832 | tf_op jit(solution)/shard_map/ppermute | solution.py:412
  31.5 0.3 gain_terms.1
  31.8 1.6 %collective-permute-start.8 = (f32[16,128]{1,0:T(8,128)S(1)}, f32[16,128]{1,0:T(8,128)S(1)}, u32[]{:S(2)}, u32[]{:S(2)}) collective-permute-start(f32[16,128]{1,0:T(8,128)S(1)} %gain_terms.1), channel_id=1, source_target_pairs={{0,1},{1,0},{2,3},{3,2},{4,5},{5,4},{6,7},{7,6},{8,9},{9,8},{10,11... | collective-permute-start | bytes 24584 | tf_op jit(solution)/shard_map/ppermute | solution.py:412
  33.5 2.1 %collective-permute-done.8 = f32[16,128]{1,0:T(8,128)S(1)} collective-permute-done((f32[16,128]{1,0:T(8,128)S(1)}, f32[16,128]{1,0:T(8,128)S(1)}, u32[]{:S(2)}, u32[]{:S(2)}) %collective-permute-start.8) | collective-permute-done | bytes 8224 | tf_op jit(solution)/shard_map/ppermute | solution.py:412
  35.6 2.7 %collective-permute-start.9 = (f32[16,128]{1,0:T(8,128)S(1)}, f32[16,128]{1,0:T(8,128)S(1)}, u32[]{:S(2)}, u32[]{:S(2)}) collective-permute-start(f32[16,128]{1,0:T(8,128)S(1)} %add.15), channel_id=1, source_target_pairs={{0,2},{1,3},{2,0},{3,1},{4,6},{5,7},{6,4},{7,5},{8,10},{9,11},{10,... | collective-permute-start | bytes 24584 | tf_op jit(solution)/shard_map/ppermute | solution.py:412
  38.2 1.9 %collective-permute-done.9 = f32[16,128]{1,0:T(8,128)S(1)} collective-permute-done((f32[16,128]{1,0:T(8,128)S(1)}, f32[16,128]{1,0:T(8,128)S(1)}, u32[]{:S(2)}, u32[]{:S(2)}) %collective-permute-start.9) | collective-permute-done | bytes 8224 | tf_op jit(solution)/shard_map/ppermute | solution.py:412
  40.1 1.2 %collective-permute-done.10 = f32[16,128]{1,0:T(8,128)S(1)} collective-permute-done((f32[16,128]{1,0:T(8,128)S(1)}, f32[16,128]{1,0:T(8,128)S(1)}, u32[]{:S(2)}, u32[]{:S(2)}) %collective-permute-start.10) | collective-permute-done | bytes 8224 | tf_op jit(solution)/shard_map/ppermute | solution.py:412
  41.3 1.5 %collective-permute-start.17 = (bf16[48,2048]{1,0:T(8,128)(2,1)S(1)}, bf16[48,2048]{1,0:T(8,128)(2,1)S(1)}, u32[]{:S(2)}, u32[]{:S(2)}) collective-permute-start(bf16[48,2048]{1,0:T(8,128)(2,1)S(1)} %get-tuple-element.97), channel_id=1, source_target_pairs={{0,12},{4,8},{8,4},{12,0},{1,13},{5,9},{9,5},{13,1},{2,14},{6,10},... | collective-permute-start | bytes 589832 | tf_op jit(solution)/shard_map/ppermute | solution.py:412
  42.8 0.6 %collective-permute-done.13.refs_3_ = bf16[48,2048]{1,0:T(8,128)(2,1)S(1)} collective-permute-done((bf16[48,2048]{1,0:T(8,128)(2,1)S(1)}, bf16[48,2048]{1,0:T(8,128)(2,1)S(1)}, u32[]{:S(2)}, u32[]{:S(2)}) %collective-permute-start.13) | collective-permute-done | bytes 196640 | tf_op jit(solution)/shard_map/ppermute | solution.py:412
  43.4 1.0 %collective-permute-start.14 = (f32[16,128]{1,0:T(8,128)S(1)}, f32[16,128]{1,0:T(8,128)S(1)}, u32[]{:S(2)}, u32[]{:S(2)}) collective-permute-start(f32[16,128]{1,0:T(8,128)S(1)} %add.17), channel_id=1, source_target_pairs={{0,4},{4,0},{8,12},{12,8},{1,5},{5,1},{9,13},{13,9},{2,6},{6,2},{1... | collective-permute-start | bytes 24584 | tf_op jit(solution)/shard_map/ppermute | solution.py:412
  44.3 3.3 %residual_attention_backward.1 = (bf16[128,2048]{1,0:T(8,128)(2,1)}, bf16[128,2048]{1,0:T(8,128)(2,1)S(1)}, f32[128,512]{1,0:T(8,128)S(1)}, bf16[128,512]{1,0:T(8,128)(2,1)S(1)}) custom-call(bf16[128,192]{1,0:T(8,128)(2,1)S(1)} %get-tuple-element.65.place_ref, f32[1,2048]{1,0:T(1,128)S(1)} %get-tuple-element.70.gain_ref, ...), custom_call_target="tpu_custom_call" | custom-call | flops 369098752 | bytes 6610944 | tf_op jit(solution)/shard_map/residual_attention_backward/pallas_call | solution.py:393
  47.7 1.7 %collective-permute-done.14 = f32[16,128]{1,0:T(8,128)S(1)} collective-permute-done((f32[16,128]{1,0:T(8,128)S(1)}, f32[16,128]{1,0:T(8,128)S(1)}, u32[]{:S(2)}, u32[]{:S(2)}) %collective-permute-start.14) | collective-permute-done | bytes 8224 | tf_op jit(solution)/shard_map/ppermute | solution.py:412
  49.4 0.5 collective-permute-start.15
  49.9 3.1 %collective-permute-done.15 = f32[16,128]{1,0:T(8,128)S(1)} collective-permute-done((f32[16,128]{1,0:T(8,128)S(1)}, f32[16,128]{1,0:T(8,128)S(1)}, u32[]{:S(2)}, u32[]{:S(2)}) %collective-permute-start.15) | collective-permute-done | bytes 8224 | tf_op jit(solution)/shard_map/ppermute | solution.py:412
  53.1 1.2 %layer_output.1 = (bf16[128,2048]{1,0:T(8,128)(2,1)}, bf16[128,2048]{1,0:T(8,128)(2,1)}, bf16[128,256]{1,0:T(8,128)(2,1)}, bf16[128,256]{1,0:T(8,128)(2,1)}, f32[1,128]{1,0:T(1,128)}, /*index=5*/f32[16,128]{1,0:T(8,128)}) custom-call(bf16[128,192]{1,0:T(8,128)(2,1)S(1)} %get-tuple-element.65.place_ref, f32[128,256]{1,0:T(8,128)S(1)} %get-tuple-element.66.weight_ref, ...), custom_call_target="tpu_custom_call" | custom-call | flops 100663296 | bytes 4522496 | tf_op jit(solution)/shard_map/layer_output/pallas_call | solution.py:393
  (16 shorter events, 0.0 us)
Async XLA Ops:
  2.2 10.0 %collective-permute-start.1 = (bf16[48,2048]{1,0:T(8,128)(2,1)S(1)}, bf16[48,2048]{1,0:T(8,128)(2,1)S(1)}, u32[]{:S(2)}, u32[]{:S(2)}) collective-permute-start(bf16[48,2048]{1,0:T(8,128)(2,1)S(1)} %get-tuple-element.62), channel_id=1, source_target_pairs={{0,4},{4,0},{8,12},{12,8},{1,5},{5,1},{9,13},{13,9},{2,6},{6,2},{1... | collective-permute-start | bytes 589832 | tf_op jit(solution)/shard_map/ppermute | solution.py:412
  5.2 2.1 %collective-permute-start = (bf16[128,256]{1,0:T(8,128)(2,1)}, bf16[128,256]{1,0:T(8,128)(2,1)S(1)}, u32[]{:S(2)}, u32[]{:S(2)}) collective-permute-start(bf16[128,256]{1,0:T(8,128)(2,1)} %bitcast.17), channel_id=1, source_target_pairs={{0,16},{16,0},{1,17},{17,1},{2,18},{18,2},{3,19},{19,3},{4,20},{20... | collective-permute-start | bytes 196616 | tf_op jit(solution)/shard_map/ppermute | solution.py:412
  5.2 2.1 %collective-permute-start.4 = (bf16[128,256]{1,0:T(8,128)(2,1)}, bf16[128,256]{1,0:T(8,128)(2,1)S(1)}, u32[]{:S(2)}, u32[]{:S(2)}) collective-permute-start(bf16[128,256]{1,0:T(8,128)(2,1)} %bitcast.19), channel_id=1, source_target_pairs={{0,16},{16,0},{1,17},{17,1},{2,18},{18,2},{3,19},{19,3},{4,20},{20... | collective-permute-start | bytes 196616 | tf_op jit(solution)/shard_map/ppermute | solution.py:412
  5.7 12.0 %collective-permute-start.2 = (bf16[48,2048]{1,0:T(8,128)(2,1)S(1)}, bf16[48,2048]{1,0:T(8,128)(2,1)S(1)}, u32[]{:S(2)}, u32[]{:S(2)}) collective-permute-start(bf16[48,2048]{1,0:T(8,128)(2,1)S(1)} %get-tuple-element.63), channel_id=1, source_target_pairs={{0,8},{4,12},{8,0},{12,4},{1,9},{5,13},{9,1},{13,5},{2,10},{6,14},... | collective-permute-start | bytes 589832 | tf_op jit(solution)/shard_map/ppermute | solution.py:412
  7.2 10.5 %collective-permute-start.3 = (bf16[48,2048]{1,0:T(8,128)(2,1)S(1)}, bf16[48,2048]{1,0:T(8,128)(2,1)S(1)}, u32[]{:S(2)}, u32[]{:S(2)}) collective-permute-start(bf16[48,2048]{1,0:T(8,128)(2,1)S(1)} %get-tuple-element.64), channel_id=1, source_target_pairs={{0,12},{4,8},{8,4},{12,0},{1,13},{5,9},{9,5},{13,1},{2,14},{6,10},... | collective-permute-start | bytes 589832 | tf_op jit(solution)/shard_map/ppermute | solution.py:412
  8.6 12.8 %collective-permute-start.5 = (bf16[48,2048]{1,0:T(8,128)(2,1)S(1)}, bf16[48,2048]{1,0:T(8,128)(2,1)S(1)}, u32[]{:S(2)}, u32[]{:S(2)}) collective-permute-start(bf16[48,2048]{1,0:T(8,128)(2,1)S(1)} %get-tuple-element.74), channel_id=1, source_target_pairs={{0,4},{4,0},{8,12},{12,8},{1,5},{5,1},{9,13},{13,9},{2,6},{6,2},{1... | collective-permute-start | bytes 589832 | tf_op jit(solution)/shard_map/ppermute | solution.py:412
  10.7 14.5 %collective-permute-start.6 = (bf16[48,2048]{1,0:T(8,128)(2,1)S(1)}, bf16[48,2048]{1,0:T(8,128)(2,1)S(1)}, u32[]{:S(2)}, u32[]{:S(2)}) collective-permute-start(bf16[48,2048]{1,0:T(8,128)(2,1)S(1)} %get-tuple-element.75), channel_id=1, source_target_pairs={{0,8},{4,12},{8,0},{12,4},{1,9},{5,13},{9,1},{13,5},{2,10},{6,14},... | collective-permute-start | bytes 589832 | tf_op jit(solution)/shard_map/ppermute | solution.py:412
  12.2 13.0 %collective-permute-start.7 = (bf16[48,2048]{1,0:T(8,128)(2,1)S(1)}, bf16[48,2048]{1,0:T(8,128)(2,1)S(1)}, u32[]{:S(2)}, u32[]{:S(2)}) collective-permute-start(bf16[48,2048]{1,0:T(8,128)(2,1)S(1)} %get-tuple-element.76), channel_id=1, source_target_pairs={{0,12},{4,8},{8,4},{12,0},{1,13},{5,9},{9,5},{13,1},{2,14},{6,10},... | collective-permute-start | bytes 589832 | tf_op jit(solution)/shard_map/ppermute | solution.py:412
  28.0 15.4 %collective-permute-start.11 = (bf16[96,2048]{1,0:T(8,128)(2,1)S(1)}, bf16[96,2048]{1,0:T(8,128)(2,1)S(1)}, u32[]{:S(2)}, u32[]{:S(2)}) collective-permute-start(bf16[96,2048]{1,0:T(8,128)(2,1)S(1)} %get-tuple-element.79.refs_5_), channel_id=1, source_target_pairs={{0,4},{4,0},{8,12},{12,8},{1,5},{5,1},{9,13},{13,9},{2,6},{6,2},{1... | collective-permute-start | bytes 1179656 | tf_op jit(solution)/shard_map/ppermute | solution.py:412
  28.4 15.0 %collective-permute-start.12 = (bf16[96,2048]{1,0:T(8,128)(2,1)S(1)}, bf16[96,2048]{1,0:T(8,128)(2,1)S(1)}, u32[]{:S(2)}, u32[]{:S(2)}) collective-permute-start(bf16[96,2048]{1,0:T(8,128)(2,1)S(1)} %get-tuple-element.80.refs_6_), channel_id=1, source_target_pairs={{0,8},{4,12},{8,0},{12,4},{1,9},{5,13},{9,1},{13,5},{2,10},{6,14},... | collective-permute-start | bytes 1179656 | tf_op jit(solution)/shard_map/ppermute | solution.py:412
  30.1 13.3 %collective-permute-start.13 = (bf16[48,2048]{1,0:T(8,128)(2,1)S(1)}, bf16[48,2048]{1,0:T(8,128)(2,1)S(1)}, u32[]{:S(2)}, u32[]{:S(2)}) collective-permute-start(bf16[48,2048]{1,0:T(8,128)(2,1)S(1)} %get-tuple-element.81.refs_7_), channel_id=1, source_target_pairs={{0,12},{4,8},{8,4},{12,0},{1,13},{5,9},{9,5},{13,1},{2,14},{6,10},... | collective-permute-start | bytes 589832 | tf_op jit(solution)/shard_map/ppermute | solution.py:412
  31.8 3.7 %collective-permute-start.8 = (f32[16,128]{1,0:T(8,128)S(1)}, f32[16,128]{1,0:T(8,128)S(1)}, u32[]{:S(2)}, u32[]{:S(2)}) collective-permute-start(f32[16,128]{1,0:T(8,128)S(1)} %gain_terms.1), channel_id=1, source_target_pairs={{0,1},{1,0},{2,3},{3,2},{4,5},{5,4},{6,7},{7,6},{8,9},{9,8},{10,11... | collective-permute-start | bytes 24584 | tf_op jit(solution)/shard_map/ppermute | solution.py:412
  35.6 4.5 %collective-permute-start.9 = (f32[16,128]{1,0:T(8,128)S(1)}, f32[16,128]{1,0:T(8,128)S(1)}, u32[]{:S(2)}, u32[]{:S(2)}) collective-permute-start(f32[16,128]{1,0:T(8,128)S(1)} %add.15), channel_id=1, source_target_pairs={{0,2},{1,3},{2,0},{3,1},{4,6},{5,7},{6,4},{7,5},{8,10},{9,11},{10,... | collective-permute-start | bytes 24584 | tf_op jit(solution)/shard_map/ppermute | solution.py:412
  40.1 1.2 %collective-permute-start.10 = (f32[16,128]{1,0:T(8,128)S(1)}, f32[16,128]{1,0:T(8,128)S(1)}, u32[]{:S(2)}, u32[]{:S(2)}) collective-permute-start(f32[16,128]{1,0:T(8,128)S(1)} %add.16), channel_id=1, source_target_pairs={{0,16},{16,0},{1,17},{17,1},{2,18},{18,2},{3,19},{19,3},{4,20},{20... | collective-permute-start | bytes 24584 | tf_op jit(solution)/shard_map/ppermute | solution.py:412
  41.3 11.8 %collective-permute-start.17 = (bf16[48,2048]{1,0:T(8,128)(2,1)S(1)}, bf16[48,2048]{1,0:T(8,128)(2,1)S(1)}, u32[]{:S(2)}, u32[]{:S(2)}) collective-permute-start(bf16[48,2048]{1,0:T(8,128)(2,1)S(1)} %get-tuple-element.97), channel_id=1, source_target_pairs={{0,12},{4,8},{8,4},{12,0},{1,13},{5,9},{9,5},{13,1},{2,14},{6,10},... | collective-permute-start | bytes 589832 | tf_op jit(solution)/shard_map/ppermute | solution.py:412
  43.4 6.0 %collective-permute-start.14 = (f32[16,128]{1,0:T(8,128)S(1)}, f32[16,128]{1,0:T(8,128)S(1)}, u32[]{:S(2)}, u32[]{:S(2)}) collective-permute-start(f32[16,128]{1,0:T(8,128)S(1)} %add.17), channel_id=1, source_target_pairs={{0,4},{4,0},{8,12},{12,8},{1,5},{5,1},{9,13},{13,9},{2,6},{6,2},{1... | collective-permute-start | bytes 24584 | tf_op jit(solution)/shard_map/ppermute | solution.py:412
  49.4 3.7 %collective-permute-start.16 = (bf16[128,512]{1,0:T(8,128)(2,1)S(1)}, bf16[128,512]{1,0:T(8,128)(2,1)S(1)}, u32[]{:S(2)}, u32[]{:S(2)}) collective-permute-start(bf16[128,512]{1,0:T(8,128)(2,1)S(1)} %get-tuple-element.95), channel_id=1, source_target_pairs={{0,16},{16,0},{1,17},{17,1},{2,18},{18,2},{3,19},{19,3},{4,20},{20... | collective-permute-start | bytes 393224 | tf_op jit(solution)/shard_map/ppermute | solution.py:412
  49.4 3.7 %collective-permute-start.15 = (f32[16,128]{1,0:T(8,128)S(1)}, f32[16,128]{1,0:T(8,128)S(1)}, u32[]{:S(2)}, u32[]{:S(2)}) collective-permute-start(f32[16,128]{1,0:T(8,128)S(1)} %add.18), channel_id=1, source_target_pairs={{0,8},{4,12},{8,0},{12,4},{1,9},{5,13},{9,1},{13,5},{2,10},{6,14},... | collective-permute-start | bytes 24584 | tf_op jit(solution)/shard_map/ppermute | solution.py:412

commit v12 on v10

--- a/solution.py
+++ b/solution.py
@@ -18,6 +18,7 @@
 LANES = 128
 GAIN_LINES = D // LANES
 WIDE_LINES = 32
+FIRST = 2
 A_COST = 4000000000
 B_COST = 0
 SCALE = HEAD_SIZE ** (-0.5)
@@ -592,10 +593,10 @@
         2 * slots * D,
     )
     terms = sum_over(sum_over(terms, "dp"), "ctx")
-    send_far, terms, dn = lax.optimization_barrier(([send_y[s] for s in far], terms, dn))
+    send_far, terms = lax.optimization_barrier(([send_y[s] for s in far], terms))
     for s, piece in zip(far, send_far):
         y[s] = pairwise(piece, "exp", s)
-    terms = doubled(terms, "exp", 1)
+    beside = pairwise(terms, "exp", FIRST)
 
     half_shape = shaped((tokens, D // 2), BF16)
     own_shape = shaped((tokens, 2 * HEAD_SIZE), F32)
@@ -617,10 +618,9 @@
             pltpu.SemaphoreType.DMA(()),
         ],
     )
-    arrived_far, terms, rest = lax.optimization_barrier(([y[s] for s in far], terms, rest))
-    for s, piece in zip(far, arrived_far):
-        y[s] = piece
-    terms = widened(doubled, terms, "exp", 2)
+    terms, rest = lax.optimization_barrier((terms, rest))
+    terms = terms + beside
+    terms = widened(doubled, terms, "exp", 3 - FIRST)
     dq_second, own_second, *shared = run(
         functools.partial(second_back_kernel, ctx_count),
         "second_group",
@@ -630,6 +630,9 @@
         B_COST,
     )
     terms = sum_over(terms, "exp", first=4)
+    arrived_far, shared = lax.optimization_barrier(([y[s] for s in far], shared))
+    for s, piece in zip(far, arrived_far):
+        y[s] = piece
     kv_arrived = [pairwise(part, "ctx", s) for s, part in enumerate(shared, 1)]
 
     kv_shape = shaped((tokens, kv_width // 2), BF16)

time: 56.7 us -> 53.3 us (0.940)
  waiting for transfers between devices: 19 us -> 16.3 us
  starting transfers between devices: 22 us -> 21.4 us
    ppermute x18, waiting for transfers between devices: 19 us -> 16.3 us  [pairwise(): return lax.ppermute(value, axis, [(i, i ^ step) for i in range(count)])]
    ppermute x18, starting transfers between devices: 22 us -> 21.4 us  [pairwise(): return lax.ppermute(value, axis, [(i, i ^ step) for i in range(count)])]
  transfers between devices with their start and end apart: 18 -> 18, of which waited for: 9 -> 8; matrix products, arithmetic and copies ran while one was open for 0% -> 0% of each run, Pallas kernels for 16% -> 17%
where the time goes in v12:
time: 53.3 us; the launch traced here: 53.1 us
  starting transfers between devices  21.4 us (40%)
  waiting for transfers between devices  16.3 us (31%)
  Pallas kernels  14.7 us (28%)
  between operations  0.73 us (1%)
    ppermute x18, starting transfers between devices, pairwise(): return lax.ppermute(value, axis, [(i, i ^ step) for i in range(count)])  21.4 us
    ppermute x18, waiting for transfers between devices, pairwise(): return lax.ppermute(value, axis, [(i, i ^ step) for i in range(count)])  16.3 us
    pallas_call x8, Pallas kernels, run(): pl.pallas_call(kernel, out_shape=[x for _, x in outputs], in_specs=[spec[...  14.7 us
  transfers between devices with their start and end apart: 18, of which 8 were waited for; matrix products, arithmetic and copies ran while one was open for 0% of the time, Pallas kernels for 17%

profile of v12, /device:TPU:0, one launch (start us, length us, event | category | flops | bytes accessed | tf_op | source)
XLA Modules:
  0.0 53.1 jit_solution(13682171517891537774)
XLA Ops:
  0.6 1.5 %dispatch_grads.1 = (bf16[128,2048]{1,0:T(8,128)(2,1)S(1)}, bf16[128,256]{1,0:T(8,128)(2,1)S(1)}, bf16[128,256]{1,0:T(8,128)(2,1)S(1)}, f32[1,2048]{1,0:T(1,128)...) custom-call(bf16[128,2048]{1,0:T(8,128)(2,1)} %bitcast.13, ...), custom_call_target="tpu_custom_call" | custom-call | flops 100663296 | bytes 4213824 | tf_op jit(solution)/shard_map/dispatch_grads/pallas_call | solution.py:420
  2.2 3.0 %collective-permute-start.1 = (bf16[48,2048]{1,0:T(8,128)(2,1)S(1)}, bf16[48,2048]{1,0:T(8,128)(2,1)S(1)}, u32[]{:S(2)}, u32[]{:S(2)}) collective-permute-start(bf16[48,2048]{1,0:T(8,128)(2,1)S(1)} %get-tuple-element.63), channel_id=1, source_target_pairs={{0,4},{4,0},{8,12},{12,8},{1,5},{5,1},{9,13},{13,9},{2,6},{6,2},{1... | collective-permute-start | bytes 589832 | tf_op jit(solution)/shard_map/ppermute | solution.py:439
  5.2 0.5 collective-permute-start.4
  5.7 1.5 %collective-permute-start.2 = (bf16[48,2048]{1,0:T(8,128)(2,1)S(1)}, bf16[48,2048]{1,0:T(8,128)(2,1)S(1)}, u32[]{:S(2)}, u32[]{:S(2)}) collective-permute-start(bf16[48,2048]{1,0:T(8,128)(2,1)S(1)} %get-tuple-element.64), channel_id=1, source_target_pairs={{0,8},{4,12},{8,0},{12,4},{1,9},{5,13},{9,1},{13,5},{2,10},{6,14},... | collective-permute-start | bytes 589832 | tf_op jit(solution)/shard_map/ppermute | solution.py:439
  7.2 0.0 collective-permute-start.3
  7.2 0.0 collective-permute-done.refs_1_
  7.2 1.4 %attention_forward.1 = (bf16[128,2048]{1,0:T(8,128)(2,1)S(1)}, bf16[48,2048]{1,0:T(8,128)(2,1)S(1)}, bf16[48,2048]{1,0:T(8,128)(2,1)S(1)}, bf16[48,2048]{1,0:T(8,128)(2,1)S(1)}, bf16[48,2048]{1,0:T(8,128)(2,1)S(1)}) custom-call(s32[2,128]{1,0:T(2,128)S(1)} %get-tuple-element.57.pos_ref, s32[1,128]{1,0:T(1,128)S(1)} %get-tuple-element.58.slot_ref, ...), custom_call_target="tpu_custom_call" | custom-call | flops 369098752 | bytes 2631168 | tf_op jit(solution)/shard_map/attention_forward/pallas_call | solution.py:420
  8.7 2.0 %collective-permute-start.5 = (bf16[48,2048]{1,0:T(8,128)(2,1)S(1)}, bf16[48,2048]{1,0:T(8,128)(2,1)S(1)}, u32[]{:S(2)}, u32[]{:S(2)}) collective-permute-start(bf16[48,2048]{1,0:T(8,128)(2,1)S(1)} %get-tuple-element.75), channel_id=1, source_target_pairs={{0,4},{4,0},{8,12},{12,8},{1,5},{5,1},{9,13},{13,9},{2,6},{6,2},{1... | collective-permute-start | bytes 589832 | tf_op jit(solution)/shard_map/ppermute | solution.py:439
  10.7 1.5 %collective-permute-start.6 = (bf16[48,2048]{1,0:T(8,128)(2,1)S(1)}, bf16[48,2048]{1,0:T(8,128)(2,1)S(1)}, u32[]{:S(2)}, u32[]{:S(2)}) collective-permute-start(bf16[48,2048]{1,0:T(8,128)(2,1)S(1)} %get-tuple-element.76), channel_id=1, source_target_pairs={{0,8},{4,12},{8,0},{12,4},{1,9},{5,13},{9,1},{13,5},{2,10},{6,14},... | collective-permute-start | bytes 589832 | tf_op jit(solution)/shard_map/ppermute | solution.py:439
  12.2 1.7 %collective-permute-start.7 = (bf16[48,2048]{1,0:T(8,128)(2,1)S(1)}, bf16[48,2048]{1,0:T(8,128)(2,1)S(1)}, u32[]{:S(2)}, u32[]{:S(2)}) collective-permute-start(bf16[48,2048]{1,0:T(8,128)(2,1)S(1)} %get-tuple-element.77), channel_id=1, source_target_pairs={{0,12},{4,8},{8,4},{12,0},{1,13},{5,9},{9,5},{13,1},{2,14},{6,10},... | collective-permute-start | bytes 589832 | tf_op jit(solution)/shard_map/ppermute | solution.py:439
  13.9 3.7 %collective-permute-done.2.refs_4_ = bf16[48,2048]{1,0:T(8,128)(2,1)S(1)} collective-permute-done((bf16[48,2048]{1,0:T(8,128)(2,1)S(1)}, bf16[48,2048]{1,0:T(8,128)(2,1)S(1)}, u32[]{:S(2)}, u32[]{:S(2)}) %collective-permute-start.2) | collective-permute-done | bytes 196640 | tf_op jit(solution)/shard_map/ppermute | solution.py:439
  17.7 3.8 %act_grads_and_probs.1 = (f32[192,384]{1,0:T(8,128)S(1)}, f32[8,256,256]{2,1,0:T(8,128)S(1)}, bf16[768,2048]{1,0:T(8,128)(2,1)S(1)}, bf16[2048,768]{1,0:T(8,128)...) custom-call(s32[2,128]{1,0:T(2,128)S(1)} %get-tuple-element.57.pos_ref, ...), custom_call_target="tpu_custom_call" | custom-call | flops 738197504 | bytes 16599040 | tf_op jit(solution)/shard_map/act_grads_and_probs/pallas_call | solution.py:420
  21.5 3.6 %collective-permute-done.6.refs_2_ = bf16[48,2048]{1,0:T(8,128)(2,1)S(1)} collective-permute-done((bf16[48,2048]{1,0:T(8,128)(2,1)S(1)}, bf16[48,2048]{1,0:T(8,128)(2,1)S(1)}, u32[]{:S(2)}, u32[]{:S(2)}) %collective-permute-start.6) | collective-permute-done | bytes 196640 | tf_op jit(solution)/shard_map/ppermute | solution.py:439
  25.1 2.8 %experts.1 = (bf16[48,2048]{1,0:T(8,128)(2,1)S(1)}, bf16[48,2048]{1,0:T(8,128)(2,1)S(1)}, bf16[96,2048]{1,0:T(8,128)(2,1)S(1)}, bf16[96,2048]{1,0:T(8,128)(2,1)S...) custom-call(bf16[2048,768]{1,0:T(8,128)(2,1)S(1)} %get-tuple-element.68.gate_ref, ...), custom_call_target="tpu_custom_call" | custom-call | flops 1811939328 | bytes 8945664 | tf_op jit(solution)/shard_map/experts/pallas_call | solution.py:420
  28.0 0.4 collective-permute-start.11
  28.4 1.7 %collective-permute-start.12 = (bf16[96,2048]{1,0:T(8,128)(2,1)S(1)}, bf16[96,2048]{1,0:T(8,128)(2,1)S(1)}, u32[]{:S(2)}, u32[]{:S(2)}) collective-permute-start(bf16[96,2048]{1,0:T(8,128)(2,1)S(1)} %get-tuple-element.81.refs_6_), channel_id=1, source_target_pairs={{0,8},{4,12},{8,0},{12,4},{1,9},{5,13},{9,1},{13,5},{2,10},{6,14},... | collective-permute-start | bytes 1179656 | tf_op jit(solution)/shard_map/ppermute | solution.py:439
  30.1 1.4 %collective-permute-start.13 = (bf16[48,2048]{1,0:T(8,128)(2,1)S(1)}, bf16[48,2048]{1,0:T(8,128)(2,1)S(1)}, u32[]{:S(2)}, u32[]{:S(2)}) collective-permute-start(bf16[48,2048]{1,0:T(8,128)(2,1)S(1)} %get-tuple-element.82.refs_7_), channel_id=1, source_target_pairs={{0,12},{4,8},{8,4},{12,0},{1,13},{5,9},{9,5},{13,1},{2,14},{6,10},... | collective-permute-start | bytes 589832 | tf_op jit(solution)/shard_map/ppermute | solution.py:439
  31.5 0.3 gain_terms.1
  31.8 1.6 %collective-permute-start.8 = (f32[16,128]{1,0:T(8,128)S(1)}, f32[16,128]{1,0:T(8,128)S(1)}, u32[]{:S(2)}, u32[]{:S(2)}) collective-permute-start(f32[16,128]{1,0:T(8,128)S(1)} %gain_terms.1), channel_id=1, source_target_pairs={{0,1},{1,0},{2,3},{3,2},{4,5},{5,4},{6,7},{7,6},{8,9},{9,8},{10,11... | collective-permute-start | bytes 24584 | tf_op jit(solution)/shard_map/ppermute | solution.py:439
  33.5 2.1 %collective-permute-done.8 = f32[16,128]{1,0:T(8,128)S(1)} collective-permute-done((f32[16,128]{1,0:T(8,128)S(1)}, f32[16,128]{1,0:T(8,128)S(1)}, u32[]{:S(2)}, u32[]{:S(2)}) %collective-permute-start.8) | collective-permute-done | bytes 8224 | tf_op jit(solution)/shard_map/ppermute | solution.py:439
  35.6 2.6 %collective-permute-start.9 = (f32[16,128]{1,0:T(8,128)S(1)}, f32[16,128]{1,0:T(8,128)S(1)}, u32[]{:S(2)}, u32[]{:S(2)}) collective-permute-start(f32[16,128]{1,0:T(8,128)S(1)} %add.17), channel_id=1, source_target_pairs={{0,2},{1,3},{2,0},{3,1},{4,6},{5,7},{6,4},{7,5},{8,10},{9,11},{10,... | collective-permute-start | bytes 24584 | tf_op jit(solution)/shard_map/ppermute | solution.py:439
  38.2 1.9 %collective-permute-done.9 = f32[16,128]{1,0:T(8,128)S(1)} collective-permute-done((f32[16,128]{1,0:T(8,128)S(1)}, f32[16,128]{1,0:T(8,128)S(1)}, u32[]{:S(2)}, u32[]{:S(2)}) %collective-permute-start.9) | collective-permute-done | bytes 8224 | tf_op jit(solution)/shard_map/ppermute | solution.py:439
  40.1 1.2 %collective-permute-done.10 = f32[16,128]{1,0:T(8,128)S(1)} collective-permute-done((f32[16,128]{1,0:T(8,128)S(1)}, f32[16,128]{1,0:T(8,128)S(1)}, u32[]{:S(2)}, u32[]{:S(2)}) %collective-permute-start.10) | collective-permute-done | bytes 8224 | tf_op jit(solution)/shard_map/ppermute | solution.py:439
  41.3 1.5 %collective-permute-start.14 = (f32[16,128]{1,0:T(8,128)S(1)}, f32[16,128]{1,0:T(8,128)S(1)}, u32[]{:S(2)}, u32[]{:S(2)}) collective-permute-start(f32[16,128]{1,0:T(8,128)S(1)} %add.19), channel_id=1, source_target_pairs={{0,8},{4,12},{8,0},{12,4},{1,9},{5,13},{9,1},{13,5},{2,10},{6,14},... | collective-permute-start | bytes 24584 | tf_op jit(solution)/shard_map/ppermute | solution.py:439
  42.8 0.3 collective-permute-start.16
  43.1 0.3 collective-permute-done.13.refs_7_
  43.4 2.1 %residual_and_first_group.1 = (bf16[128,2048]{1,0:T(8,128)(2,1)}, bf16[128,1024]{1,0:T(8,128)(2,1)S(1)}, bf16[128,1024]{1,0:T(8,128)(2,1)S(1)}, f32[128,256]{1,0:T(8,128)S(1)}, bf16[128,256]{1,0:T(8,128)(2,1)S(1)}) custom-call(bf16[128,192]{1,0:T(8,128)(2,1)S(1)} %get-tuple-element.66.place_ref, f32[1,2048]{1,0:T(1,128)S(1)} %get-tuple-element.71.gain_ref, ...), custom_call_target="tpu_custom_call" | custom-call | flops 4000000000 | bytes 6414336 | tf_op jit(solution)/shard_map/residual_and_first_group/pallas_call | solution.py:420
  45.5 1.5 %collective-permute-start.15 = (f32[32,128]{1,0:T(8,128)S(1)}, f32[32,128]{1,0:T(8,128)S(1)}, u32[]{:S(2)}, u32[]{:S(2)}) collective-permute-start(f32[32,128]{1,0:T(8,128)S(1)} %pad.4), channel_id=1, source_target_pairs={{0,4},{4,0},{8,12},{12,8},{1,5},{5,1},{9,13},{13,9},{2,6},{6,2},{1... | collective-permute-start | bytes 49160 | tf_op jit(solution)/shard_map/ppermute | solution.py:439
  47.0 1.5 %second_group.1 = (bf16[128,1024]{1,0:T(8,128)(2,1)S(1)}, f32[128,256]{1,0:T(8,128)S(1)}, bf16[128,512]{1,0:T(8,128)(2,1)S(1)}) custom-call(bf16[128,2048]{1,0:T(8,128)(2,1)S(1)} %get-tuple-element.60.query_ref, f32[8,256,256]{2,1,0:T(8,128)S(1)} %get-tuple-element.86.probs_ref, bf16[128,1024]{1,0:T(8,128)(2,1)S(1)} %get-tuple-element.90.rest_ref, ...), custom_call_target="tpu_custom_call" | custom-call | tf_op jit(solution)/shard_map/second_group/pallas_call | solution.py:420
  48.5 2.1 %collective-permute-done.16.refs_8_ = bf16[48,2048]{1,0:T(8,128)(2,1)S(1)} collective-permute-done((bf16[48,2048]{1,0:T(8,128)(2,1)S(1)}, bf16[48,2048]{1,0:T(8,128)(2,1)S(1)}, u32[]{:S(2)}, u32[]{:S(2)}) %collective-permute-start.16) | collective-permute-done | bytes 196640 | tf_op jit(solution)/shard_map/ppermute | solution.py:439
  50.6 1.3 %collective-permute-done.17.refs_4_ = bf16[128,512]{1,0:T(8,128)(2,1)S(1)} collective-permute-done((bf16[128,512]{1,0:T(8,128)(2,1)S(1)}, bf16[128,512]{1,0:T(8,128)(2,1)S(1)}, u32[]{:S(2)}, u32[]{:S(2)}) %collective-permute-start.17) | collective-permute-done | bytes 131104 | tf_op jit(solution)/shard_map/ppermute | solution.py:439
  51.9 1.2 %layer_output.1 = (bf16[128,2048]{1,0:T(8,128)(2,1)}, bf16[128,2048]{1,0:T(8,128)(2,1)}, bf16[128,256]{1,0:T(8,128)(2,1)}, bf16[128,256]{1,0:T(8,128)(2,1)}, f32[1,128]{1,0:T(1,128)}, /*index=5*/f32[16,128]{1,0:T(8,128)}) custom-call(bf16[128,192]{1,0:T(8,128)(2,1)S(1)} %get-tuple-element.66.place_ref, f32[128,256]{1,0:T(8,128)S(1)} %get-tuple-element.67.weight_ref, ...), custom_call_target="tpu_custom_call" | custom-call | flops 100663296 | bytes 4522496 | tf_op jit(solution)/shard_map/layer_output/pallas_call | solution.py:420
  (18 shorter events, 0.1 us)
Async XLA Ops:
  2.2 10.0 %collective-permute-start.1 = (bf16[48,2048]{1,0:T(8,128)(2,1)S(1)}, bf16[48,2048]{1,0:T(8,128)(2,1)S(1)}, u32[]{:S(2)}, u32[]{:S(2)}) collective-permute-start(bf16[48,2048]{1,0:T(8,128)(2,1)S(1)} %get-tuple-element.63), channel_id=1, source_target_pairs={{0,4},{4,0},{8,12},{12,8},{1,5},{5,1},{9,13},{13,9},{2,6},{6,2},{1... | collective-permute-start | bytes 589832 | tf_op jit(solution)/shard_map/ppermute | solution.py:439
  5.2 2.1 %collective-permute-start = (bf16[128,256]{1,0:T(8,128)(2,1)}, bf16[128,256]{1,0:T(8,128)(2,1)S(1)}, u32[]{:S(2)}, u32[]{:S(2)}) collective-permute-start(bf16[128,256]{1,0:T(8,128)(2,1)} %bitcast.17), channel_id=1, source_target_pairs={{0,16},{16,0},{1,17},{17,1},{2,18},{18,2},{3,19},{19,3},{4,20},{20... | collective-permute-start | bytes 196616 | tf_op jit(solution)/shard_map/ppermute | solution.py:439
  5.2 2.1 %collective-permute-start.4 = (bf16[128,256]{1,0:T(8,128)(2,1)}, bf16[128,256]{1,0:T(8,128)(2,1)S(1)}, u32[]{:S(2)}, u32[]{:S(2)}) collective-permute-start(bf16[128,256]{1,0:T(8,128)(2,1)} %bitcast.19), channel_id=1, source_target_pairs={{0,16},{16,0},{1,17},{17,1},{2,18},{18,2},{3,19},{19,3},{4,20},{20... | collective-permute-start | bytes 196616 | tf_op jit(solution)/shard_map/ppermute | solution.py:439
  5.7 12.0 %collective-permute-start.2 = (bf16[48,2048]{1,0:T(8,128)(2,1)S(1)}, bf16[48,2048]{1,0:T(8,128)(2,1)S(1)}, u32[]{:S(2)}, u32[]{:S(2)}) collective-permute-start(bf16[48,2048]{1,0:T(8,128)(2,1)S(1)} %get-tuple-element.64), channel_id=1, source_target_pairs={{0,8},{4,12},{8,0},{12,4},{1,9},{5,13},{9,1},{13,5},{2,10},{6,14},... | collective-permute-start | bytes 589832 | tf_op jit(solution)/shard_map/ppermute | solution.py:439
  7.2 10.5 %collective-permute-start.3 = (bf16[48,2048]{1,0:T(8,128)(2,1)S(1)}, bf16[48,2048]{1,0:T(8,128)(2,1)S(1)}, u32[]{:S(2)}, u32[]{:S(2)}) collective-permute-start(bf16[48,2048]{1,0:T(8,128)(2,1)S(1)} %get-tuple-element.65), channel_id=1, source_target_pairs={{0,12},{4,8},{8,4},{12,0},{1,13},{5,9},{9,5},{13,1},{2,14},{6,10},... | collective-permute-start | bytes 589832 | tf_op jit(solution)/shard_map/ppermute | solution.py:439
  8.7 12.8 %collective-permute-start.5 = (bf16[48,2048]{1,0:T(8,128)(2,1)S(1)}, bf16[48,2048]{1,0:T(8,128)(2,1)S(1)}, u32[]{:S(2)}, u32[]{:S(2)}) collective-permute-start(bf16[48,2048]{1,0:T(8,128)(2,1)S(1)} %get-tuple-element.75), channel_id=1, source_target_pairs={{0,4},{4,0},{8,12},{12,8},{1,5},{5,1},{9,13},{13,9},{2,6},{6,2},{1... | collective-permute-start | bytes 589832 | tf_op jit(solution)/shard_map/ppermute | solution.py:439
  10.7 14.5 %collective-permute-start.6 = (bf16[48,2048]{1,0:T(8,128)(2,1)S(1)}, bf16[48,2048]{1,0:T(8,128)(2,1)S(1)}, u32[]{:S(2)}, u32[]{:S(2)}) collective-permute-start(bf16[48,2048]{1,0:T(8,128)(2,1)S(1)} %get-tuple-element.76), channel_id=1, source_target_pairs={{0,8},{4,12},{8,0},{12,4},{1,9},{5,13},{9,1},{13,5},{2,10},{6,14},... | collective-permute-start | bytes 589832 | tf_op jit(solution)/shard_map/ppermute | solution.py:439
  12.2 12.9 %collective-permute-start.7 = (bf16[48,2048]{1,0:T(8,128)(2,1)S(1)}, bf16[48,2048]{1,0:T(8,128)(2,1)S(1)}, u32[]{:S(2)}, u32[]{:S(2)}) collective-permute-start(bf16[48,2048]{1,0:T(8,128)(2,1)S(1)} %get-tuple-element.77), channel_id=1, source_target_pairs={{0,12},{4,8},{8,4},{12,0},{1,13},{5,9},{9,5},{13,1},{2,14},{6,10},... | collective-permute-start | bytes 589832 | tf_op jit(solution)/shard_map/ppermute | solution.py:439
  28.0 15.4 %collective-permute-start.11 = (bf16[96,2048]{1,0:T(8,128)(2,1)S(1)}, bf16[96,2048]{1,0:T(8,128)(2,1)S(1)}, u32[]{:S(2)}, u32[]{:S(2)}) collective-permute-start(bf16[96,2048]{1,0:T(8,128)(2,1)S(1)} %get-tuple-element.80.refs_5_), channel_id=1, source_target_pairs={{0,4},{4,0},{8,12},{12,8},{1,5},{5,1},{9,13},{13,9},{2,6},{6,2},{1... | collective-permute-start | bytes 1179656 | tf_op jit(solution)/shard_map/ppermute | solution.py:439
  28.4 15.0 %collective-permute-start.12 = (bf16[96,2048]{1,0:T(8,128)(2,1)S(1)}, bf16[96,2048]{1,0:T(8,128)(2,1)S(1)}, u32[]{:S(2)}, u32[]{:S(2)}) collective-permute-start(bf16[96,2048]{1,0:T(8,128)(2,1)S(1)} %get-tuple-element.81.refs_6_), channel_id=1, source_target_pairs={{0,8},{4,12},{8,0},{12,4},{1,9},{5,13},{9,1},{13,5},{2,10},{6,14},... | collective-permute-start | bytes 1179656 | tf_op jit(solution)/shard_map/ppermute | solution.py:439
  30.1 13.3 %collective-permute-start.13 = (bf16[48,2048]{1,0:T(8,128)(2,1)S(1)}, bf16[48,2048]{1,0:T(8,128)(2,1)S(1)}, u32[]{:S(2)}, u32[]{:S(2)}) collective-permute-start(bf16[48,2048]{1,0:T(8,128)(2,1)S(1)} %get-tuple-element.82.refs_7_), channel_id=1, source_target_pairs={{0,12},{4,8},{8,4},{12,0},{1,13},{5,9},{9,5},{13,1},{2,14},{6,10},... | collective-permute-start | bytes 589832 | tf_op jit(solution)/shard_map/ppermute | solution.py:439
  31.8 3.7 %collective-permute-start.8 = (f32[16,128]{1,0:T(8,128)S(1)}, f32[16,128]{1,0:T(8,128)S(1)}, u32[]{:S(2)}, u32[]{:S(2)}) collective-permute-start(f32[16,128]{1,0:T(8,128)S(1)} %gain_terms.1), channel_id=1, source_target_pairs={{0,1},{1,0},{2,3},{3,2},{4,5},{5,4},{6,7},{7,6},{8,9},{9,8},{10,11... | collective-permute-start | bytes 24584 | tf_op jit(solution)/shard_map/ppermute | solution.py:439
  35.6 4.5 %collective-permute-start.9 = (f32[16,128]{1,0:T(8,128)S(1)}, f32[16,128]{1,0:T(8,128)S(1)}, u32[]{:S(2)}, u32[]{:S(2)}) collective-permute-start(f32[16,128]{1,0:T(8,128)S(1)} %add.17), channel_id=1, source_target_pairs={{0,2},{1,3},{2,0},{3,1},{4,6},{5,7},{6,4},{7,5},{8,10},{9,11},{10,... | collective-permute-start | bytes 24584 | tf_op jit(solution)/shard_map/ppermute | solution.py:439
  40.1 1.2 %collective-permute-start.10 = (f32[16,128]{1,0:T(8,128)S(1)}, f32[16,128]{1,0:T(8,128)S(1)}, u32[]{:S(2)}, u32[]{:S(2)}) collective-permute-start(f32[16,128]{1,0:T(8,128)S(1)} %add.18), channel_id=1, source_target_pairs={{0,16},{16,0},{1,17},{17,1},{2,18},{18,2},{3,19},{19,3},{4,20},{20... | collective-permute-start | bytes 24584 | tf_op jit(solution)/shard_map/ppermute | solution.py:439
  41.3 4.2 %collective-permute-start.14 = (f32[16,128]{1,0:T(8,128)S(1)}, f32[16,128]{1,0:T(8,128)S(1)}, u32[]{:S(2)}, u32[]{:S(2)}) collective-permute-start(f32[16,128]{1,0:T(8,128)S(1)} %add.19), channel_id=1, source_target_pairs={{0,8},{4,12},{8,0},{12,4},{1,9},{5,13},{9,1},{13,5},{2,10},{6,14},... | collective-permute-start | bytes 24584 | tf_op jit(solution)/shard_map/ppermute | solution.py:439
  42.8 7.8 %collective-permute-start.16 = (bf16[48,2048]{1,0:T(8,128)(2,1)S(1)}, bf16[48,2048]{1,0:T(8,128)(2,1)S(1)}, u32[]{:S(2)}, u32[]{:S(2)}) collective-permute-start(bf16[48,2048]{1,0:T(8,128)(2,1)S(1)} %get-tuple-element.95), channel_id=1, source_target_pairs={{0,12},{4,8},{8,4},{12,0},{1,13},{5,9},{9,5},{13,1},{2,14},{6,10},... | collective-permute-start | bytes 589832 | tf_op jit(solution)/shard_map/ppermute | solution.py:439
  45.5 5.1 %collective-permute-start.15 = (f32[32,128]{1,0:T(8,128)S(1)}, f32[32,128]{1,0:T(8,128)S(1)}, u32[]{:S(2)}, u32[]{:S(2)}) collective-permute-start(f32[32,128]{1,0:T(8,128)S(1)} %pad.4), channel_id=1, source_target_pairs={{0,4},{4,0},{8,12},{12,8},{1,5},{5,1},{9,13},{13,9},{2,6},{6,2},{1... | collective-permute-start | bytes 49160 | tf_op jit(solution)/shard_map/ppermute | solution.py:439
  50.6 1.3 %collective-permute-start.17 = (bf16[128,512]{1,0:T(8,128)(2,1)S(1)}, bf16[128,512]{1,0:T(8,128)(2,1)S(1)}, u32[]{:S(2)}, u32[]{:S(2)}) collective-permute-start(bf16[128,512]{1,0:T(8,128)(2,1)S(1)} %get-tuple-element.97), channel_id=1, source_target_pairs={{0,16},{16,0},{1,17},{17,1},{2,18},{18,2},{3,19},{19,3},{4,20},{20... | collective-permute-start | bytes 393224 | tf_op jit(solution)/shard_map/ppermute | solution.py:439

commit v13 on v12

--- a/solution.py
+++ b/solution.py
@@ -592,10 +592,11 @@
         placed(VMEM, [shaped((GAIN_LINES, LANES), F32)]),
         2 * slots * D,
     )
-    terms = sum_over(sum_over(terms, "dp"), "ctx")
+    terms = sum_over(terms, "dp")
     send_far, terms = lax.optimization_barrier(([send_y[s] for s in far], terms))
     for s, piece in zip(far, send_far):
         y[s] = pairwise(piece, "exp", s)
+    terms = sum_over(terms, "ctx")
     beside = pairwise(terms, "exp", FIRST)
 
     half_shape = shaped((tokens, D // 2), BF16)

time: 53.3 us -> 53.6 us (level)
  transfers between devices with their start and end apart: 18 -> 18, of which waited for: 8 -> 7; matrix products, arithmetic and copies ran while one was open for 0% -> 0% of each run, Pallas kernels for 17% -> 17%
where the time goes in v13:
time: 53.6 us; the launch traced here: 53.5 us
  starting transfers between devices  21.2 us (40%)
  waiting for transfers between devices  16.8 us (31%)
  Pallas kernels  14.7 us (27%)
  between operations  0.72 us (1%)
    ppermute x18, starting transfers between devices, pairwise(): return lax.ppermute(value, axis, [(i, i ^ step) for i in range(count)])  21.2 us
    ppermute x18, waiting for transfers between devices, pairwise(): return lax.ppermute(value, axis, [(i, i ^ step) for i in range(count)])  16.8 us
    pallas_call x8, Pallas kernels, run(): pl.pallas_call(kernel, out_shape=[x for _, x in outputs], in_specs=[spec[...  14.7 us
  transfers between devices with their start and end apart: 18, of which 7 were waited for; matrix products, arithmetic and copies ran while one was open for 0% of the time, Pallas kernels for 17%

profile of v13, /device:TPU:0, one launch (start us, length us, event | category | flops | bytes accessed | tf_op | source)
XLA Modules:
  0.0 53.5 jit_solution(11572001418665196069)
XLA Ops:
  0.6 1.5 %dispatch_grads.1 = (bf16[128,2048]{1,0:T(8,128)(2,1)S(1)}, bf16[128,256]{1,0:T(8,128)(2,1)S(1)}, bf16[128,256]{1,0:T(8,128)(2,1)S(1)}, f32[1,2048]{1,0:T(1,128)...) custom-call(bf16[128,2048]{1,0:T(8,128)(2,1)} %bitcast.13, ...), custom_call_target="tpu_custom_call" | custom-call | flops 100663296 | bytes 4213824 | tf_op jit(solution)/shard_map/dispatch_grads/pallas_call | solution.py:420
  2.2 3.0 %collective-permute-start.1 = (bf16[48,2048]{1,0:T(8,128)(2,1)S(1)}, bf16[48,2048]{1,0:T(8,128)(2,1)S(1)}, u32[]{:S(2)}, u32[]{:S(2)}) collective-permute-start(bf16[48,2048]{1,0:T(8,128)(2,1)S(1)} %get-tuple-element.63), channel_id=1, source_target_pairs={{0,4},{4,0},{8,12},{12,8},{1,5},{5,1},{9,13},{13,9},{2,6},{6,2},{1... | collective-permute-start | bytes 589832 | tf_op jit(solution)/shard_map/ppermute | solution.py:439
  5.2 0.5 collective-permute-start.4
  5.7 1.5 %collective-permute-start.2 = (bf16[48,2048]{1,0:T(8,128)(2,1)S(1)}, bf16[48,2048]{1,0:T(8,128)(2,1)S(1)}, u32[]{:S(2)}, u32[]{:S(2)}) collective-permute-start(bf16[48,2048]{1,0:T(8,128)(2,1)S(1)} %get-tuple-element.64), channel_id=1, source_target_pairs={{0,8},{4,12},{8,0},{12,4},{1,9},{5,13},{9,1},{13,5},{2,10},{6,14},... | collective-permute-start | bytes 589832 | tf_op jit(solution)/shard_map/ppermute | solution.py:439
  7.2 0.0 collective-permute-start.3
  7.2 0.0 collective-permute-done.refs_1_
  7.2 1.4 %attention_forward.1 = (bf16[128,2048]{1,0:T(8,128)(2,1)S(1)}, bf16[48,2048]{1,0:T(8,128)(2,1)S(1)}, bf16[48,2048]{1,0:T(8,128)(2,1)S(1)}, bf16[48,2048]{1,0:T(8,128)(2,1)S(1)}, bf16[48,2048]{1,0:T(8,128)(2,1)S(1)}) custom-call(s32[2,128]{1,0:T(2,128)S(1)} %get-tuple-element.57.pos_ref, s32[1,128]{1,0:T(1,128)S(1)} %get-tuple-element.58.slot_ref, ...), custom_call_target="tpu_custom_call" | custom-call | flops 369098752 | bytes 2631168 | tf_op jit(solution)/shard_map/attention_forward/pallas_call | solution.py:420
  8.7 2.0 %collective-permute-start.5 = (bf16[48,2048]{1,0:T(8,128)(2,1)S(1)}, bf16[48,2048]{1,0:T(8,128)(2,1)S(1)}, u32[]{:S(2)}, u32[]{:S(2)}) collective-permute-start(bf16[48,2048]{1,0:T(8,128)(2,1)S(1)} %get-tuple-element.75), channel_id=1, source_target_pairs={{0,4},{4,0},{8,12},{12,8},{1,5},{5,1},{9,13},{13,9},{2,6},{6,2},{1... | collective-permute-start | bytes 589832 | tf_op jit(solution)/shard_map/ppermute | solution.py:439
  10.7 1.5 %collective-permute-start.6 = (bf16[48,2048]{1,0:T(8,128)(2,1)S(1)}, bf16[48,2048]{1,0:T(8,128)(2,1)S(1)}, u32[]{:S(2)}, u32[]{:S(2)}) collective-permute-start(bf16[48,2048]{1,0:T(8,128)(2,1)S(1)} %get-tuple-element.76), channel_id=1, source_target_pairs={{0,8},{4,12},{8,0},{12,4},{1,9},{5,13},{9,1},{13,5},{2,10},{6,14},... | collective-permute-start | bytes 589832 | tf_op jit(solution)/shard_map/ppermute | solution.py:439
  12.2 1.7 %collective-permute-start.7 = (bf16[48,2048]{1,0:T(8,128)(2,1)S(1)}, bf16[48,2048]{1,0:T(8,128)(2,1)S(1)}, u32[]{:S(2)}, u32[]{:S(2)}) collective-permute-start(bf16[48,2048]{1,0:T(8,128)(2,1)S(1)} %get-tuple-element.77), channel_id=1, source_target_pairs={{0,12},{4,8},{8,4},{12,0},{1,13},{5,9},{9,5},{13,1},{2,14},{6,10},... | collective-permute-start | bytes 589832 | tf_op jit(solution)/shard_map/ppermute | solution.py:439
  13.9 3.7 %collective-permute-done.2.refs_4_ = bf16[48,2048]{1,0:T(8,128)(2,1)S(1)} collective-permute-done((bf16[48,2048]{1,0:T(8,128)(2,1)S(1)}, bf16[48,2048]{1,0:T(8,128)(2,1)S(1)}, u32[]{:S(2)}, u32[]{:S(2)}) %collective-permute-start.2) | collective-permute-done | bytes 196640 | tf_op jit(solution)/shard_map/ppermute | solution.py:439
  17.7 3.8 %act_grads_and_probs.1 = (f32[192,384]{1,0:T(8,128)S(1)}, f32[8,256,256]{2,1,0:T(8,128)S(1)}, bf16[768,2048]{1,0:T(8,128)(2,1)S(1)}, bf16[2048,768]{1,0:T(8,128)...) custom-call(s32[2,128]{1,0:T(2,128)S(1)} %get-tuple-element.57.pos_ref, ...), custom_call_target="tpu_custom_call" | custom-call | flops 738197504 | bytes 16599040 | tf_op jit(solution)/shard_map/act_grads_and_probs/pallas_call | solution.py:420
  21.5 3.6 %collective-permute-done.6.refs_2_ = bf16[48,2048]{1,0:T(8,128)(2,1)S(1)} collective-permute-done((bf16[48,2048]{1,0:T(8,128)(2,1)S(1)}, bf16[48,2048]{1,0:T(8,128)(2,1)S(1)}, u32[]{:S(2)}, u32[]{:S(2)}) %collective-permute-start.6) | collective-permute-done | bytes 196640 | tf_op jit(solution)/shard_map/ppermute | solution.py:439
  25.1 2.8 %experts.1 = (bf16[48,2048]{1,0:T(8,128)(2,1)S(1)}, bf16[48,2048]{1,0:T(8,128)(2,1)S(1)}, bf16[96,2048]{1,0:T(8,128)(2,1)S(1)}, bf16[96,2048]{1,0:T(8,128)(2,1)S...) custom-call(bf16[2048,768]{1,0:T(8,128)(2,1)S(1)} %get-tuple-element.68.gate_ref, ...), custom_call_target="tpu_custom_call" | custom-call | flops 1811939328 | bytes 8945664 | tf_op jit(solution)/shard_map/experts/pallas_call | solution.py:420
  28.0 0.4 collective-permute-start.11
  28.4 1.7 %collective-permute-start.12 = (bf16[96,2048]{1,0:T(8,128)(2,1)S(1)}, bf16[96,2048]{1,0:T(8,128)(2,1)S(1)}, u32[]{:S(2)}, u32[]{:S(2)}) collective-permute-start(bf16[96,2048]{1,0:T(8,128)(2,1)S(1)} %get-tuple-element.81.refs_6_), channel_id=1, source_target_pairs={{0,8},{4,12},{8,0},{12,4},{1,9},{5,13},{9,1},{13,5},{2,10},{6,14},... | collective-permute-start | bytes 1179656 | tf_op jit(solution)/shard_map/ppermute | solution.py:439
  30.1 1.4 %collective-permute-start.13 = (bf16[48,2048]{1,0:T(8,128)(2,1)S(1)}, bf16[48,2048]{1,0:T(8,128)(2,1)S(1)}, u32[]{:S(2)}, u32[]{:S(2)}) collective-permute-start(bf16[48,2048]{1,0:T(8,128)(2,1)S(1)} %get-tuple-element.82.refs_7_), channel_id=1, source_target_pairs={{0,12},{4,8},{8,4},{12,0},{1,13},{5,9},{9,5},{13,1},{2,14},{6,10},... | collective-permute-start | bytes 589832 | tf_op jit(solution)/shard_map/ppermute | solution.py:439
  31.5 0.3 gain_terms.1
  31.8 1.6 %collective-permute-start.8 = (f32[16,128]{1,0:T(8,128)S(1)}, f32[16,128]{1,0:T(8,128)S(1)}, u32[]{:S(2)}, u32[]{:S(2)}) collective-permute-start(f32[16,128]{1,0:T(8,128)S(1)} %gain_terms.1), channel_id=1, source_target_pairs={{0,1},{1,0},{2,3},{3,2},{4,5},{5,4},{6,7},{7,6},{8,9},{9,8},{10,11... | collective-permute-start | bytes 24584 | tf_op jit(solution)/shard_map/ppermute | solution.py:439
  33.5 2.1 %collective-permute-done.8 = f32[16,128]{1,0:T(8,128)S(1)} collective-permute-done((f32[16,128]{1,0:T(8,128)S(1)}, f32[16,128]{1,0:T(8,128)S(1)}, u32[]{:S(2)}, u32[]{:S(2)}) %collective-permute-start.8) | collective-permute-done | bytes 8224 | tf_op jit(solution)/shard_map/ppermute | solution.py:439
  35.6 2.6 %collective-permute-start.9 = (f32[16,128]{1,0:T(8,128)S(1)}, f32[16,128]{1,0:T(8,128)S(1)}, u32[]{:S(2)}, u32[]{:S(2)}) collective-permute-start(f32[16,128]{1,0:T(8,128)S(1)} %add.17), channel_id=1, source_target_pairs={{0,2},{1,3},{2,0},{3,1},{4,6},{5,7},{6,4},{7,5},{8,10},{9,11},{10,... | collective-permute-start | bytes 24584 | tf_op jit(solution)/shard_map/ppermute | solution.py:439
  38.2 1.9 %collective-permute-done.9 = f32[16,128]{1,0:T(8,128)S(1)} collective-permute-done((f32[16,128]{1,0:T(8,128)S(1)}, f32[16,128]{1,0:T(8,128)S(1)}, u32[]{:S(2)}, u32[]{:S(2)}) %collective-permute-start.9) | collective-permute-done | bytes 8224 | tf_op jit(solution)/shard_map/ppermute | solution.py:439
  40.1 1.5 %collective-permute-start.16 = (bf16[48,2048]{1,0:T(8,128)(2,1)S(1)}, bf16[48,2048]{1,0:T(8,128)(2,1)S(1)}, u32[]{:S(2)}, u32[]{:S(2)}) collective-permute-start(bf16[48,2048]{1,0:T(8,128)(2,1)S(1)} %get-tuple-element.95), channel_id=1, source_target_pairs={{0,12},{4,8},{8,4},{12,0},{1,13},{5,9},{9,5},{13,1},{2,14},{6,10},... | collective-permute-start | bytes 589832 | tf_op jit(solution)/shard_map/ppermute | solution.py:439
  41.6 1.2 %collective-permute-start.14 = (f32[16,128]{1,0:T(8,128)S(1)}, f32[16,128]{1,0:T(8,128)S(1)}, u32[]{:S(2)}, u32[]{:S(2)}) collective-permute-start(f32[16,128]{1,0:T(8,128)S(1)} %add.19), channel_id=1, source_target_pairs={{0,8},{4,12},{8,0},{12,4},{1,9},{5,13},{9,1},{13,5},{2,10},{6,14},... | collective-permute-start | bytes 24584 | tf_op jit(solution)/shard_map/ppermute | solution.py:439
  42.8 0.6 %collective-permute-done.13.refs_7_ = bf16[48,2048]{1,0:T(8,128)(2,1)S(1)} collective-permute-done((bf16[48,2048]{1,0:T(8,128)(2,1)S(1)}, bf16[48,2048]{1,0:T(8,128)(2,1)S(1)}, u32[]{:S(2)}, u32[]{:S(2)}) %collective-permute-start.13) | collective-permute-done | bytes 196640 | tf_op jit(solution)/shard_map/ppermute | solution.py:439
  43.4 2.1 %residual_and_first_group.1 = (bf16[128,2048]{1,0:T(8,128)(2,1)}, bf16[128,1024]{1,0:T(8,128)(2,1)S(1)}, bf16[128,1024]{1,0:T(8,128)(2,1)S(1)}, f32[128,256]{1,0:T(8,128)S(1)}, bf16[128,256]{1,0:T(8,128)(2,1)S(1)}) custom-call(bf16[128,192]{1,0:T(8,128)(2,1)S(1)} %get-tuple-element.66.place_ref, f32[1,2048]{1,0:T(1,128)S(1)} %get-tuple-element.71.gain_ref, ...), custom_call_target="tpu_custom_call" | custom-call | flops 4000000000 | bytes 6414336 | tf_op jit(solution)/shard_map/residual_and_first_group/pallas_call | solution.py:420
  45.5 3.0 %collective-permute-done.14 = f32[16,128]{1,0:T(8,128)S(1)} collective-permute-done((f32[16,128]{1,0:T(8,128)S(1)}, f32[16,128]{1,0:T(8,128)S(1)}, u32[]{:S(2)}, u32[]{:S(2)}) %collective-permute-start.14) | collective-permute-done | bytes 8224 | tf_op jit(solution)/shard_map/ppermute | solution.py:439
  48.5 0.3 collective-permute-start.15
  48.8 1.5 %second_group.1 = (bf16[128,1024]{1,0:T(8,128)(2,1)S(1)}, f32[128,256]{1,0:T(8,128)S(1)}, bf16[128,512]{1,0:T(8,128)(2,1)S(1)}) custom-call(bf16[128,2048]{1,0:T(8,128)(2,1)S(1)} %get-tuple-element.60.query_ref, f32[8,256,256]{2,1,0:T(8,128)S(1)} %get-tuple-element.86.probs_ref, bf16[128,1024]{1,0:T(8,128)(2,1)S(1)} %get-tuple-element.90.rest_ref, ...), custom_call_target="tpu_custom_call" | custom-call | tf_op jit(solution)/shard_map/second_group/pallas_call | solution.py:420
  50.4 0.1 collective-permute-start.17
  50.5 1.8 %collective-permute-done.15 = f32[32,128]{1,0:T(8,128)S(1)} collective-permute-done((f32[32,128]{1,0:T(8,128)S(1)}, f32[32,128]{1,0:T(8,128)S(1)}, u32[]{:S(2)}, u32[]{:S(2)}) %collective-permute-start.15) | collective-permute-done | bytes 16416 | tf_op jit(solution)/shard_map/ppermute | solution.py:439
  52.3 1.2 %layer_output.1 = (bf16[128,2048]{1,0:T(8,128)(2,1)}, bf16[128,2048]{1,0:T(8,128)(2,1)}, bf16[128,256]{1,0:T(8,128)(2,1)}, bf16[128,256]{1,0:T(8,128)(2,1)}, f32[1,128]{1,0:T(1,128)}, /*index=5*/f32[16,128]{1,0:T(8,128)}) custom-call(bf16[128,192]{1,0:T(8,128)(2,1)S(1)} %get-tuple-element.66.place_ref, f32[128,256]{1,0:T(8,128)S(1)} %get-tuple-element.67.weight_ref, ...), custom_call_target="tpu_custom_call" | custom-call | flops 100663296 | bytes 4522496 | tf_op jit(solution)/shard_map/layer_output/pallas_call | solution.py:420
  (18 shorter events, 0.1 us)
Async XLA Ops:
  2.2 10.0 %collective-permute-start.1 = (bf16[48,2048]{1,0:T(8,128)(2,1)S(1)}, bf16[48,2048]{1,0:T(8,128)(2,1)S(1)}, u32[]{:S(2)}, u32[]{:S(2)}) collective-permute-start(bf16[48,2048]{1,0:T(8,128)(2,1)S(1)} %get-tuple-element.63), channel_id=1, source_target_pairs={{0,4},{4,0},{8,12},{12,8},{1,5},{5,1},{9,13},{13,9},{2,6},{6,2},{1... | collective-permute-start | bytes 589832 | tf_op jit(solution)/shard_map/ppermute | solution.py:439
  5.2 2.1 %collective-permute-start = (bf16[128,256]{1,0:T(8,128)(2,1)}, bf16[128,256]{1,0:T(8,128)(2,1)S(1)}, u32[]{:S(2)}, u32[]{:S(2)}) collective-permute-start(bf16[128,256]{1,0:T(8,128)(2,1)} %bitcast.17), channel_id=1, source_target_pairs={{0,16},{16,0},{1,17},{17,1},{2,18},{18,2},{3,19},{19,3},{4,20},{20... | collective-permute-start | bytes 196616 | tf_op jit(solution)/shard_map/ppermute | solution.py:439
  5.2 2.1 %collective-permute-start.4 = (bf16[128,256]{1,0:T(8,128)(2,1)}, bf16[128,256]{1,0:T(8,128)(2,1)S(1)}, u32[]{:S(2)}, u32[]{:S(2)}) collective-permute-start(bf16[128,256]{1,0:T(8,128)(2,1)} %bitcast.19), channel_id=1, source_target_pairs={{0,16},{16,0},{1,17},{17,1},{2,18},{18,2},{3,19},{19,3},{4,20},{20... | collective-permute-start | bytes 196616 | tf_op jit(solution)/shard_map/ppermute | solution.py:439
  5.7 12.0 %collective-permute-start.2 = (bf16[48,2048]{1,0:T(8,128)(2,1)S(1)}, bf16[48,2048]{1,0:T(8,128)(2,1)S(1)}, u32[]{:S(2)}, u32[]{:S(2)}) collective-permute-start(bf16[48,2048]{1,0:T(8,128)(2,1)S(1)} %get-tuple-element.64), channel_id=1, source_target_pairs={{0,8},{4,12},{8,0},{12,4},{1,9},{5,13},{9,1},{13,5},{2,10},{6,14},... | collective-permute-start | bytes 589832 | tf_op jit(solution)/shard_map/ppermute | solution.py:439
  7.2 10.5 %collective-permute-start.3 = (bf16[48,2048]{1,0:T(8,128)(2,1)S(1)}, bf16[48,2048]{1,0:T(8,128)(2,1)S(1)}, u32[]{:S(2)}, u32[]{:S(2)}) collective-permute-start(bf16[48,2048]{1,0:T(8,128)(2,1)S(1)} %get-tuple-element.65), channel_id=1, source_target_pairs={{0,12},{4,8},{8,4},{12,0},{1,13},{5,9},{9,5},{13,1},{2,14},{6,10},... | collective-permute-start | bytes 589832 | tf_op jit(solution)/shard_map/ppermute | solution.py:439
  8.7 12.8 %collective-permute-start.5 = (bf16[48,2048]{1,0:T(8,128)(2,1)S(1)}, bf16[48,2048]{1,0:T(8,128)(2,1)S(1)}, u32[]{:S(2)}, u32[]{:S(2)}) collective-permute-start(bf16[48,2048]{1,0:T(8,128)(2,1)S(1)} %get-tuple-element.75), channel_id=1, source_target_pairs={{0,4},{4,0},{8,12},{12,8},{1,5},{5,1},{9,13},{13,9},{2,6},{6,2},{1... | collective-permute-start | bytes 589832 | tf_op jit(solution)/shard_map/ppermute | solution.py:439
  10.7 14.5 %collective-permute-start.6 = (bf16[48,2048]{1,0:T(8,128)(2,1)S(1)}, bf16[48,2048]{1,0:T(8,128)(2,1)S(1)}, u32[]{:S(2)}, u32[]{:S(2)}) collective-permute-start(bf16[48,2048]{1,0:T(8,128)(2,1)S(1)} %get-tuple-element.76), channel_id=1, source_target_pairs={{0,8},{4,12},{8,0},{12,4},{1,9},{5,13},{9,1},{13,5},{2,10},{6,14},... | collective-permute-start | bytes 589832 | tf_op jit(solution)/shard_map/ppermute | solution.py:439
  12.2 12.9 %collective-permute-start.7 = (bf16[48,2048]{1,0:T(8,128)(2,1)S(1)}, bf16[48,2048]{1,0:T(8,128)(2,1)S(1)}, u32[]{:S(2)}, u32[]{:S(2)}) collective-permute-start(bf16[48,2048]{1,0:T(8,128)(2,1)S(1)} %get-tuple-element.77), channel_id=1, source_target_pairs={{0,12},{4,8},{8,4},{12,0},{1,13},{5,9},{9,5},{13,1},{2,14},{6,10},... | collective-permute-start | bytes 589832 | tf_op jit(solution)/shard_map/ppermute | solution.py:439
  28.0 15.4 %collective-permute-start.11 = (bf16[96,2048]{1,0:T(8,128)(2,1)S(1)}, bf16[96,2048]{1,0:T(8,128)(2,1)S(1)}, u32[]{:S(2)}, u32[]{:S(2)}) collective-permute-start(bf16[96,2048]{1,0:T(8,128)(2,1)S(1)} %get-tuple-element.80.refs_5_), channel_id=1, source_target_pairs={{0,4},{4,0},{8,12},{12,8},{1,5},{5,1},{9,13},{13,9},{2,6},{6,2},{1... | collective-permute-start | bytes 1179656 | tf_op jit(solution)/shard_map/ppermute | solution.py:439
  28.4 15.0 %collective-permute-start.12 = (bf16[96,2048]{1,0:T(8,128)(2,1)S(1)}, bf16[96,2048]{1,0:T(8,128)(2,1)S(1)}, u32[]{:S(2)}, u32[]{:S(2)}) collective-permute-start(bf16[96,2048]{1,0:T(8,128)(2,1)S(1)} %get-tuple-element.81.refs_6_), channel_id=1, source_target_pairs={{0,8},{4,12},{8,0},{12,4},{1,9},{5,13},{9,1},{13,5},{2,10},{6,14},... | collective-permute-start | bytes 1179656 | tf_op jit(solution)/shard_map/ppermute | solution.py:439
  30.1 13.3 %collective-permute-start.13 = (bf16[48,2048]{1,0:T(8,128)(2,1)S(1)}, bf16[48,2048]{1,0:T(8,128)(2,1)S(1)}, u32[]{:S(2)}, u32[]{:S(2)}) collective-permute-start(bf16[48,2048]{1,0:T(8,128)(2,1)S(1)} %get-tuple-element.82.refs_7_), channel_id=1, source_target_pairs={{0,12},{4,8},{8,4},{12,0},{1,13},{5,9},{9,5},{13,1},{2,14},{6,10},... | collective-permute-start | bytes 589832 | tf_op jit(solution)/shard_map/ppermute | solution.py:439
  31.8 3.7 %collective-permute-start.8 = (f32[16,128]{1,0:T(8,128)S(1)}, f32[16,128]{1,0:T(8,128)S(1)}, u32[]{:S(2)}, u32[]{:S(2)}) collective-permute-start(f32[16,128]{1,0:T(8,128)S(1)} %gain_terms.1), channel_id=1, source_target_pairs={{0,1},{1,0},{2,3},{3,2},{4,5},{5,4},{6,7},{7,6},{8,9},{9,8},{10,11... | collective-permute-start | bytes 24584 | tf_op jit(solution)/shard_map/ppermute | solution.py:439
  35.6 4.5 %collective-permute-start.9 = (f32[16,128]{1,0:T(8,128)S(1)}, f32[16,128]{1,0:T(8,128)S(1)}, u32[]{:S(2)}, u32[]{:S(2)}) collective-permute-start(f32[16,128]{1,0:T(8,128)S(1)} %add.17), channel_id=1, source_target_pairs={{0,2},{1,3},{2,0},{3,1},{4,6},{5,7},{6,4},{7,5},{8,10},{9,11},{10,... | collective-permute-start | bytes 24584 | tf_op jit(solution)/shard_map/ppermute | solution.py:439
  40.1 1.5 %collective-permute-start.10 = (f32[16,128]{1,0:T(8,128)S(1)}, f32[16,128]{1,0:T(8,128)S(1)}, u32[]{:S(2)}, u32[]{:S(2)}) collective-permute-start(f32[16,128]{1,0:T(8,128)S(1)} %add.18), channel_id=1, source_target_pairs={{0,16},{16,0},{1,17},{17,1},{2,18},{18,2},{3,19},{19,3},{4,20},{20... | collective-permute-start | bytes 24584 | tf_op jit(solution)/shard_map/ppermute | solution.py:439
  40.1 10.3 %collective-permute-start.16 = (bf16[48,2048]{1,0:T(8,128)(2,1)S(1)}, bf16[48,2048]{1,0:T(8,128)(2,1)S(1)}, u32[]{:S(2)}, u32[]{:S(2)}) collective-permute-start(bf16[48,2048]{1,0:T(8,128)(2,1)S(1)} %get-tuple-element.95), channel_id=1, source_target_pairs={{0,12},{4,8},{8,4},{12,0},{1,13},{5,9},{9,5},{13,1},{2,14},{6,10},... | collective-permute-start | bytes 589832 | tf_op jit(solution)/shard_map/ppermute | solution.py:439
  41.6 6.9 %collective-permute-start.14 = (f32[16,128]{1,0:T(8,128)S(1)}, f32[16,128]{1,0:T(8,128)S(1)}, u32[]{:S(2)}, u32[]{:S(2)}) collective-permute-start(f32[16,128]{1,0:T(8,128)S(1)} %add.19), channel_id=1, source_target_pairs={{0,8},{4,12},{8,0},{12,4},{1,9},{5,13},{9,1},{13,5},{2,10},{6,14},... | collective-permute-start | bytes 24584 | tf_op jit(solution)/shard_map/ppermute | solution.py:439
  48.5 3.7 %collective-permute-start.15 = (f32[32,128]{1,0:T(8,128)S(1)}, f32[32,128]{1,0:T(8,128)S(1)}, u32[]{:S(2)}, u32[]{:S(2)}) collective-permute-start(f32[32,128]{1,0:T(8,128)S(1)} %pad.4), channel_id=1, source_target_pairs={{0,4},{4,0},{8,12},{12,8},{1,5},{5,1},{9,13},{13,9},{2,6},{6,2},{1... | collective-permute-start | bytes 49160 | tf_op jit(solution)/shard_map/ppermute | solution.py:439
  50.4 1.9 %collective-permute-start.17 = (bf16[128,512]{1,0:T(8,128)(2,1)S(1)}, bf16[128,512]{1,0:T(8,128)(2,1)S(1)}, u32[]{:S(2)}, u32[]{:S(2)}) collective-permute-start(bf16[128,512]{1,0:T(8,128)(2,1)S(1)} %get-tuple-element.97), channel_id=1, source_target_pairs={{0,16},{16,0},{1,17},{17,1},{2,18},{18,2},{3,19},{19,3},{4,20},{20... | collective-permute-start | bytes 393224 | tf_op jit(solution)/shard_map/ppermute | solution.py:439

commit v14 on v12

--- a/solution.py
+++ b/solution.py
@@ -18,7 +18,7 @@
 LANES = 128
 GAIN_LINES = D // LANES
 WIDE_LINES = 32
-FIRST = 2
+FIRST = 1
 A_COST = 4000000000
 B_COST = 0
 SCALE = HEAD_SIZE ** (-0.5)

time: 53.3 us -> 52.2 us (0.979)
  waiting for transfers between devices: 16.3 us -> 14.9 us
    ppermute x18, waiting for transfers between devices: 16.3 us -> 14.9 us  [pairwise(): return lax.ppermute(value, axis, [(i, i ^ step) for i in range(count)])]
  transfers between devices with their start and end apart: 18 -> 18, of which waited for: 8 -> 8; matrix products, arithmetic and copies ran while one was open for 0% -> 0% of each run, Pallas kernels for 17% -> 18%
where the time goes in v14:
time: 52.2 us; the launch traced here: 52 us
  starting transfers between devices  21.7 us (42%)
  waiting for transfers between devices  14.9 us (29%)
  Pallas kernels  14.7 us (28%)
  between operations  0.73 us (1%)
    ppermute x18, starting transfers between devices, pairwise(): return lax.ppermute(value, axis, [(i, i ^ step) for i in range(count)])  21.7 us
    ppermute x18, waiting for transfers between devices, pairwise(): return lax.ppermute(value, axis, [(i, i ^ step) for i in range(count)])  14.9 us
    pallas_call x8, Pallas kernels, run(): pl.pallas_call(kernel, out_shape=[x for _, x in outputs], in_specs=[spec[...  14.7 us
  transfers between devices with their start and end apart: 18, of which 8 were waited for; matrix products, arithmetic and copies ran while one was open for 0% of the time, Pallas kernels for 18%

profile of v14, /device:TPU:0, one launch (start us, length us, event | category | flops | bytes accessed | tf_op | source)
XLA Modules:
  0.0 52.0 jit_solution(4792677430992010160)
XLA Ops:
  0.6 1.5 %dispatch_grads.1 = (bf16[128,2048]{1,0:T(8,128)(2,1)S(1)}, bf16[128,256]{1,0:T(8,128)(2,1)S(1)}, bf16[128,256]{1,0:T(8,128)(2,1)S(1)}, f32[1,2048]{1,0:T(1,128)...) custom-call(bf16[128,2048]{1,0:T(8,128)(2,1)} %bitcast.13, ...), custom_call_target="tpu_custom_call" | custom-call | flops 100663296 | bytes 4213824 | tf_op jit(solution)/shard_map/dispatch_grads/pallas_call | solution.py:420
  2.2 3.0 %collective-permute-start.1 = (bf16[48,2048]{1,0:T(8,128)(2,1)S(1)}, bf16[48,2048]{1,0:T(8,128)(2,1)S(1)}, u32[]{:S(2)}, u32[]{:S(2)}) collective-permute-start(bf16[48,2048]{1,0:T(8,128)(2,1)S(1)} %get-tuple-element.63), channel_id=1, source_target_pairs={{0,4},{4,0},{8,12},{12,8},{1,5},{5,1},{9,13},{13,9},{2,6},{6,2},{1... | collective-permute-start | bytes 589832 | tf_op jit(solution)/shard_map/ppermute | solution.py:439
  5.2 0.0 collective-permute-start
  5.2 0.5 collective-permute-start.4
  5.7 1.5 %collective-permute-start.2 = (bf16[48,2048]{1,0:T(8,128)(2,1)S(1)}, bf16[48,2048]{1,0:T(8,128)(2,1)S(1)}, u32[]{:S(2)}, u32[]{:S(2)}) collective-permute-start(bf16[48,2048]{1,0:T(8,128)(2,1)S(1)} %get-tuple-element.64), channel_id=1, source_target_pairs={{0,8},{4,12},{8,0},{12,4},{1,9},{5,13},{9,1},{13,5},{2,10},{6,14},... | collective-permute-start | bytes 589832 | tf_op jit(solution)/shard_map/ppermute | solution.py:439
  7.2 0.0 collective-permute-start.3
  7.2 1.4 %attention_forward.1 = (bf16[128,2048]{1,0:T(8,128)(2,1)S(1)}, bf16[48,2048]{1,0:T(8,128)(2,1)S(1)}, bf16[48,2048]{1,0:T(8,128)(2,1)S(1)}, bf16[48,2048]{1,0:T(8,128)(2,1)S(1)}, bf16[48,2048]{1,0:T(8,128)(2,1)S(1)}) custom-call(s32[2,128]{1,0:T(2,128)S(1)} %get-tuple-element.57.pos_ref, s32[1,128]{1,0:T(1,128)S(1)} %get-tuple-element.58.slot_ref, ...), custom_call_target="tpu_custom_call" | custom-call | flops 369098752 | bytes 2631168 | tf_op jit(solution)/shard_map/attention_forward/pallas_call | solution.py:420
  8.7 2.0 %collective-permute-start.5 = (bf16[48,2048]{1,0:T(8,128)(2,1)S(1)}, bf16[48,2048]{1,0:T(8,128)(2,1)S(1)}, u32[]{:S(2)}, u32[]{:S(2)}) collective-permute-start(bf16[48,2048]{1,0:T(8,128)(2,1)S(1)} %get-tuple-element.75), channel_id=1, source_target_pairs={{0,4},{4,0},{8,12},{12,8},{1,5},{5,1},{9,13},{13,9},{2,6},{6,2},{1... | collective-permute-start | bytes 589832 | tf_op jit(solution)/shard_map/ppermute | solution.py:439
  10.7 1.5 %collective-permute-start.6 = (bf16[48,2048]{1,0:T(8,128)(2,1)S(1)}, bf16[48,2048]{1,0:T(8,128)(2,1)S(1)}, u32[]{:S(2)}, u32[]{:S(2)}) collective-permute-start(bf16[48,2048]{1,0:T(8,128)(2,1)S(1)} %get-tuple-element.76), channel_id=1, source_target_pairs={{0,8},{4,12},{8,0},{12,4},{1,9},{5,13},{9,1},{13,5},{2,10},{6,14},... | collective-permute-start | bytes 589832 | tf_op jit(solution)/shard_map/ppermute | solution.py:439
  12.2 1.7 %collective-permute-start.7 = (bf16[48,2048]{1,0:T(8,128)(2,1)S(1)}, bf16[48,2048]{1,0:T(8,128)(2,1)S(1)}, u32[]{:S(2)}, u32[]{:S(2)}) collective-permute-start(bf16[48,2048]{1,0:T(8,128)(2,1)S(1)} %get-tuple-element.77), channel_id=1, source_target_pairs={{0,12},{4,8},{8,4},{12,0},{1,13},{5,9},{9,5},{13,1},{2,14},{6,10},... | collective-permute-start | bytes 589832 | tf_op jit(solution)/shard_map/ppermute | solution.py:439
  13.9 3.7 %collective-permute-done.2.refs_4_ = bf16[48,2048]{1,0:T(8,128)(2,1)S(1)} collective-permute-done((bf16[48,2048]{1,0:T(8,128)(2,1)S(1)}, bf16[48,2048]{1,0:T(8,128)(2,1)S(1)}, u32[]{:S(2)}, u32[]{:S(2)}) %collective-permute-start.2) | collective-permute-done | bytes 196640 | tf_op jit(solution)/shard_map/ppermute | solution.py:439
  17.7 3.8 %act_grads_and_probs.1 = (f32[192,384]{1,0:T(8,128)S(1)}, f32[8,256,256]{2,1,0:T(8,128)S(1)}, bf16[768,2048]{1,0:T(8,128)(2,1)S(1)}, bf16[2048,768]{1,0:T(8,128)...) custom-call(s32[2,128]{1,0:T(2,128)S(1)} %get-tuple-element.57.pos_ref, ...), custom_call_target="tpu_custom_call" | custom-call | flops 738197504 | bytes 16599040 | tf_op jit(solution)/shard_map/act_grads_and_probs/pallas_call | solution.py:420
  21.5 3.6 %collective-permute-done.6.refs_2_ = bf16[48,2048]{1,0:T(8,128)(2,1)S(1)} collective-permute-done((bf16[48,2048]{1,0:T(8,128)(2,1)S(1)}, bf16[48,2048]{1,0:T(8,128)(2,1)S(1)}, u32[]{:S(2)}, u32[]{:S(2)}) %collective-permute-start.6) | collective-permute-done | bytes 196640 | tf_op jit(solution)/shard_map/ppermute | solution.py:439
  25.1 2.8 %experts.1 = (bf16[48,2048]{1,0:T(8,128)(2,1)S(1)}, bf16[48,2048]{1,0:T(8,128)(2,1)S(1)}, bf16[96,2048]{1,0:T(8,128)(2,1)S(1)}, bf16[96,2048]{1,0:T(8,128)(2,1)S...) custom-call(bf16[2048,768]{1,0:T(8,128)(2,1)S(1)} %get-tuple-element.68.gate_ref, ...), custom_call_target="tpu_custom_call" | custom-call | flops 1811939328 | bytes 8945664 | tf_op jit(solution)/shard_map/experts/pallas_call | solution.py:420
  28.0 0.4 collective-permute-start.11
  28.4 1.7 %collective-permute-start.12 = (bf16[96,2048]{1,0:T(8,128)(2,1)S(1)}, bf16[96,2048]{1,0:T(8,128)(2,1)S(1)}, u32[]{:S(2)}, u32[]{:S(2)}) collective-permute-start(bf16[96,2048]{1,0:T(8,128)(2,1)S(1)} %get-tuple-element.81.refs_6_), channel_id=1, source_target_pairs={{0,8},{4,12},{8,0},{12,4},{1,9},{5,13},{9,1},{13,5},{2,10},{6,14},... | collective-permute-start | bytes 1179656 | tf_op jit(solution)/shard_map/ppermute | solution.py:439
  30.1 1.4 %collective-permute-start.13 = (bf16[48,2048]{1,0:T(8,128)(2,1)S(1)}, bf16[48,2048]{1,0:T(8,128)(2,1)S(1)}, u32[]{:S(2)}, u32[]{:S(2)}) collective-permute-start(bf16[48,2048]{1,0:T(8,128)(2,1)S(1)} %get-tuple-element.82.refs_7_), channel_id=1, source_target_pairs={{0,12},{4,8},{8,4},{12,0},{1,13},{5,9},{9,5},{13,1},{2,14},{6,10},... | collective-permute-start | bytes 589832 | tf_op jit(solution)/shard_map/ppermute | solution.py:439
  31.5 0.3 gain_terms.1
  31.8 1.6 %collective-permute-start.8 = (f32[16,128]{1,0:T(8,128)S(1)}, f32[16,128]{1,0:T(8,128)S(1)}, u32[]{:S(2)}, u32[]{:S(2)}) collective-permute-start(f32[16,128]{1,0:T(8,128)S(1)} %gain_terms.1), channel_id=1, source_target_pairs={{0,1},{1,0},{2,3},{3,2},{4,5},{5,4},{6,7},{7,6},{8,9},{9,8},{10,11... | collective-permute-start | bytes 24584 | tf_op jit(solution)/shard_map/ppermute | solution.py:439
  33.5 2.1 %collective-permute-done.8 = f32[16,128]{1,0:T(8,128)S(1)} collective-permute-done((f32[16,128]{1,0:T(8,128)S(1)}, f32[16,128]{1,0:T(8,128)S(1)}, u32[]{:S(2)}, u32[]{:S(2)}) %collective-permute-start.8) | collective-permute-done | bytes 8224 | tf_op jit(solution)/shard_map/ppermute | solution.py:439
  35.6 2.6 %collective-permute-start.9 = (f32[16,128]{1,0:T(8,128)S(1)}, f32[16,128]{1,0:T(8,128)S(1)}, u32[]{:S(2)}, u32[]{:S(2)}) collective-permute-start(f32[16,128]{1,0:T(8,128)S(1)} %add.17), channel_id=1, source_target_pairs={{0,2},{1,3},{2,0},{3,1},{4,6},{5,7},{6,4},{7,5},{8,10},{9,11},{10,... | collective-permute-start | bytes 24584 | tf_op jit(solution)/shard_map/ppermute | solution.py:439
  38.2 1.9 %collective-permute-done.9 = f32[16,128]{1,0:T(8,128)S(1)} collective-permute-done((f32[16,128]{1,0:T(8,128)S(1)}, f32[16,128]{1,0:T(8,128)S(1)}, u32[]{:S(2)}, u32[]{:S(2)}) %collective-permute-start.9) | collective-permute-done | bytes 8224 | tf_op jit(solution)/shard_map/ppermute | solution.py:439
  40.1 1.2 %collective-permute-done.10 = f32[16,128]{1,0:T(8,128)S(1)} collective-permute-done((f32[16,128]{1,0:T(8,128)S(1)}, f32[16,128]{1,0:T(8,128)S(1)}, u32[]{:S(2)}, u32[]{:S(2)}) %collective-permute-start.10) | collective-permute-done | bytes 8224 | tf_op jit(solution)/shard_map/ppermute | solution.py:439
  41.3 0.3 collective-permute-start.14
  41.6 2.7 %collective-permute-start.16 = (bf16[48,2048]{1,0:T(8,128)(2,1)S(1)}, bf16[48,2048]{1,0:T(8,128)(2,1)S(1)}, u32[]{:S(2)}, u32[]{:S(2)}) collective-permute-start(bf16[48,2048]{1,0:T(8,128)(2,1)S(1)} %get-tuple-element.95), channel_id=1, source_target_pairs={{0,12},{4,8},{8,4},{12,0},{1,13},{5,9},{9,5},{13,1},{2,14},{6,10},... | collective-permute-start | bytes 589832 | tf_op jit(solution)/shard_map/ppermute | solution.py:439
  44.3 2.1 %residual_and_first_group.1 = (bf16[128,2048]{1,0:T(8,128)(2,1)}, bf16[128,1024]{1,0:T(8,128)(2,1)S(1)}, bf16[128,1024]{1,0:T(8,128)(2,1)S(1)}, f32[128,256]{1,0:T(8,128)S(1)}, bf16[128,256]{1,0:T(8,128)(2,1)S(1)}) custom-call(bf16[128,192]{1,0:T(8,128)(2,1)S(1)} %get-tuple-element.66.place_ref, f32[1,2048]{1,0:T(1,128)S(1)} %get-tuple-element.71.gain_ref, ...), custom_call_target="tpu_custom_call" | custom-call | flops 4000000000 | bytes 6414336 | tf_op jit(solution)/shard_map/residual_and_first_group/pallas_call | solution.py:420
  46.4 0.6 %collective-permute-start.15 = (f32[32,128]{1,0:T(8,128)S(1)}, f32[32,128]{1,0:T(8,128)S(1)}, u32[]{:S(2)}, u32[]{:S(2)}) collective-permute-start(f32[32,128]{1,0:T(8,128)S(1)} %pad.4), channel_id=1, source_target_pairs={{0,8},{4,12},{8,0},{12,4},{1,9},{5,13},{9,1},{13,5},{2,10},{6,14},... | collective-permute-start | bytes 49160 | tf_op jit(solution)/shard_map/ppermute | solution.py:439
  47.0 1.5 %second_group.1 = (bf16[128,1024]{1,0:T(8,128)(2,1)S(1)}, f32[128,256]{1,0:T(8,128)S(1)}, bf16[128,512]{1,0:T(8,128)(2,1)S(1)}) custom-call(bf16[128,2048]{1,0:T(8,128)(2,1)S(1)} %get-tuple-element.60.query_ref, f32[8,256,256]{2,1,0:T(8,128)S(1)} %get-tuple-element.86.probs_ref, bf16[128,1024]{1,0:T(8,128)(2,1)S(1)} %get-tuple-element.90.rest_ref, ...), custom_call_target="tpu_custom_call" | custom-call | tf_op jit(solution)/shard_map/second_group/pallas_call | solution.py:420
  48.5 1.0 %collective-permute-done.16.refs_8_ = bf16[48,2048]{1,0:T(8,128)(2,1)S(1)} collective-permute-done((bf16[48,2048]{1,0:T(8,128)(2,1)S(1)}, bf16[48,2048]{1,0:T(8,128)(2,1)S(1)}, u32[]{:S(2)}, u32[]{:S(2)}) %collective-permute-start.16) | collective-permute-done | bytes 196640 | tf_op jit(solution)/shard_map/ppermute | solution.py:439
  49.5 0.7 %collective-permute-done.15 = f32[32,128]{1,0:T(8,128)S(1)} collective-permute-done((f32[32,128]{1,0:T(8,128)S(1)}, f32[32,128]{1,0:T(8,128)S(1)}, u32[]{:S(2)}, u32[]{:S(2)}) %collective-permute-start.15) | collective-permute-done | bytes 16416 | tf_op jit(solution)/shard_map/ppermute | solution.py:439
  50.2 0.6 %collective-permute-done.17.refs_4_ = bf16[128,512]{1,0:T(8,128)(2,1)S(1)} collective-permute-done((bf16[128,512]{1,0:T(8,128)(2,1)S(1)}, bf16[128,512]{1,0:T(8,128)(2,1)S(1)}, u32[]{:S(2)}, u32[]{:S(2)}) %collective-permute-start.17) | collective-permute-done | bytes 131104 | tf_op jit(solution)/shard_map/ppermute | solution.py:439
  50.8 1.2 %layer_output.1 = (bf16[128,2048]{1,0:T(8,128)(2,1)}, bf16[128,2048]{1,0:T(8,128)(2,1)}, bf16[128,256]{1,0:T(8,128)(2,1)}, bf16[128,256]{1,0:T(8,128)(2,1)}, f32[1,128]{1,0:T(1,128)}, /*index=5*/f32[16,128]{1,0:T(8,128)}) custom-call(bf16[128,192]{1,0:T(8,128)(2,1)S(1)} %get-tuple-element.66.place_ref, f32[128,256]{1,0:T(8,128)S(1)} %get-tuple-element.67.weight_ref, ...), custom_call_target="tpu_custom_call" | custom-call | flops 100663296 | bytes 4522496 | tf_op jit(solution)/shard_map/layer_output/pallas_call | solution.py:420
  (18 shorter events, 0.1 us)
Async XLA Ops:
  2.2 10.0 %collective-permute-start.1 = (bf16[48,2048]{1,0:T(8,128)(2,1)S(1)}, bf16[48,2048]{1,0:T(8,128)(2,1)S(1)}, u32[]{:S(2)}, u32[]{:S(2)}) collective-permute-start(bf16[48,2048]{1,0:T(8,128)(2,1)S(1)} %get-tuple-element.63), channel_id=1, source_target_pairs={{0,4},{4,0},{8,12},{12,8},{1,5},{5,1},{9,13},{13,9},{2,6},{6,2},{1... | collective-permute-start | bytes 589832 | tf_op jit(solution)/shard_map/ppermute | solution.py:439
  5.2 2.1 %collective-permute-start = (bf16[128,256]{1,0:T(8,128)(2,1)}, bf16[128,256]{1,0:T(8,128)(2,1)S(1)}, u32[]{:S(2)}, u32[]{:S(2)}) collective-permute-start(bf16[128,256]{1,0:T(8,128)(2,1)} %bitcast.17), channel_id=1, source_target_pairs={{0,16},{16,0},{1,17},{17,1},{2,18},{18,2},{3,19},{19,3},{4,20},{20... | collective-permute-start | bytes 196616 | tf_op jit(solution)/shard_map/ppermute | solution.py:439
  5.2 2.1 %collective-permute-start.4 = (bf16[128,256]{1,0:T(8,128)(2,1)}, bf16[128,256]{1,0:T(8,128)(2,1)S(1)}, u32[]{:S(2)}, u32[]{:S(2)}) collective-permute-start(bf16[128,256]{1,0:T(8,128)(2,1)} %bitcast.19), channel_id=1, source_target_pairs={{0,16},{16,0},{1,17},{17,1},{2,18},{18,2},{3,19},{19,3},{4,20},{20... | collective-permute-start | bytes 196616 | tf_op jit(solution)/shard_map/ppermute | solution.py:439
  5.7 12.0 %collective-permute-start.2 = (bf16[48,2048]{1,0:T(8,128)(2,1)S(1)}, bf16[48,2048]{1,0:T(8,128)(2,1)S(1)}, u32[]{:S(2)}, u32[]{:S(2)}) collective-permute-start(bf16[48,2048]{1,0:T(8,128)(2,1)S(1)} %get-tuple-element.64), channel_id=1, source_target_pairs={{0,8},{4,12},{8,0},{12,4},{1,9},{5,13},{9,1},{13,5},{2,10},{6,14},... | collective-permute-start | bytes 589832 | tf_op jit(solution)/shard_map/ppermute | solution.py:439
  7.2 10.5 %collective-permute-start.3 = (bf16[48,2048]{1,0:T(8,128)(2,1)S(1)}, bf16[48,2048]{1,0:T(8,128)(2,1)S(1)}, u32[]{:S(2)}, u32[]{:S(2)}) collective-permute-start(bf16[48,2048]{1,0:T(8,128)(2,1)S(1)} %get-tuple-element.65), channel_id=1, source_target_pairs={{0,12},{4,8},{8,4},{12,0},{1,13},{5,9},{9,5},{13,1},{2,14},{6,10},... | collective-permute-start | bytes 589832 | tf_op jit(solution)/shard_map/ppermute | solution.py:439
  8.7 12.8 %collective-permute-start.5 = (bf16[48,2048]{1,0:T(8,128)(2,1)S(1)}, bf16[48,2048]{1,0:T(8,128)(2,1)S(1)}, u32[]{:S(2)}, u32[]{:S(2)}) collective-permute-start(bf16[48,2048]{1,0:T(8,128)(2,1)S(1)} %get-tuple-element.75), channel_id=1, source_target_pairs={{0,4},{4,0},{8,12},{12,8},{1,5},{5,1},{9,13},{13,9},{2,6},{6,2},{1... | collective-permute-start | bytes 589832 | tf_op jit(solution)/shard_map/ppermute | solution.py:439
  10.7 14.5 %collective-permute-start.6 = (bf16[48,2048]{1,0:T(8,128)(2,1)S(1)}, bf16[48,2048]{1,0:T(8,128)(2,1)S(1)}, u32[]{:S(2)}, u32[]{:S(2)}) collective-permute-start(bf16[48,2048]{1,0:T(8,128)(2,1)S(1)} %get-tuple-element.76), channel_id=1, source_target_pairs={{0,8},{4,12},{8,0},{12,4},{1,9},{5,13},{9,1},{13,5},{2,10},{6,14},... | collective-permute-start | bytes 589832 | tf_op jit(solution)/shard_map/ppermute | solution.py:439
  12.2 12.9 %collective-permute-start.7 = (bf16[48,2048]{1,0:T(8,128)(2,1)S(1)}, bf16[48,2048]{1,0:T(8,128)(2,1)S(1)}, u32[]{:S(2)}, u32[]{:S(2)}) collective-permute-start(bf16[48,2048]{1,0:T(8,128)(2,1)S(1)} %get-tuple-element.77), channel_id=1, source_target_pairs={{0,12},{4,8},{8,4},{12,0},{1,13},{5,9},{9,5},{13,1},{2,14},{6,10},... | collective-permute-start | bytes 589832 | tf_op jit(solution)/shard_map/ppermute | solution.py:439
  28.0 16.3 %collective-permute-start.11 = (bf16[96,2048]{1,0:T(8,128)(2,1)S(1)}, bf16[96,2048]{1,0:T(8,128)(2,1)S(1)}, u32[]{:S(2)}, u32[]{:S(2)}) collective-permute-start(bf16[96,2048]{1,0:T(8,128)(2,1)S(1)} %get-tuple-element.80.refs_5_), channel_id=1, source_target_pairs={{0,4},{4,0},{8,12},{12,8},{1,5},{5,1},{9,13},{13,9},{2,6},{6,2},{1... | collective-permute-start | bytes 1179656 | tf_op jit(solution)/shard_map/ppermute | solution.py:439
  28.4 15.9 %collective-permute-start.12 = (bf16[96,2048]{1,0:T(8,128)(2,1)S(1)}, bf16[96,2048]{1,0:T(8,128)(2,1)S(1)}, u32[]{:S(2)}, u32[]{:S(2)}) collective-permute-start(bf16[96,2048]{1,0:T(8,128)(2,1)S(1)} %get-tuple-element.81.refs_6_), channel_id=1, source_target_pairs={{0,8},{4,12},{8,0},{12,4},{1,9},{5,13},{9,1},{13,5},{2,10},{6,14},... | collective-permute-start | bytes 1179656 | tf_op jit(solution)/shard_map/ppermute | solution.py:439
  30.1 14.2 %collective-permute-start.13 = (bf16[48,2048]{1,0:T(8,128)(2,1)S(1)}, bf16[48,2048]{1,0:T(8,128)(2,1)S(1)}, u32[]{:S(2)}, u32[]{:S(2)}) collective-permute-start(bf16[48,2048]{1,0:T(8,128)(2,1)S(1)} %get-tuple-element.82.refs_7_), channel_id=1, source_target_pairs={{0,12},{4,8},{8,4},{12,0},{1,13},{5,9},{9,5},{13,1},{2,14},{6,10},... | collective-permute-start | bytes 589832 | tf_op jit(solution)/shard_map/ppermute | solution.py:439
  31.8 3.7 %collective-permute-start.8 = (f32[16,128]{1,0:T(8,128)S(1)}, f32[16,128]{1,0:T(8,128)S(1)}, u32[]{:S(2)}, u32[]{:S(2)}) collective-permute-start(f32[16,128]{1,0:T(8,128)S(1)} %gain_terms.1), channel_id=1, source_target_pairs={{0,1},{1,0},{2,3},{3,2},{4,5},{5,4},{6,7},{7,6},{8,9},{9,8},{10,11... | collective-permute-start | bytes 24584 | tf_op jit(solution)/shard_map/ppermute | solution.py:439
  35.6 4.5 %collective-permute-start.9 = (f32[16,128]{1,0:T(8,128)S(1)}, f32[16,128]{1,0:T(8,128)S(1)}, u32[]{:S(2)}, u32[]{:S(2)}) collective-permute-start(f32[16,128]{1,0:T(8,128)S(1)} %add.17), channel_id=1, source_target_pairs={{0,2},{1,3},{2,0},{3,1},{4,6},{5,7},{6,4},{7,5},{8,10},{9,11},{10,... | collective-permute-start | bytes 24584 | tf_op jit(solution)/shard_map/ppermute | solution.py:439
  40.1 1.2 %collective-permute-start.10 = (f32[16,128]{1,0:T(8,128)S(1)}, f32[16,128]{1,0:T(8,128)S(1)}, u32[]{:S(2)}, u32[]{:S(2)}) collective-permute-start(f32[16,128]{1,0:T(8,128)S(1)} %add.18), channel_id=1, source_target_pairs={{0,16},{16,0},{1,17},{17,1},{2,18},{18,2},{3,19},{19,3},{4,20},{20... | collective-permute-start | bytes 24584 | tf_op jit(solution)/shard_map/ppermute | solution.py:439
  41.3 5.1 %collective-permute-start.14 = (f32[16,128]{1,0:T(8,128)S(1)}, f32[16,128]{1,0:T(8,128)S(1)}, u32[]{:S(2)}, u32[]{:S(2)}) collective-permute-start(f32[16,128]{1,0:T(8,128)S(1)} %add.19), channel_id=1, source_target_pairs={{0,4},{4,0},{8,12},{12,8},{1,5},{5,1},{9,13},{13,9},{2,6},{6,2},{1... | collective-permute-start | bytes 24584 | tf_op jit(solution)/shard_map/ppermute | solution.py:439
  41.6 7.9 %collective-permute-start.16 = (bf16[48,2048]{1,0:T(8,128)(2,1)S(1)}, bf16[48,2048]{1,0:T(8,128)(2,1)S(1)}, u32[]{:S(2)}, u32[]{:S(2)}) collective-permute-start(bf16[48,2048]{1,0:T(8,128)(2,1)S(1)} %get-tuple-element.95), channel_id=1, source_target_pairs={{0,12},{4,8},{8,4},{12,0},{1,13},{5,9},{9,5},{13,1},{2,14},{6,10},... | collective-permute-start | bytes 589832 | tf_op jit(solution)/shard_map/ppermute | solution.py:439
  46.4 3.8 %collective-permute-start.15 = (f32[32,128]{1,0:T(8,128)S(1)}, f32[32,128]{1,0:T(8,128)S(1)}, u32[]{:S(2)}, u32[]{:S(2)}) collective-permute-start(f32[32,128]{1,0:T(8,128)S(1)} %pad.4), channel_id=1, source_target_pairs={{0,8},{4,12},{8,0},{12,4},{1,9},{5,13},{9,1},{13,5},{2,10},{6,14},... | collective-permute-start | bytes 49160 | tf_op jit(solution)/shard_map/ppermute | solution.py:439
  49.5 1.3 %collective-permute-start.17 = (bf16[128,512]{1,0:T(8,128)(2,1)S(1)}, bf16[128,512]{1,0:T(8,128)(2,1)S(1)}, u32[]{:S(2)}, u32[]{:S(2)}) collective-permute-start(bf16[128,512]{1,0:T(8,128)(2,1)S(1)} %get-tuple-element.97), channel_id=1, source_target_pairs={{0,16},{16,0},{1,17},{17,1},{2,18},{18,2},{3,19},{19,3},{4,20},{20... | collective-permute-start | bytes 393224 | tf_op jit(solution)/shard_map/ppermute | solution.py:439

commit v15 on v14

--- a/solution.py
+++ b/solution.py
@@ -592,7 +592,7 @@
         placed(VMEM, [shaped((GAIN_LINES, LANES), F32)]),
         2 * slots * D,
     )
-    terms = sum_over(sum_over(terms, "dp"), "ctx")
+    terms = sum_over(terms, "dp")
     send_far, terms = lax.optimization_barrier(([send_y[s] for s in far], terms))
     for s, piece in zip(far, send_far):
         y[s] = pairwise(piece, "exp", s)
@@ -629,7 +629,7 @@
         + placed(VMEM, [shaped((tokens, kv_width), BF16)] * (ctx_count - 1)),
         B_COST,
     )
-    terms = sum_over(terms, "exp", first=4)
+    terms = sum_over(sum_over(terms, "exp", first=4), "ctx")
     arrived_far, shared = lax.optimization_barrier(([y[s] for s in far], shared))
     for s, piece in zip(far, arrived_far):
         y[s] = piece

time: 52.2 us -> 53.8 us (1.031)
  waiting for transfers between devices: 14.9 us -> 15.8 us
  starting transfers between devices: 21.7 us -> 22.3 us
    ppermute x18, waiting for transfers between devices: 14.9 us -> 15.8 us  [pairwise(): return lax.ppermute(value, axis, [(i, i ^ step) for i in range(count)])]
    ppermute x18, starting transfers between devices: 21.7 us -> 22.3 us  [pairwise(): return lax.ppermute(value, axis, [(i, i ^ step) for i in range(count)])]
  transfers between devices with their start and end apart: 18 -> 18, of which waited for: 8 -> 7; matrix products, arithmetic and copies ran while one was open for 0% -> 0% of each run, Pallas kernels for 18% -> 17%
where the time goes in v15:
time: 53.8 us; the launch traced here: 53.6 us
  starting transfers between devices  22.3 us (41%)
  waiting for transfers between devices  15.8 us (29%)
  Pallas kernels  14.7 us (27%)
  between operations  0.75 us (1%)
    ppermute x18, starting transfers between devices, pairwise(): return lax.ppermute(value, axis, [(i, i ^ step) for i in range(count)])  22.3 us
    ppermute x18, waiting for transfers between devices, pairwise(): return lax.ppermute(value, axis, [(i, i ^ step) for i in range(count)])  15.8 us
    pallas_call x8, Pallas kernels, run(): pl.pallas_call(kernel, out_shape=[x for _, x in outputs], in_specs=[spec[...  14.7 us
  transfers between devices with their start and end apart: 18, of which 7 were waited for; matrix products, arithmetic and copies ran while one was open for 0% of the time, Pallas kernels for 17%

profile of v15, /device:TPU:0, one launch (start us, length us, event | category | flops | bytes accessed | tf_op | source)
XLA Modules:
  0.0 53.6 jit_solution(11947567734124411231)
XLA Ops:
  0.6 1.5 %dispatch_grads.1 = (bf16[128,2048]{1,0:T(8,128)(2,1)S(1)}, bf16[128,256]{1,0:T(8,128)(2,1)S(1)}, bf16[128,256]{1,0:T(8,128)(2,1)S(1)}, f32[1,2048]{1,0:T(1,128)...) custom-call(bf16[128,2048]{1,0:T(8,128)(2,1)} %bitcast.13, ...), custom_call_target="tpu_custom_call" | custom-call | flops 100663296 | bytes 4213824 | tf_op jit(solution)/shard_map/dispatch_grads/pallas_call | solution.py:420
  2.2 3.0 %collective-permute-start.1 = (bf16[48,2048]{1,0:T(8,128)(2,1)S(1)}, bf16[48,2048]{1,0:T(8,128)(2,1)S(1)}, u32[]{:S(2)}, u32[]{:S(2)}) collective-permute-start(bf16[48,2048]{1,0:T(8,128)(2,1)S(1)} %get-tuple-element.63), channel_id=1, source_target_pairs={{0,4},{4,0},{8,12},{12,8},{1,5},{5,1},{9,13},{13,9},{2,6},{6,2},{1... | collective-permute-start | bytes 589832 | tf_op jit(solution)/shard_map/ppermute | solution.py:439
  5.2 0.0 collective-permute-start
  5.2 0.5 collective-permute-start.4
  5.7 1.5 %collective-permute-start.2 = (bf16[48,2048]{1,0:T(8,128)(2,1)S(1)}, bf16[48,2048]{1,0:T(8,128)(2,1)S(1)}, u32[]{:S(2)}, u32[]{:S(2)}) collective-permute-start(bf16[48,2048]{1,0:T(8,128)(2,1)S(1)} %get-tuple-element.64), channel_id=1, source_target_pairs={{0,8},{4,12},{8,0},{12,4},{1,9},{5,13},{9,1},{13,5},{2,10},{6,14},... | collective-permute-start | bytes 589832 | tf_op jit(solution)/shard_map/ppermute | solution.py:439
  7.2 0.0 collective-permute-start.3
  7.2 1.4 %attention_forward.1 = (bf16[128,2048]{1,0:T(8,128)(2,1)S(1)}, bf16[48,2048]{1,0:T(8,128)(2,1)S(1)}, bf16[48,2048]{1,0:T(8,128)(2,1)S(1)}, bf16[48,2048]{1,0:T(8,128)(2,1)S(1)}, bf16[48,2048]{1,0:T(8,128)(2,1)S(1)}) custom-call(s32[2,128]{1,0:T(2,128)S(1)} %get-tuple-element.57.pos_ref, s32[1,128]{1,0:T(1,128)S(1)} %get-tuple-element.58.slot_ref, ...), custom_call_target="tpu_custom_call" | custom-call | flops 369098752 | bytes 2631168 | tf_op jit(solution)/shard_map/attention_forward/pallas_call | solution.py:420
  8.7 2.0 %collective-permute-start.5 = (bf16[48,2048]{1,0:T(8,128)(2,1)S(1)}, bf16[48,2048]{1,0:T(8,128)(2,1)S(1)}, u32[]{:S(2)}, u32[]{:S(2)}) collective-permute-start(bf16[48,2048]{1,0:T(8,128)(2,1)S(1)} %get-tuple-element.75), channel_id=1, source_target_pairs={{0,4},{4,0},{8,12},{12,8},{1,5},{5,1},{9,13},{13,9},{2,6},{6,2},{1... | collective-permute-start | bytes 589832 | tf_op jit(solution)/shard_map/ppermute | solution.py:439
  10.7 1.5 %collective-permute-start.6 = (bf16[48,2048]{1,0:T(8,128)(2,1)S(1)}, bf16[48,2048]{1,0:T(8,128)(2,1)S(1)}, u32[]{:S(2)}, u32[]{:S(2)}) collective-permute-start(bf16[48,2048]{1,0:T(8,128)(2,1)S(1)} %get-tuple-element.76), channel_id=1, source_target_pairs={{0,8},{4,12},{8,0},{12,4},{1,9},{5,13},{9,1},{13,5},{2,10},{6,14},... | collective-permute-start | bytes 589832 | tf_op jit(solution)/shard_map/ppermute | solution.py:439
  12.2 1.7 %collective-permute-start.7 = (bf16[48,2048]{1,0:T(8,128)(2,1)S(1)}, bf16[48,2048]{1,0:T(8,128)(2,1)S(1)}, u32[]{:S(2)}, u32[]{:S(2)}) collective-permute-start(bf16[48,2048]{1,0:T(8,128)(2,1)S(1)} %get-tuple-element.77), channel_id=1, source_target_pairs={{0,12},{4,8},{8,4},{12,0},{1,13},{5,9},{9,5},{13,1},{2,14},{6,10},... | collective-permute-start | bytes 589832 | tf_op jit(solution)/shard_map/ppermute | solution.py:439
  13.9 3.7 %collective-permute-done.2.refs_4_ = bf16[48,2048]{1,0:T(8,128)(2,1)S(1)} collective-permute-done((bf16[48,2048]{1,0:T(8,128)(2,1)S(1)}, bf16[48,2048]{1,0:T(8,128)(2,1)S(1)}, u32[]{:S(2)}, u32[]{:S(2)}) %collective-permute-start.2) | collective-permute-done | bytes 196640 | tf_op jit(solution)/shard_map/ppermute | solution.py:439
  17.7 3.8 %act_grads_and_probs.1 = (f32[192,384]{1,0:T(8,128)S(1)}, f32[8,256,256]{2,1,0:T(8,128)S(1)}, bf16[768,2048]{1,0:T(8,128)(2,1)S(1)}, bf16[2048,768]{1,0:T(8,128)...) custom-call(s32[2,128]{1,0:T(2,128)S(1)} %get-tuple-element.57.pos_ref, ...), custom_call_target="tpu_custom_call" | custom-call | flops 738197504 | bytes 16599040 | tf_op jit(solution)/shard_map/act_grads_and_probs/pallas_call | solution.py:420
  21.5 3.6 %collective-permute-done.6.refs_2_ = bf16[48,2048]{1,0:T(8,128)(2,1)S(1)} collective-permute-done((bf16[48,2048]{1,0:T(8,128)(2,1)S(1)}, bf16[48,2048]{1,0:T(8,128)(2,1)S(1)}, u32[]{:S(2)}, u32[]{:S(2)}) %collective-permute-start.6) | collective-permute-done | bytes 196640 | tf_op jit(solution)/shard_map/ppermute | solution.py:439
  25.1 2.8 %experts.1 = (bf16[48,2048]{1,0:T(8,128)(2,1)S(1)}, bf16[48,2048]{1,0:T(8,128)(2,1)S(1)}, bf16[96,2048]{1,0:T(8,128)(2,1)S(1)}, bf16[96,2048]{1,0:T(8,128)(2,1)S...) custom-call(bf16[2048,768]{1,0:T(8,128)(2,1)S(1)} %get-tuple-element.68.gate_ref, ...), custom_call_target="tpu_custom_call" | custom-call | flops 1811939328 | bytes 8945664 | tf_op jit(solution)/shard_map/experts/pallas_call | solution.py:420
  28.0 0.4 collective-permute-start.10
  28.4 1.7 %collective-permute-start.11 = (bf16[96,2048]{1,0:T(8,128)(2,1)S(1)}, bf16[96,2048]{1,0:T(8,128)(2,1)S(1)}, u32[]{:S(2)}, u32[]{:S(2)}) collective-permute-start(bf16[96,2048]{1,0:T(8,128)(2,1)S(1)} %get-tuple-element.81.refs_6_), channel_id=1, source_target_pairs={{0,8},{4,12},{8,0},{12,4},{1,9},{5,13},{9,1},{13,5},{2,10},{6,14},... | collective-permute-start | bytes 1179656 | tf_op jit(solution)/shard_map/ppermute | solution.py:439
  30.1 1.4 %collective-permute-start.12 = (bf16[48,2048]{1,0:T(8,128)(2,1)S(1)}, bf16[48,2048]{1,0:T(8,128)(2,1)S(1)}, u32[]{:S(2)}, u32[]{:S(2)}) collective-permute-start(bf16[48,2048]{1,0:T(8,128)(2,1)S(1)} %get-tuple-element.82.refs_7_), channel_id=1, source_target_pairs={{0,12},{4,8},{8,4},{12,0},{1,13},{5,9},{9,5},{13,1},{2,14},{6,10},... | collective-permute-start | bytes 589832 | tf_op jit(solution)/shard_map/ppermute | solution.py:439
  31.5 0.3 gain_terms.1
  31.8 1.6 %collective-permute-start.8 = (f32[16,128]{1,0:T(8,128)S(1)}, f32[16,128]{1,0:T(8,128)S(1)}, u32[]{:S(2)}, u32[]{:S(2)}) collective-permute-start(f32[16,128]{1,0:T(8,128)S(1)} %gain_terms.1), channel_id=1, source_target_pairs={{0,1},{1,0},{2,3},{3,2},{4,5},{5,4},{6,7},{7,6},{8,9},{9,8},{10,11... | collective-permute-start | bytes 24584 | tf_op jit(solution)/shard_map/ppermute | solution.py:439
  33.5 2.1 %collective-permute-done.8 = f32[16,128]{1,0:T(8,128)S(1)} collective-permute-done((f32[16,128]{1,0:T(8,128)S(1)}, f32[16,128]{1,0:T(8,128)S(1)}, u32[]{:S(2)}, u32[]{:S(2)}) %collective-permute-start.8) | collective-permute-done | bytes 8224 | tf_op jit(solution)/shard_map/ppermute | solution.py:439
  35.6 2.6 %collective-permute-start.9 = (f32[16,128]{1,0:T(8,128)S(1)}, f32[16,128]{1,0:T(8,128)S(1)}, u32[]{:S(2)}, u32[]{:S(2)}) collective-permute-start(f32[16,128]{1,0:T(8,128)S(1)} %add.17), channel_id=1, source_target_pairs={{0,2},{1,3},{2,0},{3,1},{4,6},{5,7},{6,4},{7,5},{8,10},{9,11},{10,... | collective-permute-start | bytes 24584 | tf_op jit(solution)/shard_map/ppermute | solution.py:439
  38.2 1.9 %collective-permute-done.9 = f32[16,128]{1,0:T(8,128)S(1)} collective-permute-done((f32[16,128]{1,0:T(8,128)S(1)}, f32[16,128]{1,0:T(8,128)S(1)}, u32[]{:S(2)}, u32[]{:S(2)}) %collective-permute-start.9) | collective-permute-done | bytes 8224 | tf_op jit(solution)/shard_map/ppermute | solution.py:439
  40.1 0.3 collective-permute-start.13
  40.4 2.7 %collective-permute-start.16 = (bf16[48,2048]{1,0:T(8,128)(2,1)S(1)}, bf16[48,2048]{1,0:T(8,128)(2,1)S(1)}, u32[]{:S(2)}, u32[]{:S(2)}) collective-permute-start(bf16[48,2048]{1,0:T(8,128)(2,1)S(1)} %get-tuple-element.95), channel_id=1, source_target_pairs={{0,12},{4,8},{8,4},{12,0},{1,13},{5,9},{9,5},{13,1},{2,14},{6,10},... | collective-permute-start | bytes 589832 | tf_op jit(solution)/shard_map/ppermute | solution.py:439
  43.1 2.2 %collective-permute-done.12.refs_7_ = bf16[48,2048]{1,0:T(8,128)(2,1)S(1)} collective-permute-done((bf16[48,2048]{1,0:T(8,128)(2,1)S(1)}, bf16[48,2048]{1,0:T(8,128)(2,1)S(1)}, u32[]{:S(2)}, u32[]{:S(2)}) %collective-permute-start.12) | collective-permute-done | bytes 196640 | tf_op jit(solution)/shard_map/ppermute | solution.py:439
  45.3 2.1 %residual_and_first_group.1 = (bf16[128,2048]{1,0:T(8,128)(2,1)}, bf16[128,1024]{1,0:T(8,128)(2,1)S(1)}, bf16[128,1024]{1,0:T(8,128)(2,1)S(1)}, f32[128,256]{1,0:T(8,128)S(1)}, bf16[128,256]{1,0:T(8,128)(2,1)S(1)}) custom-call(bf16[128,192]{1,0:T(8,128)(2,1)S(1)} %get-tuple-element.66.place_ref, f32[1,2048]{1,0:T(1,128)S(1)} %get-tuple-element.71.gain_ref, ...), custom_call_target="tpu_custom_call" | custom-call | flops 4000000000 | bytes 6414336 | tf_op jit(solution)/shard_map/residual_and_first_group/pallas_call | solution.py:420
  47.4 1.1 %collective-permute-start.14 = (f32[32,128]{1,0:T(8,128)S(1)}, f32[32,128]{1,0:T(8,128)S(1)}, u32[]{:S(2)}, u32[]{:S(2)}) collective-permute-start(f32[32,128]{1,0:T(8,128)S(1)} %pad.4), channel_id=1, source_target_pairs={{0,8},{4,12},{8,0},{12,4},{1,9},{5,13},{9,1},{13,5},{2,10},{6,14},... | collective-permute-start | bytes 49160 | tf_op jit(solution)/shard_map/ppermute | solution.py:439
  48.5 1.5 %second_group.1 = (bf16[128,1024]{1,0:T(8,128)(2,1)S(1)}, f32[128,256]{1,0:T(8,128)S(1)}, bf16[128,512]{1,0:T(8,128)(2,1)S(1)}) custom-call(bf16[128,2048]{1,0:T(8,128)(2,1)S(1)} %get-tuple-element.60.query_ref, f32[8,256,256]{2,1,0:T(8,128)S(1)} %get-tuple-element.86.probs_ref, bf16[128,1024]{1,0:T(8,128)(2,1)S(1)} %get-tuple-element.90.rest_ref, ...), custom_call_target="tpu_custom_call" | custom-call | tf_op jit(solution)/shard_map/second_group/pallas_call | solution.py:420
  50.0 0.1 collective-permute-start.17
  50.1 1.1 %collective-permute-done.14 = f32[32,128]{1,0:T(8,128)S(1)} collective-permute-done((f32[32,128]{1,0:T(8,128)S(1)}, f32[32,128]{1,0:T(8,128)S(1)}, u32[]{:S(2)}, u32[]{:S(2)}) %collective-permute-start.14) | collective-permute-done | bytes 16416 | tf_op jit(solution)/shard_map/ppermute | solution.py:439
  51.2 1.2 %collective-permute-done.15 = f32[16,128]{1,0:T(8,128)S(1)} collective-permute-done((f32[16,128]{1,0:T(8,128)S(1)}, f32[16,128]{1,0:T(8,128)S(1)}, u32[]{:S(2)}, u32[]{:S(2)}) %collective-permute-start.15) | collective-permute-done | bytes 8224 | tf_op jit(solution)/shard_map/ppermute | solution.py:439
  52.4 1.2 %layer_output.1 = (bf16[128,2048]{1,0:T(8,128)(2,1)}, bf16[128,2048]{1,0:T(8,128)(2,1)}, bf16[128,256]{1,0:T(8,128)(2,1)}, bf16[128,256]{1,0:T(8,128)(2,1)}, f32[1,128]{1,0:T(1,128)}, /*index=5*/f32[16,128]{1,0:T(8,128)}) custom-call(bf16[128,192]{1,0:T(8,128)(2,1)S(1)} %get-tuple-element.66.place_ref, f32[128,256]{1,0:T(8,128)S(1)} %get-tuple-element.67.weight_ref, ...), custom_call_target="tpu_custom_call" | custom-call | flops 100663296 | bytes 4522496 | tf_op jit(solution)/shard_map/layer_output/pallas_call | solution.py:420
  (18 shorter events, 0.1 us)
Async XLA Ops:
  2.2 10.0 %collective-permute-start.1 = (bf16[48,2048]{1,0:T(8,128)(2,1)S(1)}, bf16[48,2048]{1,0:T(8,128)(2,1)S(1)}, u32[]{:S(2)}, u32[]{:S(2)}) collective-permute-start(bf16[48,2048]{1,0:T(8,128)(2,1)S(1)} %get-tuple-element.63), channel_id=1, source_target_pairs={{0,4},{4,0},{8,12},{12,8},{1,5},{5,1},{9,13},{13,9},{2,6},{6,2},{1... | collective-permute-start | bytes 589832 | tf_op jit(solution)/shard_map/ppermute | solution.py:439
  5.2 2.1 %collective-permute-start = (bf16[128,256]{1,0:T(8,128)(2,1)}, bf16[128,256]{1,0:T(8,128)(2,1)S(1)}, u32[]{:S(2)}, u32[]{:S(2)}) collective-permute-start(bf16[128,256]{1,0:T(8,128)(2,1)} %bitcast.17), channel_id=1, source_target_pairs={{0,16},{16,0},{1,17},{17,1},{2,18},{18,2},{3,19},{19,3},{4,20},{20... | collective-permute-start | bytes 196616 | tf_op jit(solution)/shard_map/ppermute | solution.py:439
  5.2 2.1 %collective-permute-start.4 = (bf16[128,256]{1,0:T(8,128)(2,1)}, bf16[128,256]{1,0:T(8,128)(2,1)S(1)}, u32[]{:S(2)}, u32[]{:S(2)}) collective-permute-start(bf16[128,256]{1,0:T(8,128)(2,1)} %bitcast.19), channel_id=1, source_target_pairs={{0,16},{16,0},{1,17},{17,1},{2,18},{18,2},{3,19},{19,3},{4,20},{20... | collective-permute-start | bytes 196616 | tf_op jit(solution)/shard_map/ppermute | solution.py:439
  5.7 12.0 %collective-permute-start.2 = (bf16[48,2048]{1,0:T(8,128)(2,1)S(1)}, bf16[48,2048]{1,0:T(8,128)(2,1)S(1)}, u32[]{:S(2)}, u32[]{:S(2)}) collective-permute-start(bf16[48,2048]{1,0:T(8,128)(2,1)S(1)} %get-tuple-element.64), channel_id=1, source_target_pairs={{0,8},{4,12},{8,0},{12,4},{1,9},{5,13},{9,1},{13,5},{2,10},{6,14},... | collective-permute-start | bytes 589832 | tf_op jit(solution)/shard_map/ppermute | solution.py:439
  7.2 10.5 %collective-permute-start.3 = (bf16[48,2048]{1,0:T(8,128)(2,1)S(1)}, bf16[48,2048]{1,0:T(8,128)(2,1)S(1)}, u32[]{:S(2)}, u32[]{:S(2)}) collective-permute-start(bf16[48,2048]{1,0:T(8,128)(2,1)S(1)} %get-tuple-element.65), channel_id=1, source_target_pairs={{0,12},{4,8},{8,4},{12,0},{1,13},{5,9},{9,5},{13,1},{2,14},{6,10},... | collective-permute-start | bytes 589832 | tf_op jit(solution)/shard_map/ppermute | solution.py:439
  8.7 12.8 %collective-permute-start.5 = (bf16[48,2048]{1,0:T(8,128)(2,1)S(1)}, bf16[48,2048]{1,0:T(8,128)(2,1)S(1)}, u32[]{:S(2)}, u32[]{:S(2)}) collective-permute-start(bf16[48,2048]{1,0:T(8,128)(2,1)S(1)} %get-tuple-element.75), channel_id=1, source_target_pairs={{0,4},{4,0},{8,12},{12,8},{1,5},{5,1},{9,13},{13,9},{2,6},{6,2},{1... | collective-permute-start | bytes 589832 | tf_op jit(solution)/shard_map/ppermute | solution.py:439
  10.7 14.5 %collective-permute-start.6 = (bf16[48,2048]{1,0:T(8,128)(2,1)S(1)}, bf16[48,2048]{1,0:T(8,128)(2,1)S(1)}, u32[]{:S(2)}, u32[]{:S(2)}) collective-permute-start(bf16[48,2048]{1,0:T(8,128)(2,1)S(1)} %get-tuple-element.76), channel_id=1, source_target_pairs={{0,8},{4,12},{8,0},{12,4},{1,9},{5,13},{9,1},{13,5},{2,10},{6,14},... | collective-permute-start | bytes 589832 | tf_op jit(solution)/shard_map/ppermute | solution.py:439
  12.2 12.9 %collective-permute-start.7 = (bf16[48,2048]{1,0:T(8,128)(2,1)S(1)}, bf16[48,2048]{1,0:T(8,128)(2,1)S(1)}, u32[]{:S(2)}, u32[]{:S(2)}) collective-permute-start(bf16[48,2048]{1,0:T(8,128)(2,1)S(1)} %get-tuple-element.77), channel_id=1, source_target_pairs={{0,12},{4,8},{8,4},{12,0},{1,13},{5,9},{9,5},{13,1},{2,14},{6,10},... | collective-permute-start | bytes 589832 | tf_op jit(solution)/shard_map/ppermute | solution.py:439
  28.0 17.3 %collective-permute-start.10 = (bf16[96,2048]{1,0:T(8,128)(2,1)S(1)}, bf16[96,2048]{1,0:T(8,128)(2,1)S(1)}, u32[]{:S(2)}, u32[]{:S(2)}) collective-permute-start(bf16[96,2048]{1,0:T(8,128)(2,1)S(1)} %get-tuple-element.80.refs_5_), channel_id=1, source_target_pairs={{0,4},{4,0},{8,12},{12,8},{1,5},{5,1},{9,13},{13,9},{2,6},{6,2},{1... | collective-permute-start | bytes 1179656 | tf_op jit(solution)/shard_map/ppermute | solution.py:439
  28.4 16.9 %collective-permute-start.11 = (bf16[96,2048]{1,0:T(8,128)(2,1)S(1)}, bf16[96,2048]{1,0:T(8,128)(2,1)S(1)}, u32[]{:S(2)}, u32[]{:S(2)}) collective-permute-start(bf16[96,2048]{1,0:T(8,128)(2,1)S(1)} %get-tuple-element.81.refs_6_), channel_id=1, source_target_pairs={{0,8},{4,12},{8,0},{12,4},{1,9},{5,13},{9,1},{13,5},{2,10},{6,14},... | collective-permute-start | bytes 1179656 | tf_op jit(solution)/shard_map/ppermute | solution.py:439
  30.1 15.2 %collective-permute-start.12 = (bf16[48,2048]{1,0:T(8,128)(2,1)S(1)}, bf16[48,2048]{1,0:T(8,128)(2,1)S(1)}, u32[]{:S(2)}, u32[]{:S(2)}) collective-permute-start(bf16[48,2048]{1,0:T(8,128)(2,1)S(1)} %get-tuple-element.82.refs_7_), channel_id=1, source_target_pairs={{0,12},{4,8},{8,4},{12,0},{1,13},{5,9},{9,5},{13,1},{2,14},{6,10},... | collective-permute-start | bytes 589832 | tf_op jit(solution)/shard_map/ppermute | solution.py:439
  31.8 3.7 %collective-permute-start.8 = (f32[16,128]{1,0:T(8,128)S(1)}, f32[16,128]{1,0:T(8,128)S(1)}, u32[]{:S(2)}, u32[]{:S(2)}) collective-permute-start(f32[16,128]{1,0:T(8,128)S(1)} %gain_terms.1), channel_id=1, source_target_pairs={{0,1},{1,0},{2,3},{3,2},{4,5},{5,4},{6,7},{7,6},{8,9},{9,8},{10,11... | collective-permute-start | bytes 24584 | tf_op jit(solution)/shard_map/ppermute | solution.py:439
  35.6 4.5 %collective-permute-start.9 = (f32[16,128]{1,0:T(8,128)S(1)}, f32[16,128]{1,0:T(8,128)S(1)}, u32[]{:S(2)}, u32[]{:S(2)}) collective-permute-start(f32[16,128]{1,0:T(8,128)S(1)} %add.17), channel_id=1, source_target_pairs={{0,2},{1,3},{2,0},{3,1},{4,6},{5,7},{6,4},{7,5},{8,10},{9,11},{10,... | collective-permute-start | bytes 24584 | tf_op jit(solution)/shard_map/ppermute | solution.py:439
  40.1 7.2 %collective-permute-start.13 = (f32[16,128]{1,0:T(8,128)S(1)}, f32[16,128]{1,0:T(8,128)S(1)}, u32[]{:S(2)}, u32[]{:S(2)}) collective-permute-start(f32[16,128]{1,0:T(8,128)S(1)} %add.18), channel_id=1, source_target_pairs={{0,4},{4,0},{8,12},{12,8},{1,5},{5,1},{9,13},{13,9},{2,6},{6,2},{1... | collective-permute-start | bytes 24584 | tf_op jit(solution)/shard_map/ppermute | solution.py:439
  40.4 9.6 %collective-permute-start.16 = (bf16[48,2048]{1,0:T(8,128)(2,1)S(1)}, bf16[48,2048]{1,0:T(8,128)(2,1)S(1)}, u32[]{:S(2)}, u32[]{:S(2)}) collective-permute-start(bf16[48,2048]{1,0:T(8,128)(2,1)S(1)} %get-tuple-element.95), channel_id=1, source_target_pairs={{0,12},{4,8},{8,4},{12,0},{1,13},{5,9},{9,5},{13,1},{2,14},{6,10},... | collective-permute-start | bytes 589832 | tf_op jit(solution)/shard_map/ppermute | solution.py:439
  47.4 3.8 %collective-permute-start.14 = (f32[32,128]{1,0:T(8,128)S(1)}, f32[32,128]{1,0:T(8,128)S(1)}, u32[]{:S(2)}, u32[]{:S(2)}) collective-permute-start(f32[32,128]{1,0:T(8,128)S(1)} %pad.4), channel_id=1, source_target_pairs={{0,8},{4,12},{8,0},{12,4},{1,9},{5,13},{9,1},{13,5},{2,10},{6,14},... | collective-permute-start | bytes 49160 | tf_op jit(solution)/shard_map/ppermute | solution.py:439
  50.0 2.4 %collective-permute-start.17 = (bf16[128,512]{1,0:T(8,128)(2,1)S(1)}, bf16[128,512]{1,0:T(8,128)(2,1)S(1)}, u32[]{:S(2)}, u32[]{:S(2)}) collective-permute-start(bf16[128,512]{1,0:T(8,128)(2,1)S(1)} %get-tuple-element.97), channel_id=1, source_target_pairs={{0,16},{16,0},{1,17},{17,1},{2,18},{18,2},{3,19},{19,3},{4,20},{20... | collective-permute-start | bytes 393224 | tf_op jit(solution)/shard_map/ppermute | solution.py:439
  51.2 1.2 %collective-permute-start.15 = (f32[16,128]{1,0:T(8,128)S(1)}, f32[16,128]{1,0:T(8,128)S(1)}, u32[]{:S(2)}, u32[]{:S(2)}) collective-permute-start(f32[16,128]{1,0:T(8,128)S(1)} %slice_add_fusion), channel_id=1, source_target_pairs={{0,16},{16,0},{1,17},{17,1},{2,18},{18,2},{3,19},{19,3},{4,20},{20... | collective-permute-start | bytes 24584 | tf_op jit(solution)/shard_map/ppermute | solution.py:439

commit v16 on v14

--- a/solution.py
+++ b/solution.py
@@ -248,22 +248,13 @@
     return pieces > 1 and step > 0 and step & (step - 1) == 0
 
 
-def split_parts(refs, pieces):
-    back, out = [], []
-    at = 0
-    for s in range(pieces):
-        back.append(refs[at])
-        at += not joined(s, pieces)
-        out.append(refs[at])
-        at += 1
-    return back, out
-
-
 def expert_kernel(capacity, pieces, gate_ref, down_ref, d_act_ref, *refs):
     rows = stacked(refs[:pieces])
-    back_refs, out_refs = split_parts(refs[pieces:], pieces)
-    back_refs = part_views(back_refs, EXP_DEV * capacity, 0)
-    out_refs = part_views(out_refs, EXP_DEV * capacity, 1)
+    act_ref, piece_refs = refs[pieces], refs[pieces + 1 :]
+    span = EXP_DEV * capacity
+    back_refs = part_views(piece_refs, span, 0)
+    near = [s for s in range(pieces) if joined(s, pieces)]
+    out_refs = part_views([piece_refs[s] for s in near], span, 1)
     first = first_expert_rows(rows.shape[0], capacity)
     both = mm(rows, gate_ref[...])
     pre = jnp.where(first, both[:, :FFE], both[:, FFE:])
@@ -274,15 +265,27 @@
         jnp.concatenate([jnp.where(first, x, 0.0), jnp.where(first, 0.0, x)], axis=1).astype(BF16)
         for x in (act, d_pre)
     ]
+    act_ref[...] = act
+    near_act = [act[s * span : (s + 1) * span] for s in near]
+    near_act = jnp.concatenate(near_act, axis=0) if near else None
     for cols in column_blocks():
         store_pieces(back_refs, cols, mm(d_pre, gate_ref[cols, :], NT).astype(BF16))
+        if near:
+            store_pieces(out_refs, cols, mm(near_act, down_ref[:, cols]).astype(BF16))
+
+
+def gain_kernel(pieces, rows, gain_ref, down_ref, act_ref, *refs):
+    row_refs = refs[:pieces]
+    back_refs = part_views(refs[pieces : 2 * pieces], rows, 0)
+    terms_ref, out_refs = refs[2 * pieces], refs[2 * pieces + 1 :]
+    act = [act_ref[...]]
+    if pieces > 1:
+        act = [
+            act_ref[s * rows : (s + 1) * rows, :] for s in range(pieces) if not joined(s, pieces)
+        ]
+    act = jnp.concatenate(act, axis=0)
+    for cols in column_blocks():
         store_pieces(out_refs, cols, mm(act, down_ref[:, cols]).astype(BF16))
-
-
-def gain_kernel(pieces, rows, gain_ref, *refs):
-    row_refs = refs[:pieces]
-    back_refs = part_views(refs[pieces:-1], rows, 0)
-    terms_ref = refs[-1]
     for cols in column_blocks():
         products = stacked(row_refs, cols).astype(F32) * stacked(back_refs, cols).astype(F32)
         terms = jnp.sum(products, axis=0, keepdims=True) / gain_ref[:, cols]
@@ -567,31 +570,30 @@
         scratch=[pltpu.SemaphoreType.DMA((2 * EXP_DEV,))],
     )
 
-    return_shapes = []
-    for s in range(piece_count):
-        if joined(s, piece_count):
-            return_shapes.append(shaped((2 * rows, D), BF16))
-        else:
-            return_shapes.extend([piece_shapes[0]] * 2)
-    sent = run(
+    steps = range(piece_count)
+    apart = [s for s in steps if not joined(s, piece_count)]
+    far = [s for s in apart if s > 0]
+    return_shapes = [
+        piece_shapes[s] if s in apart else shaped((2 * rows, D), BF16) for s in steps
+    ]
+    act, *send_dn = run(
         functools.partial(expert_kernel, capacity, piece_count),
         "experts",
         placed(VMEM, [gate_near, down_near, d_act] + arrived_x),
-        placed(VMEM, return_shapes),
-        3 * expert_flops,
-    )
-    send_dn, send_y = split_parts(sent, piece_count)
+        placed(VMEM, [shaped((slots, EXP_DEV * FFE), BF16)] + return_shapes),
+        5 * expert_flops // 2,
+    )
     dn = exchange(send_dn, capacity)
-    far = [s for s in range(1, piece_count) if not joined(s, piece_count)]
+    terms, *outs = run(
+        functools.partial(gain_kernel, piece_count, rows),
+        "gain_terms",
+        placed(VMEM, [gain, down_near, act] + arrived_x + send_dn),
+        placed(VMEM, [shaped((GAIN_LINES, LANES), F32)] + [piece_shapes[s] for s in apart]),
+        expert_flops // 2,
+    )
+    send_y = dict(zip(apart, outs))
     y = list(dn) if piece_count > 1 else [exchange_flat(send_y[0], capacity)]
     y[0] = send_y[0] if piece_count > 1 else y[0]
-    (terms,) = run(
-        functools.partial(gain_kernel, piece_count, rows),
-        "gain_terms",
-        placed(VMEM, [gain] + arrived_x + send_dn),
-        placed(VMEM, [shaped((GAIN_LINES, LANES), F32)]),
-        2 * slots * D,
-    )
     terms = sum_over(sum_over(terms, "dp"), "ctx")
     send_far, terms = lax.optimization_barrier(([send_y[s] for s in far], terms))
     for s, piece in zip(far, send_far):

time: 52.2 us -> 52.7 us (level)
  no operation moved by 1% of the time
where the time goes in v16:
time: 52.7 us; the launch traced here: 52.5 us
  starting transfers between devices  21.7 us (41%)
  Pallas kernels  15.2 us (29%)
  waiting for transfers between devices  14.9 us (28%)
  between operations  0.74 us (1%)
    ppermute x18, starting transfers between devices, pairwise(): return lax.ppermute(value, axis, [(i, i ^ step) for i in range(count)])  21.7 us
    pallas_call x8, Pallas kernels, run(): pl.pallas_call(kernel, out_shape=[x for _, x in outputs], in_specs=[spec[...  15.2 us
    ppermute x18, waiting for transfers between devices, pairwise(): return lax.ppermute(value, axis, [(i, i ^ step) for i in range(count)])  14.9 us
  transfers between devices with their start and end apart: 18, of which 8 were waited for; matrix products, arithmetic and copies ran while one was open for 0% of the time, Pallas kernels for 18%

profile of v16, /device:TPU:0, one launch (start us, length us, event | category | flops | bytes accessed | tf_op | source)
XLA Modules:
  0.0 52.5 jit_solution(9196950686861779866)
XLA Ops:
  0.6 1.5 %dispatch_grads.1 = (bf16[128,2048]{1,0:T(8,128)(2,1)S(1)}, bf16[128,256]{1,0:T(8,128)(2,1)S(1)}, bf16[128,256]{1,0:T(8,128)(2,1)S(1)}, f32[1,2048]{1,0:T(1,128)...) custom-call(bf16[128,2048]{1,0:T(8,128)(2,1)} %bitcast.13, ...), custom_call_target="tpu_custom_call" | custom-call | flops 100663296 | bytes 4213824 | tf_op jit(solution)/shard_map/dispatch_grads/pallas_call | solution.py:423
  2.2 3.0 %collective-permute-start.1 = (bf16[48,2048]{1,0:T(8,128)(2,1)S(1)}, bf16[48,2048]{1,0:T(8,128)(2,1)S(1)}, u32[]{:S(2)}, u32[]{:S(2)}) collective-permute-start(bf16[48,2048]{1,0:T(8,128)(2,1)S(1)} %get-tuple-element.65), channel_id=1, source_target_pairs={{0,4},{4,0},{8,12},{12,8},{1,5},{5,1},{9,13},{13,9},{2,6},{6,2},{1... | collective-permute-start | bytes 589832 | tf_op jit(solution)/shard_map/ppermute | solution.py:442
  5.2 0.0 collective-permute-start
  5.2 0.5 collective-permute-start.4
  5.7 1.5 %collective-permute-start.2 = (bf16[48,2048]{1,0:T(8,128)(2,1)S(1)}, bf16[48,2048]{1,0:T(8,128)(2,1)S(1)}, u32[]{:S(2)}, u32[]{:S(2)}) collective-permute-start(bf16[48,2048]{1,0:T(8,128)(2,1)S(1)} %get-tuple-element.66), channel_id=1, source_target_pairs={{0,8},{4,12},{8,0},{12,4},{1,9},{5,13},{9,1},{13,5},{2,10},{6,14},... | collective-permute-start | bytes 589832 | tf_op jit(solution)/shard_map/ppermute | solution.py:442
  7.2 0.0 collective-permute-start.3
  7.2 1.4 %attention_forward.1 = (bf16[128,2048]{1,0:T(8,128)(2,1)S(1)}, bf16[48,2048]{1,0:T(8,128)(2,1)S(1)}, bf16[48,2048]{1,0:T(8,128)(2,1)S(1)}, bf16[48,2048]{1,0:T(8,128)(2,1)S(1)}, bf16[48,2048]{1,0:T(8,128)(2,1)S(1)}) custom-call(s32[2,128]{1,0:T(2,128)S(1)} %get-tuple-element.59.pos_ref, s32[1,128]{1,0:T(1,128)S(1)} %get-tuple-element.60.slot_ref, ...), custom_call_target="tpu_custom_call" | custom-call | flops 369098752 | bytes 2631168 | tf_op jit(solution)/shard_map/attention_forward/pallas_call | solution.py:423
  8.7 2.0 %collective-permute-start.5 = (bf16[48,2048]{1,0:T(8,128)(2,1)S(1)}, bf16[48,2048]{1,0:T(8,128)(2,1)S(1)}, u32[]{:S(2)}, u32[]{:S(2)}) collective-permute-start(bf16[48,2048]{1,0:T(8,128)(2,1)S(1)} %get-tuple-element.77), channel_id=1, source_target_pairs={{0,4},{4,0},{8,12},{12,8},{1,5},{5,1},{9,13},{13,9},{2,6},{6,2},{1... | collective-permute-start | bytes 589832 | tf_op jit(solution)/shard_map/ppermute | solution.py:442
  10.7 1.5 %collective-permute-start.6 = (bf16[48,2048]{1,0:T(8,128)(2,1)S(1)}, bf16[48,2048]{1,0:T(8,128)(2,1)S(1)}, u32[]{:S(2)}, u32[]{:S(2)}) collective-permute-start(bf16[48,2048]{1,0:T(8,128)(2,1)S(1)} %get-tuple-element.78), channel_id=1, source_target_pairs={{0,8},{4,12},{8,0},{12,4},{1,9},{5,13},{9,1},{13,5},{2,10},{6,14},... | collective-permute-start | bytes 589832 | tf_op jit(solution)/shard_map/ppermute | solution.py:442
  12.2 1.7 %collective-permute-start.7 = (bf16[48,2048]{1,0:T(8,128)(2,1)S(1)}, bf16[48,2048]{1,0:T(8,128)(2,1)S(1)}, u32[]{:S(2)}, u32[]{:S(2)}) collective-permute-start(bf16[48,2048]{1,0:T(8,128)(2,1)S(1)} %get-tuple-element.79), channel_id=1, source_target_pairs={{0,12},{4,8},{8,4},{12,0},{1,13},{5,9},{9,5},{13,1},{2,14},{6,10},... | collective-permute-start | bytes 589832 | tf_op jit(solution)/shard_map/ppermute | solution.py:442
  13.9 3.7 %collective-permute-done.2.refs_4_ = bf16[48,2048]{1,0:T(8,128)(2,1)S(1)} collective-permute-done((bf16[48,2048]{1,0:T(8,128)(2,1)S(1)}, bf16[48,2048]{1,0:T(8,128)(2,1)S(1)}, u32[]{:S(2)}, u32[]{:S(2)}) %collective-permute-start.2) | collective-permute-done | bytes 196640 | tf_op jit(solution)/shard_map/ppermute | solution.py:442
  17.7 3.8 %act_grads_and_probs.1 = (f32[192,384]{1,0:T(8,128)S(1)}, f32[8,256,256]{2,1,0:T(8,128)S(1)}, bf16[768,2048]{1,0:T(8,128)(2,1)S(1)}, bf16[2048,768]{1,0:T(8,128)...) custom-call(s32[2,128]{1,0:T(2,128)S(1)} %get-tuple-element.59.pos_ref, ...), custom_call_target="tpu_custom_call" | custom-call | flops 738197504 | bytes 16599040 | tf_op jit(solution)/shard_map/act_grads_and_probs/pallas_call | solution.py:423
  21.5 3.6 %collective-permute-done.6.refs_2_ = bf16[48,2048]{1,0:T(8,128)(2,1)S(1)} collective-permute-done((bf16[48,2048]{1,0:T(8,128)(2,1)S(1)}, bf16[48,2048]{1,0:T(8,128)(2,1)S(1)}, u32[]{:S(2)}, u32[]{:S(2)}) %collective-permute-start.6) | collective-permute-done | bytes 196640 | tf_op jit(solution)/shard_map/ppermute | solution.py:442
  25.1 2.7 %experts.1 = (bf16[192,768]{1,0:T(8,128)(2,1)S(1)}, bf16[48,2048]{1,0:T(8,128)(2,1)S(1)}, bf16[96,2048]{1,0:T(8,128)(2,1)S(1)}, bf16[96,2048]{1,0:T(8,128)(2,1)S(1)}, bf16[48,2048]{1,0:T(8,128)(2,1)S(1)}) custom-call(bf16[2048,768]{1,0:T(8,128)(2,1)S(1)} %get-tuple-element.72.gate_ref, bf16[768,2048]{1,0:T(8,128)(2,1)S(1)} %get-tuple-element.71.down_ref, ...), custom_call_target="tpu_custom_call" | custom-call | flops 1509949440 | bytes 8847360 | tf_op jit(solution)/shard_map/experts/pallas_call | solution.py:423
  27.9 0.4 collective-permute-start.11
  28.3 1.7 %collective-permute-start.12 = (bf16[96,2048]{1,0:T(8,128)(2,1)S(1)}, bf16[96,2048]{1,0:T(8,128)(2,1)S(1)}, u32[]{:S(2)}, u32[]{:S(2)}) collective-permute-start(bf16[96,2048]{1,0:T(8,128)(2,1)S(1)} %get-tuple-element.83.refs_6_), channel_id=1, source_target_pairs={{0,8},{4,12},{8,0},{12,4},{1,9},{5,13},{9,1},{13,5},{2,10},{6,14},... | collective-permute-start | bytes 1179656 | tf_op jit(solution)/shard_map/ppermute | solution.py:442
  30.0 1.4 %collective-permute-start.13 = (bf16[48,2048]{1,0:T(8,128)(2,1)S(1)}, bf16[48,2048]{1,0:T(8,128)(2,1)S(1)}, u32[]{:S(2)}, u32[]{:S(2)}) collective-permute-start(bf16[48,2048]{1,0:T(8,128)(2,1)S(1)} %get-tuple-element.84.refs_7_), channel_id=1, source_target_pairs={{0,12},{4,8},{8,4},{12,0},{1,13},{5,9},{9,5},{13,1},{2,14},{6,10},... | collective-permute-start | bytes 589832 | tf_op jit(solution)/shard_map/ppermute | solution.py:442
  31.5 0.9 %gain_terms.1 = (f32[16,128]{1,0:T(8,128)S(1)}, bf16[48,2048]{1,0:T(8,128)(2,1)S(1)}, bf16[48,2048]{1,0:T(8,128)(2,1)S(1)}) custom-call(f32[1,2048]{1,0:T(1,128)S(1)} %get-tuple-element.70.gain_ref, bf16[768,2048]{1,0:T(8,128)(2,1)S(1)} %get-tuple-element.71.down_ref, bf16[192,768]{1,0:T(8,128)(2,1)S(1)} %get-tuple-element.80.act_ref, ...), custom_call_target="tpu_custom_call" | custom-call | flops 301989888 | bytes 5816320 | tf_op jit(solution)/shard_map/gain_terms/pallas_call | solution.py:423
  32.3 1.6 %collective-permute-start.8 = (f32[16,128]{1,0:T(8,128)S(1)}, f32[16,128]{1,0:T(8,128)S(1)}, u32[]{:S(2)}, u32[]{:S(2)}) collective-permute-start(f32[16,128]{1,0:T(8,128)S(1)} %get-tuple-element.86), channel_id=1, source_target_pairs={{0,1},{1,0},{2,3},{3,2},{4,5},{5,4},{6,7},{7,6},{8,9},{9,8},{10,11... | collective-permute-start | bytes 24584 | tf_op jit(solution)/shard_map/ppermute | solution.py:442
  34.0 2.1 %collective-permute-done.8 = f32[16,128]{1,0:T(8,128)S(1)} collective-permute-done((f32[16,128]{1,0:T(8,128)S(1)}, f32[16,128]{1,0:T(8,128)S(1)}, u32[]{:S(2)}, u32[]{:S(2)}) %collective-permute-start.8) | collective-permute-done | bytes 8224 | tf_op jit(solution)/shard_map/ppermute | solution.py:442
  36.0 2.7 %collective-permute-start.9 = (f32[16,128]{1,0:T(8,128)S(1)}, f32[16,128]{1,0:T(8,128)S(1)}, u32[]{:S(2)}, u32[]{:S(2)}) collective-permute-start(f32[16,128]{1,0:T(8,128)S(1)} %add.17), channel_id=1, source_target_pairs={{0,2},{1,3},{2,0},{3,1},{4,6},{5,7},{6,4},{7,5},{8,10},{9,11},{10,... | collective-permute-start | bytes 24584 | tf_op jit(solution)/shard_map/ppermute | solution.py:442
  38.7 1.9 %collective-permute-done.9 = f32[16,128]{1,0:T(8,128)S(1)} collective-permute-done((f32[16,128]{1,0:T(8,128)S(1)}, f32[16,128]{1,0:T(8,128)S(1)}, u32[]{:S(2)}, u32[]{:S(2)}) %collective-permute-start.9) | collective-permute-done | bytes 8224 | tf_op jit(solution)/shard_map/ppermute | solution.py:442
  40.6 1.2 %collective-permute-done.10 = f32[16,128]{1,0:T(8,128)S(1)} collective-permute-done((f32[16,128]{1,0:T(8,128)S(1)}, f32[16,128]{1,0:T(8,128)S(1)}, u32[]{:S(2)}, u32[]{:S(2)}) %collective-permute-start.10) | collective-permute-done | bytes 8224 | tf_op jit(solution)/shard_map/ppermute | solution.py:442
  41.8 0.3 collective-permute-start.14
  42.1 2.7 %collective-permute-start.16 = (bf16[48,2048]{1,0:T(8,128)(2,1)S(1)}, bf16[48,2048]{1,0:T(8,128)(2,1)S(1)}, u32[]{:S(2)}, u32[]{:S(2)}) collective-permute-start(bf16[48,2048]{1,0:T(8,128)(2,1)S(1)} %get-tuple-element.99), channel_id=1, source_target_pairs={{0,12},{4,8},{8,4},{12,0},{1,13},{5,9},{9,5},{13,1},{2,14},{6,10},... | collective-permute-start | bytes 589832 | tf_op jit(solution)/shard_map/ppermute | solution.py:442
  44.8 2.1 %residual_and_first_group.1 = (bf16[128,2048]{1,0:T(8,128)(2,1)}, bf16[128,1024]{1,0:T(8,128)(2,1)S(1)}, bf16[128,1024]{1,0:T(8,128)(2,1)S(1)}, f32[128,256]{1,0:T(8,128)S(1)}, bf16[128,256]{1,0:T(8,128)(2,1)S(1)}) custom-call(bf16[128,192]{1,0:T(8,128)(2,1)S(1)} %get-tuple-element.68.place_ref, f32[1,2048]{1,0:T(1,128)S(1)} %get-tuple-element.70.gain_ref, ...), custom_call_target="tpu_custom_call" | custom-call | flops 4000000000 | bytes 6414336 | tf_op jit(solution)/shard_map/residual_and_first_group/pallas_call | solution.py:423
  46.9 0.6 %collective-permute-start.15 = (f32[32,128]{1,0:T(8,128)S(1)}, f32[32,128]{1,0:T(8,128)S(1)}, u32[]{:S(2)}, u32[]{:S(2)}) collective-permute-start(f32[32,128]{1,0:T(8,128)S(1)} %pad.4), channel_id=1, source_target_pairs={{0,8},{4,12},{8,0},{12,4},{1,9},{5,13},{9,1},{13,5},{2,10},{6,14},... | collective-permute-start | bytes 49160 | tf_op jit(solution)/shard_map/ppermute | solution.py:442
  47.4 1.5 %second_group.1 = (bf16[128,1024]{1,0:T(8,128)(2,1)S(1)}, f32[128,256]{1,0:T(8,128)S(1)}, bf16[128,512]{1,0:T(8,128)(2,1)S(1)}) custom-call(bf16[128,2048]{1,0:T(8,128)(2,1)S(1)} %get-tuple-element.62.query_ref, f32[8,256,256]{2,1,0:T(8,128)S(1)} %get-tuple-element.90.probs_ref, bf16[128,1024]{1,0:T(8,128)(2,1)S(1)} %get-tuple-element.94.rest_ref, ...), custom_call_target="tpu_custom_call" | custom-call | tf_op jit(solution)/shard_map/second_group/pallas_call | solution.py:423
  49.0 1.0 %collective-permute-done.16.refs_8_ = bf16[48,2048]{1,0:T(8,128)(2,1)S(1)} collective-permute-done((bf16[48,2048]{1,0:T(8,128)(2,1)S(1)}, bf16[48,2048]{1,0:T(8,128)(2,1)S(1)}, u32[]{:S(2)}, u32[]{:S(2)}) %collective-permute-start.16) | collective-permute-done | bytes 196640 | tf_op jit(solution)/shard_map/ppermute | solution.py:442
  49.9 0.7 %collective-permute-done.15 = f32[32,128]{1,0:T(8,128)S(1)} collective-permute-done((f32[32,128]{1,0:T(8,128)S(1)}, f32[32,128]{1,0:T(8,128)S(1)}, u32[]{:S(2)}, u32[]{:S(2)}) %collective-permute-start.15) | collective-permute-done | bytes 16416 | tf_op jit(solution)/shard_map/ppermute | solution.py:442
  50.7 0.6 %collective-permute-done.17.refs_4_ = bf16[128,512]{1,0:T(8,128)(2,1)S(1)} collective-permute-done((bf16[128,512]{1,0:T(8,128)(2,1)S(1)}, bf16[128,512]{1,0:T(8,128)(2,1)S(1)}, u32[]{:S(2)}, u32[]{:S(2)}) %collective-permute-start.17) | collective-permute-done | bytes 131104 | tf_op jit(solution)/shard_map/ppermute | solution.py:442
  51.3 1.2 %layer_output.1 = (bf16[128,2048]{1,0:T(8,128)(2,1)}, bf16[128,2048]{1,0:T(8,128)(2,1)}, bf16[128,256]{1,0:T(8,128)(2,1)}, bf16[128,256]{1,0:T(8,128)(2,1)}, f32[1,128]{1,0:T(1,128)}, /*index=5*/f32[16,128]{1,0:T(8,128)}) custom-call(bf16[128,192]{1,0:T(8,128)(2,1)S(1)} %get-tuple-element.68.place_ref, f32[128,256]{1,0:T(8,128)S(1)} %get-tuple-element.69.weight_ref, ...), custom_call_target="tpu_custom_call" | custom-call | flops 100663296 | bytes 4522496 | tf_op jit(solution)/shard_map/layer_output/pallas_call | solution.py:423
  (18 shorter events, 0.1 us)
Async XLA Ops:
  2.2 10.0 %collective-permute-start.1 = (bf16[48,2048]{1,0:T(8,128)(2,1)S(1)}, bf16[48,2048]{1,0:T(8,128)(2,1)S(1)}, u32[]{:S(2)}, u32[]{:S(2)}) collective-permute-start(bf16[48,2048]{1,0:T(8,128)(2,1)S(1)} %get-tuple-element.65), channel_id=1, source_target_pairs={{0,4},{4,0},{8,12},{12,8},{1,5},{5,1},{9,13},{13,9},{2,6},{6,2},{1... | collective-permute-start | bytes 589832 | tf_op jit(solution)/shard_map/ppermute | solution.py:442
  5.2 2.1 %collective-permute-start = (bf16[128,256]{1,0:T(8,128)(2,1)}, bf16[128,256]{1,0:T(8,128)(2,1)S(1)}, u32[]{:S(2)}, u32[]{:S(2)}) collective-permute-start(bf16[128,256]{1,0:T(8,128)(2,1)} %bitcast.17), channel_id=1, source_target_pairs={{0,16},{16,0},{1,17},{17,1},{2,18},{18,2},{3,19},{19,3},{4,20},{20... | collective-permute-start | bytes 196616 | tf_op jit(solution)/shard_map/ppermute | solution.py:442
  5.2 2.1 %collective-permute-start.4 = (bf16[128,256]{1,0:T(8,128)(2,1)}, bf16[128,256]{1,0:T(8,128)(2,1)S(1)}, u32[]{:S(2)}, u32[]{:S(2)}) collective-permute-start(bf16[128,256]{1,0:T(8,128)(2,1)} %bitcast.19), channel_id=1, source_target_pairs={{0,16},{16,0},{1,17},{17,1},{2,18},{18,2},{3,19},{19,3},{4,20},{20... | collective-permute-start | bytes 196616 | tf_op jit(solution)/shard_map/ppermute | solution.py:442
  5.7 12.0 %collective-permute-start.2 = (bf16[48,2048]{1,0:T(8,128)(2,1)S(1)}, bf16[48,2048]{1,0:T(8,128)(2,1)S(1)}, u32[]{:S(2)}, u32[]{:S(2)}) collective-permute-start(bf16[48,2048]{1,0:T(8,128)(2,1)S(1)} %get-tuple-element.66), channel_id=1, source_target_pairs={{0,8},{4,12},{8,0},{12,4},{1,9},{5,13},{9,1},{13,5},{2,10},{6,14},... | collective-permute-start | bytes 589832 | tf_op jit(solution)/shard_map/ppermute | solution.py:442
  7.2 10.5 %collective-permute-start.3 = (bf16[48,2048]{1,0:T(8,128)(2,1)S(1)}, bf16[48,2048]{1,0:T(8,128)(2,1)S(1)}, u32[]{:S(2)}, u32[]{:S(2)}) collective-permute-start(bf16[48,2048]{1,0:T(8,128)(2,1)S(1)} %get-tuple-element.67), channel_id=1, source_target_pairs={{0,12},{4,8},{8,4},{12,0},{1,13},{5,9},{9,5},{13,1},{2,14},{6,10},... | collective-permute-start | bytes 589832 | tf_op jit(solution)/shard_map/ppermute | solution.py:442
  8.7 12.8 %collective-permute-start.5 = (bf16[48,2048]{1,0:T(8,128)(2,1)S(1)}, bf16[48,2048]{1,0:T(8,128)(2,1)S(1)}, u32[]{:S(2)}, u32[]{:S(2)}) collective-permute-start(bf16[48,2048]{1,0:T(8,128)(2,1)S(1)} %get-tuple-element.77), channel_id=1, source_target_pairs={{0,4},{4,0},{8,12},{12,8},{1,5},{5,1},{9,13},{13,9},{2,6},{6,2},{1... | collective-permute-start | bytes 589832 | tf_op jit(solution)/shard_map/ppermute | solution.py:442
  10.7 14.5 %collective-permute-start.6 = (bf16[48,2048]{1,0:T(8,128)(2,1)S(1)}, bf16[48,2048]{1,0:T(8,128)(2,1)S(1)}, u32[]{:S(2)}, u32[]{:S(2)}) collective-permute-start(bf16[48,2048]{1,0:T(8,128)(2,1)S(1)} %get-tuple-element.78), channel_id=1, source_target_pairs={{0,8},{4,12},{8,0},{12,4},{1,9},{5,13},{9,1},{13,5},{2,10},{6,14},... | collective-permute-start | bytes 589832 | tf_op jit(solution)/shard_map/ppermute | solution.py:442
  12.2 12.9 %collective-permute-start.7 = (bf16[48,2048]{1,0:T(8,128)(2,1)S(1)}, bf16[48,2048]{1,0:T(8,128)(2,1)S(1)}, u32[]{:S(2)}, u32[]{:S(2)}) collective-permute-start(bf16[48,2048]{1,0:T(8,128)(2,1)S(1)} %get-tuple-element.79), channel_id=1, source_target_pairs={{0,12},{4,8},{8,4},{12,0},{1,13},{5,9},{9,5},{13,1},{2,14},{6,10},... | collective-permute-start | bytes 589832 | tf_op jit(solution)/shard_map/ppermute | solution.py:442
  27.9 16.8 %collective-permute-start.11 = (bf16[96,2048]{1,0:T(8,128)(2,1)S(1)}, bf16[96,2048]{1,0:T(8,128)(2,1)S(1)}, u32[]{:S(2)}, u32[]{:S(2)}) collective-permute-start(bf16[96,2048]{1,0:T(8,128)(2,1)S(1)} %get-tuple-element.82.refs_5_), channel_id=1, source_target_pairs={{0,4},{4,0},{8,12},{12,8},{1,5},{5,1},{9,13},{13,9},{2,6},{6,2},{1... | collective-permute-start | bytes 1179656 | tf_op jit(solution)/shard_map/ppermute | solution.py:442
  28.3 16.5 %collective-permute-start.12 = (bf16[96,2048]{1,0:T(8,128)(2,1)S(1)}, bf16[96,2048]{1,0:T(8,128)(2,1)S(1)}, u32[]{:S(2)}, u32[]{:S(2)}) collective-permute-start(bf16[96,2048]{1,0:T(8,128)(2,1)S(1)} %get-tuple-element.83.refs_6_), channel_id=1, source_target_pairs={{0,8},{4,12},{8,0},{12,4},{1,9},{5,13},{9,1},{13,5},{2,10},{6,14},... | collective-permute-start | bytes 1179656 | tf_op jit(solution)/shard_map/ppermute | solution.py:442
  30.0 14.7 %collective-permute-start.13 = (bf16[48,2048]{1,0:T(8,128)(2,1)S(1)}, bf16[48,2048]{1,0:T(8,128)(2,1)S(1)}, u32[]{:S(2)}, u32[]{:S(2)}) collective-permute-start(bf16[48,2048]{1,0:T(8,128)(2,1)S(1)} %get-tuple-element.84.refs_7_), channel_id=1, source_target_pairs={{0,12},{4,8},{8,4},{12,0},{1,13},{5,9},{9,5},{13,1},{2,14},{6,10},... | collective-permute-start | bytes 589832 | tf_op jit(solution)/shard_map/ppermute | solution.py:442
  32.3 3.7 %collective-permute-start.8 = (f32[16,128]{1,0:T(8,128)S(1)}, f32[16,128]{1,0:T(8,128)S(1)}, u32[]{:S(2)}, u32[]{:S(2)}) collective-permute-start(f32[16,128]{1,0:T(8,128)S(1)} %get-tuple-element.86), channel_id=1, source_target_pairs={{0,1},{1,0},{2,3},{3,2},{4,5},{5,4},{6,7},{7,6},{8,9},{9,8},{10,11... | collective-permute-start | bytes 24584 | tf_op jit(solution)/shard_map/ppermute | solution.py:442
  36.0 4.5 %collective-permute-start.9 = (f32[16,128]{1,0:T(8,128)S(1)}, f32[16,128]{1,0:T(8,128)S(1)}, u32[]{:S(2)}, u32[]{:S(2)}) collective-permute-start(f32[16,128]{1,0:T(8,128)S(1)} %add.17), channel_id=1, source_target_pairs={{0,2},{1,3},{2,0},{3,1},{4,6},{5,7},{6,4},{7,5},{8,10},{9,11},{10,... | collective-permute-start | bytes 24584 | tf_op jit(solution)/shard_map/ppermute | solution.py:442
  40.6 1.2 %collective-permute-start.10 = (f32[16,128]{1,0:T(8,128)S(1)}, f32[16,128]{1,0:T(8,128)S(1)}, u32[]{:S(2)}, u32[]{:S(2)}) collective-permute-start(f32[16,128]{1,0:T(8,128)S(1)} %add.18), channel_id=1, source_target_pairs={{0,16},{16,0},{1,17},{17,1},{2,18},{18,2},{3,19},{19,3},{4,20},{20... | collective-permute-start | bytes 24584 | tf_op jit(solution)/shard_map/ppermute | solution.py:442
  41.8 5.1 %collective-permute-start.14 = (f32[16,128]{1,0:T(8,128)S(1)}, f32[16,128]{1,0:T(8,128)S(1)}, u32[]{:S(2)}, u32[]{:S(2)}) collective-permute-start(f32[16,128]{1,0:T(8,128)S(1)} %add.19), channel_id=1, source_target_pairs={{0,4},{4,0},{8,12},{12,8},{1,5},{5,1},{9,13},{13,9},{2,6},{6,2},{1... | collective-permute-start | bytes 24584 | tf_op jit(solution)/shard_map/ppermute | solution.py:442
  42.1 7.8 %collective-permute-start.16 = (bf16[48,2048]{1,0:T(8,128)(2,1)S(1)}, bf16[48,2048]{1,0:T(8,128)(2,1)S(1)}, u32[]{:S(2)}, u32[]{:S(2)}) collective-permute-start(bf16[48,2048]{1,0:T(8,128)(2,1)S(1)} %get-tuple-element.99), channel_id=1, source_target_pairs={{0,12},{4,8},{8,4},{12,0},{1,13},{5,9},{9,5},{13,1},{2,14},{6,10},... | collective-permute-start | bytes 589832 | tf_op jit(solution)/shard_map/ppermute | solution.py:442
  46.9 3.8 %collective-permute-start.15 = (f32[32,128]{1,0:T(8,128)S(1)}, f32[32,128]{1,0:T(8,128)S(1)}, u32[]{:S(2)}, u32[]{:S(2)}) collective-permute-start(f32[32,128]{1,0:T(8,128)S(1)} %pad.4), channel_id=1, source_target_pairs={{0,8},{4,12},{8,0},{12,4},{1,9},{5,13},{9,1},{13,5},{2,10},{6,14},... | collective-permute-start | bytes 49160 | tf_op jit(solution)/shard_map/ppermute | solution.py:442
  49.9 1.3 %collective-permute-start.17 = (bf16[128,512]{1,0:T(8,128)(2,1)S(1)}, bf16[128,512]{1,0:T(8,128)(2,1)S(1)}, u32[]{:S(2)}, u32[]{:S(2)}) collective-permute-start(bf16[128,512]{1,0:T(8,128)(2,1)S(1)} %get-tuple-element.101), channel_id=1, source_target_pairs={{0,16},{16,0},{1,17},{17,1},{2,18},{18,2},{3,19},{19,3},{4,20},{20... | collective-permute-start | bytes 393224 | tf_op jit(solution)/shard_map/ppermute | solution.py:442

commit v17 on v14

--- a/solution.py
+++ b/solution.py
@@ -14,7 +14,7 @@
 GROUP = QUERY_HEADS // KEY_VALUE_HEADS
 FFE = 384
 EXP_DEV = 2
-COLS = 256
+COLS = 512
 LANES = 128
 GAIN_LINES = D // LANES
 WIDE_LINES = 32

time: 52.2 us -> 52.2 us (level)
  no operation moved by 1% of the time
where the time goes in v17:
time: 52.2 us; the launch traced here: 52 us
  starting transfers between devices  21.7 us (42%)
  waiting for transfers between devices  14.9 us (29%)
  Pallas kernels  14.7 us (28%)
  between operations  0.73 us (1%)
    ppermute x18, starting transfers between devices, pairwise(): return lax.ppermute(value, axis, [(i, i ^ step) for i in range(count)])  21.7 us
    ppermute x18, waiting for transfers between devices, pairwise(): return lax.ppermute(value, axis, [(i, i ^ step) for i in range(count)])  14.9 us
    pallas_call x8, Pallas kernels, run(): pl.pallas_call(kernel, out_shape=[x for _, x in outputs], in_specs=[spec[...  14.7 us
  transfers between devices with their start and end apart: 18, of which 8 were waited for; matrix products, arithmetic and copies ran while one was open for 0% of the time, Pallas kernels for 18%

profile of v17, /device:TPU:0, one launch (start us, length us, event | category | flops | bytes accessed | tf_op | source)
XLA Modules:
  0.0 52.0 jit_solution(10158952238155914989)
XLA Ops:
  0.6 1.5 %dispatch_grads.1 = (bf16[128,2048]{1,0:T(8,128)(2,1)S(1)}, bf16[128,256]{1,0:T(8,128)(2,1)S(1)}, bf16[128,256]{1,0:T(8,128)(2,1)S(1)}, f32[1,2048]{1,0:T(1,128)...) custom-call(bf16[128,2048]{1,0:T(8,128)(2,1)} %bitcast.13, ...), custom_call_target="tpu_custom_call" | custom-call | flops 100663296 | bytes 4213824 | tf_op jit(solution)/shard_map/dispatch_grads/pallas_call | solution.py:420
  2.2 3.0 %collective-permute-start.1 = (bf16[48,2048]{1,0:T(8,128)(2,1)S(1)}, bf16[48,2048]{1,0:T(8,128)(2,1)S(1)}, u32[]{:S(2)}, u32[]{:S(2)}) collective-permute-start(bf16[48,2048]{1,0:T(8,128)(2,1)S(1)} %get-tuple-element.63), channel_id=1, source_target_pairs={{0,4},{4,0},{8,12},{12,8},{1,5},{5,1},{9,13},{13,9},{2,6},{6,2},{1... | collective-permute-start | bytes 589832 | tf_op jit(solution)/shard_map/ppermute | solution.py:439
  5.2 0.5 collective-permute-start.4
  5.7 1.5 %collective-permute-start.2 = (bf16[48,2048]{1,0:T(8,128)(2,1)S(1)}, bf16[48,2048]{1,0:T(8,128)(2,1)S(1)}, u32[]{:S(2)}, u32[]{:S(2)}) collective-permute-start(bf16[48,2048]{1,0:T(8,128)(2,1)S(1)} %get-tuple-element.64), channel_id=1, source_target_pairs={{0,8},{4,12},{8,0},{12,4},{1,9},{5,13},{9,1},{13,5},{2,10},{6,14},... | collective-permute-start | bytes 589832 | tf_op jit(solution)/shard_map/ppermute | solution.py:439
  7.2 0.0 collective-permute-start.3
  7.2 0.0 collective-permute-done.refs_1_
  7.2 1.4 %attention_forward.1 = (bf16[128,2048]{1,0:T(8,128)(2,1)S(1)}, bf16[48,2048]{1,0:T(8,128)(2,1)S(1)}, bf16[48,2048]{1,0:T(8,128)(2,1)S(1)}, bf16[48,2048]{1,0:T(8,128)(2,1)S(1)}, bf16[48,2048]{1,0:T(8,128)(2,1)S(1)}) custom-call(s32[2,128]{1,0:T(2,128)S(1)} %get-tuple-element.57.pos_ref, s32[1,128]{1,0:T(1,128)S(1)} %get-tuple-element.58.slot_ref, ...), custom_call_target="tpu_custom_call" | custom-call | flops 369098752 | bytes 2631168 | tf_op jit(solution)/shard_map/attention_forward/pallas_call | solution.py:420
  8.7 2.0 %collective-permute-start.5 = (bf16[48,2048]{1,0:T(8,128)(2,1)S(1)}, bf16[48,2048]{1,0:T(8,128)(2,1)S(1)}, u32[]{:S(2)}, u32[]{:S(2)}) collective-permute-start(bf16[48,2048]{1,0:T(8,128)(2,1)S(1)} %get-tuple-element.75), channel_id=1, source_target_pairs={{0,4},{4,0},{8,12},{12,8},{1,5},{5,1},{9,13},{13,9},{2,6},{6,2},{1... | collective-permute-start | bytes 589832 | tf_op jit(solution)/shard_map/ppermute | solution.py:439
  10.7 1.5 %collective-permute-start.6 = (bf16[48,2048]{1,0:T(8,128)(2,1)S(1)}, bf16[48,2048]{1,0:T(8,128)(2,1)S(1)}, u32[]{:S(2)}, u32[]{:S(2)}) collective-permute-start(bf16[48,2048]{1,0:T(8,128)(2,1)S(1)} %get-tuple-element.76), channel_id=1, source_target_pairs={{0,8},{4,12},{8,0},{12,4},{1,9},{5,13},{9,1},{13,5},{2,10},{6,14},... | collective-permute-start | bytes 589832 | tf_op jit(solution)/shard_map/ppermute | solution.py:439
  12.2 1.7 %collective-permute-start.7 = (bf16[48,2048]{1,0:T(8,128)(2,1)S(1)}, bf16[48,2048]{1,0:T(8,128)(2,1)S(1)}, u32[]{:S(2)}, u32[]{:S(2)}) collective-permute-start(bf16[48,2048]{1,0:T(8,128)(2,1)S(1)} %get-tuple-element.77), channel_id=1, source_target_pairs={{0,12},{4,8},{8,4},{12,0},{1,13},{5,9},{9,5},{13,1},{2,14},{6,10},... | collective-permute-start | bytes 589832 | tf_op jit(solution)/shard_map/ppermute | solution.py:439
  13.9 3.7 %collective-permute-done.2.refs_4_ = bf16[48,2048]{1,0:T(8,128)(2,1)S(1)} collective-permute-done((bf16[48,2048]{1,0:T(8,128)(2,1)S(1)}, bf16[48,2048]{1,0:T(8,128)(2,1)S(1)}, u32[]{:S(2)}, u32[]{:S(2)}) %collective-permute-start.2) | collective-permute-done | bytes 196640 | tf_op jit(solution)/shard_map/ppermute | solution.py:439
  17.7 3.8 %act_grads_and_probs.1 = (f32[192,384]{1,0:T(8,128)S(1)}, f32[8,256,256]{2,1,0:T(8,128)S(1)}, bf16[768,2048]{1,0:T(8,128)(2,1)S(1)}, bf16[2048,768]{1,0:T(8,128)...) custom-call(s32[2,128]{1,0:T(2,128)S(1)} %get-tuple-element.57.pos_ref, ...), custom_call_target="tpu_custom_call" | custom-call | flops 738197504 | bytes 16730112 | tf_op jit(solution)/shard_map/act_grads_and_probs/pallas_call | solution.py:420
  21.5 3.6 %collective-permute-done.6.refs_2_ = bf16[48,2048]{1,0:T(8,128)(2,1)S(1)} collective-permute-done((bf16[48,2048]{1,0:T(8,128)(2,1)S(1)}, bf16[48,2048]{1,0:T(8,128)(2,1)S(1)}, u32[]{:S(2)}, u32[]{:S(2)}) %collective-permute-start.6) | collective-permute-done | bytes 196640 | tf_op jit(solution)/shard_map/ppermute | solution.py:439
  25.1 2.8 %experts.1 = (bf16[48,2048]{1,0:T(8,128)(2,1)S(1)}, bf16[48,2048]{1,0:T(8,128)(2,1)S(1)}, bf16[96,2048]{1,0:T(8,128)(2,1)S(1)}, bf16[96,2048]{1,0:T(8,128)(2,1)S...) custom-call(bf16[2048,768]{1,0:T(8,128)(2,1)S(1)} %get-tuple-element.68.gate_ref, ...), custom_call_target="tpu_custom_call" | custom-call | flops 1811939328 | bytes 8945664 | tf_op jit(solution)/shard_map/experts/pallas_call | solution.py:420
  27.9 0.4 collective-permute-start.11
  28.3 1.7 %collective-permute-start.12 = (bf16[96,2048]{1,0:T(8,128)(2,1)S(1)}, bf16[96,2048]{1,0:T(8,128)(2,1)S(1)}, u32[]{:S(2)}, u32[]{:S(2)}) collective-permute-start(bf16[96,2048]{1,0:T(8,128)(2,1)S(1)} %get-tuple-element.81.refs_6_), channel_id=1, source_target_pairs={{0,8},{4,12},{8,0},{12,4},{1,9},{5,13},{9,1},{13,5},{2,10},{6,14},... | collective-permute-start | bytes 1179656 | tf_op jit(solution)/shard_map/ppermute | solution.py:439
  30.1 1.4 %collective-permute-start.13 = (bf16[48,2048]{1,0:T(8,128)(2,1)S(1)}, bf16[48,2048]{1,0:T(8,128)(2,1)S(1)}, u32[]{:S(2)}, u32[]{:S(2)}) collective-permute-start(bf16[48,2048]{1,0:T(8,128)(2,1)S(1)} %get-tuple-element.82.refs_7_), channel_id=1, source_target_pairs={{0,12},{4,8},{8,4},{12,0},{1,13},{5,9},{9,5},{13,1},{2,14},{6,10},... | collective-permute-start | bytes 589832 | tf_op jit(solution)/shard_map/ppermute | solution.py:439
  31.5 0.3 gain_terms.1
  31.8 1.6 %collective-permute-start.8 = (f32[16,128]{1,0:T(8,128)S(1)}, f32[16,128]{1,0:T(8,128)S(1)}, u32[]{:S(2)}, u32[]{:S(2)}) collective-permute-start(f32[16,128]{1,0:T(8,128)S(1)} %gain_terms.1), channel_id=1, source_target_pairs={{0,1},{1,0},{2,3},{3,2},{4,5},{5,4},{6,7},{7,6},{8,9},{9,8},{10,11... | collective-permute-start | bytes 24584 | tf_op jit(solution)/shard_map/ppermute | solution.py:439
  33.4 2.1 %collective-permute-done.8 = f32[16,128]{1,0:T(8,128)S(1)} collective-permute-done((f32[16,128]{1,0:T(8,128)S(1)}, f32[16,128]{1,0:T(8,128)S(1)}, u32[]{:S(2)}, u32[]{:S(2)}) %collective-permute-start.8) | collective-permute-done | bytes 8224 | tf_op jit(solution)/shard_map/ppermute | solution.py:439
  35.5 2.7 %collective-permute-start.9 = (f32[16,128]{1,0:T(8,128)S(1)}, f32[16,128]{1,0:T(8,128)S(1)}, u32[]{:S(2)}, u32[]{:S(2)}) collective-permute-start(f32[16,128]{1,0:T(8,128)S(1)} %add.17), channel_id=1, source_target_pairs={{0,2},{1,3},{2,0},{3,1},{4,6},{5,7},{6,4},{7,5},{8,10},{9,11},{10,... | collective-permute-start | bytes 24584 | tf_op jit(solution)/shard_map/ppermute | solution.py:439
  38.2 1.9 %collective-permute-done.9 = f32[16,128]{1,0:T(8,128)S(1)} collective-permute-done((f32[16,128]{1,0:T(8,128)S(1)}, f32[16,128]{1,0:T(8,128)S(1)}, u32[]{:S(2)}, u32[]{:S(2)}) %collective-permute-start.9) | collective-permute-done | bytes 8224 | tf_op jit(solution)/shard_map/ppermute | solution.py:439
  40.1 1.2 %collective-permute-done.10 = f32[16,128]{1,0:T(8,128)S(1)} collective-permute-done((f32[16,128]{1,0:T(8,128)S(1)}, f32[16,128]{1,0:T(8,128)S(1)}, u32[]{:S(2)}, u32[]{:S(2)}) %collective-permute-start.10) | collective-permute-done | bytes 8224 | tf_op jit(solution)/shard_map/ppermute | solution.py:439
  41.2 0.3 collective-permute-start.14
  41.6 2.7 %collective-permute-start.16 = (bf16[48,2048]{1,0:T(8,128)(2,1)S(1)}, bf16[48,2048]{1,0:T(8,128)(2,1)S(1)}, u32[]{:S(2)}, u32[]{:S(2)}) collective-permute-start(bf16[48,2048]{1,0:T(8,128)(2,1)S(1)} %get-tuple-element.95), channel_id=1, source_target_pairs={{0,12},{4,8},{8,4},{12,0},{1,13},{5,9},{9,5},{13,1},{2,14},{6,10},... | collective-permute-start | bytes 589832 | tf_op jit(solution)/shard_map/ppermute | solution.py:439
  44.2 2.1 %residual_and_first_group.1 = (bf16[128,2048]{1,0:T(8,128)(2,1)}, bf16[128,1024]{1,0:T(8,128)(2,1)S(1)}, bf16[128,1024]{1,0:T(8,128)(2,1)S(1)}, f32[128,256]{1,0:T(8,128)S(1)}, bf16[128,256]{1,0:T(8,128)(2,1)S(1)}) custom-call(bf16[128,192]{1,0:T(8,128)(2,1)S(1)} %get-tuple-element.66.place_ref, f32[1,2048]{1,0:T(1,128)S(1)} %get-tuple-element.71.gain_ref, ...), custom_call_target="tpu_custom_call" | custom-call | flops 4000000000 | bytes 6414336 | tf_op jit(solution)/shard_map/residual_and_first_group/pallas_call | solution.py:420
  46.4 0.6 %collective-permute-start.15 = (f32[32,128]{1,0:T(8,128)S(1)}, f32[32,128]{1,0:T(8,128)S(1)}, u32[]{:S(2)}, u32[]{:S(2)}) collective-permute-start(f32[32,128]{1,0:T(8,128)S(1)} %pad.4), channel_id=1, source_target_pairs={{0,8},{4,12},{8,0},{12,4},{1,9},{5,13},{9,1},{13,5},{2,10},{6,14},... | collective-permute-start | bytes 49160 | tf_op jit(solution)/shard_map/ppermute | solution.py:439
  46.9 1.5 %second_group.1 = (bf16[128,1024]{1,0:T(8,128)(2,1)S(1)}, f32[128,256]{1,0:T(8,128)S(1)}, bf16[128,512]{1,0:T(8,128)(2,1)S(1)}) custom-call(bf16[128,2048]{1,0:T(8,128)(2,1)S(1)} %get-tuple-element.60.query_ref, f32[8,256,256]{2,1,0:T(8,128)S(1)} %get-tuple-element.86.probs_ref, bf16[128,1024]{1,0:T(8,128)(2,1)S(1)} %get-tuple-element.90.rest_ref, ...), custom_call_target="tpu_custom_call" | custom-call | tf_op jit(solution)/shard_map/second_group/pallas_call | solution.py:420
  48.5 1.0 %collective-permute-done.16.refs_8_ = bf16[48,2048]{1,0:T(8,128)(2,1)S(1)} collective-permute-done((bf16[48,2048]{1,0:T(8,128)(2,1)S(1)}, bf16[48,2048]{1,0:T(8,128)(2,1)S(1)}, u32[]{:S(2)}, u32[]{:S(2)}) %collective-permute-start.16) | collective-permute-done | bytes 196640 | tf_op jit(solution)/shard_map/ppermute | solution.py:439
  49.4 0.7 %collective-permute-done.15 = f32[32,128]{1,0:T(8,128)S(1)} collective-permute-done((f32[32,128]{1,0:T(8,128)S(1)}, f32[32,128]{1,0:T(8,128)S(1)}, u32[]{:S(2)}, u32[]{:S(2)}) %collective-permute-start.15) | collective-permute-done | bytes 16416 | tf_op jit(solution)/shard_map/ppermute | solution.py:439
  50.2 0.6 %collective-permute-done.17.refs_4_ = bf16[128,512]{1,0:T(8,128)(2,1)S(1)} collective-permute-done((bf16[128,512]{1,0:T(8,128)(2,1)S(1)}, bf16[128,512]{1,0:T(8,128)(2,1)S(1)}, u32[]{:S(2)}, u32[]{:S(2)}) %collective-permute-start.17) | collective-permute-done | bytes 131104 | tf_op jit(solution)/shard_map/ppermute | solution.py:439
  50.8 1.2 %layer_output.1 = (bf16[128,2048]{1,0:T(8,128)(2,1)}, bf16[128,2048]{1,0:T(8,128)(2,1)}, bf16[128,256]{1,0:T(8,128)(2,1)}, bf16[128,256]{1,0:T(8,128)(2,1)}, f32[1,128]{1,0:T(1,128)}, /*index=5*/f32[16,128]{1,0:T(8,128)}) custom-call(bf16[128,192]{1,0:T(8,128)(2,1)S(1)} %get-tuple-element.66.place_ref, f32[128,512]{1,0:T(8,128)S(1)} %get-tuple-element.67.weight_ref, ...), custom_call_target="tpu_custom_call" | custom-call | flops 100663296 | bytes 4653568 | tf_op jit(solution)/shard_map/layer_output/pallas_call | solution.py:420
  (18 shorter events, 0.1 us)
Async XLA Ops:
  2.2 10.0 %collective-permute-start.1 = (bf16[48,2048]{1,0:T(8,128)(2,1)S(1)}, bf16[48,2048]{1,0:T(8,128)(2,1)S(1)}, u32[]{:S(2)}, u32[]{:S(2)}) collective-permute-start(bf16[48,2048]{1,0:T(8,128)(2,1)S(1)} %get-tuple-element.63), channel_id=1, source_target_pairs={{0,4},{4,0},{8,12},{12,8},{1,5},{5,1},{9,13},{13,9},{2,6},{6,2},{1... | collective-permute-start | bytes 589832 | tf_op jit(solution)/shard_map/ppermute | solution.py:439
  5.2 2.1 %collective-permute-start = (bf16[128,256]{1,0:T(8,128)(2,1)}, bf16[128,256]{1,0:T(8,128)(2,1)S(1)}, u32[]{:S(2)}, u32[]{:S(2)}) collective-permute-start(bf16[128,256]{1,0:T(8,128)(2,1)} %bitcast.17), channel_id=1, source_target_pairs={{0,16},{16,0},{1,17},{17,1},{2,18},{18,2},{3,19},{19,3},{4,20},{20... | collective-permute-start | bytes 196616 | tf_op jit(solution)/shard_map/ppermute | solution.py:439
  5.2 2.1 %collective-permute-start.4 = (bf16[128,256]{1,0:T(8,128)(2,1)}, bf16[128,256]{1,0:T(8,128)(2,1)S(1)}, u32[]{:S(2)}, u32[]{:S(2)}) collective-permute-start(bf16[128,256]{1,0:T(8,128)(2,1)} %bitcast.19), channel_id=1, source_target_pairs={{0,16},{16,0},{1,17},{17,1},{2,18},{18,2},{3,19},{19,3},{4,20},{20... | collective-permute-start | bytes 196616 | tf_op jit(solution)/shard_map/ppermute | solution.py:439
  5.7 12.0 %collective-permute-start.2 = (bf16[48,2048]{1,0:T(8,128)(2,1)S(1)}, bf16[48,2048]{1,0:T(8,128)(2,1)S(1)}, u32[]{:S(2)}, u32[]{:S(2)}) collective-permute-start(bf16[48,2048]{1,0:T(8,128)(2,1)S(1)} %get-tuple-element.64), channel_id=1, source_target_pairs={{0,8},{4,12},{8,0},{12,4},{1,9},{5,13},{9,1},{13,5},{2,10},{6,14},... | collective-permute-start | bytes 589832 | tf_op jit(solution)/shard_map/ppermute | solution.py:439
  7.2 10.5 %collective-permute-start.3 = (bf16[48,2048]{1,0:T(8,128)(2,1)S(1)}, bf16[48,2048]{1,0:T(8,128)(2,1)S(1)}, u32[]{:S(2)}, u32[]{:S(2)}) collective-permute-start(bf16[48,2048]{1,0:T(8,128)(2,1)S(1)} %get-tuple-element.65), channel_id=1, source_target_pairs={{0,12},{4,8},{8,4},{12,0},{1,13},{5,9},{9,5},{13,1},{2,14},{6,10},... | collective-permute-start | bytes 589832 | tf_op jit(solution)/shard_map/ppermute | solution.py:439
  8.7 12.8 %collective-permute-start.5 = (bf16[48,2048]{1,0:T(8,128)(2,1)S(1)}, bf16[48,2048]{1,0:T(8,128)(2,1)S(1)}, u32[]{:S(2)}, u32[]{:S(2)}) collective-permute-start(bf16[48,2048]{1,0:T(8,128)(2,1)S(1)} %get-tuple-element.75), channel_id=1, source_target_pairs={{0,4},{4,0},{8,12},{12,8},{1,5},{5,1},{9,13},{13,9},{2,6},{6,2},{1... | collective-permute-start | bytes 589832 | tf_op jit(solution)/shard_map/ppermute | solution.py:439
  10.7 14.5 %collective-permute-start.6 = (bf16[48,2048]{1,0:T(8,128)(2,1)S(1)}, bf16[48,2048]{1,0:T(8,128)(2,1)S(1)}, u32[]{:S(2)}, u32[]{:S(2)}) collective-permute-start(bf16[48,2048]{1,0:T(8,128)(2,1)S(1)} %get-tuple-element.76), channel_id=1, source_target_pairs={{0,8},{4,12},{8,0},{12,4},{1,9},{5,13},{9,1},{13,5},{2,10},{6,14},... | collective-permute-start | bytes 589832 | tf_op jit(solution)/shard_map/ppermute | solution.py:439
  12.2 12.9 %collective-permute-start.7 = (bf16[48,2048]{1,0:T(8,128)(2,1)S(1)}, bf16[48,2048]{1,0:T(8,128)(2,1)S(1)}, u32[]{:S(2)}, u32[]{:S(2)}) collective-permute-start(bf16[48,2048]{1,0:T(8,128)(2,1)S(1)} %get-tuple-element.77), channel_id=1, source_target_pairs={{0,12},{4,8},{8,4},{12,0},{1,13},{5,9},{9,5},{13,1},{2,14},{6,10},... | collective-permute-start | bytes 589832 | tf_op jit(solution)/shard_map/ppermute | solution.py:439
  27.9 16.3 %collective-permute-start.11 = (bf16[96,2048]{1,0:T(8,128)(2,1)S(1)}, bf16[96,2048]{1,0:T(8,128)(2,1)S(1)}, u32[]{:S(2)}, u32[]{:S(2)}) collective-permute-start(bf16[96,2048]{1,0:T(8,128)(2,1)S(1)} %get-tuple-element.80.refs_5_), channel_id=1, source_target_pairs={{0,4},{4,0},{8,12},{12,8},{1,5},{5,1},{9,13},{13,9},{2,6},{6,2},{1... | collective-permute-start | bytes 1179656 | tf_op jit(solution)/shard_map/ppermute | solution.py:439
  28.3 15.9 %collective-permute-start.12 = (bf16[96,2048]{1,0:T(8,128)(2,1)S(1)}, bf16[96,2048]{1,0:T(8,128)(2,1)S(1)}, u32[]{:S(2)}, u32[]{:S(2)}) collective-permute-start(bf16[96,2048]{1,0:T(8,128)(2,1)S(1)} %get-tuple-element.81.refs_6_), channel_id=1, source_target_pairs={{0,8},{4,12},{8,0},{12,4},{1,9},{5,13},{9,1},{13,5},{2,10},{6,14},... | collective-permute-start | bytes 1179656 | tf_op jit(solution)/shard_map/ppermute | solution.py:439
  30.1 14.2 %collective-permute-start.13 = (bf16[48,2048]{1,0:T(8,128)(2,1)S(1)}, bf16[48,2048]{1,0:T(8,128)(2,1)S(1)}, u32[]{:S(2)}, u32[]{:S(2)}) collective-permute-start(bf16[48,2048]{1,0:T(8,128)(2,1)S(1)} %get-tuple-element.82.refs_7_), channel_id=1, source_target_pairs={{0,12},{4,8},{8,4},{12,0},{1,13},{5,9},{9,5},{13,1},{2,14},{6,10},... | collective-permute-start | bytes 589832 | tf_op jit(solution)/shard_map/ppermute | solution.py:439
  31.8 3.7 %collective-permute-start.8 = (f32[16,128]{1,0:T(8,128)S(1)}, f32[16,128]{1,0:T(8,128)S(1)}, u32[]{:S(2)}, u32[]{:S(2)}) collective-permute-start(f32[16,128]{1,0:T(8,128)S(1)} %gain_terms.1), channel_id=1, source_target_pairs={{0,1},{1,0},{2,3},{3,2},{4,5},{5,4},{6,7},{7,6},{8,9},{9,8},{10,11... | collective-permute-start | bytes 24584 | tf_op jit(solution)/shard_map/ppermute | solution.py:439
  35.5 4.5 %collective-permute-start.9 = (f32[16,128]{1,0:T(8,128)S(1)}, f32[16,128]{1,0:T(8,128)S(1)}, u32[]{:S(2)}, u32[]{:S(2)}) collective-permute-start(f32[16,128]{1,0:T(8,128)S(1)} %add.17), channel_id=1, source_target_pairs={{0,2},{1,3},{2,0},{3,1},{4,6},{5,7},{6,4},{7,5},{8,10},{9,11},{10,... | collective-permute-start | bytes 24584 | tf_op jit(solution)/shard_map/ppermute | solution.py:439
  40.1 1.2 %collective-permute-start.10 = (f32[16,128]{1,0:T(8,128)S(1)}, f32[16,128]{1,0:T(8,128)S(1)}, u32[]{:S(2)}, u32[]{:S(2)}) collective-permute-start(f32[16,128]{1,0:T(8,128)S(1)} %add.18), channel_id=1, source_target_pairs={{0,16},{16,0},{1,17},{17,1},{2,18},{18,2},{3,19},{19,3},{4,20},{20... | collective-permute-start | bytes 24584 | tf_op jit(solution)/shard_map/ppermute | solution.py:439
  41.2 5.1 %collective-permute-start.14 = (f32[16,128]{1,0:T(8,128)S(1)}, f32[16,128]{1,0:T(8,128)S(1)}, u32[]{:S(2)}, u32[]{:S(2)}) collective-permute-start(f32[16,128]{1,0:T(8,128)S(1)} %add.19), channel_id=1, source_target_pairs={{0,4},{4,0},{8,12},{12,8},{1,5},{5,1},{9,13},{13,9},{2,6},{6,2},{1... | collective-permute-start | bytes 24584 | tf_op jit(solution)/shard_map/ppermute | solution.py:439
  41.6 7.9 %collective-permute-start.16 = (bf16[48,2048]{1,0:T(8,128)(2,1)S(1)}, bf16[48,2048]{1,0:T(8,128)(2,1)S(1)}, u32[]{:S(2)}, u32[]{:S(2)}) collective-permute-start(bf16[48,2048]{1,0:T(8,128)(2,1)S(1)} %get-tuple-element.95), channel_id=1, source_target_pairs={{0,12},{4,8},{8,4},{12,0},{1,13},{5,9},{9,5},{13,1},{2,14},{6,10},... | collective-permute-start | bytes 589832 | tf_op jit(solution)/shard_map/ppermute | solution.py:439
  46.4 3.8 %collective-permute-start.15 = (f32[32,128]{1,0:T(8,128)S(1)}, f32[32,128]{1,0:T(8,128)S(1)}, u32[]{:S(2)}, u32[]{:S(2)}) collective-permute-start(f32[32,128]{1,0:T(8,128)S(1)} %pad.4), channel_id=1, source_target_pairs={{0,8},{4,12},{8,0},{12,4},{1,9},{5,13},{9,1},{13,5},{2,10},{6,14},... | collective-permute-start | bytes 49160 | tf_op jit(solution)/shard_map/ppermute | solution.py:439
  49.4 1.3 %collective-permute-start.17 = (bf16[128,512]{1,0:T(8,128)(2,1)S(1)}, bf16[128,512]{1,0:T(8,128)(2,1)S(1)}, u32[]{:S(2)}, u32[]{:S(2)}) collective-permute-start(bf16[128,512]{1,0:T(8,128)(2,1)S(1)} %get-tuple-element.97), channel_id=1, source_target_pairs={{0,16},{16,0},{1,17},{17,1},{2,18},{18,2},{3,19},{19,3},{4,20},{20... | collective-permute-start | bytes 393224 | tf_op jit(solution)/shard_map/ppermute | solution.py:439
